TPU v7x, 32 devices: a whole 2x2x4 slice. The times are simulated.
32 devices in a mesh: groups: 2 (over x), wide: 16 (over z, y, core).
Axes of the slice: x: 2, y: 2, z: 4, core: 2. Of those that a mesh axis runs over, the one named last changes fastest.
Arguments:
- embeddings: bfloat16 [65536, 1024], P(('groups', 'wide')), parts along dimension 0
- basis: bfloat16 [1024, 256], replicated, may hold values from -0.1875 to 0.1875
- list_owner: int32 [65536], P(('groups', 'wide')), parts along dimension 0, may hold values from 0 to 15, as said below
- list_slot: int32 [65536], P(('groups', 'wide')), parts along dimension 0, may hold values from 0 to 1023
- centroids: bfloat16 [16384, 256], P('wide'), may hold values from -6 to 6
- rotation: bfloat16 [256, 256], replicated, may hold values from -0.375 to 0.375
Outputs:
- encoded: bfloat16 [65536, 256], P(('groups', 'wide')), parts along dimension 0
- covariance: float32 [2048, 1024], P(('groups', 'wide')), parts along dimension 0
There are 2 independent parts, one for each index of `groups`. A program takes and returns all parts, laid end to end along the dimension named above; an argument that names none is the same for every part. Nothing has to cross between parts.
Inputs may be any that keep to these rules, and one draw needn't show every extreme that they name: `list_owner`: among the rows of one device each owner is named at most 128 times; one owner, drawn from the seed, is named exactly 128 times by the rows of every device.
All inputs are finite; a program needn't handle non-finite values.
Results may differ from a plain program's by a relative error of at most 0.0055.
Values may be sent and summed in bfloat16 or wider, within the bound.
No kernel may reach another device: no remote copies, remote signals or barrier semaphores. Data moves between devices by JAX's collectives and lax.ppermute only.
A program may use at most 64 MiB of HBM per device.

v0:
```python
import jax
import jax.numpy as jnp
from jax import lax
from jax.sharding import PartitionSpec as P

CAP = 128


def local(embeddings, basis, list_owner, list_slot, centroids, rotation):
    width = lax.axis_size("wide")
    rows_here = embeddings.shape[0]
    feat = embeddings.shape[1]
    total = rows_here * width
    block = feat // width
    first = lax.axis_index("wide") * block
    basis_full = basis.astype(jnp.float32)
    local_sum = jnp.sum(embeddings, 0, dtype=jnp.float32)
    moment_part = lax.psum_scatter(
        lax.dot_general(
            embeddings, embeddings, (((0,), (0,)), ((), ())), preferred_element_type=jnp.float32
        ),
        "wide",
        scatter_dimension=0,
        tiled=True,
    )
    column_sum = lax.psum(local_sum, "wide")
    mean = column_sum / total
    mean_part = lax.dynamic_slice_in_dim(mean, first, block, 0)
    basis_part = lax.dynamic_slice_in_dim(basis_full, first, block, 0)
    cov_rows = moment_part / total - mean_part[:, None] * mean[None, :]
    terms = jnp.sum(basis_part * jnp.dot(cov_rows, basis_full, precision=lax.Precision.HIGHEST), 0)
    variance = lax.psum(terms, "wide")
    scale = lax.rsqrt(variance + 1e-05)
    shift = jnp.dot(mean, basis_full, precision=lax.Precision.HIGHEST)
    projected = (
        (jnp.dot(embeddings, basis, preferred_element_type=jnp.float32) - shift) * scale
    ).astype(jnp.bfloat16)
    proj_width = projected.shape[1]
    hits = (list_owner[:, None] == jnp.arange(width, dtype=jnp.int32)[None, :]).astype(jnp.int32)
    rank = jnp.sum(hits * (jnp.cumsum(hits, 0) - 1), 1)
    target = list_owner * CAP + rank
    outgoing = (
        jnp.zeros((width * CAP, proj_width), jnp.bfloat16)
        .at[target]
        .set(projected)
        .reshape(width, CAP, proj_width)
    )
    out_lists = (
        jnp.full((width * CAP,), -1, jnp.int32).at[target].set(list_slot).reshape(width, CAP)
    )
    owned = centroids.shape[0]
    got_rows = lax.all_to_all(outgoing, "wide", split_axis=0, concat_axis=0, tiled=True)
    got_lists = lax.all_to_all(out_lists, "wide", split_axis=0, concat_axis=0, tiled=True)
    flat_rows = got_rows.reshape(-1, proj_width)
    onehot = (got_lists.reshape(-1)[:, None] == jnp.arange(owned, dtype=jnp.int32)[None, :]).astype(
        jnp.bfloat16
    )
    centre = jnp.dot(onehot, centroids, preferred_element_type=jnp.float32)
    residual = (flat_rows.astype(jnp.float32) - centre).astype(jnp.bfloat16)
    rotated = jnp.dot(residual, rotation, preferred_element_type=jnp.float32).astype(jnp.bfloat16)
    received = rotated.reshape(got_rows.shape[0], got_rows.shape[1], proj_width)
    return (received.reshape(-1, proj_width), cov_rows)


def solution(mesh):
    in_specs = (
        P(("groups", "wide"), None),
        P(),
        P(("groups", "wide")),
        P(("groups", "wide")),
        P("wide", None),
        P(),
    )
    out_specs = (P(("groups", "wide"), None), P(("groups", "wide"), None))
    return jax.shard_map(local, mesh=mesh, in_specs=in_specs, out_specs=out_specs, check_vma=False)
```

profile of v0, /device:TPU:0, one launch (start us, length us, event | category | flops | bytes accessed | tf_op | source)
XLA Modules:
  0.0 176.0 jit_solution(14217361229257181824)
XLA Ops:
  7.2 0.0 copy-start
  7.2 0.0 reduce-scatter.2.cloned.1.call-start
  7.2 10.0 %fusion.15 = f32[1024,1024]{1,0:T(8,128)} fusion(bf16[2048,1024]{1,0:T(8,128)(2,1)} %param.6), kind=kOutput, calls=%fused_computation.31 | convolution fusion | flops 4294967296 | bytes 8388608 | tf_op jit(solution)/shard_map/dot_general | solution.py:19
  17.2 0.0 copy-start.3
  17.2 0.0 copy-start.1
  17.2 0.0 reduce-scatter.2.cloned.1.call-update
  17.2 0.7 copy-done.3
  17.9 4.5 %reduce-window.6 = s32[16,16,128]{2,1,0:T(8,128)S(1)} reduce-window(s32[16,16,128]{2,1,0:T(8,128)S(1)} %fusion.11, s32[]{:T(128)} %constant.13.clone.1), window={size=1x1x128 pad=0_0x0_0x127_0}, to_apply=%region_0.0 | reduce-window | flops 4161536 | bytes 262148 | tf_op jit(solution)/shard_map/reduce-window
  22.5 0.4 slice_reduce_fusion
  22.9 0.2 reduce-window.9
  23.1 0.1 add_add_fusion
  23.2 0.1 fusion.10
  23.3 8.8 %scatter_custom_fusion.1 = s32[2048]{0:T(1024)} fusion(s32[2048]{0:T(1024)S(1)} %compare_select_fusion, s32[2048]{0:T(1024)} %param.9, s32[]{:T(128)} %constant.14.clone.1), kind=kCustom, calls=%fused_computation.26 | custom fusion | bytes 8704 | tf_op jit(solution)/shard_map/scatter | solution.py:49
  32.1 7.4 %all-to-all-start.1 = ((s32[16,1,128]{2,1,0:T(1,128)}), s32[16,1,128]{2,1,0:T(1,128)S(1)}, u32[]{:S(2)}, u32[]{:S(2)}) async-start(s32[16,1,128]{2,1,0:T(1,128)} %bitcast.6), calls=%async_computation.2 | async-start | bytes 16384 | tf_op jit(solution)/shard_map/all_to_all | solution.py:53
  39.5 3.0 %convert_reduce_fusion = f32[1024]{0:T(1024)S(1)} fusion(bf16[2048,1024]{1,0:T(8,128)(2,1)} %param.6), kind=kLoop, calls=%fused_computation.3 | loop fusion | flops 4193280 | bytes 4198400 | tf_op jit(solution)/shard_map/reduce_sum | solution.py:17
  42.4 34.4 %psum.14 = f32[1024]{0:T(1024)S(1)} all-reduce(f32[1024]{0:T(1024)S(1)} %convert_reduce_fusion), channel_id=1, replica_groups=mesh['groups'=2,'wide'=16] {'wide'}, use_global_device_ids=true, to_apply=%region_4.0 | all-reduce | flops 1024 | bytes 8192 | tf_op jit(solution)/shard_map/psum | solution.py:26
  76.8 0.1 dynamic_slice.7
  76.9 0.0 copy-done.1
  76.9 0.3 fusion.14
  77.2 16.1 %reduce-scatter.2.cloned.1.call-done = f32[64,1024]{1,0:T(8,128)} async-done(((f32[1024,1024]{1,0:T(8,128)}), f32[64,1024]{1,0:T(8,128)}) %reduce-scatter.2.cloned.1.call-update) | async-done | bytes 262160 | tf_op jit(solution)/shard_map/reduce_scatter | solution.py:18
  93.3 1.0 multiply_subtract_fusion
  94.3 0.0 copy-start.2
  94.3 0.4 fusion.6
  94.7 30.1 %psum.15 = f32[256]{0:T(256)S(1)} all-reduce(f32[256]{0:T(256)S(1)} %fusion.6), channel_id=1, replica_groups=mesh['groups'=2,'wide'=16] {'wide'}, use_global_device_ids=true, to_apply=%region_7.8 | all-reduce | flops 256 | bytes 2048 | tf_op jit(solution)/shard_map/psum | solution.py:32
  124.8 3.4 %fusion.5 = bf16[2048,256]{1,0:T(8,128)(2,1)S(1)} fusion(bf16[2048,1024]{1,0:T(8,128)(2,1)} %param.6, bf16[1024,256]{1,0:T(8,128)(2,1)S(1)} %copy-done.1, f32[256]{0:T(256)S(1)} %add_rsqrt_fusion, f32[256]{0:T(256)S(1)} %bitcast.39), kind=kOutput, calls=%fused_computation.10 | convolution fusion | flops 1075314688 | bytes 5769216 | tf_op jit(solution)/shard_map/dot_general | solution.py:36
  128.3 0.0 copy-done.2
  128.3 9.6 %scatter_custom_fusion = bf16[2048,256]{1,0:T(8,128)(2,1)S(1)} fusion(s32[2048]{0:T(1024)S(1)} %compare_select_fusion, bf16[2048,256]{1,0:T(8,128)(2,1)S(1)} %fusion.5, bf16[]{:T(256)} %constant.11.clone.1), kind=kCustom, calls=%fused_computation.14 | custom fusion | bytes 1048578 | tf_op jit(solution)/shard_map/scatter | solution.py:45
  137.8 0.0 all-to-all-done.1
  137.9 27.4 %all_to_all.14 = bf16[16,128,256]{2,1,0:T(8,128)(2,1)S(1)} all-to-all(bf16[16,128,256]{2,1,0:T(8,128)(2,1)S(1)} %bitcast.32), channel_id=1, replica_groups=mesh['groups'=2,'wide'=16] {'wide'}, dimensions={0} | all-to-all | bytes 2097152 | tf_op jit(solution)/shard_map/all_to_all | solution.py:52
  165.3 0.0 copy-done
  165.3 3.8 %convolution_convert_fusion = bf16[2048,256]{1,0:T(8,128)(2,1)} fusion(bf16[256,256]{1,0:T(8,128)(2,1)} %param.11, bf16[1024,256]{1,0:T(8,128)(2,1)S(1)} %copy-done, s32[2048]{0:T(1024)S(1)} %bitcast.38, bf16[2048,256]{1,0:T(8,128)(2,1)S(1)} %bitcast.33), kind=kOutput, calls=%fused_computation.11 | convolution fusion | flops 1346371584 | bytes 2760704 | tf_op jit(solution)/shard_map/dot_general | solution.py:60
  (4 shorter events, 0.0 us)
Async XLA Ops:
  7.2 158.1 %copy-start = (bf16[1024,256]{1,0:T(8,128)(2,1)S(1)}, bf16[1024,256]{1,0:T(8,128)(2,1)}, u32[]{:S(2)}) copy-start(bf16[1024,256]{1,0:T(8,128)(2,1)} %param.10) | copy-start | bytes 1572868
  7.2 86.1 %reduce-scatter.2.cloned.1.call-start = ((), (), s32[]{:S(2)}) async-start(), calls=%async_computation.3 | async-start | bytes 4456448 | tf_op jit(solution)/shard_map/reduce_scatter | solution.py:18
  17.2 0.7 copy-start.3
  17.2 59.7 %copy-start.1 = (bf16[1024,256]{1,0:T(8,128)(2,1)S(1)}, bf16[1024,256]{1,0:T(8,128)(2,1)}, u32[]{:S(2)}) copy-start(bf16[1024,256]{1,0:T(8,128)(2,1)} %param.7) | copy-start | bytes 1572868
  32.1 105.8 %all-to-all-start.1 = ((s32[16,1,128]{2,1,0:T(1,128)}), s32[16,1,128]{2,1,0:T(1,128)S(1)}, u32[]{:S(2)}, u32[]{:S(2)}) async-start(s32[16,1,128]{2,1,0:T(1,128)} %bitcast.6), calls=%async_computation.2 | async-start | bytes 16384 | tf_op jit(solution)/shard_map/all_to_all | solution.py:53
  94.3 33.9 %copy-start.2 = (f32[64,1024]{1,0:T(8,128)}, f32[64,1024]{1,0:T(8,128)S(1)}, u32[]{:S(2)}) copy-start(f32[64,1024]{1,0:T(8,128)S(1)} %multiply_subtract_fusion) | copy-start | bytes 786436
Sparse Core Ops, SparseCore 0:
  17.4 75.8 reduce-scatter.1
where the time goes:
time: 177 us; the launch traced here: 176 us
  blocking collectives  91.9 us (52%)
  local copies, waits for them, and re-layouts  19.5 us (11%)
  matrix products  18 us (10%)
  waiting for transfers between devices  16.1 us (9%)
  between operations  14.1 us (8%)
  other arithmetic  8.91 us (5%)
  starting transfers between devices  7.42 us (4%)
    psum x1, blocking collectives, local(): column_sum = lax.psum(local_sum, 'wide')  34.4 us
    psum x1, blocking collectives, local(): variance = lax.psum(terms, 'wide')  30.1 us
    all_to_all x1, blocking collectives, local(): lax.all_to_all(outgoing, 'wide', split_axis=0, concat_axis=0, tiled=True)  27.4 us
    reduce_scatter x1, waiting for transfers between devices, local(): lax.psum_scatter(lax.dot_general(embeddings, embeddings, (((0,), (0,)), (...  16.1 us
    dot_general x1, matrix products, local(): lax.dot_general(embeddings, embeddings, (((0,), (0,)), ((), ())), preferr...  9.99 us
    scatter x1, local copies, waits for them, and re-layouts, local(): outgoing = jnp.zeros((width * CAP, proj_width), jnp.bfloat16).at[target]....  9.57 us
    scatter x1, local copies, waits for them, and re-layouts, local(): jnp.full((width * CAP,), -1, jnp.int32).at[target].set(list_slot)  8.78 us
    all_to_all x1, starting transfers between devices, local(): lax.all_to_all(out_lists, 'wide', split_axis=0, concat_axis=0, tiled=True)  7.38 us
  transfers between devices with their start and end apart: 2, of which 1 were waited for; matrix products, arithmetic and copies ran while one was open for 18% of the time, Pallas kernels for 0%

commit v1 on v0

v1 whole, which is shorter than its diff:
```python
import functools

import jax
import jax.numpy as jnp
from jax import lax
from jax.experimental import pallas as pl
from jax.experimental.pallas import tpu as pltpu
from jax.sharding import PartitionSpec as P

CAP = 128
LANES = 128
CHUNK = 256
GROUP = 512
VMEM_LIMIT = 50 * 1024 * 1024


def rows_kernel(width, e_ref, basis_ref, owner_ref, slot_ref, rows_ref, lists_ref, stat_ref, y_ref, yb_ref, sum_ref):
    step = pl.program_id(0)
    rows_here, feats = y_ref.shape
    y = jnp.dot(e_ref[...], basis_ref[...], preferred_element_type=jnp.float32)
    y_ref[pl.ds(pl.multiple_of(step * CHUNK, CHUNK), CHUNK), :] = y
    part = jnp.sum(y.reshape(CHUNK // 8, 8, feats), 0)

    @pl.when(step == 0)
    def _():
        sum_ref[...] = part

    @pl.when(step > 0)
    def _():
        sum_ref[...] += part

    @pl.when(step == pl.num_programs(0) - 1)
    def _():
        mean = jnp.sum(sum_ref[...], 0, keepdims=True) / rows_here
        square = jnp.zeros((8, feats), jnp.float32)
        for c in range(rows_here // CHUNK):
            centred = y_ref[c * CHUNK:(c + 1) * CHUNK, :] - mean
            square = square + jnp.sum((centred * centred).reshape(CHUNK // 8, 8, feats), 0)
            yb_ref[c * CHUNK:(c + 1) * CHUNK, :] = centred.astype(jnp.bfloat16)
        stat_ref[0:1, :] = mean
        stat_ref[1:2, :] = jnp.sum(square, 0, keepdims=True)

        chunks = rows_here // LANES
        owner = owner_ref[...]
        wanted = lax.broadcasted_iota(jnp.int32, (width, LANES), 0)
        hits = [owner[c:c + 1, :] == wanted for c in range(chunks)]
        hits_f = [jnp.where(h, 1.0, 0.0) for h in hits]
        flat = jnp.concatenate(hits_f, 0).astype(jnp.bfloat16)
        up = lax.broadcasted_iota(jnp.int32, (LANES, LANES), 0)
        to = lax.broadcasted_iota(jnp.int32, (LANES, LANES), 1)
        before = jnp.where(up < to, 1.0, 0.0).astype(jnp.bfloat16)
        every = jnp.ones((LANES, LANES), jnp.bfloat16)
        within = jnp.dot(flat, before, preferred_element_type=jnp.float32)
        totals = jnp.dot(flat, every, preferred_element_type=jnp.float32)
        carry = jnp.zeros((width, LANES), jnp.float32)
        ranks = []
        for c in range(chunks):
            at = slice(c * width, (c + 1) * width)
            ranks.append(jnp.sum(hits_f[c] * (within[at] + carry), 0, keepdims=True).astype(jnp.int32))
            carry = carry + totals[at]

        slot = slot_ref[...] + 1
        high, low = (slot >> 5).astype(jnp.float32), (slot & 31).astype(jnp.float32)
        spots = lax.broadcasted_iota(jnp.int32, (CAP, LANES), 0)
        placed = jnp.concatenate([jnp.where(ranks[c] == spots, 1.0, 0.0) for c in range(chunks)], 1).astype(jnp.bfloat16)
        digits = jnp.concatenate(
            [
                jnp.concatenate([hits_f[c] * high[c:c + 1, :] for c in range(chunks)], 1),
                jnp.concatenate([hits_f[c] * low[c:c + 1, :] for c in range(chunks)], 1),
            ],
            0,
        ).astype(jnp.bfloat16)
        found = lax.dot_general(digits, placed, (((1,), (1,)), ((), ())), preferred_element_type=jnp.float32)
        lists_ref[...] = found[:width] * 32.0 + found[width:] - 1.0

        targets = [owner[c:c + 1, :] * CAP + ranks[c] for c in range(chunks)]
        place = lax.broadcasted_iota(jnp.int32, (GROUP, LANES), 0)

        def sort_group(g, _):
            first = pl.multiple_of(g * GROUP, GROUP)
            pick = jnp.concatenate(
                [jnp.where(targets[c] - first == place, 1.0, 0.0).astype(jnp.bfloat16) for c in range(chunks)], 1
            )
            rows_ref[pl.ds(first, GROUP), :] = jnp.dot(
                pick, yb_ref[...], preferred_element_type=jnp.float32
            ).astype(jnp.bfloat16)
            return 0

        lax.fori_loop(0, width * CAP // GROUP, sort_group, 0)


def project_and_sort(width, embeddings, basis, list_owner, list_slot):
    rows_here, wide = embeddings.shape
    feats = basis.shape[1]
    lanes = rows_here // LANES
    slots = width * CAP
    return pl.pallas_call(
        functools.partial(rows_kernel, width),
        grid=(rows_here // CHUNK,),
        in_specs=[
            pl.BlockSpec((CHUNK, wide), lambda i: (i, 0)),
            pl.BlockSpec((wide, feats), lambda i: (0, 0)),
            pl.BlockSpec((lanes, LANES), lambda i: (0, 0)),
            pl.BlockSpec((lanes, LANES), lambda i: (0, 0)),
        ],
        out_specs=[
            pl.BlockSpec((slots, feats), lambda i: (0, 0)),
            pl.BlockSpec((width, CAP), lambda i: (0, 0)),
            pl.BlockSpec((2, feats), lambda i: (0, 0)),
        ],
        out_shape=[
            jax.ShapeDtypeStruct((slots, feats), jnp.bfloat16),
            jax.ShapeDtypeStruct((width, CAP), jnp.float32),
            jax.ShapeDtypeStruct((2, feats), jnp.float32),
        ],
        scratch_shapes=[
            pltpu.VMEM((rows_here, feats), jnp.float32),
            pltpu.VMEM((rows_here, feats), jnp.bfloat16),
            pltpu.VMEM((8, feats), jnp.float32),
        ],
        compiler_params=pltpu.CompilerParams(vmem_limit_bytes=VMEM_LIMIT),
        cost_estimate=pl.CostEstimate(
            flops=2 * rows_here * feats * (wide + slots), bytes_accessed=2 * rows_here * wide + 2 * slots * feats, transcendentals=0
        ),
        name="project_sort",
    )(embeddings, basis, list_owner.reshape(lanes, LANES), list_slot.reshape(lanes, LANES))


def moments_kernel(width, me_ref, e_ref, keep_ref, send_ref, mean_ref, m_ref):
    rows_here, wide = e_ref.shape
    block = wide // width
    bits = width.bit_length() - 1
    me = me_ref[0]
    total = jnp.zeros((8, wide), jnp.float32)
    for c in range(rows_here // CHUNK):
        rows = e_ref[c * CHUNK:(c + 1) * CHUNK, :].astype(jnp.float32)
        total = total + jnp.sum(rows.reshape(CHUNK // 8, 8, wide), 0)
    mean = jnp.sum(total, 0, keepdims=True) / rows_here
    mean_ref[...] = mean
    for t in range(wide // CHUNK):
        at = slice(t * CHUNK, (t + 1) * CHUNK)
        product = lax.dot_general(
            e_ref[:, at], e_ref[...], (((0,), (0,)), ((), ())), preferred_element_type=jnp.float32
        )
        down = jnp.transpose(jnp.broadcast_to(mean[:, at] * rows_here, (LANES, CHUNK)))
        for j in range(wide // LANES):
            across = slice(j * LANES, (j + 1) * LANES)
            m_ref[:, across] = product[:, across] - down * mean[:, across]
        for b in range(CHUNK // block):
            apart = (t * (CHUNK // block) + b) ^ me
            place = 0
            for k in range(1, bits):
                place = place + (((apart >> k) & 1) << (bits - 1 - k))
            first = pl.multiple_of(place * block, block)

            @pl.when((apart & 1) == 0)
            def _():
                keep_ref[pl.ds(first, block), :] = m_ref[b * block:(b + 1) * block, :]

            @pl.when((apart & 1) == 1)
            def _():
                send_ref[pl.ds(first, block), :] = m_ref[b * block:(b + 1) * block, :].astype(jnp.bfloat16)


def moments(width, me, embeddings):
    rows_here, wide = embeddings.shape
    return pl.pallas_call(
        functools.partial(moments_kernel, width),
        in_specs=[
            pl.BlockSpec(memory_space=pltpu.SMEM),
            pl.BlockSpec(memory_space=pltpu.VMEM),
        ],
        out_specs=[pl.BlockSpec(memory_space=pltpu.VMEM)] * 3,
        out_shape=[
            jax.ShapeDtypeStruct((wide // 2, wide), jnp.float32),
            jax.ShapeDtypeStruct((wide // 2, wide), jnp.bfloat16),
            jax.ShapeDtypeStruct((1, wide), jnp.float32),
        ],
        scratch_shapes=[pltpu.VMEM((CHUNK, wide), jnp.float32)],
        compiler_params=pltpu.CompilerParams(vmem_limit_bytes=VMEM_LIMIT),
        cost_estimate=pl.CostEstimate(
            flops=2 * rows_here * wide * wide, bytes_accessed=2 * rows_here * wide + 3 * wide * wide, transcendentals=0
        ),
        name="moments",
    )(me.reshape(1), embeddings)


def encode_kernel(total, rows_ref, lists_ref, stat_ref, centroid_ref, rotation_ref, out_ref, delta_ref, scale_ref):
    step = pl.program_id(0)
    width = lists_ref.shape[0]
    feats = out_ref.shape[1]
    owned = centroid_ref.shape[0]
    share = total // width

    @pl.when(step == 0)
    def _():
        means, squares = stat_ref[:, :feats], stat_ref[:, feats:]
        shift = jnp.sum(means, 0, keepdims=True) / width
        delta = means - shift
        variance = jnp.sum(squares + share * (delta * delta), 0, keepdims=True) / total
        scale_ref[...] = lax.rsqrt(variance + 1e-05)
        delta_ref[...] = delta

    senders = rows_ref.shape[0] // CAP
    first = step * senders
    columns = jnp.transpose(lists_ref[pl.ds(first, senders), :])
    names = lax.broadcasted_iota(jnp.int32, (CAP, owned), 1).astype(jnp.float32)
    for s in range(senders):
        at = slice(s * CAP, (s + 1) * CAP)
        listed = columns[:, s:s + 1]
        onehot = jnp.where(listed == names, 1.0, 0.0).astype(jnp.bfloat16)
        centre = jnp.dot(onehot, centroid_ref[...], preferred_element_type=jnp.float32)
        projected = (rows_ref[at, :].astype(jnp.float32) + delta_ref[pl.ds(first + s, 1), :]) * scale_ref[...]
        residual = jnp.where(listed >= 0, projected - centre, 0.0).astype(jnp.bfloat16)
        out_ref[at, :] = jnp.dot(residual, rotation_ref[...], preferred_element_type=jnp.float32).astype(jnp.bfloat16)


def encode(total, rows, lists, stats, centroids, rotation):
    slots, feats = rows.shape
    width = lists.shape[0]
    owned = centroids.shape[0]
    size = 8 * CAP
    whole = lambda i: (0, 0)
    return pl.pallas_call(
        functools.partial(encode_kernel, total),
        grid=(slots // size,),
        in_specs=[
            pl.BlockSpec((size, feats), lambda i: (i, 0)),
            pl.BlockSpec((width, CAP), whole),
            pl.BlockSpec((width, 2 * feats), whole),
            pl.BlockSpec((owned, feats), whole),
            pl.BlockSpec((feats, feats), whole),
        ],
        out_specs=pl.BlockSpec((size, feats), lambda i: (i, 0)),
        out_shape=jax.ShapeDtypeStruct((slots, feats), jnp.bfloat16),
        scratch_shapes=[pltpu.VMEM((width, feats), jnp.float32), pltpu.VMEM((1, feats), jnp.float32)],
        compiler_params=pltpu.CompilerParams(vmem_limit_bytes=VMEM_LIMIT),
        cost_estimate=pl.CostEstimate(
            flops=2 * slots * feats * (owned + feats), bytes_accessed=4 * slots * feats, transcendentals=0
        ),
        name="encode",
    )(rows, lists, stats, centroids, rotation)


def local(embeddings, basis, list_owner, list_slot, centroids, rotation):
    width = lax.axis_size("wide")
    me = lax.axis_index("wide")
    rows_here, wide = embeddings.shape
    feats = basis.shape[1]
    total = rows_here * width
    block = wide // width

    rows, lists, stats = project_and_sort(width, embeddings, basis, list_owner, list_slot)
    got = lax.all_to_all(rows.reshape(width, CAP, feats), "wide", split_axis=0, concat_axis=0, tiled=True)

    keep, send, mean = moments(width, me, embeddings)
    notes = jnp.concatenate(
        [lists, jnp.broadcast_to(stats.reshape(1, -1), (width, 2 * feats)), jnp.broadcast_to(mean, (width, wide))], 1
    )
    notes = lax.all_to_all(notes[:, None, :], "wide", split_axis=0, concat_axis=0, tiled=True)[:, 0, :]
    got_lists, got_stats, got_means = notes[:, :CAP], notes[:, CAP:CAP + 2 * feats], notes[:, CAP + 2 * feats:]

    step = 1
    while step < width:
        came = lax.ppermute(send, "wide", [(i, i ^ step) for i in range(width)])
        held = keep + came.astype(jnp.float32)
        half = held.shape[0] // 2
        keep, send = held[:half], held[half:].astype(jnp.bfloat16)
        step *= 2
    apart = got_means - jnp.mean(got_means, 0, keepdims=True)
    apart_here = lax.dynamic_slice_in_dim(apart, me * block, block, 1)
    between = lax.dot_general(
        apart_here, apart, (((0,), (0,)), ((), ())), precision=lax.Precision.HIGHEST, preferred_element_type=jnp.float32
    )
    covariance = (held + rows_here * between) / total

    encoded = encode(total, got.reshape(width * CAP, feats), got_lists, got_stats, centroids, rotation)
    return (encoded, covariance)


def solution(mesh):
    in_specs = (
        P(("groups", "wide"), None),
        P(),
        P(("groups", "wide")),
        P(("groups", "wide")),
        P("wide", None),
        P(),
    )
    out_specs = (P(("groups", "wide"), None), P(("groups", "wide"), None))
    return jax.shard_map(local, mesh=mesh, in_specs=in_specs, out_specs=out_specs, check_vma=False)
```

time: 177 us -> 80.4 us (0.45)
  blocking collectives: 91.9 us -> 0 us
  Pallas kernels: 0 us -> 24.5 us
  matrix products: 18 us -> 0.48 us
  local copies, waits for them, and re-layouts: 19.5 us -> 3.03 us
  waiting for transfers between devices: 16.1 us -> 31.6 us
  between operations: 14.1 us -> 0.84 us
  starting transfers between devices: 7.42 us -> 15.8 us
  other arithmetic: 8.91 us -> 3.6 us
    psum x2 -> x0, blocking collectives: 64.4 us -> none  [the longest x1 34.4 us: local(): column_sum = lax.psum(local_sum, 'wide')]
    ppermute x0 -> x4, waiting for transfers between devices: none -> 29.8 us  [local(): came = lax.ppermute(send, 'wide', [(i, i ^ step) for i in range(width)])]
    all_to_all x1 -> x0, blocking collectives: 27.4 us -> none  [local(): lax.all_to_all(outgoing, 'wide', split_axis=0, concat_axis=0, tiled=True)]
    pallas_call x0 -> x3, Pallas kernels: none -> 24.5 us  [the longest x1 10.5 us: project_and_sort(): pl.pallas_call(functools.partial(rows_kernel, width), grid=(rows_here //...]
    scatter x2 -> x0, local copies, waits for them, and re-layouts: 18.3 us -> none  [the longest x1 9.57 us: local(): outgoing = jnp.zeros((width * CAP, proj_width), jnp.bfloat16).at[target]....]
    dot_general x5 -> x1, matrix products: 18 us -> 0.48 us  [local(): lax.dot_general(apart_here, apart, (((0,), (0,)), ((), ())), precision=la...]
    reduce_scatter x1 -> x0, waiting for transfers between devices: 16.1 us -> none  [local(): lax.psum_scatter(lax.dot_general(embeddings, embeddings, (((0,), (0,)), (...]
    ppermute x0 -> x4, starting transfers between devices: none -> 5.14 us  [local(): came = lax.ppermute(send, 'wide', [(i, i ^ step) for i in range(width)])]
  transfers between devices with their start and end apart: 2 -> 6, of which waited for: 1 -> 4; matrix products, arithmetic and copies ran while one was open for 18% -> 7% of each run, Pallas kernels for 0% -> 13%
where the time goes in v1:
time: 80.4 us; the launch traced here: 79.9 us
  waiting for transfers between devices  31.6 us (39%)
  Pallas kernels  24.5 us (30%)
  starting transfers between devices  15.8 us (20%)
  other arithmetic  3.6 us (4%)
  local copies, waits for them, and re-layouts  3.03 us (4%)
  between operations  0.84 us (1%)
    ppermute x4, waiting for transfers between devices, local(): came = lax.ppermute(send, 'wide', [(i, i ^ step) for i in range(width)])  29.8 us
    pallas_call x1, Pallas kernels, project_and_sort(): pl.pallas_call(functools.partial(rows_kernel, width), grid=(rows_here //...  10.5 us
    pallas_call x1, Pallas kernels, moments(): pl.pallas_call(functools.partial(moments_kernel, width), in_specs=[pl.Blo...  8.45 us
    all_to_all x1, starting transfers between devices, local(): lax.all_to_all(notes[:, None, :], 'wide', split_axis=0, concat_axis=0, ti...  7.04 us
    pallas_call x1, Pallas kernels, encode(): pl.pallas_call(functools.partial(encode_kernel, total), grid=(slots // si...  5.57 us
    ppermute x4, starting transfers between devices, local(): came = lax.ppermute(send, 'wide', [(i, i ^ step) for i in range(width)])  5.14 us
    all_to_all x1, starting transfers between devices, local(): lax.all_to_all(rows.reshape(width, CAP, feats), 'wide', split_axis=0, con...  3.66 us
    add x3, other arithmetic, local(): held = keep + came.astype(jnp.float32)  2.81 us
  transfers between devices with their start and end apart: 6, of which 4 were waited for; matrix products, arithmetic and copies ran while one was open for 7% of the time, Pallas kernels for 13%

profile of v1, /device:TPU:0, one launch (start us, length us, event | category | flops | bytes accessed | tf_op | source)
XLA Modules:
  0.0 79.9 jit_solution(9281783717164027996)
XLA Ops:
  0.6 0.0 copy-start
  0.6 0.0 copy-start.3
  0.7 0.0 copy-start.4
  0.7 8.5 %moments.1 = (f32[512,1024]{1,0:T(8,128)S(1)}, bf16[512,1024]{1,0:T(8,128)(2,1)S(1)}, f32[1,1024]{1,0:T(1,128)S(1)}) custom-call(s32[1]{0:T(128)} %bitcast.4.me_ref, bf16[2048,1024]{1,0:T(8,128)(2,1)} %e_ref.3), custom_call_target="tpu_custom_call" | custom-call | flops 4294967296 | bytes 7340032 | tf_op jit(solution)/shard_map/moments/pallas_call | solution.py:167
  9.1 0.5 collective-permute-start
  9.7 0.0 copy-done
  9.7 0.0 copy-done.3
  9.7 0.0 copy-done.4
  9.7 10.5 %project_sort.1 = (bf16[2048,256]{1,0:T(8,128)(2,1)}, f32[16,128]{1,0:T(8,128)S(1)}, f32[2,256]{1,0:T(2,128)S(1)}) custom-call(bf16[2048,1024]{1,0:T(8,128)(2,1)} %e_ref.3, bf16[1024,256]{1,0:T(8,128)(2,1)S(1)} %copy-done, s32[16,128]{1,0:T(8,128)S(1)} %bitcast.15, s32[16,128]{1,0:T(8,128)S(1)} %bitcast.16), custom_call_target="tpu_custom_call" | custom-call | flops 3221225472 | bytes 5242880 | tf_op jit(solution)/shard_map/project_sort/pallas_call | solution.py:97
  20.2 0.7 broadcast_in_dim.22
  20.9 7.0 %all-to-all-start.1 = ((f32[16,1,1664]{2,1,0:T(1,128)}), f32[16,1,1664]{2,1,0:T(1,128)S(1)}, u32[]{:S(2)}, u32[]{:S(2)}) async-start(f32[16,1,1664]{2,1,0:T(1,128)} %broadcast_in_dim.22), calls=%async_computation.1 | async-start | bytes 212992 | tf_op jit(solution)/shard_map/all_to_all | solution.py:260
  27.9 0.0 collective-permute-done
  27.9 1.5 %convert_add_fusion = f32[512,1024]{1,0:T(8,128)S(1)} fusion(f32[512,1024]{1,0:T(8,128)S(1)} %get-tuple-element.12, bf16[512,1024]{1,0:T(8,128)(2,1)} %collective-permute-done), kind=kLoop, calls=%fused_computation | loop fusion | flops 1048576 | bytes 5242880 | tf_op jit(solution)/shard_map/add | solution.py:266
  29.5 0.0 copy-start.5
  29.5 1.3 %copy-done.5 = f32[512,1024]{1,0:T(8,128)} copy-done((f32[512,1024]{1,0:T(8,128)}, f32[512,1024]{1,0:T(8,128)S(1)}, u32[]{:S(2)}) %copy-start.5) | copy-done | bytes 2097176
  30.8 0.9 %slice.60 = bf16[256,1024]{1,0:T(8,128)(2,1)} slice(f32[512,1024]{1,0:T(8,128)S(1)} %convert_add_fusion), slice={[256:512], [0:1024]} | slice | bytes 1048576 | tf_op jit(solution)/shard_map/slice | solution.py:268
  31.7 1.9 %collective-permute-start.1 = (bf16[256,1024]{1,0:T(8,128)(2,1)}, bf16[256,1024]{1,0:T(8,128)(2,1)}, u32[]{:S(2)}, u32[]{:S(2)}) collective-permute-start(bf16[256,1024]{1,0:T(8,128)(2,1)} %slice.60), channel_id=1, source_target_pairs={{0,2},{1,3},{2,0},{3,1},{4,6},{5,7},{6,4},{7,5},{8,10},{9,11},{10,... | collective-permute-start | bytes 1572872 | tf_op jit(solution)/shard_map/ppermute | solution.py:265
  33.6 1.9 %all-to-all-done.1 = f32[16,1,1664]{2,1,0:T(1,128)S(1)} async-done(((f32[16,1,1664]{2,1,0:T(1,128)}), f32[16,1,1664]{2,1,0:T(1,128)S(1)}, u32[]{:S(2)}, u32[]{:S(2)}) %all-to-all-start.1) | async-done | bytes 106528 | tf_op jit(solution)/shard_map/all_to_all | solution.py:260
  35.5 3.7 %all-to-all-start = ((bf16[16,128,256]{2,1,0:T(8,128)(2,1)}), bf16[16,128,256]{2,1,0:T(8,128)(2,1)S(1)}, u32[]{:S(2)}, u32[]{:S(2)}) async-start(bf16[16,128,256]{2,1,0:T(8,128)(2,1)} %bitcast.2), calls=%async_computation | async-start | bytes 2097152 | tf_op jit(solution)/shard_map/all_to_all | solution.py:254
  39.2 11.4 %collective-permute-done.1 = bf16[256,1024]{1,0:T(8,128)(2,1)} collective-permute-done((bf16[256,1024]{1,0:T(8,128)(2,1)}, bf16[256,1024]{1,0:T(8,128)(2,1)}, u32[]{:S(2)}, u32[]{:S(2)}) %collective-permute-start.1) | collective-permute-done | bytes 524320 | tf_op jit(solution)/shard_map/ppermute | solution.py:265
  50.6 1.2 %slice_add_fusion = f32[256,1024]{1,0:T(8,128)S(1)} fusion(f32[512,1024]{1,0:T(8,128)S(1)} %copy-done.6, bf16[256,1024]{1,0:T(8,128)(2,1)} %collective-permute-done.1), kind=kLoop, calls=%fused_computation.3 | loop fusion | flops 524288 | bytes 2621440 | tf_op jit(solution)/shard_map/add | solution.py:266
  51.8 0.0 copy-start.1
  51.8 0.0 copy-start.2
  51.9 0.1 collective-permute-start.2
  52.0 12.7 %collective-permute-done.2 = bf16[128,1024]{1,0:T(8,128)(2,1)S(1)} collective-permute-done((bf16[128,1024]{1,0:T(8,128)(2,1)S(1)}, bf16[128,1024]{1,0:T(8,128)(2,1)S(1)}, u32[]{:S(2)}, u32[]{:S(2)}) %collective-permute-start.2) | collective-permute-done | bytes 262176 | tf_op jit(solution)/shard_map/ppermute | solution.py:265
  64.7 0.1 slice_add_fusion.1
  64.8 2.6 %collective-permute-start.3 = (bf16[64,1024]{1,0:T(8,128)(2,1)S(1)}, bf16[64,1024]{1,0:T(8,128)(2,1)S(1)}, u32[]{:S(2)}, u32[]{:S(2)}) collective-permute-start(bf16[64,1024]{1,0:T(8,128)(2,1)S(1)} %slice.62), channel_id=1, source_target_pairs={{0,8},{1,9},{2,10},{3,11},{4,12},{5,13},{6,14},{7,15},{8,0},{9,1},... | collective-permute-start | bytes 393224 | tf_op jit(solution)/shard_map/ppermute | solution.py:265
  67.4 0.5 convolution_multiply_fusion
  67.9 5.7 %collective-permute-done.3 = bf16[64,1024]{1,0:T(8,128)(2,1)S(1)} collective-permute-done((bf16[64,1024]{1,0:T(8,128)(2,1)S(1)}, bf16[64,1024]{1,0:T(8,128)(2,1)S(1)}, u32[]{:S(2)}, u32[]{:S(2)}) %collective-permute-start.3) | collective-permute-done | bytes 131104 | tf_op jit(solution)/shard_map/ppermute | solution.py:265
  73.6 0.7 fusion.1
  74.3 0.0 all-to-all-done
  74.3 5.6 %encode.1 = bf16[2048,256]{1,0:T(8,128)(2,1)} custom-call(bf16[2048,256]{1,0:T(8,128)(2,1)S(1)} %bitcast.12, f32[16,128]{1,0:T(8,128)S(1)} %slice.39.lists_ref, f32[16,512]{1,0:T(8,128)S(1)} %slice.40.stat_ref, bf16[1024,256]{1,0:T(8,128)(2,1)S(1)} %copy-done.1, bf16[256,256]{1,0:T(8,128)(2,1)S(1)} %copy-done.2), custom_call_target="tpu_custom_call" | custom-call | flops 1342177280 | bytes 2097152 | tf_op jit(solution)/shard_map/encode/pallas_call | solution.py:224
  (16 shorter events, 0.1 us)
Async XLA Ops:
  0.6 9.0 %copy-start = (bf16[1024,256]{1,0:T(8,128)(2,1)S(1)}, bf16[1024,256]{1,0:T(8,128)(2,1)}, u32[]{:S(2)}) copy-start(bf16[1024,256]{1,0:T(8,128)(2,1)} %basis_ref.1) | copy-start | bytes 1572868
  0.6 9.0 %copy-start.3 = (s32[2048]{0:T(1024)S(1)}, s32[2048]{0:T(1024)}, u32[]{:S(2)}) copy-start(s32[2048]{0:T(1024)} %param.8) | copy-start | bytes 24580
  0.7 9.0 %copy-start.4 = (s32[2048]{0:T(1024)S(1)}, s32[2048]{0:T(1024)}, u32[]{:S(2)}) copy-start(s32[2048]{0:T(1024)} %param.9) | copy-start | bytes 24580
  9.1 18.8 %collective-permute-start = (bf16[512,1024]{1,0:T(8,128)(2,1)S(1)}, bf16[512,1024]{1,0:T(8,128)(2,1)}, u32[]{:S(2)}, u32[]{:S(2)}) collective-permute-start(bf16[512,1024]{1,0:T(8,128)(2,1)S(1)} %get-tuple-element.13), channel_id=1, source_target_pairs={{0,1},{1,0},{2,3},{3,2},{4,5},{5,4},{6,7},{7,6},{8,9},{9,8},{10,11... | collective-permute-start | bytes 3145736 | tf_op jit(solution)/shard_map/ppermute | solution.py:265
  20.9 14.6 %all-to-all-start.1 = ((f32[16,1,1664]{2,1,0:T(1,128)}), f32[16,1,1664]{2,1,0:T(1,128)S(1)}, u32[]{:S(2)}, u32[]{:S(2)}) async-start(f32[16,1,1664]{2,1,0:T(1,128)} %broadcast_in_dim.22), calls=%async_computation.1 | async-start | bytes 212992 | tf_op jit(solution)/shard_map/all_to_all | solution.py:260
  29.5 1.3 %copy-start.5 = (f32[512,1024]{1,0:T(8,128)}, f32[512,1024]{1,0:T(8,128)S(1)}, u32[]{:S(2)}) copy-start(f32[512,1024]{1,0:T(8,128)S(1)} %convert_add_fusion) | copy-start | bytes 6291460
  31.7 18.9 %copy-start.6 = (f32[512,1024]{1,0:T(8,128)S(1)}, f32[512,1024]{1,0:T(8,128)}, u32[]{:S(2)}) copy-start(f32[512,1024]{1,0:T(8,128)} %copy-done.5) | copy-start | bytes 6291460
  31.7 18.9 %collective-permute-start.1 = (bf16[256,1024]{1,0:T(8,128)(2,1)}, bf16[256,1024]{1,0:T(8,128)(2,1)}, u32[]{:S(2)}, u32[]{:S(2)}) collective-permute-start(bf16[256,1024]{1,0:T(8,128)(2,1)} %slice.60), channel_id=1, source_target_pairs={{0,2},{1,3},{2,0},{3,1},{4,6},{5,7},{6,4},{7,5},{8,10},{9,11},{10,... | collective-permute-start | bytes 1572872 | tf_op jit(solution)/shard_map/ppermute | solution.py:265
  35.5 38.8 %all-to-all-start = ((bf16[16,128,256]{2,1,0:T(8,128)(2,1)}), bf16[16,128,256]{2,1,0:T(8,128)(2,1)S(1)}, u32[]{:S(2)}, u32[]{:S(2)}) async-start(bf16[16,128,256]{2,1,0:T(8,128)(2,1)} %bitcast.2), calls=%async_computation | async-start | bytes 2097152 | tf_op jit(solution)/shard_map/all_to_all | solution.py:254
  51.8 22.5 %copy-start.1 = (bf16[1024,256]{1,0:T(8,128)(2,1)S(1)}, bf16[1024,256]{1,0:T(8,128)(2,1)}, u32[]{:S(2)}) copy-start(bf16[1024,256]{1,0:T(8,128)(2,1)} %centroid_ref.1) | copy-start | bytes 1572868
  51.8 22.5 %copy-start.2 = (bf16[256,256]{1,0:T(8,128)(2,1)S(1)}, bf16[256,256]{1,0:T(8,128)(2,1)}, u32[]{:S(2)}) copy-start(bf16[256,256]{1,0:T(8,128)(2,1)} %rotation_ref.1) | copy-start | bytes 393220
  51.9 12.8 %collective-permute-start.2 = (bf16[128,1024]{1,0:T(8,128)(2,1)S(1)}, bf16[128,1024]{1,0:T(8,128)(2,1)S(1)}, u32[]{:S(2)}, u32[]{:S(2)}) collective-permute-start(bf16[128,1024]{1,0:T(8,128)(2,1)S(1)} %slice.61), channel_id=1, source_target_pairs={{0,4},{1,5},{2,6},{3,7},{4,0},{5,1},{6,2},{7,3},{8,12},{9,13},{10,... | collective-permute-start | bytes 786440 | tf_op jit(solution)/shard_map/ppermute | solution.py:265
  64.8 8.8 %collective-permute-start.3 = (bf16[64,1024]{1,0:T(8,128)(2,1)S(1)}, bf16[64,1024]{1,0:T(8,128)(2,1)S(1)}, u32[]{:S(2)}, u32[]{:S(2)}) collective-permute-start(bf16[64,1024]{1,0:T(8,128)(2,1)S(1)} %slice.62), channel_id=1, source_target_pairs={{0,8},{1,9},{2,10},{3,11},{4,12},{5,13},{6,14},{7,15},{8,0},{9,1},... | collective-permute-start | bytes 393224 | tf_op jit(solution)/shard_map/ppermute | solution.py:265

commit v2 on v1

v2 whole, which is shorter than its diff:
```python
import functools

import jax
import jax.numpy as jnp
from jax import lax
from jax.experimental import pallas as pl
from jax.experimental.pallas import tpu as pltpu
from jax.sharding import PartitionSpec as P

CAP = 128
LANES = 128
NOTES = 16
SPAN = CAP + NOTES
CHUNK = 512
TILE = 256
GROUP = 4
VMEM_LIMIT = 40 * 1024 * 1024


def in_three(x):
    high = x.astype(jnp.bfloat16).astype(jnp.float32)
    rest = x - high
    middle = rest.astype(jnp.bfloat16).astype(jnp.float32)
    return high, middle, (rest - middle).astype(jnp.bfloat16).astype(jnp.float32)


def rows_kernel(width, e_ref, basis_ref, owner_ref, slot_ref, rows_ref, mean_ref, y_ref, yb_ref, sum_ref, total_ref, target_ref, list_ref):
    step = pl.program_id(0)
    rows_here, feats = y_ref.shape
    wide = e_ref.shape[1]
    chunks = rows_here // LANES

    @pl.when(step == 0)
    def _():
        sum_ref[...] = jnp.zeros_like(sum_ref)
        total_ref[...] = jnp.zeros_like(total_ref)
        owner = owner_ref[...]
        wanted = lax.broadcasted_iota(jnp.int32, (width, LANES), 0)
        hits = [jnp.where(owner[c:c + 1, :] == wanted, 1.0, 0.0) for c in range(chunks)]
        flat = jnp.concatenate(hits, 0).astype(jnp.bfloat16)
        up = lax.broadcasted_iota(jnp.int32, (LANES, LANES), 0)
        to = lax.broadcasted_iota(jnp.int32, (LANES, LANES), 1)
        before = jnp.where(up < to, 1.0, 0.0).astype(jnp.bfloat16)
        every = jnp.ones((LANES, LANES), jnp.bfloat16)
        within = jnp.dot(flat, before, preferred_element_type=jnp.float32)
        counts = jnp.dot(flat, every, preferred_element_type=jnp.float32)
        carry = jnp.zeros((width, LANES), jnp.float32)
        ranks = []
        for c in range(chunks):
            at = slice(c * width, (c + 1) * width)
            ranks.append(jnp.sum(hits[c] * (within[at] + carry), 0, keepdims=True).astype(jnp.int32))
            carry = carry + counts[at]
            target_ref[c:c + 1, :] = owner[c:c + 1, :] * CAP + ranks[c]

        slot = slot_ref[...] + 1
        high, low = (slot >> 5).astype(jnp.float32), (slot & 31).astype(jnp.float32)
        spots = lax.broadcasted_iota(jnp.int32, (CAP, LANES), 0)
        placed = jnp.concatenate([jnp.where(ranks[c] == spots, 1.0, 0.0) for c in range(chunks)], 1).astype(jnp.bfloat16)
        digits = jnp.concatenate(
            [
                jnp.concatenate([hits[c] * high[c:c + 1, :] for c in range(chunks)], 1),
                jnp.concatenate([hits[c] * low[c:c + 1, :] for c in range(chunks)], 1),
            ],
            0,
        ).astype(jnp.bfloat16)
        found = lax.dot_general(digits, placed, (((1,), (1,)), ((), ())), preferred_element_type=jnp.float32)
        list_ref[:, :CAP] = found[:width]
        list_ref[:, CAP:] = found[width:]

    y = jnp.dot(e_ref[...], basis_ref[...], preferred_element_type=jnp.float32)
    y_ref[pl.ds(pl.multiple_of(step * CHUNK, CHUNK), CHUNK), :] = y
    sum_ref[...] += jnp.sum(y.reshape(CHUNK // 8, 8, feats), 0)
    total_ref[...] += jnp.sum(e_ref[...].astype(jnp.float32).reshape(CHUNK // 8, 8, wide), 0)

    @pl.when(step == pl.num_programs(0) - 1)
    def _():
        mean_y = jnp.sum(sum_ref[...], 0, keepdims=True) / rows_here
        square = jnp.zeros((8, feats), jnp.float32)
        for c in range(rows_here // CHUNK):
            at = slice(c * CHUNK, (c + 1) * CHUNK)
            centred = y_ref[at, :] - mean_y
            square = square + jnp.sum((centred * centred).reshape(CHUNK // 8, 8, feats), 0)
            yb_ref[at, :] = centred.astype(jnp.bfloat16)
        mean = jnp.sum(total_ref[...], 0, keepdims=True) / rows_here
        mean_ref[...] = mean
        parts = in_three(mean)
        common = [part[:, q * feats:(q + 1) * feats] for part in parts for q in range(wide // feats)]
        common = jnp.concatenate(common + list(in_three(jnp.sum(square, 0, keepdims=True))), 0)

        place = lax.broadcasted_iota(jnp.int32, (GROUP * CAP, LANES), 0).astype(jnp.int16)

        def sort_group(g, _):
            first = g * GROUP
            pieces = []
            for c in range(chunks):
                wanted = (target_ref[c:c + 1, :] - first * CAP).astype(jnp.int32)
                wanted = jnp.broadcast_to(wanted, (16, LANES)).astype(jnp.int16)
                wanted = jnp.concatenate([wanted] * (GROUP * CAP // 16), 0)
                pieces.append(jnp.where(wanted == place, jnp.ones((), jnp.bfloat16), jnp.zeros((), jnp.bfloat16)))
            pick = jnp.concatenate(pieces, 1)
            rows = jnp.dot(pick, yb_ref[...], preferred_element_type=jnp.float32).astype(jnp.bfloat16)
            for j in range(GROUP):
                base = pl.multiple_of((first + j) * SPAN, 16)
                rows_ref[pl.ds(base, CAP), :] = rows[j * CAP:(j + 1) * CAP]
                notes = jnp.concatenate([common, list_ref[pl.ds(first + j, 1), :]], 0)
                rows_ref[pl.ds(pl.multiple_of(base + CAP, 16), NOTES), :] = notes.astype(jnp.bfloat16)
            return 0

        groups = width // GROUP
        if groups <= 4:
            for g in range(groups):
                sort_group(g, 0)
        else:
            lax.fori_loop(0, groups, sort_group, 0)


def project_and_sort(width, embeddings, basis, list_owner, list_slot):
    rows_here, wide = embeddings.shape
    feats = basis.shape[1]
    lanes = rows_here // LANES
    slots = width * SPAN
    return pl.pallas_call(
        functools.partial(rows_kernel, width),
        grid=(rows_here // CHUNK,),
        in_specs=[
            pl.BlockSpec((CHUNK, wide), lambda i: (i, 0)),
            pl.BlockSpec((wide, feats), lambda i: (0, 0)),
            pl.BlockSpec((lanes, LANES), lambda i: (0, 0)),
            pl.BlockSpec((lanes, LANES), lambda i: (0, 0)),
        ],
        out_specs=[
            pl.BlockSpec((slots, feats), lambda i: (0, 0)),
            pl.BlockSpec((1, wide), lambda i: (0, 0)),
        ],
        out_shape=[
            jax.ShapeDtypeStruct((slots, feats), jnp.bfloat16),
            jax.ShapeDtypeStruct((1, wide), jnp.float32),
        ],
        scratch_shapes=[
            pltpu.VMEM((rows_here, feats), jnp.float32),
            pltpu.VMEM((rows_here, feats), jnp.bfloat16),
            pltpu.VMEM((8, feats), jnp.float32),
            pltpu.VMEM((8, wide), jnp.float32),
            pltpu.VMEM((lanes, LANES), jnp.int32),
            pltpu.VMEM((width, 2 * CAP), jnp.float32),
        ],
        compiler_params=pltpu.CompilerParams(vmem_limit_bytes=VMEM_LIMIT),
        cost_estimate=pl.CostEstimate(
            flops=2 * rows_here * feats * (wide + slots), bytes_accessed=2 * rows_here * wide + 2 * slots * feats, transcendentals=0
        ),
        name="project_sort",
    )(embeddings, basis, list_owner.reshape(lanes, LANES), list_slot.reshape(lanes, LANES))


def moments_kernel(width, me_ref, e_ref, mean_ref, keep_ref, send_ref, m_ref):
    step = pl.program_id(0)
    wide = e_ref.shape[1]
    rows_here = e_ref.shape[0] * pl.num_programs(0)
    block = wide // width
    bits = width.bit_length() - 1
    tiles = wide // TILE

    for t in range(tiles):
        rows, columns = slice(t * TILE, (t + 1) * TILE), slice(t * TILE, wide)
        product = lax.dot_general(
            e_ref[:, rows], e_ref[:, columns], (((0,), (0,)), ((), ())), preferred_element_type=jnp.float32
        )

        @pl.when(step == 0)
        def _():
            m_ref[rows, columns] = product

        @pl.when(step > 0)
        def _():
            m_ref[rows, columns] += product

    @pl.when(step == pl.num_programs(0) - 1)
    def _():
        me = me_ref[0]
        mean = mean_ref[...]
        for t in range(tiles):
            rows = slice(t * TILE, (t + 1) * TILE)
            for u in range(t):
                columns = slice(u * TILE, (u + 1) * TILE)
                m_ref[rows, columns] = jnp.transpose(m_ref[columns, rows])
            down = jnp.transpose(jnp.broadcast_to(mean[:, rows] * rows_here, (LANES, TILE)))
            for b in range(TILE // block):
                part = slice(b * block, (b + 1) * block)
                here = slice(t * TILE + b * block, t * TILE + (b + 1) * block)
                apart = (t * (TILE // block) + b) ^ me
                place = 0
                for k in range(1, bits):
                    place = place + (((apart >> k) & 1) << (bits - 1 - k))
                first = pl.multiple_of(place * block, block)
                centred = [
                    m_ref[here, j * LANES:(j + 1) * LANES] - down[part] * mean[:, j * LANES:(j + 1) * LANES]
                    for j in range(wide // LANES)
                ]
                centred = jnp.concatenate(centred, 1)

                @pl.when((apart & 1) == 0)
                def _():
                    keep_ref[pl.ds(first, block), :] = centred

                @pl.when((apart & 1) == 1)
                def _():
                    send_ref[pl.ds(first, block), :] = centred.astype(jnp.bfloat16)


def moments(width, me, embeddings, mean):
    rows_here, wide = embeddings.shape
    return pl.pallas_call(
        functools.partial(moments_kernel, width),
        grid=(rows_here // CHUNK,),
        in_specs=[
            pl.BlockSpec(memory_space=pltpu.SMEM),
            pl.BlockSpec((CHUNK, wide), lambda i: (i, 0)),
            pl.BlockSpec((1, wide), lambda i: (0, 0)),
        ],
        out_specs=[pl.BlockSpec((wide // 2, wide), lambda i: (0, 0))] * 2,
        out_shape=[
            jax.ShapeDtypeStruct((wide // 2, wide), jnp.float32),
            jax.ShapeDtypeStruct((wide // 2, wide), jnp.bfloat16),
        ],
        scratch_shapes=[pltpu.VMEM((wide, wide), jnp.float32)],
        compiler_params=pltpu.CompilerParams(vmem_limit_bytes=VMEM_LIMIT),
        cost_estimate=pl.CostEstimate(
            flops=2 * rows_here * wide * wide, bytes_accessed=2 * rows_here * wide + 3 * wide * wide, transcendentals=0
        ),
        name="moments",
    )(me.reshape(1), embeddings, mean)


def halve_kernel(keep_ref, came_ref, held_ref, send_ref):
    half = held_ref.shape[0]
    held_ref[...] = keep_ref[:half] + came_ref[:half].astype(jnp.float32)
    send_ref[...] = (keep_ref[half:] + came_ref[half:].astype(jnp.float32)).astype(jnp.bfloat16)


def halve(keep, came):
    rows, wide = keep.shape
    return pl.pallas_call(
        halve_kernel,
        in_specs=[pl.BlockSpec(memory_space=pltpu.VMEM)] * 2,
        out_specs=[pl.BlockSpec(memory_space=pltpu.VMEM)] * 2,
        out_shape=[
            jax.ShapeDtypeStruct((rows // 2, wide), jnp.float32),
            jax.ShapeDtypeStruct((rows // 2, wide), jnp.bfloat16),
        ],
        compiler_params=pltpu.CompilerParams(vmem_limit_bytes=VMEM_LIMIT),
        cost_estimate=pl.CostEstimate(flops=rows * wide, bytes_accessed=9 * rows * wide, transcendentals=0),
        name="halve",
    )(keep, came)


def encode_kernel(total, me_ref, got_ref, all_ref, basis_ref, centroid_ref, rotation_ref, out_ref, between_ref, delta_ref, scale_ref, list_ref, apart_ref):
    step = pl.program_id(0)
    width = delta_ref.shape[0]
    feats = out_ref.shape[1]
    owned = centroid_ref.shape[0]
    wide = basis_ref.shape[0]
    block = wide // width
    share = total // width

    @pl.when(step == 0)
    def _():
        notes = jnp.concatenate([all_ref[s * SPAN + CAP:(s + 1) * SPAN, :] for s in range(width)], 0)
        size = width * NOTES
        to = lax.broadcasted_iota(jnp.int32, (size, size), 0)
        of = lax.broadcasted_iota(jnp.int32, (size, size), 1)
        turn = jnp.where((to % width) * NOTES + to // width == of, 1.0, 0.0).astype(jnp.bfloat16)
        turned = jnp.dot(turn, notes, preferred_element_type=jnp.float32)
        row = [turned[r * width:(r + 1) * width] for r in range(NOTES)]
        quarters = wide // feats
        shifts = jnp.zeros((width, feats), jnp.float32)
        for q in range(quarters):
            parts = [row[p * quarters + q] for p in range(3)]
            mean = parts[0] + (parts[1] + parts[2])
            apart_ref[:, q * feats:(q + 1) * feats] = mean - jnp.mean(mean, 0, keepdims=True)
            terms = jnp.dot(
                jnp.concatenate(parts, 0).astype(jnp.bfloat16),
                basis_ref[q * feats:(q + 1) * feats, :],
                preferred_element_type=jnp.float32,
            )
            shifts = shifts + (terms[:width] + (terms[width:2 * width] + terms[2 * width:]))
        square = row[3 * quarters] + (row[3 * quarters + 1] + row[3 * quarters + 2])
        delta = shifts - jnp.mean(shifts, 0, keepdims=True)
        variance = jnp.sum(square + share * (delta * delta), 0, keepdims=True) / total
        scale_ref[...] = lax.rsqrt(variance + 1e-05)
        delta_ref[...] = delta
        digits = row[NOTES - 1]
        list_ref[...] = digits[:, :CAP] * 32.0 + digits[:, CAP:] - 1.0

        me = me_ref[0]
        first = me * block
        near = apart_ref[:, pl.ds(pl.multiple_of(first // LANES * LANES, LANES), LANES)]
        near = pltpu.roll(near, (LANES - first % LANES) % LANES, 1)[:, :block]
        between_ref[...] = share * lax.dot_general(
            near,
            apart_ref[...],
            (((0,), (0,)), ((), ())),
            precision=lax.Precision.HIGHEST,
            preferred_element_type=jnp.float32,
        )

    columns = jnp.transpose(list_ref[pl.ds(step * GROUP, GROUP), :])
    names = lax.broadcasted_iota(jnp.int32, (CAP, owned), 1).astype(jnp.int16)
    hits, projected, held = [], [], []
    for s in range(GROUP):
        listed = jnp.broadcast_to(columns[:, s:s + 1], (CAP, LANES))
        held.append(jnp.concatenate([listed] * (feats // LANES), 1) >= 0)
        wanted = jnp.concatenate([listed.astype(jnp.int32).astype(jnp.int16)] * (owned // LANES), 1)
        hits.append(jnp.where(wanted == names, jnp.ones((), jnp.bfloat16), jnp.zeros((), jnp.bfloat16)))
        rows = got_ref[s * SPAN:s * SPAN + CAP, :].astype(jnp.float32)
        projected.append((rows + delta_ref[pl.ds(step * GROUP + s, 1), :]) * scale_ref[...])
    centre = jnp.dot(jnp.concatenate(hits, 0), centroid_ref[...], preferred_element_type=jnp.float32)
    residual = jnp.where(jnp.concatenate(held, 0), jnp.concatenate(projected, 0) - centre, 0.0)
    out_ref[...] = jnp.dot(
        residual.astype(jnp.bfloat16), rotation_ref[...], preferred_element_type=jnp.float32
    ).astype(jnp.bfloat16)


def encode(width, total, me, got, basis, centroids, rotation):
    wide, feats = basis.shape
    owned = centroids.shape[0]
    slots = width * CAP
    whole = lambda i: (0, 0)
    return pl.pallas_call(
        functools.partial(encode_kernel, total),
        grid=(width // GROUP,),
        in_specs=[
            pl.BlockSpec(memory_space=pltpu.SMEM),
            pl.BlockSpec((GROUP * SPAN, feats), lambda i: (i, 0)),
            pl.BlockSpec((width * SPAN, feats), whole),
            pl.BlockSpec((wide, feats), whole),
            pl.BlockSpec((owned, feats), whole),
            pl.BlockSpec((feats, feats), whole),
        ],
        out_specs=[
            pl.BlockSpec((GROUP * CAP, feats), lambda i: (i, 0)),
            pl.BlockSpec((wide // width, wide), whole),
        ],
        out_shape=[
            jax.ShapeDtypeStruct((slots, feats), jnp.bfloat16),
            jax.ShapeDtypeStruct((wide // width, wide), jnp.float32),
        ],
        scratch_shapes=[
            pltpu.VMEM((width, feats), jnp.float32),
            pltpu.VMEM((1, feats), jnp.float32),
            pltpu.VMEM((width, CAP), jnp.float32),
            pltpu.VMEM((width, wide), jnp.float32),
        ],
        compiler_params=pltpu.CompilerParams(vmem_limit_bytes=VMEM_LIMIT),
        cost_estimate=pl.CostEstimate(
            flops=2 * slots * feats * (owned + feats), bytes_accessed=4 * slots * feats, transcendentals=0
        ),
        name="encode",
    )(me.reshape(1), got, got, basis, centroids, rotation)


def local(embeddings, basis, list_owner, list_slot, centroids, rotation):
    width = lax.axis_size("wide")
    me = lax.axis_index("wide")
    rows_here, wide = embeddings.shape
    feats = basis.shape[1]
    total = rows_here * width

    rows, mean = project_and_sort(width, embeddings, basis, list_owner, list_slot)
    got = lax.all_to_all(rows.reshape(width, SPAN, feats), "wide", split_axis=0, concat_axis=0, tiled=True)

    keep, send = moments(width, me, embeddings, mean)
    step = 1
    while step < width:
        came = lax.ppermute(send, "wide", [(i, i ^ step) for i in range(width)])
        step *= 2
        if step < width:
            keep, send = halve(keep, came)
    encoded, between = encode(width, total, me, got.reshape(width * SPAN, feats), basis, centroids, rotation)
    covariance = (keep + came.astype(jnp.float32) + between) / total
    return (encoded, covariance)


def solution(mesh):
    in_specs = (
        P(("groups", "wide"), None),
        P(),
        P(("groups", "wide")),
        P(("groups", "wide")),
        P("wide", None),
        P(),
    )
    out_specs = (P(("groups", "wide"), None), P(("groups", "wide"), None))
    return jax.shard_map(local, mesh=mesh, in_specs=in_specs, out_specs=out_specs, check_vma=False)
```

time: 80.4 us -> 69.4 us (0.86)
  Pallas kernels: 24.5 us -> 19.3 us
  waiting for transfers between devices: 31.6 us -> 26.5 us
  local copies, waits for them, and re-layouts: 3.03 us -> 6.81 us
  other arithmetic: 3.6 us -> 0.76 us
  starting transfers between devices: 15.8 us -> 14.9 us
    unnamed x16, local copies, waits for them, and re-layouts: 1.37 us -> 6.81 us
    pallas_call x1, Pallas kernels: 10.5 us -> 6.05 us  [project_and_sort(): pl.pallas_call(functools.partial(rows_kernel, width), grid=(rows_here //...]
    all_to_all x2 -> x1, starting transfers between devices: 10.7 us -> 7.38 us  [local(): lax.all_to_all(rows.reshape(width, SPAN, feats), 'wide', split_axis=0, co...]
    ppermute x4, waiting for transfers between devices: 29.8 us -> 26.5 us  [local(): came = lax.ppermute(send, 'wide', [(i, i ^ step) for i in range(width)])]
    add x3 -> x0, other arithmetic: 2.81 us -> none  [local(): held = keep + came.astype(jnp.float32)]
    ppermute x4, starting transfers between devices: 5.14 us -> 7.5 us  [local(): came = lax.ppermute(send, 'wide', [(i, i ^ step) for i in range(width)])]
    all_to_all x2 -> x1, waiting for transfers between devices: 1.87 us -> 0.01 us  [local(): lax.all_to_all(rows.reshape(width, SPAN, feats), 'wide', split_axis=0, co...]
    slice x5 -> x0, local copies, waits for them, and re-layouts: 0.93 us -> none  [the longest x3 0.92 us: local(): keep, send = (held[:half], held[half:].astype(jnp.bfloat16))]
  transfers between devices with their start and end apart: 6 -> 5, of which waited for: 4 -> 4; matrix products, arithmetic and copies ran while one was open for 7% -> 0% of each run, Pallas kernels for 13% -> 19%
where the time goes in v2:
time: 69.4 us; the launch traced here: 69 us
  waiting for transfers between devices  26.5 us (38%)
  Pallas kernels  19.3 us (28%)
  starting transfers between devices  14.9 us (21%)
  local copies, waits for them, and re-layouts  6.81 us (10%)
  other arithmetic  0.76 us (1%)
  between operations  0.7 us (1%)
    ppermute x4, waiting for transfers between devices, local(): came = lax.ppermute(send, 'wide', [(i, i ^ step) for i in range(width)])  26.5 us
    pallas_call x1, Pallas kernels, moments(): pl.pallas_call(functools.partial(moments_kernel, width), grid=(rows_here...  8.37 us
    ppermute x4, starting transfers between devices, local(): came = lax.ppermute(send, 'wide', [(i, i ^ step) for i in range(width)])  7.5 us
    all_to_all x1, starting transfers between devices, local(): lax.all_to_all(rows.reshape(width, SPAN, feats), 'wide', split_axis=0, co...  7.38 us
    unnamed x16, local copies, waits for them, and re-layouts  6.81 us
    pallas_call x1, Pallas kernels, project_and_sort(): pl.pallas_call(functools.partial(rows_kernel, width), grid=(rows_here //...  6.05 us
    pallas_call x1, Pallas kernels, encode(): pl.pallas_call(functools.partial(encode_kernel, total), grid=(width // GR...  4.47 us
  transfers between devices with their start and end apart: 5, of which 4 were waited for; matrix products, arithmetic and copies ran while one was open for 0% of the time, Pallas kernels for 19%

profile of v2, /device:TPU:0, one launch (start us, length us, event | category | flops | bytes accessed | tf_op | source)
XLA Modules:
  0.0 69.0 jit_solution(7721644648849118393)
XLA Ops:
  0.6 0.0 copy-start
  0.6 2.2 %copy-done = bf16[2048,1024]{1,0:T(8,128)(2,1)S(1)} copy-done((bf16[2048,1024]{1,0:T(8,128)(2,1)S(1)}, bf16[2048,1024]{1,0:T(8,128)(2,1)}, u32[]{:S(2)}) %copy-start) | copy-done | bytes 4194328
  2.8 0.0 copy-start.2
  2.8 1.0 %copy-done.2 = bf16[1024,256]{1,0:T(8,128)(2,1)S(1)} copy-done((bf16[1024,256]{1,0:T(8,128)(2,1)S(1)}, bf16[1024,256]{1,0:T(8,128)(2,1)}, u32[]{:S(2)}) %copy-start.2) | copy-done | bytes 524312
  3.9 0.0 copy-start.6
  3.9 0.7 %copy-done.6 = s32[2048]{0:T(1024)S(1)} copy-done((s32[2048]{0:T(1024)S(1)}, s32[2048]{0:T(1024)}, u32[]{:S(2)}) %copy-start.6) | copy-done | bytes 8216
  4.6 0.0 copy-start.7
  4.6 0.7 %copy-done.7 = s32[2048]{0:T(1024)S(1)} copy-done((s32[2048]{0:T(1024)S(1)}, s32[2048]{0:T(1024)}, u32[]{:S(2)}) %copy-start.7) | copy-done | bytes 8216
  5.3 6.1 %project_sort.1 = (bf16[2304,256]{1,0:T(8,128)(2,1)}, f32[1,1024]{1,0:T(1,128)S(1)}) custom-call(bf16[2048,1024]{1,0:T(8,128)(2,1)S(1)} %copy-done, bf16[1024,256]{1,0:T(8,128)(2,1)S(1)} %copy-done.2, s32[16,128]{1,0:T(8,128)S(1)} %bitcast.7, s32[16,128]{1,0:T(8,128)S(1)} %bitcast.8), custom_call_target="tpu_custom_call" | custom-call | flops 3489660928 | bytes 5373952 | tf_op jit(solution)/shard_map/project_sort/pallas_call | solution.py:122
  11.3 7.4 %all-to-all-start = ((bf16[16,144,256]{2,1,0:T(8,128)(2,1)}), bf16[16,144,256]{2,1,0:T(8,128)(2,1)S(1)}, u32[]{:S(2)}, u32[]{:S(2)}) async-start(bf16[16,144,256]{2,1,0:T(8,128)(2,1)} %bitcast.3), calls=%async_computation | async-start | bytes 2359296 | tf_op jit(solution)/shard_map/all_to_all | solution.py:369
  18.7 0.0 copy-start.1
  18.7 2.2 %copy-done.1 = bf16[2048,1024]{1,0:T(8,128)(2,1)S(1)} copy-done((bf16[2048,1024]{1,0:T(8,128)(2,1)S(1)}, bf16[2048,1024]{1,0:T(8,128)(2,1)}, u32[]{:S(2)}) %copy-start.1) | copy-done | bytes 4194328
  20.9 8.4 %moments.1 = (f32[512,1024]{1,0:T(8,128)S(1)}, bf16[512,1024]{1,0:T(8,128)(2,1)S(1)}) custom-call(s32[1]{0:T(128)} %bitcast.me_ref, bf16[2048,1024]{1,0:T(8,128)(2,1)S(1)} %copy-done.1, f32[1,1024]{1,0:T(1,128)S(1)} %get-tuple-element.16.mean_ref), custom_call_target="tpu_custom_call" | custom-call | flops 4294967296 | bytes 7340032 | tf_op jit(solution)/shard_map/moments/pallas_call | solution.py:212
  29.3 0.5 collective-permute-start
  29.8 2.3 %collective-permute-done.came_ref = bf16[512,1024]{1,0:T(8,128)(2,1)S(1)} collective-permute-done((bf16[512,1024]{1,0:T(8,128)(2,1)S(1)}, bf16[512,1024]{1,0:T(8,128)(2,1)S(1)}, u32[]{:S(2)}, u32[]{:S(2)}) %collective-permute-start) | collective-permute-done | bytes 1048608 | tf_op jit(solution)/shard_map/ppermute | solution.py:374
  32.0 0.0 copy-start.3
  32.1 0.0 copy-start.4
  32.1 0.0 copy-start.5
  32.1 0.2 halve.3
  32.3 1.9 %collective-permute-start.1 = (bf16[256,1024]{1,0:T(8,128)(2,1)S(1)}, bf16[256,1024]{1,0:T(8,128)(2,1)S(1)}, u32[]{:S(2)}, u32[]{:S(2)}) collective-permute-start(bf16[256,1024]{1,0:T(8,128)(2,1)S(1)} %get-tuple-element.20), channel_id=1, source_target_pairs={{0,2},{1,3},{2,0},{3,1},{4,6},{5,7},{6,4},{7,5},{8,10},{9,11},{10,... | collective-permute-start | bytes 1572872 | tf_op jit(solution)/shard_map/ppermute | solution.py:374
  34.2 15.5 %collective-permute-done.1.came_ref = bf16[256,1024]{1,0:T(8,128)(2,1)S(1)} collective-permute-done((bf16[256,1024]{1,0:T(8,128)(2,1)S(1)}, bf16[256,1024]{1,0:T(8,128)(2,1)S(1)}, u32[]{:S(2)}, u32[]{:S(2)}) %collective-permute-start.1) | collective-permute-done | bytes 524320 | tf_op jit(solution)/shard_map/ppermute | solution.py:374
  49.8 0.1 halve.4
  49.9 3.3 %collective-permute-start.2 = (bf16[128,1024]{1,0:T(8,128)(2,1)S(1)}, bf16[128,1024]{1,0:T(8,128)(2,1)S(1)}, u32[]{:S(2)}, u32[]{:S(2)}) collective-permute-start(bf16[128,1024]{1,0:T(8,128)(2,1)S(1)} %get-tuple-element.22), channel_id=1, source_target_pairs={{0,4},{1,5},{2,6},{3,7},{4,0},{5,1},{6,2},{7,3},{8,12},{9,13},{10,... | collective-permute-start | bytes 786440 | tf_op jit(solution)/shard_map/ppermute | solution.py:374
  53.1 6.4 %collective-permute-done.2.came_ref = bf16[128,1024]{1,0:T(8,128)(2,1)S(1)} collective-permute-done((bf16[128,1024]{1,0:T(8,128)(2,1)S(1)}, bf16[128,1024]{1,0:T(8,128)(2,1)S(1)}, u32[]{:S(2)}, u32[]{:S(2)}) %collective-permute-start.2) | collective-permute-done | bytes 262176 | tf_op jit(solution)/shard_map/ppermute | solution.py:374
  59.6 1.8 %collective-permute-start.3 = (bf16[64,1024]{1,0:T(8,128)(2,1)S(1)}, bf16[64,1024]{1,0:T(8,128)(2,1)S(1)}, u32[]{:S(2)}, u32[]{:S(2)}) collective-permute-start(bf16[64,1024]{1,0:T(8,128)(2,1)S(1)} %get-tuple-element.24), channel_id=1, source_target_pairs={{0,8},{1,9},{2,10},{3,11},{4,12},{5,13},{6,14},{7,15},{8,0},{9,1},... | collective-permute-start | bytes 393224 | tf_op jit(solution)/shard_map/ppermute | solution.py:374
  61.4 0.0 all-to-all-done
  61.4 0.0 copy-done.3
  61.4 0.0 copy-done.4
  61.4 0.0 copy-done.5
  61.4 4.5 %encode.1 = (bf16[2048,256]{1,0:T(8,128)(2,1)}, f32[64,1024]{1,0:T(8,128)S(1)}) custom-call(s32[1]{0:T(128)} %bitcast.me_ref, bf16[2304,256]{1,0:T(8,128)(2,1)S(1)} %bitcast.5, bf16[2304,256]{1,0:T(8,128)(2,1)S(1)} %bitcast.6, bf16[1024,256]{1,0:T(8,128)(2,1)S(1)} %copy-done.3, bf16[1024,256]{1,0:T(8,128)(2,1)S(1)} %copy-done.4, bf16[256,256]{1,0:T(8,128)(2,1)S(1)} %copy-done.5), custom_call_target="tpu_custom_call" | custom-call | flops 1342177280 | bytes 2097152 | tf_op jit(solution)/shard_map/encode/pallas_call | solution.py:328
  65.9 2.3 %collective-permute-done.3 = bf16[64,1024]{1,0:T(8,128)(2,1)S(1)} collective-permute-done((bf16[64,1024]{1,0:T(8,128)(2,1)S(1)}, bf16[64,1024]{1,0:T(8,128)(2,1)S(1)}, u32[]{:S(2)}, u32[]{:S(2)}) %collective-permute-start.3) | collective-permute-done | bytes 131104 | tf_op jit(solution)/shard_map/ppermute | solution.py:374
  68.2 0.8 %add_multiply_fusion = f32[64,1024]{1,0:T(8,128)} fusion(f32[64,1024]{1,0:T(8,128)S(1)} %get-tuple-element.25, f32[64,1024]{1,0:T(8,128)S(1)} %get-tuple-element.23, bf16[64,1024]{1,0:T(8,128)(2,1)S(1)} %collective-permute-done.3), kind=kLoop, calls=%fused_computation | loop fusion | flops 262144 | bytes 917504 | tf_op jit(solution)/shard_map/div | solution.py:379
  (1 shorter events, 0.0 us)
Async XLA Ops:
  0.6 2.2 %copy-start = (bf16[2048,1024]{1,0:T(8,128)(2,1)S(1)}, bf16[2048,1024]{1,0:T(8,128)(2,1)}, u32[]{:S(2)}) copy-start(bf16[2048,1024]{1,0:T(8,128)(2,1)} %e_ref.3) | copy-start | bytes 12582916
  2.8 1.0 %copy-start.2 = (bf16[1024,256]{1,0:T(8,128)(2,1)S(1)}, bf16[1024,256]{1,0:T(8,128)(2,1)}, u32[]{:S(2)}) copy-start(bf16[1024,256]{1,0:T(8,128)(2,1)} %basis_ref.3) | copy-start | bytes 1572868
  3.9 0.7 %copy-start.6 = (s32[2048]{0:T(1024)S(1)}, s32[2048]{0:T(1024)}, u32[]{:S(2)}) copy-start(s32[2048]{0:T(1024)} %param.8) | copy-start | bytes 24580
  4.6 0.7 %copy-start.7 = (s32[2048]{0:T(1024)S(1)}, s32[2048]{0:T(1024)}, u32[]{:S(2)}) copy-start(s32[2048]{0:T(1024)} %param.9) | copy-start | bytes 24580
  11.3 50.1 %all-to-all-start = ((bf16[16,144,256]{2,1,0:T(8,128)(2,1)}), bf16[16,144,256]{2,1,0:T(8,128)(2,1)S(1)}, u32[]{:S(2)}, u32[]{:S(2)}) async-start(bf16[16,144,256]{2,1,0:T(8,128)(2,1)} %bitcast.3), calls=%async_computation | async-start | bytes 2359296 | tf_op jit(solution)/shard_map/all_to_all | solution.py:369
  18.7 2.2 %copy-start.1 = (bf16[2048,1024]{1,0:T(8,128)(2,1)S(1)}, bf16[2048,1024]{1,0:T(8,128)(2,1)}, u32[]{:S(2)}) copy-start(bf16[2048,1024]{1,0:T(8,128)(2,1)} %e_ref.3) | copy-start | bytes 12582916
  29.3 2.8 %collective-permute-start = (bf16[512,1024]{1,0:T(8,128)(2,1)S(1)}, bf16[512,1024]{1,0:T(8,128)(2,1)S(1)}, u32[]{:S(2)}, u32[]{:S(2)}) collective-permute-start(bf16[512,1024]{1,0:T(8,128)(2,1)S(1)} %get-tuple-element.18), channel_id=1, source_target_pairs={{0,1},{1,0},{2,3},{3,2},{4,5},{5,4},{6,7},{7,6},{8,9},{9,8},{10,11... | collective-permute-start | bytes 3145736 | tf_op jit(solution)/shard_map/ppermute | solution.py:374
  32.0 29.4 %copy-start.3 = (bf16[1024,256]{1,0:T(8,128)(2,1)S(1)}, bf16[1024,256]{1,0:T(8,128)(2,1)}, u32[]{:S(2)}) copy-start(bf16[1024,256]{1,0:T(8,128)(2,1)} %basis_ref.3) | copy-start | bytes 1572868
  32.1 29.4 %copy-start.4 = (bf16[1024,256]{1,0:T(8,128)(2,1)S(1)}, bf16[1024,256]{1,0:T(8,128)(2,1)}, u32[]{:S(2)}) copy-start(bf16[1024,256]{1,0:T(8,128)(2,1)} %centroid_ref.1) | copy-start | bytes 1572868
  32.1 29.4 %copy-start.5 = (bf16[256,256]{1,0:T(8,128)(2,1)S(1)}, bf16[256,256]{1,0:T(8,128)(2,1)}, u32[]{:S(2)}) copy-start(bf16[256,256]{1,0:T(8,128)(2,1)} %rotation_ref.1) | copy-start | bytes 393220
  32.3 17.5 %collective-permute-start.1 = (bf16[256,1024]{1,0:T(8,128)(2,1)S(1)}, bf16[256,1024]{1,0:T(8,128)(2,1)S(1)}, u32[]{:S(2)}, u32[]{:S(2)}) collective-permute-start(bf16[256,1024]{1,0:T(8,128)(2,1)S(1)} %get-tuple-element.20), channel_id=1, source_target_pairs={{0,2},{1,3},{2,0},{3,1},{4,6},{5,7},{6,4},{7,5},{8,10},{9,11},{10,... | collective-permute-start | bytes 1572872 | tf_op jit(solution)/shard_map/ppermute | solution.py:374
  49.9 9.7 %collective-permute-start.2 = (bf16[128,1024]{1,0:T(8,128)(2,1)S(1)}, bf16[128,1024]{1,0:T(8,128)(2,1)S(1)}, u32[]{:S(2)}, u32[]{:S(2)}) collective-permute-start(bf16[128,1024]{1,0:T(8,128)(2,1)S(1)} %get-tuple-element.22), channel_id=1, source_target_pairs={{0,4},{1,5},{2,6},{3,7},{4,0},{5,1},{6,2},{7,3},{8,12},{9,13},{10,... | collective-permute-start | bytes 786440 | tf_op jit(solution)/shard_map/ppermute | solution.py:374
  59.6 8.6 %collective-permute-start.3 = (bf16[64,1024]{1,0:T(8,128)(2,1)S(1)}, bf16[64,1024]{1,0:T(8,128)(2,1)S(1)}, u32[]{:S(2)}, u32[]{:S(2)}) collective-permute-start(bf16[64,1024]{1,0:T(8,128)(2,1)S(1)} %get-tuple-element.24), channel_id=1, source_target_pairs={{0,8},{1,9},{2,10},{3,11},{4,12},{5,13},{6,14},{7,15},{8,0},{9,1},... | collective-permute-start | bytes 393224 | tf_op jit(solution)/shard_map/ppermute | solution.py:374

commit v3 on v2

--- a/solution.py
+++ b/solution.py
@@ -14,7 +14,9 @@
 CHUNK = 512
 TILE = 256
 GROUP = 4
-VMEM_LIMIT = 40 * 1024 * 1024
+VMEM_ALL = 60 * 1024 * 1024
+VMEM_SOME = 24 * 1024 * 1024
+VMEM_MOST = 48 * 1024 * 1024
 
 
 def in_three(x):
@@ -144,7 +146,7 @@
             pltpu.VMEM((lanes, LANES), jnp.int32),
             pltpu.VMEM((width, 2 * CAP), jnp.float32),
         ],
-        compiler_params=pltpu.CompilerParams(vmem_limit_bytes=VMEM_LIMIT),
+        compiler_params=pltpu.CompilerParams(vmem_limit_bytes=VMEM_ALL),
         cost_estimate=pl.CostEstimate(
             flops=2 * rows_here * feats * (wide + slots), bytes_accessed=2 * rows_here * wide + 2 * slots * feats, transcendentals=0
         ),
@@ -152,105 +154,124 @@
     )(embeddings, basis, list_owner.reshape(lanes, LANES), list_slot.reshape(lanes, LANES))
 
 
-def moments_kernel(width, me_ref, e_ref, mean_ref, keep_ref, send_ref, m_ref):
-    step = pl.program_id(0)
-    wide = e_ref.shape[1]
-    rows_here = e_ref.shape[0] * pl.num_programs(0)
+def moments_kernel(width, me_ref, mean_hbm, e_hbm, keep_ref, send_ref, e_ref, mean_ref, m_ref, sem, mean_sem):
+    rows_here, wide = e_ref.shape
     block = wide // width
     bits = width.bit_length() - 1
-    tiles = wide // TILE
-
-    for t in range(tiles):
-        rows, columns = slice(t * TILE, (t + 1) * TILE), slice(t * TILE, wide)
-        product = lax.dot_general(
-            e_ref[:, rows], e_ref[:, columns], (((0,), (0,)), ((), ())), preferred_element_type=jnp.float32
-        )
-
-        @pl.when(step == 0)
-        def _():
-            m_ref[rows, columns] = product
-
-        @pl.when(step > 0)
-        def _():
-            m_ref[rows, columns] += product
-
-    @pl.when(step == pl.num_programs(0) - 1)
-    def _():
-        me = me_ref[0]
-        mean = mean_ref[...]
-        for t in range(tiles):
-            rows = slice(t * TILE, (t + 1) * TILE)
-            for u in range(t):
-                columns = slice(u * TILE, (u + 1) * TILE)
-                m_ref[rows, columns] = jnp.transpose(m_ref[columns, rows])
-            down = jnp.transpose(jnp.broadcast_to(mean[:, rows] * rows_here, (LANES, TILE)))
-            for b in range(TILE // block):
-                part = slice(b * block, (b + 1) * block)
-                here = slice(t * TILE + b * block, t * TILE + (b + 1) * block)
-                apart = (t * (TILE // block) + b) ^ me
-                place = 0
-                for k in range(1, bits):
-                    place = place + (((apart >> k) & 1) << (bits - 1 - k))
-                first = pl.multiple_of(place * block, block)
-                centred = [
-                    m_ref[here, j * LANES:(j + 1) * LANES] - down[part] * mean[:, j * LANES:(j + 1) * LANES]
-                    for j in range(wide // LANES)
-                ]
-                centred = jnp.concatenate(centred, 1)
-
-                @pl.when((apart & 1) == 0)
-                def _():
-                    keep_ref[pl.ds(first, block), :] = centred
-
-                @pl.when((apart & 1) == 1)
-                def _():
-                    send_ref[pl.ds(first, block), :] = centred.astype(jnp.bfloat16)
+    mean_copy = pltpu.make_async_copy(mean_hbm, mean_ref, mean_sem)
+    mean_copy.start()
+    copies = []
+    for c in range(rows_here // CHUNK):
+        at = pl.ds(c * CHUNK, CHUNK)
+        copies.append(pltpu.make_async_copy(e_hbm.at[at], e_ref.at[at], sem.at[c]))
+        copies[c].start()
+    me = me_ref[0]
+    mean_copy.wait()
+    mean = mean_ref[...]
+    for t in range(wide // TILE):
+        rows = slice(t * TILE, (t + 1) * TILE)
+        if t == 0:
+            product = jnp.zeros((TILE, wide), jnp.float32)
+            for c in range(rows_here // CHUNK):
+                copies[c].wait()
+                at = slice(c * CHUNK, (c + 1) * CHUNK)
+                product = product + lax.dot_general(
+                    e_ref[at, rows], e_ref[at, :], (((0,), (0,)), ((), ())), preferred_element_type=jnp.float32
+                )
+        else:
+            product = lax.dot_general(
+                e_ref[:, rows], e_ref[...], (((0,), (0,)), ((), ())), preferred_element_type=jnp.float32
+            )
+        down = jnp.transpose(jnp.broadcast_to(mean[:, rows] * rows_here, (LANES, TILE)))
+        for j in range(wide // LANES):
+            across = slice(j * LANES, (j + 1) * LANES)
+            m_ref[rows, across] = product[:, across] - down * mean[:, across]
+        for pair in range(TILE // block // 2):
+            first = t * (TILE // block) + 2 * pair
+            apart = (first ^ me) >> 1
+            place = 0
+            for k in range(bits - 1):
+                place = place + (((apart >> k) & 1) << (bits - 2 - k))
+            to = pl.ds(pl.multiple_of(place * block, block), block)
+            kept = pl.multiple_of((first + (me & 1)) * block, block)
+            sent = pl.multiple_of((first + 1 - (me & 1)) * block, block)
+            keep_ref[to, :] = m_ref[pl.ds(kept, block), :]
+            send_ref[to, :] = m_ref[pl.ds(sent, block), :].astype(jnp.bfloat16)
 
 
 def moments(width, me, embeddings, mean):
     rows_here, wide = embeddings.shape
+    vmem = pl.BlockSpec(memory_space=pltpu.VMEM)
     return pl.pallas_call(
         functools.partial(moments_kernel, width),
-        grid=(rows_here // CHUNK,),
-        in_specs=[
-            pl.BlockSpec(memory_space=pltpu.SMEM),
-            pl.BlockSpec((CHUNK, wide), lambda i: (i, 0)),
-            pl.BlockSpec((1, wide), lambda i: (0, 0)),
-        ],
-        out_specs=[pl.BlockSpec((wide // 2, wide), lambda i: (0, 0))] * 2,
+        in_specs=[pl.BlockSpec(memory_space=pltpu.SMEM)] + [pl.BlockSpec(memory_space=pl.ANY)] * 2,
+        out_specs=[vmem] * 2,
         out_shape=[
             jax.ShapeDtypeStruct((wide // 2, wide), jnp.float32),
             jax.ShapeDtypeStruct((wide // 2, wide), jnp.bfloat16),
         ],
-        scratch_shapes=[pltpu.VMEM((wide, wide), jnp.float32)],
-        compiler_params=pltpu.CompilerParams(vmem_limit_bytes=VMEM_LIMIT),
+        scratch_shapes=[
+            pltpu.VMEM((rows_here, wide), jnp.bfloat16),
+            pltpu.VMEM((1, wide), jnp.float32),
+            pltpu.VMEM((wide, wide), jnp.float32),
+            pltpu.SemaphoreType.DMA((rows_here // CHUNK,)),
+            pltpu.SemaphoreType.DMA,
+        ],
+        compiler_params=pltpu.CompilerParams(vmem_limit_bytes=VMEM_MOST),
         cost_estimate=pl.CostEstimate(
             flops=2 * rows_here * wide * wide, bytes_accessed=2 * rows_here * wide + 3 * wide * wide, transcendentals=0
         ),
         name="moments",
-    )(me.reshape(1), embeddings, mean)
-
-
-def halve_kernel(keep_ref, came_ref, held_ref, send_ref):
-    half = held_ref.shape[0]
-    held_ref[...] = keep_ref[:half] + came_ref[:half].astype(jnp.float32)
-    send_ref[...] = (keep_ref[half:] + came_ref[half:].astype(jnp.float32)).astype(jnp.bfloat16)
-
-
-def halve(keep, came):
+    )(me.reshape(1), mean, embeddings)
+
+
+def add_kernel(pieces, keep_ref, *refs):
+    came, outs = refs[:-pieces], refs[-pieces:]
+    size = outs[0].shape[0]
+    for p in range(pieces):
+        at = slice(p * size, (p + 1) * size)
+        held = keep_ref[at]
+        for ref in came:
+            held = held + ref[at].astype(jnp.float32)
+        outs[p][...] = held.astype(outs[p].dtype)
+
+
+def add_and_split(keep, came, pieces):
     rows, wide = keep.shape
+    vmem = pl.BlockSpec(memory_space=pltpu.VMEM)
     return pl.pallas_call(
-        halve_kernel,
-        in_specs=[pl.BlockSpec(memory_space=pltpu.VMEM)] * 2,
-        out_specs=[pl.BlockSpec(memory_space=pltpu.VMEM)] * 2,
+        functools.partial(add_kernel, pieces),
+        in_specs=[vmem] * (1 + len(came)),
+        out_specs=[vmem] * pieces,
         out_shape=[
-            jax.ShapeDtypeStruct((rows // 2, wide), jnp.float32),
-            jax.ShapeDtypeStruct((rows // 2, wide), jnp.bfloat16),
-        ],
-        compiler_params=pltpu.CompilerParams(vmem_limit_bytes=VMEM_LIMIT),
-        cost_estimate=pl.CostEstimate(flops=rows * wide, bytes_accessed=9 * rows * wide, transcendentals=0),
-        name="halve",
-    )(keep, came)
+            jax.ShapeDtypeStruct((rows // pieces, wide), jnp.float32 if p == 0 else jnp.bfloat16) for p in range(pieces)
+        ],
+        compiler_params=pltpu.CompilerParams(vmem_limit_bytes=VMEM_SOME),
+        cost_estimate=pl.CostEstimate(flops=2 * rows * wide, bytes_accessed=10 * rows * wide, transcendentals=0),
+        name="add_and_split",
+    )(keep, *came)
+
+
+def partners(width, apart):
+    return [(i, i ^ apart) for i in range(width)]
+
+
+def halving_stages(width):
+    strides = [1 << k for k in range(width.bit_length() - 1)]
+    return [strides[:1], strides[1:3]] + [[s] for s in strides[3:]]
+
+
+def reduce_blocks(width, keep, send):
+    stages = halving_stages(width)
+    out = [send]
+    for n, stage in enumerate(stages):
+        came = []
+        for p in range(1, 1 << len(stage)):
+            apart = sum(s for k, s in enumerate(stage) if (p >> (len(stage) - 1 - k)) & 1)
+            came.append(lax.ppermute(out[p - 1], "wide", partners(width, apart)))
+        if n + 1 < len(stages):
+            keep, *out = add_and_split(keep, came, 1 << len(stages[n + 1]))
+    return keep, came
 
 
 def encode_kernel(total, me_ref, got_ref, all_ref, basis_ref, centroid_ref, rotation_ref, out_ref, between_ref, delta_ref, scale_ref, list_ref, apart_ref):
@@ -350,7 +371,7 @@
             pltpu.VMEM((width, CAP), jnp.float32),
             pltpu.VMEM((width, wide), jnp.float32),
         ],
-        compiler_params=pltpu.CompilerParams(vmem_limit_bytes=VMEM_LIMIT),
+        compiler_params=pltpu.CompilerParams(vmem_limit_bytes=VMEM_SOME),
         cost_estimate=pl.CostEstimate(
             flops=2 * slots * feats * (owned + feats), bytes_accessed=4 * slots * feats, transcendentals=0
         ),
@@ -369,14 +390,11 @@
     got = lax.all_to_all(rows.reshape(width, SPAN, feats), "wide", split_axis=0, concat_axis=0, tiled=True)
 
     keep, send = moments(width, me, embeddings, mean)
-    step = 1
-    while step < width:
-        came = lax.ppermute(send, "wide", [(i, i ^ step) for i in range(width)])
-        step *= 2
-        if step < width:
-            keep, send = halve(keep, came)
+    keep, came = reduce_blocks(width, keep, send)
     encoded, between = encode(width, total, me, got.reshape(width * SPAN, feats), basis, centroids, rotation)
-    covariance = (keep + came.astype(jnp.float32) + between) / total
+    for block in came:
+        keep = keep + block.astype(jnp.float32)
+    covariance = (keep + between) / total
     return (encoded, covariance)
 
 

time: 69.4 us -> 60.6 us (0.87)
  local copies, waits for them, and re-layouts: 6.81 us -> 0.01 us
  waiting for transfers between devices: 26.5 us -> 24.6 us
  Pallas kernels: 19.3 us -> 20.1 us
  starting transfers between devices: 14.9 us -> 14.1 us
    unnamed x16 -> x8, local copies, waits for them, and re-layouts: 6.81 us -> 0.01 us
    pallas_call x1, Pallas kernels: 6.05 us -> 8.19 us  [project_and_sort(): pl.pallas_call(functools.partial(rows_kernel, width), grid=(rows_here //...]
    ppermute x4 -> x5, waiting for transfers between devices: 26.5 us -> 24.6 us  [reduce_blocks(): came.append(lax.ppermute(out[p - 1], 'wide', partners(width, apart)))]
    pallas_call x4 -> x3, Pallas kernels: 8.75 us -> 7.45 us  [the longest x1 7.16 us: moments(): pl.pallas_call(functools.partial(moments_kernel, width), in_specs=[pl.Blo...]
    ppermute x4 -> x5, starting transfers between devices: 7.5 us -> 6.6 us  [reduce_blocks(): came.append(lax.ppermute(out[p - 1], 'wide', partners(width, apart)))]
  transfers between devices with their start and end apart: 5 -> 6, of which waited for: 4 -> 4; matrix products, arithmetic and copies ran while one was open for 0% -> 0% of each run, Pallas kernels for 19% -> 20%
where the time goes in v3:
time: 60.6 us; the launch traced here: 60.3 us
  waiting for transfers between devices  24.6 us (41%)
  Pallas kernels  20.1 us (33%)
  starting transfers between devices  14.1 us (23%)
  other arithmetic  0.74 us (1%)
  between operations  0.68 us (1%)
    ppermute x5, waiting for transfers between devices, reduce_blocks(): came.append(lax.ppermute(out[p - 1], 'wide', partners(width, apart)))  24.6 us
    pallas_call x1, Pallas kernels, project_and_sort(): pl.pallas_call(functools.partial(rows_kernel, width), grid=(rows_here //...  8.19 us
    all_to_all x1, starting transfers between devices, local(): lax.all_to_all(rows.reshape(width, SPAN, feats), 'wide', split_axis=0, co...  7.53 us
    pallas_call x1, Pallas kernels, moments(): pl.pallas_call(functools.partial(moments_kernel, width), in_specs=[pl.Blo...  7.16 us
    ppermute x5, starting transfers between devices, reduce_blocks(): came.append(lax.ppermute(out[p - 1], 'wide', partners(width, apart)))  6.6 us
    pallas_call x1, Pallas kernels, encode(): pl.pallas_call(functools.partial(encode_kernel, total), grid=(width // GR...  4.47 us
  transfers between devices with their start and end apart: 6, of which 4 were waited for; matrix products, arithmetic and copies ran while one was open for 0% of the time, Pallas kernels for 20%

profile of v3, /device:TPU:0, one launch (start us, length us, event | category | flops | bytes accessed | tf_op | source)
XLA Modules:
  0.0 60.3 jit_solution(13477623244767793248)
XLA Ops:
  0.6 8.2 %project_sort.1 = (bf16[2304,256]{1,0:T(8,128)(2,1)}, f32[1,1024]{1,0:T(1,128)}) custom-call(bf16[2048,1024]{1,0:T(8,128)(2,1)} %e_hbm.1, bf16[1024,256]{1,0:T(8,128)(2,1)} %basis_ref.3, s32[16,128]{1,0:T(8,128)} %bitcast.8, s32[16,128]{1,0:T(8,128)} %bitcast.9), custom_call_target="tpu_custom_call" | custom-call | flops 3489660928 | bytes 5373952 | tf_op jit(solution)/shard_map/project_sort/pallas_call | solution.py:124
  8.8 0.0 copy-start.3
  8.8 7.5 %all-to-all-start = ((bf16[16,144,256]{2,1,0:T(8,128)(2,1)}), bf16[16,144,256]{2,1,0:T(8,128)(2,1)S(1)}, u32[]{:S(2)}, u32[]{:S(2)}) async-start(bf16[16,144,256]{2,1,0:T(8,128)(2,1)} %bitcast.7), calls=%async_computation | async-start | bytes 2359296 | tf_op jit(solution)/shard_map/all_to_all | solution.py:390
  16.4 0.0 copy-done.3
  16.4 7.2 %moments.1 = (f32[512,1024]{1,0:T(8,128)S(1)}, bf16[512,1024]{1,0:T(8,128)(2,1)S(1)}) custom-call(s32[1]{0:T(128)} %bitcast.me_ref, f32[1,1024]{1,0:T(1,128)S(1)} %copy-done.3, bf16[2048,1024]{1,0:T(8,128)(2,1)} %e_hbm.1), custom_call_target="tpu_custom_call" | custom-call | flops 4294967296 | bytes 7340032 | tf_op jit(solution)/shard_map/moments/pallas_call | solution.py:205
  23.5 0.5 collective-permute-start
  24.0 2.3 %collective-permute-done.refs_0_ = bf16[512,1024]{1,0:T(8,128)(2,1)S(1)} collective-permute-done((bf16[512,1024]{1,0:T(8,128)(2,1)S(1)}, bf16[512,1024]{1,0:T(8,128)(2,1)S(1)}, u32[]{:S(2)}, u32[]{:S(2)}) %collective-permute-start) | collective-permute-done | bytes 1048608 | tf_op jit(solution)/shard_map/ppermute | solution.py:271
  26.3 0.0 copy-start
  26.3 0.0 copy-start.1
  26.3 0.0 copy-start.2
  26.3 0.2 add_and_split.2
  26.5 2.0 %collective-permute-start.1 = (bf16[128,1024]{1,0:T(8,128)(2,1)S(1)}, bf16[128,1024]{1,0:T(8,128)(2,1)S(1)}, u32[]{:S(2)}, u32[]{:S(2)}) collective-permute-start(bf16[128,1024]{1,0:T(8,128)(2,1)S(1)} %get-tuple-element.20), channel_id=1, source_target_pairs={{0,4},{1,5},{2,6},{3,7},{4,0},{5,1},{6,2},{7,3},{8,12},{9,13},{10,... | collective-permute-start | bytes 786440 | tf_op jit(solution)/shard_map/ppermute | solution.py:271
  28.4 1.5 %collective-permute-start.2 = (bf16[128,1024]{1,0:T(8,128)(2,1)S(1)}, bf16[128,1024]{1,0:T(8,128)(2,1)S(1)}, u32[]{:S(2)}, u32[]{:S(2)}) collective-permute-start(bf16[128,1024]{1,0:T(8,128)(2,1)S(1)} %get-tuple-element.21), channel_id=1, source_target_pairs={{0,2},{1,3},{2,0},{3,1},{4,6},{5,7},{6,4},{7,5},{8,10},{9,11},{10,... | collective-permute-start | bytes 786440 | tf_op jit(solution)/shard_map/ppermute | solution.py:271
  29.9 0.1 collective-permute-start.3
  30.0 14.5 %collective-permute-done.1.refs_0_ = bf16[128,1024]{1,0:T(8,128)(2,1)S(1)} collective-permute-done((bf16[128,1024]{1,0:T(8,128)(2,1)S(1)}, bf16[128,1024]{1,0:T(8,128)(2,1)S(1)}, u32[]{:S(2)}, u32[]{:S(2)}) %collective-permute-start.1) | collective-permute-done | bytes 262176 | tf_op jit(solution)/shard_map/ppermute | solution.py:271
  44.6 0.0 collective-permute-done.2.refs_1_
  44.6 6.1 %collective-permute-done.3.refs_2_ = bf16[128,1024]{1,0:T(8,128)(2,1)S(1)} collective-permute-done((bf16[128,1024]{1,0:T(8,128)(2,1)S(1)}, bf16[128,1024]{1,0:T(8,128)(2,1)S(1)}, u32[]{:S(2)}, u32[]{:S(2)}) %collective-permute-start.3) | collective-permute-done | bytes 262176 | tf_op jit(solution)/shard_map/ppermute | solution.py:271
  50.6 0.1 add_and_split.3
  50.7 2.6 %collective-permute-start.4 = (bf16[64,1024]{1,0:T(8,128)(2,1)S(1)}, bf16[64,1024]{1,0:T(8,128)(2,1)S(1)}, u32[]{:S(2)}, u32[]{:S(2)}) collective-permute-start(bf16[64,1024]{1,0:T(8,128)(2,1)S(1)} %get-tuple-element.24), channel_id=1, source_target_pairs={{0,8},{1,9},{2,10},{3,11},{4,12},{5,13},{6,14},{7,15},{8,0},{9,1},... | collective-permute-start | bytes 393224 | tf_op jit(solution)/shard_map/ppermute | solution.py:271
  53.3 0.0 all-to-all-done
  53.3 0.0 copy-done
  53.3 0.0 copy-done.1
  53.3 0.0 copy-done.2
  53.3 4.5 %encode.1 = (bf16[2048,256]{1,0:T(8,128)(2,1)}, f32[64,1024]{1,0:T(8,128)S(1)}) custom-call(s32[1]{0:T(128)} %bitcast.me_ref, bf16[2304,256]{1,0:T(8,128)(2,1)S(1)} %bitcast.5, bf16[2304,256]{1,0:T(8,128)(2,1)S(1)} %bitcast.6, bf16[1024,256]{1,0:T(8,128)(2,1)S(1)} %copy-done, bf16[1024,256]{1,0:T(8,128)(2,1)S(1)} %copy-done.1, bf16[256,256]{1,0:T(8,128)(2,1)S(1)} %copy-done.2), custom_call_target="tpu_custom_call" | custom-call | flops 1342177280 | bytes 2097152 | tf_op jit(solution)/shard_map/encode/pallas_call | solution.py:349
  57.8 1.8 %collective-permute-done.4 = bf16[64,1024]{1,0:T(8,128)(2,1)S(1)} collective-permute-done((bf16[64,1024]{1,0:T(8,128)(2,1)S(1)}, bf16[64,1024]{1,0:T(8,128)(2,1)S(1)}, u32[]{:S(2)}, u32[]{:S(2)}) %collective-permute-start.4) | collective-permute-done | bytes 131104 | tf_op jit(solution)/shard_map/ppermute | solution.py:271
  59.6 0.7 %add_multiply_fusion = f32[64,1024]{1,0:T(8,128)} fusion(f32[64,1024]{1,0:T(8,128)S(1)} %get-tuple-element.25, f32[64,1024]{1,0:T(8,128)S(1)} %get-tuple-element.23, bf16[64,1024]{1,0:T(8,128)(2,1)S(1)} %collective-permute-done.4), kind=kLoop, calls=%fused_computation | loop fusion | flops 262144 | bytes 917504 | tf_op jit(solution)/shard_map/div | solution.py:397
Async XLA Ops:
  8.8 7.5 %copy-start.3 = (f32[1,1024]{1,0:T(1,128)S(1)}, f32[1,1024]{1,0:T(1,128)}, u32[]{:S(2)}) copy-start(f32[1,1024]{1,0:T(1,128)} %get-tuple-element.16.mean_hbm) | copy-start | bytes 12292
  8.8 44.5 %all-to-all-start = ((bf16[16,144,256]{2,1,0:T(8,128)(2,1)}), bf16[16,144,256]{2,1,0:T(8,128)(2,1)S(1)}, u32[]{:S(2)}, u32[]{:S(2)}) async-start(bf16[16,144,256]{2,1,0:T(8,128)(2,1)} %bitcast.7), calls=%async_computation | async-start | bytes 2359296 | tf_op jit(solution)/shard_map/all_to_all | solution.py:390
  23.5 2.7 %collective-permute-start = (bf16[512,1024]{1,0:T(8,128)(2,1)S(1)}, bf16[512,1024]{1,0:T(8,128)(2,1)S(1)}, u32[]{:S(2)}, u32[]{:S(2)}) collective-permute-start(bf16[512,1024]{1,0:T(8,128)(2,1)S(1)} %get-tuple-element.18), channel_id=1, source_target_pairs={{0,1},{1,0},{2,3},{3,2},{4,5},{5,4},{6,7},{7,6},{8,9},{9,8},{10,11... | collective-permute-start | bytes 3145736 | tf_op jit(solution)/shard_map/ppermute | solution.py:271
  26.3 27.0 %copy-start = (bf16[1024,256]{1,0:T(8,128)(2,1)S(1)}, bf16[1024,256]{1,0:T(8,128)(2,1)}, u32[]{:S(2)}) copy-start(bf16[1024,256]{1,0:T(8,128)(2,1)} %basis_ref.3) | copy-start | bytes 1572868
  26.3 27.0 %copy-start.1 = (bf16[1024,256]{1,0:T(8,128)(2,1)S(1)}, bf16[1024,256]{1,0:T(8,128)(2,1)}, u32[]{:S(2)}) copy-start(bf16[1024,256]{1,0:T(8,128)(2,1)} %centroid_ref.1) | copy-start | bytes 1572868
  26.3 27.0 %copy-start.2 = (bf16[256,256]{1,0:T(8,128)(2,1)S(1)}, bf16[256,256]{1,0:T(8,128)(2,1)}, u32[]{:S(2)}) copy-start(bf16[256,256]{1,0:T(8,128)(2,1)} %rotation_ref.1) | copy-start | bytes 393220
  26.5 18.1 %collective-permute-start.1 = (bf16[128,1024]{1,0:T(8,128)(2,1)S(1)}, bf16[128,1024]{1,0:T(8,128)(2,1)S(1)}, u32[]{:S(2)}, u32[]{:S(2)}) collective-permute-start(bf16[128,1024]{1,0:T(8,128)(2,1)S(1)} %get-tuple-element.20), channel_id=1, source_target_pairs={{0,4},{1,5},{2,6},{3,7},{4,0},{5,1},{6,2},{7,3},{8,12},{9,13},{10,... | collective-permute-start | bytes 786440 | tf_op jit(solution)/shard_map/ppermute | solution.py:271
  28.4 16.1 %collective-permute-start.2 = (bf16[128,1024]{1,0:T(8,128)(2,1)S(1)}, bf16[128,1024]{1,0:T(8,128)(2,1)S(1)}, u32[]{:S(2)}, u32[]{:S(2)}) collective-permute-start(bf16[128,1024]{1,0:T(8,128)(2,1)S(1)} %get-tuple-element.21), channel_id=1, source_target_pairs={{0,2},{1,3},{2,0},{3,1},{4,6},{5,7},{6,4},{7,5},{8,10},{9,11},{10,... | collective-permute-start | bytes 786440 | tf_op jit(solution)/shard_map/ppermute | solution.py:271
  29.9 20.7 %collective-permute-start.3 = (bf16[128,1024]{1,0:T(8,128)(2,1)S(1)}, bf16[128,1024]{1,0:T(8,128)(2,1)S(1)}, u32[]{:S(2)}, u32[]{:S(2)}) collective-permute-start(bf16[128,1024]{1,0:T(8,128)(2,1)S(1)} %get-tuple-element.22), channel_id=1, source_target_pairs={{0,6},{1,7},{2,4},{3,5},{4,2},{5,3},{6,0},{7,1},{8,14},{9,15},{10,... | collective-permute-start | bytes 786440 | tf_op jit(solution)/shard_map/ppermute | solution.py:271
  50.7 8.8 %collective-permute-start.4 = (bf16[64,1024]{1,0:T(8,128)(2,1)S(1)}, bf16[64,1024]{1,0:T(8,128)(2,1)S(1)}, u32[]{:S(2)}, u32[]{:S(2)}) collective-permute-start(bf16[64,1024]{1,0:T(8,128)(2,1)S(1)} %get-tuple-element.24), channel_id=1, source_target_pairs={{0,8},{1,9},{2,10},{3,11},{4,12},{5,13},{6,14},{7,15},{8,0},{9,1},... | collective-permute-start | bytes 393224 | tf_op jit(solution)/shard_map/ppermute | solution.py:271

commit v4 on v3

v4 whole, which is shorter than its diff:
```python
import functools

import jax
import jax.numpy as jnp
from jax import lax
from jax.experimental import pallas as pl
from jax.experimental.pallas import tpu as pltpu
from jax.sharding import PartitionSpec as P

CAP = 128
LANES = 128
NOTES = 16
SPAN = CAP + NOTES
CHUNK = 512
TILE = 256
GROUP = 4
VMEM_SOME = 24 * 1024 * 1024
VMEM_MOST = 57 * 1024 * 1024


def in_three(x):
    high = x.astype(jnp.bfloat16).astype(jnp.float32)
    rest = x - high
    middle = rest.astype(jnp.bfloat16).astype(jnp.float32)
    return high, middle, (rest - middle).astype(jnp.bfloat16).astype(jnp.float32)


def first_kernel(
    width, me_ref, e_hbm, basis_hbm, owner_ref, slot_ref,
    rows_hbm, keep_hbm, send_hbm,
    e_ref, basis_ref, y_ref, yb_ref, pick_ref, rows_ref, m_ref, list_ref, e_sem, basis_sem, rows_sem, block_sem,
):
    rows_here, wide = e_ref.shape
    feats = basis_ref.shape[1]
    chunks = rows_here // LANES
    parts = rows_here // CHUNK
    block = wide // width
    bits = width.bit_length() - 1

    e_copies = []
    for c in range(parts):
        at = pl.ds(c * CHUNK, CHUNK)
        e_copies.append(pltpu.make_async_copy(e_hbm.at[at], e_ref.at[at], e_sem.at[c]))
        e_copies[c].start()
        if c == 0:
            basis_copy = pltpu.make_async_copy(basis_hbm, basis_ref, basis_sem)
            basis_copy.start()

    owner = owner_ref[...]
    wanted = lax.broadcasted_iota(jnp.int32, (width, LANES), 0)
    hits = [jnp.where(owner[c:c + 1, :] == wanted, 1.0, 0.0) for c in range(chunks)]
    flat = jnp.concatenate(hits, 0).astype(jnp.bfloat16)
    up = lax.broadcasted_iota(jnp.int32, (LANES, LANES), 0)
    to = lax.broadcasted_iota(jnp.int32, (LANES, LANES), 1)
    before = jnp.where(up < to, 1.0, 0.0).astype(jnp.bfloat16)
    every = jnp.ones((LANES, LANES), jnp.bfloat16)
    within = jnp.dot(flat, before, preferred_element_type=jnp.float32)
    counts = jnp.dot(flat, every, preferred_element_type=jnp.float32)
    carry = jnp.zeros((width, LANES), jnp.float32)
    ranks, targets = [], []
    for c in range(chunks):
        at = slice(c * width, (c + 1) * width)
        ranks.append(jnp.sum(hits[c] * (within[at] + carry), 0, keepdims=True).astype(jnp.int32))
        carry = carry + counts[at]
        targets.append(owner[c:c + 1, :] * CAP + ranks[c])
    slot = slot_ref[...] + 1
    high, low = (slot >> 5).astype(jnp.float32), (slot & 31).astype(jnp.float32)
    spots = lax.broadcasted_iota(jnp.int32, (CAP, LANES), 0)
    placed = jnp.concatenate([jnp.where(ranks[c] == spots, 1.0, 0.0) for c in range(chunks)], 1).astype(jnp.bfloat16)
    digits = jnp.concatenate(
        [
            jnp.concatenate([hits[c] * high[c:c + 1, :] for c in range(chunks)], 1),
            jnp.concatenate([hits[c] * low[c:c + 1, :] for c in range(chunks)], 1),
        ],
        0,
    ).astype(jnp.bfloat16)
    found = lax.dot_general(digits, placed, (((1,), (1,)), ((), ())), preferred_element_type=jnp.float32)
    list_ref[:, :CAP] = found[:width]
    list_ref[:, CAP:] = found[width:]

    groups = width // GROUP
    held = pick_ref.shape[0]
    place = lax.broadcasted_iota(jnp.int32, (GROUP * CAP, LANES), 0).astype(jnp.int16)

    def pick_group(g, into):
        for c in range(chunks):
            aim = jnp.broadcast_to(targets[c] - g * (GROUP * CAP), (16, LANES)).astype(jnp.int16)
            aim = jnp.concatenate([aim] * (GROUP * CAP // 16), 0)
            pick_ref[into, :, c * LANES:(c + 1) * LANES] = jnp.where(
                aim == place, jnp.ones((), jnp.bfloat16), jnp.zeros((), jnp.bfloat16)
            )

    basis_copy.wait()
    sum_y = jnp.zeros((8, feats), jnp.float32)
    sum_e = jnp.zeros((8, wide), jnp.float32)
    for c in range(parts):
        at = slice(c * CHUNK, (c + 1) * CHUNK)
        e_copies[c].wait()
        rows = e_ref[at, :]
        y = jnp.dot(rows, basis_ref[...], preferred_element_type=jnp.float32)
        y_ref[at, :] = y
        sum_y = sum_y + jnp.sum(y.reshape(CHUNK // 8, 8, feats), 0)
        sum_e = sum_e + jnp.sum(rows.astype(jnp.float32).reshape(CHUNK // 8, 8, wide), 0)
        if c < held:
            pick_group(c, c)

    mean_y = jnp.sum(sum_y, 0, keepdims=True) / rows_here
    square = jnp.zeros((8, feats), jnp.float32)
    for c in range(parts):
        at = slice(c * CHUNK, (c + 1) * CHUNK)
        centred = y_ref[at, :] - mean_y
        square = square + jnp.sum((centred * centred).reshape(CHUNK // 8, 8, feats), 0)
        yb_ref[at, :] = centred.astype(jnp.bfloat16)
    mean = jnp.sum(sum_e, 0, keepdims=True) / rows_here
    common = [part[:, q * feats:(q + 1) * feats] for part in in_three(mean) for q in range(wide // feats)]
    common = jnp.concatenate(common + list(in_three(jnp.sum(square, 0, keepdims=True))), 0)

    def sort_group(g, into):
        rows = jnp.dot(pick_ref[into], yb_ref[...], preferred_element_type=jnp.float32).astype(jnp.bfloat16)
        for j in range(GROUP):
            base = pl.multiple_of((g * GROUP + j) * SPAN, 16)
            rows_ref[pl.ds(base, CAP), :] = rows[j * CAP:(j + 1) * CAP]
            notes = jnp.concatenate([common, list_ref[pl.ds(g * GROUP + j, 1), :]], 0)
            rows_ref[pl.ds(pl.multiple_of(base + CAP, 16), NOTES), :] = notes.astype(jnp.bfloat16)

    if groups <= held:
        for g in range(groups):
            sort_group(g, g)
    else:

        @pl.loop(0, groups)
        def _(g):
            pick_group(g, 0)
            sort_group(g, 0)

    whole_copy = pltpu.make_async_copy(rows_ref, rows_hbm, rows_sem)
    whole_copy.start()

    me = me_ref[0]
    copies = []
    for t in range(wide // TILE):
        rows = slice(t * TILE, (t + 1) * TILE)
        product = lax.dot_general(
            e_ref[:, rows], e_ref[...], (((0,), (0,)), ((), ())), preferred_element_type=jnp.float32
        )
        down = jnp.transpose(jnp.broadcast_to(mean[:, rows] * rows_here, (LANES, TILE)))
        for j in range(wide // LANES):
            across = slice(j * LANES, (j + 1) * LANES)
            m_ref[rows, across] = (product[:, across] - down * mean[:, across]).astype(jnp.bfloat16)
        for pair in range(TILE // block // 2):
            first = t * (TILE // block) + 2 * pair
            apart = (first ^ me) >> 1
            spot = 0
            for k in range(bits - 1):
                spot = spot + (((apart >> k) & 1) << (bits - 2 - k))
            at = pl.ds(pl.multiple_of(spot * block, block), block)
            kept = pl.multiple_of((first + (me & 1)) * block, block)
            sent = pl.multiple_of((first + 1 - (me & 1)) * block, block)
            for here, there in ((kept, keep_hbm), (sent, send_hbm)):
                copy = pltpu.make_async_copy(m_ref.at[pl.ds(here, block)], there.at[at], block_sem.at[len(copies)])
                copy.start()
                copies.append(copy)
    for copy in copies:
        copy.wait()
    whole_copy.wait()


def first(width, me, embeddings, basis, list_owner, list_slot):
    rows_here, wide = embeddings.shape
    feats = basis.shape[1]
    lanes = rows_here // LANES
    slots = width * SPAN
    groups = width // GROUP
    vmem, anywhere = pl.BlockSpec(memory_space=pltpu.VMEM), pl.BlockSpec(memory_space=pl.ANY)
    return pl.pallas_call(
        functools.partial(first_kernel, width),
        in_specs=[pl.BlockSpec(memory_space=pltpu.SMEM), anywhere, anywhere, vmem, vmem],
        out_specs=[anywhere] * 3,
        out_shape=[jax.ShapeDtypeStruct((slots, feats), jnp.bfloat16)]
        + [jax.ShapeDtypeStruct((wide // 2, wide), jnp.bfloat16)] * 2,
        scratch_shapes=[
            pltpu.VMEM((rows_here, wide), jnp.bfloat16),
            pltpu.VMEM((wide, feats), jnp.bfloat16),
            pltpu.VMEM((rows_here, feats), jnp.float32),
            pltpu.VMEM((rows_here, feats), jnp.bfloat16),
            pltpu.VMEM((groups if groups <= rows_here // CHUNK else 1, GROUP * CAP, rows_here), jnp.bfloat16),
            pltpu.VMEM((slots, feats), jnp.bfloat16),
            pltpu.VMEM((wide, wide), jnp.bfloat16),
            pltpu.VMEM((width, 2 * CAP), jnp.float32),
            pltpu.SemaphoreType.DMA((rows_here // CHUNK,)),
            pltpu.SemaphoreType.DMA,
            pltpu.SemaphoreType.DMA,
            pltpu.SemaphoreType.DMA((width,)),
        ],
        compiler_params=pltpu.CompilerParams(vmem_limit_bytes=VMEM_MOST),
        cost_estimate=pl.CostEstimate(
            flops=2 * rows_here * (feats * (wide + slots) + wide * wide),
            bytes_accessed=2 * rows_here * wide + 2 * slots * feats + 2 * wide * wide,
            transcendentals=0,
        ),
        name="first",
    )(me.reshape(1), embeddings, basis, list_owner.reshape(lanes, LANES), list_slot.reshape(lanes, LANES))


def add_kernel(pieces, keep_ref, *refs):
    came, outs = refs[:-pieces], refs[-pieces:]
    size = outs[0].shape[0]
    for p in range(pieces):
        at = slice(p * size, (p + 1) * size)
        held = keep_ref[at].astype(jnp.float32)
        for ref in came:
            held = held + ref[at].astype(jnp.float32)
        outs[p][...] = held.astype(outs[p].dtype)


def add_and_split(keep, came, pieces):
    rows, wide = keep.shape
    vmem = pl.BlockSpec(memory_space=pltpu.VMEM)
    return pl.pallas_call(
        functools.partial(add_kernel, pieces),
        in_specs=[vmem] * (1 + len(came)),
        out_specs=[vmem] * pieces,
        out_shape=[
            jax.ShapeDtypeStruct((rows // pieces, wide), jnp.float32 if p == 0 else jnp.bfloat16) for p in range(pieces)
        ],
        compiler_params=pltpu.CompilerParams(vmem_limit_bytes=VMEM_SOME),
        cost_estimate=pl.CostEstimate(flops=2 * rows * wide, bytes_accessed=10 * rows * wide, transcendentals=0),
        name="add_and_split",
    )(keep, *came)


def partners(width, apart):
    return [(i, i ^ apart) for i in range(width)]


def halving_stages(width):
    strides = [1 << k for k in range(width.bit_length() - 1)]
    return [strides[:1], strides[1:3]] + [[s] for s in strides[3:]]


def reduce_blocks(width, keep, send):
    stages = halving_stages(width)
    out = [send]
    for n, stage in enumerate(stages):
        came = []
        for p in range(1, 1 << len(stage)):
            apart = sum(s for k, s in enumerate(stage) if (p >> (len(stage) - 1 - k)) & 1)
            came.append(lax.ppermute(out[p - 1], "wide", partners(width, apart)))
        if n + 1 < len(stages):
            keep, *out = add_and_split(keep, came, 1 << len(stages[n + 1]))
    return keep, came


def encode_kernel(total, me_ref, got_ref, all_ref, basis_ref, centroid_ref, rotation_ref, out_ref, between_ref, delta_ref, scale_ref, list_ref, apart_ref):
    step = pl.program_id(0)
    width = delta_ref.shape[0]
    feats = out_ref.shape[1]
    owned = centroid_ref.shape[0]
    wide = basis_ref.shape[0]
    block = wide // width
    share = total // width

    @pl.when(step == 0)
    def _():
        notes = jnp.concatenate([all_ref[s * SPAN + CAP:(s + 1) * SPAN, :] for s in range(width)], 0)
        size = width * NOTES
        to = lax.broadcasted_iota(jnp.int32, (size, size), 0)
        of = lax.broadcasted_iota(jnp.int32, (size, size), 1)
        turn = jnp.where((to % width) * NOTES + to // width == of, 1.0, 0.0).astype(jnp.bfloat16)
        turned = jnp.dot(turn, notes, preferred_element_type=jnp.float32)
        row = [turned[r * width:(r + 1) * width] for r in range(NOTES)]
        quarters = wide // feats
        shifts = jnp.zeros((width, feats), jnp.float32)
        for q in range(quarters):
            parts = [row[p * quarters + q] for p in range(3)]
            mean = parts[0] + (parts[1] + parts[2])
            apart_ref[:, q * feats:(q + 1) * feats] = mean - jnp.mean(mean, 0, keepdims=True)
            terms = jnp.dot(
                jnp.concatenate(parts, 0).astype(jnp.bfloat16),
                basis_ref[q * feats:(q + 1) * feats, :],
                preferred_element_type=jnp.float32,
            )
            shifts = shifts + (terms[:width] + (terms[width:2 * width] + terms[2 * width:]))
        square = row[3 * quarters] + (row[3 * quarters + 1] + row[3 * quarters + 2])
        delta = shifts - jnp.mean(shifts, 0, keepdims=True)
        variance = jnp.sum(square + share * (delta * delta), 0, keepdims=True) / total
        scale_ref[...] = lax.rsqrt(variance + 1e-05)
        delta_ref[...] = delta
        digits = row[NOTES - 1]
        list_ref[...] = digits[:, :CAP] * 32.0 + digits[:, CAP:] - 1.0

        me = me_ref[0]
        first = me * block
        near = apart_ref[:, pl.ds(pl.multiple_of(first // LANES * LANES, LANES), LANES)]
        near = pltpu.roll(near, (LANES - first % LANES) % LANES, 1)[:, :block]
        between_ref[...] = share * lax.dot_general(
            near,
            apart_ref[...],
            (((0,), (0,)), ((), ())),
            precision=lax.Precision.HIGHEST,
            preferred_element_type=jnp.float32,
        )

    columns = jnp.transpose(list_ref[pl.ds(step * GROUP, GROUP), :])
    names = lax.broadcasted_iota(jnp.int32, (CAP, owned), 1).astype(jnp.int16)
    hits, projected, held = [], [], []
    for s in range(GROUP):
        listed = jnp.broadcast_to(columns[:, s:s + 1], (CAP, LANES))
        held.append(jnp.concatenate([listed] * (feats // LANES), 1) >= 0)
        wanted = jnp.concatenate([listed.astype(jnp.int32).astype(jnp.int16)] * (owned // LANES), 1)
        hits.append(jnp.where(wanted == names, jnp.ones((), jnp.bfloat16), jnp.zeros((), jnp.bfloat16)))
        rows = got_ref[s * SPAN:s * SPAN + CAP, :].astype(jnp.float32)
        projected.append((rows + delta_ref[pl.ds(step * GROUP + s, 1), :]) * scale_ref[...])
    centre = jnp.dot(jnp.concatenate(hits, 0), centroid_ref[...], preferred_element_type=jnp.float32)
    residual = jnp.where(jnp.concatenate(held, 0), jnp.concatenate(projected, 0) - centre, 0.0)
    out_ref[...] = jnp.dot(
        residual.astype(jnp.bfloat16), rotation_ref[...], preferred_element_type=jnp.float32
    ).astype(jnp.bfloat16)


def encode(width, total, me, got, basis, centroids, rotation):
    wide, feats = basis.shape
    owned = centroids.shape[0]
    slots = width * CAP
    whole = lambda i: (0, 0)
    return pl.pallas_call(
        functools.partial(encode_kernel, total),
        grid=(width // GROUP,),
        in_specs=[
            pl.BlockSpec(memory_space=pltpu.SMEM),
            pl.BlockSpec((GROUP * SPAN, feats), lambda i: (i, 0)),
            pl.BlockSpec((width * SPAN, feats), whole),
            pl.BlockSpec((wide, feats), whole),
            pl.BlockSpec((owned, feats), whole),
            pl.BlockSpec((feats, feats), whole),
        ],
        out_specs=[
            pl.BlockSpec((GROUP * CAP, feats), lambda i: (i, 0)),
            pl.BlockSpec((wide // width, wide), whole),
        ],
        out_shape=[
            jax.ShapeDtypeStruct((slots, feats), jnp.bfloat16),
            jax.ShapeDtypeStruct((wide // width, wide), jnp.float32),
        ],
        scratch_shapes=[
            pltpu.VMEM((width, feats), jnp.float32),
            pltpu.VMEM((1, feats), jnp.float32),
            pltpu.VMEM((width, CAP), jnp.float32),
            pltpu.VMEM((width, wide), jnp.float32),
        ],
        compiler_params=pltpu.CompilerParams(vmem_limit_bytes=VMEM_SOME),
        cost_estimate=pl.CostEstimate(
            flops=2 * slots * feats * (owned + feats), bytes_accessed=4 * slots * feats, transcendentals=0
        ),
        name="encode",
    )(me.reshape(1), got, got, basis, centroids, rotation)


def local(embeddings, basis, list_owner, list_slot, centroids, rotation):
    width = lax.axis_size("wide")
    me = lax.axis_index("wide")
    rows_here, wide = embeddings.shape
    feats = basis.shape[1]
    total = rows_here * width

    rows, keep, send = first(width, me, embeddings, basis, list_owner, list_slot)
    got = lax.all_to_all(rows.reshape(width, SPAN, feats), "wide", split_axis=0, concat_axis=0, tiled=True)
    keep, came = reduce_blocks(width, keep, send)
    encoded, between = encode(width, total, me, got.reshape(width * SPAN, feats), basis, centroids, rotation)
    for block in came:
        keep = keep + block.astype(jnp.float32)
    covariance = (keep + between) / total
    return (encoded, covariance)


def solution(mesh):
    in_specs = (
        P(("groups", "wide"), None),
        P(),
        P(("groups", "wide")),
        P(("groups", "wide")),
        P("wide", None),
        P(),
    )
    out_specs = (P(("groups", "wide"), None), P(("groups", "wide"), None))
    return jax.shard_map(local, mesh=mesh, in_specs=in_specs, out_specs=out_specs, check_vma=False)
```

time: 60.6 us -> 67.1 us (1.11)
  waiting for transfers between devices: 24.6 us -> 31.7 us
    ppermute x5, waiting for transfers between devices: 24.6 us -> 31.7 us  [reduce_blocks(): came.append(lax.ppermute(out[p - 1], 'wide', partners(width, apart)))]
    pallas_call x2 -> x1, Pallas kernels: 15.4 us -> 14.7 us  [first(): pl.pallas_call(functools.partial(first_kernel, width), in_specs=[pl.Block...]
  transfers between devices with their start and end apart: 6 -> 6, of which waited for: 4 -> 4; matrix products, arithmetic and copies ran while one was open for 0% -> 0% of each run, Pallas kernels for 20% -> 7%
where the time goes in v4:
time: 67.1 us; the launch traced here: 66.8 us
  waiting for transfers between devices  31.7 us (47%)
  Pallas kernels  19.5 us (29%)
  starting transfers between devices  14.1 us (21%)
  other arithmetic  0.74 us (1%)
  between operations  0.72 us (1%)
    ppermute x5, waiting for transfers between devices, reduce_blocks(): came.append(lax.ppermute(out[p - 1], 'wide', partners(width, apart)))  31.7 us
    pallas_call x1, Pallas kernels, first(): pl.pallas_call(functools.partial(first_kernel, width), in_specs=[pl.Block...  14.7 us
    all_to_all x1, starting transfers between devices, local(): lax.all_to_all(rows.reshape(width, SPAN, feats), 'wide', split_axis=0, co...  7.54 us
    ppermute x5, starting transfers between devices, reduce_blocks(): came.append(lax.ppermute(out[p - 1], 'wide', partners(width, apart)))  6.61 us
    pallas_call x1, Pallas kernels, encode(): pl.pallas_call(functools.partial(encode_kernel, total), grid=(width // GR...  4.48 us
  transfers between devices with their start and end apart: 6, of which 4 were waited for; matrix products, arithmetic and copies ran while one was open for 0% of the time, Pallas kernels for 7%

profile of v4, /device:TPU:0, one launch (start us, length us, event | category | flops | bytes accessed | tf_op | source)
XLA Modules:
  0.0 66.8 jit_solution(8811357706580271548)
XLA Ops:
  0.6 14.7 %first.1 = (bf16[2304,256]{1,0:T(8,128)(2,1)}, bf16[512,1024]{1,0:T(8,128)(2,1)}, bf16[512,1024]{1,0:T(8,128)(2,1)}) custom-call(s32[1]{0:T(128)} %bitcast.me_ref, bf16[2048,1024]{1,0:T(8,128)(2,1)} %e_hbm.1, bf16[1024,256]{1,0:T(8,128)(2,1)} %basis_ref.1, s32[16,128]{1,0:T(8,128)} %bitcast.8, s32[16,128]{1,0:T(8,128)} %bitcast.9), custom_call_target="tpu_custom_call" | custom-call | flops 7784628224 | bytes 7471104 | tf_op jit(solution)/shard_map/first/pallas_call | solution.py:175
  15.3 0.0 copy-start.4
  15.3 0.0 copy-start
  15.3 7.5 %all-to-all-start = ((bf16[16,144,256]{2,1,0:T(8,128)(2,1)}), bf16[16,144,256]{2,1,0:T(8,128)(2,1)S(1)}, u32[]{:S(2)}, u32[]{:S(2)}) async-start(bf16[16,144,256]{2,1,0:T(8,128)(2,1)} %bitcast.7), calls=%async_computation | async-start | bytes 2359296 | tf_op jit(solution)/shard_map/all_to_all | solution.py:367
  22.9 0.0 copy-done.4
  22.9 0.5 collective-permute-start
  23.4 2.3 %collective-permute-done.refs_0_ = bf16[512,1024]{1,0:T(8,128)(2,1)S(1)} collective-permute-done((bf16[512,1024]{1,0:T(8,128)(2,1)S(1)}, bf16[512,1024]{1,0:T(8,128)(2,1)S(1)}, u32[]{:S(2)}, u32[]{:S(2)}) %collective-permute-start) | collective-permute-done | bytes 1048608 | tf_op jit(solution)/shard_map/ppermute | solution.py:248
  25.7 0.0 copy-done
  25.7 0.2 add_and_split.2
  25.9 0.0 copy-start.1
  25.9 0.0 copy-start.2
  25.9 0.0 copy-start.3
  25.9 2.0 %collective-permute-start.1 = (bf16[128,1024]{1,0:T(8,128)(2,1)S(1)}, bf16[128,1024]{1,0:T(8,128)(2,1)S(1)}, u32[]{:S(2)}, u32[]{:S(2)}) collective-permute-start(bf16[128,1024]{1,0:T(8,128)(2,1)S(1)} %get-tuple-element.18), channel_id=1, source_target_pairs={{0,4},{1,5},{2,6},{3,7},{4,0},{5,1},{6,2},{7,3},{8,12},{9,13},{10,... | collective-permute-start | bytes 786440 | tf_op jit(solution)/shard_map/ppermute | solution.py:248
  27.9 1.5 %collective-permute-start.2 = (bf16[128,1024]{1,0:T(8,128)(2,1)S(1)}, bf16[128,1024]{1,0:T(8,128)(2,1)S(1)}, u32[]{:S(2)}, u32[]{:S(2)}) collective-permute-start(bf16[128,1024]{1,0:T(8,128)(2,1)S(1)} %get-tuple-element.19), channel_id=1, source_target_pairs={{0,2},{1,3},{2,0},{3,1},{4,6},{5,7},{6,4},{7,5},{8,10},{9,11},{10,... | collective-permute-start | bytes 786440 | tf_op jit(solution)/shard_map/ppermute | solution.py:248
  29.4 0.1 collective-permute-start.3
  29.5 21.6 %collective-permute-done.1.refs_0_ = bf16[128,1024]{1,0:T(8,128)(2,1)S(1)} collective-permute-done((bf16[128,1024]{1,0:T(8,128)(2,1)S(1)}, bf16[128,1024]{1,0:T(8,128)(2,1)S(1)}, u32[]{:S(2)}, u32[]{:S(2)}) %collective-permute-start.1) | collective-permute-done | bytes 262176 | tf_op jit(solution)/shard_map/ppermute | solution.py:248
  51.1 0.0 collective-permute-done.2.refs_1_
  51.1 6.1 %collective-permute-done.3.refs_2_ = bf16[128,1024]{1,0:T(8,128)(2,1)S(1)} collective-permute-done((bf16[128,1024]{1,0:T(8,128)(2,1)S(1)}, bf16[128,1024]{1,0:T(8,128)(2,1)S(1)}, u32[]{:S(2)}, u32[]{:S(2)}) %collective-permute-start.3) | collective-permute-done | bytes 262176 | tf_op jit(solution)/shard_map/ppermute | solution.py:248
  57.2 0.1 add_and_split.3
  57.3 2.6 %collective-permute-start.4 = (bf16[64,1024]{1,0:T(8,128)(2,1)S(1)}, bf16[64,1024]{1,0:T(8,128)(2,1)S(1)}, u32[]{:S(2)}, u32[]{:S(2)}) collective-permute-start(bf16[64,1024]{1,0:T(8,128)(2,1)S(1)} %get-tuple-element.22), channel_id=1, source_target_pairs={{0,8},{1,9},{2,10},{3,11},{4,12},{5,13},{6,14},{7,15},{8,0},{9,1},... | collective-permute-start | bytes 393224 | tf_op jit(solution)/shard_map/ppermute | solution.py:248
  59.9 0.0 all-to-all-done
  59.9 0.0 copy-done.1
  59.9 0.0 copy-done.2
  59.9 0.0 copy-done.3
  59.9 4.5 %encode.1 = (bf16[2048,256]{1,0:T(8,128)(2,1)}, f32[64,1024]{1,0:T(8,128)S(1)}) custom-call(s32[1]{0:T(128)} %bitcast.me_ref, bf16[2304,256]{1,0:T(8,128)(2,1)S(1)} %bitcast.5, bf16[2304,256]{1,0:T(8,128)(2,1)S(1)} %bitcast.6, bf16[1024,256]{1,0:T(8,128)(2,1)S(1)} %copy-done.1, bf16[1024,256]{1,0:T(8,128)(2,1)S(1)} %copy-done.2, bf16[256,256]{1,0:T(8,128)(2,1)S(1)} %copy-done.3), custom_call_target="tpu_custom_call" | custom-call | flops 1342177280 | bytes 2097152 | tf_op jit(solution)/shard_map/encode/pallas_call | solution.py:326
  64.4 1.7 %collective-permute-done.4 = bf16[64,1024]{1,0:T(8,128)(2,1)S(1)} collective-permute-done((bf16[64,1024]{1,0:T(8,128)(2,1)S(1)}, bf16[64,1024]{1,0:T(8,128)(2,1)S(1)}, u32[]{:S(2)}, u32[]{:S(2)}) %collective-permute-start.4) | collective-permute-done | bytes 131104 | tf_op jit(solution)/shard_map/ppermute | solution.py:248
  66.1 0.7 %add_multiply_fusion = f32[64,1024]{1,0:T(8,128)} fusion(f32[64,1024]{1,0:T(8,128)S(1)} %get-tuple-element.23, f32[64,1024]{1,0:T(8,128)S(1)} %get-tuple-element.21, bf16[64,1024]{1,0:T(8,128)(2,1)S(1)} %collective-permute-done.4), kind=kLoop, calls=%fused_computation | loop fusion | flops 262144 | bytes 917504 | tf_op jit(solution)/shard_map/div | solution.py:372
Async XLA Ops:
  15.3 7.6 %copy-start.4 = (bf16[512,1024]{1,0:T(8,128)(2,1)S(1)}, bf16[512,1024]{1,0:T(8,128)(2,1)}, u32[]{:S(2)}) copy-start(bf16[512,1024]{1,0:T(8,128)(2,1)} %get-tuple-element.16) | copy-start | bytes 3145732
  15.3 10.3 %copy-start = (bf16[512,1024]{1,0:T(8,128)(2,1)S(1)}, bf16[512,1024]{1,0:T(8,128)(2,1)}, u32[]{:S(2)}) copy-start(bf16[512,1024]{1,0:T(8,128)(2,1)} %get-tuple-element.15.keep_ref) | copy-start | bytes 3145732
  15.3 44.5 %all-to-all-start = ((bf16[16,144,256]{2,1,0:T(8,128)(2,1)}), bf16[16,144,256]{2,1,0:T(8,128)(2,1)S(1)}, u32[]{:S(2)}, u32[]{:S(2)}) async-start(bf16[16,144,256]{2,1,0:T(8,128)(2,1)} %bitcast.7), calls=%async_computation | async-start | bytes 2359296 | tf_op jit(solution)/shard_map/all_to_all | solution.py:367
  22.9 2.8 %collective-permute-start = (bf16[512,1024]{1,0:T(8,128)(2,1)S(1)}, bf16[512,1024]{1,0:T(8,128)(2,1)S(1)}, u32[]{:S(2)}, u32[]{:S(2)}) collective-permute-start(bf16[512,1024]{1,0:T(8,128)(2,1)S(1)} %copy-done.4), channel_id=1, source_target_pairs={{0,1},{1,0},{2,3},{3,2},{4,5},{5,4},{6,7},{7,6},{8,9},{9,8},{10,11... | collective-permute-start | bytes 3145736 | tf_op jit(solution)/shard_map/ppermute | solution.py:248
  25.9 34.0 %copy-start.1 = (bf16[1024,256]{1,0:T(8,128)(2,1)S(1)}, bf16[1024,256]{1,0:T(8,128)(2,1)}, u32[]{:S(2)}) copy-start(bf16[1024,256]{1,0:T(8,128)(2,1)} %basis_ref.1) | copy-start | bytes 1572868
  25.9 33.9 %copy-start.2 = (bf16[1024,256]{1,0:T(8,128)(2,1)S(1)}, bf16[1024,256]{1,0:T(8,128)(2,1)}, u32[]{:S(2)}) copy-start(bf16[1024,256]{1,0:T(8,128)(2,1)} %centroid_ref.1) | copy-start | bytes 1572868
  25.9 33.9 %copy-start.3 = (bf16[256,256]{1,0:T(8,128)(2,1)S(1)}, bf16[256,256]{1,0:T(8,128)(2,1)}, u32[]{:S(2)}) copy-start(bf16[256,256]{1,0:T(8,128)(2,1)} %rotation_ref.1) | copy-start | bytes 393220
  25.9 25.2 %collective-permute-start.1 = (bf16[128,1024]{1,0:T(8,128)(2,1)S(1)}, bf16[128,1024]{1,0:T(8,128)(2,1)S(1)}, u32[]{:S(2)}, u32[]{:S(2)}) collective-permute-start(bf16[128,1024]{1,0:T(8,128)(2,1)S(1)} %get-tuple-element.18), channel_id=1, source_target_pairs={{0,4},{1,5},{2,6},{3,7},{4,0},{5,1},{6,2},{7,3},{8,12},{9,13},{10,... | collective-permute-start | bytes 786440 | tf_op jit(solution)/shard_map/ppermute | solution.py:248
  27.9 23.2 %collective-permute-start.2 = (bf16[128,1024]{1,0:T(8,128)(2,1)S(1)}, bf16[128,1024]{1,0:T(8,128)(2,1)S(1)}, u32[]{:S(2)}, u32[]{:S(2)}) collective-permute-start(bf16[128,1024]{1,0:T(8,128)(2,1)S(1)} %get-tuple-element.19), channel_id=1, source_target_pairs={{0,2},{1,3},{2,0},{3,1},{4,6},{5,7},{6,4},{7,5},{8,10},{9,11},{10,... | collective-permute-start | bytes 786440 | tf_op jit(solution)/shard_map/ppermute | solution.py:248
  29.4 27.8 %collective-permute-start.3 = (bf16[128,1024]{1,0:T(8,128)(2,1)S(1)}, bf16[128,1024]{1,0:T(8,128)(2,1)S(1)}, u32[]{:S(2)}, u32[]{:S(2)}) collective-permute-start(bf16[128,1024]{1,0:T(8,128)(2,1)S(1)} %get-tuple-element.20), channel_id=1, source_target_pairs={{0,6},{1,7},{2,4},{3,5},{4,2},{5,3},{6,0},{7,1},{8,14},{9,15},{10,... | collective-permute-start | bytes 786440 | tf_op jit(solution)/shard_map/ppermute | solution.py:248
  57.3 8.8 %collective-permute-start.4 = (bf16[64,1024]{1,0:T(8,128)(2,1)S(1)}, bf16[64,1024]{1,0:T(8,128)(2,1)S(1)}, u32[]{:S(2)}, u32[]{:S(2)}) collective-permute-start(bf16[64,1024]{1,0:T(8,128)(2,1)S(1)} %get-tuple-element.22), channel_id=1, source_target_pairs={{0,8},{1,9},{2,10},{3,11},{4,12},{5,13},{6,14},{7,15},{8,0},{9,1},... | collective-permute-start | bytes 393224 | tf_op jit(solution)/shard_map/ppermute | solution.py:248

commit v5 on v4

v5 whole, which is shorter than its diff:
```python
import functools

import jax
import jax.numpy as jnp
from jax import lax
from jax.experimental import pallas as pl
from jax.experimental.pallas import tpu as pltpu
from jax.sharding import PartitionSpec as P

CAP = 128
LANES = 128
NOTES = 16
SPAN = CAP + NOTES
CHUNK = 512
TILE = 256
GROUP = 4
VMEM_SOME = 24 * 1024 * 1024
VMEM_MOST = 57 * 1024 * 1024
VMEM_MUCH = 48 * 1024 * 1024


def in_three(x):
    high = x.astype(jnp.bfloat16).astype(jnp.float32)
    rest = x - high
    middle = rest.astype(jnp.bfloat16).astype(jnp.float32)
    return high, middle, (rest - middle).astype(jnp.bfloat16).astype(jnp.float32)


def moments_kernel(width, me_ref, e_hbm, keep_hbm, send_hbm, mean_ref, e_ref, m_ref, e_sem, block_sem):
    rows_here, wide = e_ref.shape
    block = wide // width
    bits = width.bit_length() - 1
    parts = rows_here // CHUNK
    tiles = wide // TILE
    e_copies = []
    for c in range(parts):
        at = pl.ds(c * CHUNK, CHUNK)
        e_copies.append(pltpu.make_async_copy(e_hbm.at[at], e_ref.at[at], e_sem.at[c]))
        e_copies[c].start()
    me = me_ref[0]
    copies = []
    for t in range(tiles):
        rows, columns = slice(t * TILE, (t + 1) * TILE), slice(t * TILE, wide)
        if t == 0:
            product = jnp.zeros((TILE, wide), jnp.float32)
            sum_e = jnp.zeros((8, wide), jnp.float32)
            for c in range(parts):
                e_copies[c].wait()
                at = slice(c * CHUNK, (c + 1) * CHUNK)
                product = product + lax.dot_general(
                    e_ref[at, rows], e_ref[at, :], (((0,), (0,)), ((), ())), preferred_element_type=jnp.float32
                )
                sum_e = sum_e + jnp.sum(e_ref[at, :].astype(jnp.float32).reshape(CHUNK // 8, 8, wide), 0)
            mean = jnp.sum(sum_e, 0, keepdims=True) / rows_here
            mean_ref[...] = mean
        else:
            product = lax.dot_general(
                e_ref[:, rows], e_ref[:, columns], (((0,), (0,)), ((), ())), preferred_element_type=jnp.float32
            )
        down = jnp.transpose(jnp.broadcast_to(mean[:, rows] * rows_here, (LANES, TILE)))
        for u in range(t, tiles):
            pieces = []
            for j in range(u * TILE // LANES, (u + 1) * TILE // LANES):
                across = slice(j * LANES, (j + 1) * LANES)
                within = slice(j * LANES - t * TILE, (j + 1) * LANES - t * TILE)
                pieces.append((product[:, within] - down * mean[:, across]).astype(jnp.bfloat16))
            piece = jnp.concatenate(pieces, 1)
            other = slice(u * TILE, (u + 1) * TILE)
            m_ref[rows, other] = piece
            if u > t:
                m_ref[other, rows] = jnp.transpose(piece)
        for pair in range(TILE // block // 2):
            first = t * (TILE // block) + 2 * pair
            apart = (first ^ me) >> 1
            spot = 0
            for k in range(bits - 1):
                spot = spot + (((apart >> k) & 1) << (bits - 2 - k))
            at = pl.ds(pl.multiple_of(spot * block, block), block)
            kept = pl.multiple_of((first + (me & 1)) * block, block)
            sent = pl.multiple_of((first + 1 - (me & 1)) * block, block)
            for here, there in ((kept, keep_hbm), (sent, send_hbm)):
                copy = pltpu.make_async_copy(m_ref.at[pl.ds(here, block)], there.at[at], block_sem.at[len(copies)])
                copy.start()
                copies.append(copy)
    for copy in copies:
        copy.wait()


def moments(width, me, embeddings):
    rows_here, wide = embeddings.shape
    anywhere = pl.BlockSpec(memory_space=pl.ANY)
    return pl.pallas_call(
        functools.partial(moments_kernel, width),
        in_specs=[pl.BlockSpec(memory_space=pltpu.SMEM), anywhere],
        out_specs=[anywhere, anywhere, pl.BlockSpec(memory_space=pltpu.VMEM)],
        out_shape=[jax.ShapeDtypeStruct((wide // 2, wide), jnp.bfloat16)] * 2 + [jax.ShapeDtypeStruct((1, wide), jnp.float32)],
        scratch_shapes=[
            pltpu.VMEM((rows_here, wide), jnp.bfloat16),
            pltpu.VMEM((wide, wide), jnp.bfloat16),
            pltpu.SemaphoreType.DMA((rows_here // CHUNK,)),
            pltpu.SemaphoreType.DMA((width,)),
        ],
        compiler_params=pltpu.CompilerParams(vmem_limit_bytes=VMEM_MOST),
        cost_estimate=pl.CostEstimate(
            flops=2 * rows_here * wide * wide, bytes_accessed=2 * rows_here * wide + 2 * wide * wide, transcendentals=0
        ),
        name="moments",
    )(me.reshape(1), embeddings)


def project_kernel(
    width, e_hbm, basis_ref, owner_ref, slot_ref, mean_ref,
    yb_ref, target_ref, list_ref, notes_ref,
    e_ref, y_ref, e_sem,
):
    rows_here, wide = e_ref.shape
    feats = basis_ref.shape[1]
    chunks = rows_here // LANES
    parts = rows_here // CHUNK

    e_copies = []
    for c in range(parts):
        at = pl.ds(c * CHUNK, CHUNK)
        e_copies.append(pltpu.make_async_copy(e_hbm.at[at], e_ref.at[at], e_sem.at[c]))
        e_copies[c].start()

    owner = owner_ref[...]
    wanted = lax.broadcasted_iota(jnp.int32, (width, LANES), 0)
    hits = [jnp.where(owner[c:c + 1, :] == wanted, 1.0, 0.0) for c in range(chunks)]
    flat = jnp.concatenate(hits, 0).astype(jnp.bfloat16)
    up = lax.broadcasted_iota(jnp.int32, (LANES, LANES), 0)
    to = lax.broadcasted_iota(jnp.int32, (LANES, LANES), 1)
    before = jnp.where(up < to, 1.0, 0.0).astype(jnp.bfloat16)
    every = jnp.ones((LANES, LANES), jnp.bfloat16)
    within = jnp.dot(flat, before, preferred_element_type=jnp.float32)
    counts = jnp.dot(flat, every, preferred_element_type=jnp.float32)
    carry = jnp.zeros((width, LANES), jnp.float32)
    ranks = []
    for c in range(chunks):
        at = slice(c * width, (c + 1) * width)
        ranks.append(jnp.sum(hits[c] * (within[at] + carry), 0, keepdims=True).astype(jnp.int32))
        carry = carry + counts[at]
        target_ref[c:c + 1, :] = owner[c:c + 1, :] * CAP + ranks[c]
    slot = slot_ref[...] + 1
    high, low = (slot >> 5).astype(jnp.float32), (slot & 31).astype(jnp.float32)
    spots = lax.broadcasted_iota(jnp.int32, (CAP, LANES), 0)
    placed = jnp.concatenate([jnp.where(ranks[c] == spots, 1.0, 0.0) for c in range(chunks)], 1).astype(jnp.bfloat16)
    digits = jnp.concatenate(
        [
            jnp.concatenate([hits[c] * high[c:c + 1, :] for c in range(chunks)], 1),
            jnp.concatenate([hits[c] * low[c:c + 1, :] for c in range(chunks)], 1),
        ],
        0,
    ).astype(jnp.bfloat16)
    found = lax.dot_general(digits, placed, (((1,), (1,)), ((), ())), preferred_element_type=jnp.float32)
    list_ref[:, :CAP] = found[:width]
    list_ref[:, CAP:] = found[width:]

    sum_y = jnp.zeros((8, feats), jnp.float32)
    for c in range(parts):
        at = slice(c * CHUNK, (c + 1) * CHUNK)
        e_copies[c].wait()
        y = jnp.dot(e_ref[at, :], basis_ref[...], preferred_element_type=jnp.float32)
        y_ref[at, :] = y
        sum_y = sum_y + jnp.sum(y.reshape(CHUNK // 8, 8, feats), 0)
    mean_y = jnp.sum(sum_y, 0, keepdims=True) / rows_here
    square = jnp.zeros((8, feats), jnp.float32)
    for c in range(parts):
        at = slice(c * CHUNK, (c + 1) * CHUNK)
        centred = y_ref[at, :] - mean_y
        square = square + jnp.sum((centred * centred).reshape(CHUNK // 8, 8, feats), 0)
        yb_ref[at, :] = centred.astype(jnp.bfloat16)
    notes = [part[:, q * feats:(q + 1) * feats] for part in in_three(mean_ref[...]) for q in range(wide // feats)]
    notes = notes + list(in_three(jnp.sum(square, 0, keepdims=True)))
    notes_ref[:len(notes), :] = jnp.concatenate(notes, 0)
    notes_ref[len(notes):, :] = jnp.zeros((NOTES - len(notes), feats), jnp.float32)


def project(width, embeddings, basis, list_owner, list_slot, mean):
    rows_here, wide = embeddings.shape
    feats = basis.shape[1]
    lanes = rows_here // LANES
    vmem, anywhere = pl.BlockSpec(memory_space=pltpu.VMEM), pl.BlockSpec(memory_space=pl.ANY)
    return pl.pallas_call(
        functools.partial(project_kernel, width),
        in_specs=[anywhere, vmem, vmem, vmem, vmem],
        out_specs=[vmem] * 4,
        out_shape=[
            jax.ShapeDtypeStruct((rows_here, feats), jnp.bfloat16),
            jax.ShapeDtypeStruct((lanes, LANES), jnp.int32),
            jax.ShapeDtypeStruct((width, 2 * CAP), jnp.float32),
            jax.ShapeDtypeStruct((NOTES, feats), jnp.float32),
        ],
        scratch_shapes=[
            pltpu.VMEM((rows_here, wide), jnp.bfloat16),
            pltpu.VMEM((rows_here, feats), jnp.float32),
            pltpu.SemaphoreType.DMA((rows_here // CHUNK,)),
        ],
        compiler_params=pltpu.CompilerParams(vmem_limit_bytes=VMEM_MUCH),
        cost_estimate=pl.CostEstimate(
            flops=2 * rows_here * feats * wide, bytes_accessed=2 * rows_here * (wide + feats), transcendentals=0
        ),
        name="project",
    )(embeddings, basis, list_owner.reshape(lanes, LANES), list_slot.reshape(lanes, LANES), mean)


def sort_kernel(yb_ref, target_ref, list_ref, notes_ref, after_hbm, rows_hbm, rows_ref, sem):
    rows_here, feats = yb_ref.shape
    width = list_ref.shape[0]
    chunks = rows_here // LANES
    groups = width // GROUP
    place = lax.broadcasted_iota(jnp.int32, (GROUP * CAP, LANES), 0).astype(jnp.int16)

    def sort_group(g):
        pieces = []
        for c in range(chunks):
            aim = jnp.broadcast_to(target_ref[c:c + 1, :] - g * (GROUP * CAP), (16, LANES)).astype(jnp.int16)
            aim = jnp.concatenate([aim] * (GROUP * CAP // 16), 0)
            pieces.append(jnp.where(aim == place, jnp.ones((), jnp.bfloat16), jnp.zeros((), jnp.bfloat16)))
        rows = jnp.dot(jnp.concatenate(pieces, 1), yb_ref[...], preferred_element_type=jnp.float32).astype(jnp.bfloat16)
        for j in range(GROUP):
            base = pl.multiple_of((g * GROUP + j) * SPAN, 16)
            rows_ref[pl.ds(base, CAP), :] = rows[j * CAP:(j + 1) * CAP]
            notes = jnp.concatenate([notes_ref[:NOTES - 1, :], list_ref[pl.ds(g * GROUP + j, 1), :]], 0)
            rows_ref[pl.ds(pl.multiple_of(base + CAP, 16), NOTES), :] = notes.astype(jnp.bfloat16)
        at = pl.ds(pl.multiple_of(g * (GROUP * SPAN), 16), GROUP * SPAN)
        return pltpu.make_async_copy(rows_ref.at[at], rows_hbm.at[at], sem.at[g])

    if groups <= 4:
        copies = []
        for g in range(groups):
            copies.append(sort_group(g))
            copies[g].start()
        for copy in copies:
            copy.wait()
    else:

        @pl.loop(0, groups)
        def _(g):
            copy = sort_group(g)
            copy.start()
            copy.wait()


def sort(yb, targets, lists, notes, after):
    rows_here, feats = yb.shape
    width = lists.shape[0]
    slots = width * SPAN
    vmem, anywhere = pl.BlockSpec(memory_space=pltpu.VMEM), pl.BlockSpec(memory_space=pl.ANY)
    return pl.pallas_call(
        sort_kernel,
        in_specs=[vmem] * 4 + [anywhere],
        out_specs=anywhere,
        out_shape=jax.ShapeDtypeStruct((slots, feats), jnp.bfloat16),
        scratch_shapes=[pltpu.VMEM((slots, feats), jnp.bfloat16), pltpu.SemaphoreType.DMA((width // GROUP,))],
        compiler_params=pltpu.CompilerParams(vmem_limit_bytes=VMEM_SOME),
        cost_estimate=pl.CostEstimate(
            flops=2 * rows_here * feats * slots, bytes_accessed=2 * (rows_here + slots) * feats, transcendentals=0
        ),
        name="sort",
    )(yb, targets, lists, notes, after)


def add_kernel(pieces, arrived, keep_ref, *refs):
    came, outs = refs[:arrived], refs[-pieces:]
    size = outs[0].shape[0]
    for p in range(pieces):
        at = slice(p * size, (p + 1) * size)
        held = keep_ref[at].astype(jnp.float32)
        for ref in came:
            held = held + ref[at].astype(jnp.float32)
        outs[p][...] = held.astype(outs[p].dtype)


def add_and_split(keep, came, pieces, after=()):
    rows, wide = keep.shape
    vmem, anywhere = pl.BlockSpec(memory_space=pltpu.VMEM), pl.BlockSpec(memory_space=pl.ANY)
    return pl.pallas_call(
        functools.partial(add_kernel, pieces, len(came)),
        in_specs=[vmem] * (1 + len(came)) + [anywhere] * len(after),
        out_specs=[vmem] * pieces,
        out_shape=[
            jax.ShapeDtypeStruct((rows // pieces, wide), jnp.float32 if p == 0 else jnp.bfloat16) for p in range(pieces)
        ],
        compiler_params=pltpu.CompilerParams(vmem_limit_bytes=VMEM_SOME),
        cost_estimate=pl.CostEstimate(flops=2 * rows * wide, bytes_accessed=10 * rows * wide, transcendentals=0),
        name="add_and_split",
    )(keep, *came, *after)


def partners(width, apart):
    return [(i, i ^ apart) for i in range(width)]


def halving_stages(width):
    strides = [1 << k for k in range(width.bit_length() - 1)]
    return [strides[:1], strides[1:3]] + [[s] for s in strides[3:]]


def exchange(width, stage, out):
    came = []
    for p in range(1, 1 << len(stage)):
        apart = sum(s for k, s in enumerate(stage) if (p >> (len(stage) - 1 - k)) & 1)
        came.append(lax.ppermute(out[p - 1], "wide", partners(width, apart)))
    return came


def encode_kernel(total, me_ref, got_ref, all_ref, basis_ref, centroid_ref, rotation_ref, out_ref, between_ref, delta_ref, scale_ref, list_ref, apart_ref):
    step = pl.program_id(0)
    width = delta_ref.shape[0]
    feats = out_ref.shape[1]
    owned = centroid_ref.shape[0]
    wide = basis_ref.shape[0]
    block = wide // width
    share = total // width

    @pl.when(step == 0)
    def _():
        notes = jnp.concatenate([all_ref[s * SPAN + CAP:(s + 1) * SPAN, :] for s in range(width)], 0)
        size = width * NOTES
        to = lax.broadcasted_iota(jnp.int32, (size, size), 0)
        of = lax.broadcasted_iota(jnp.int32, (size, size), 1)
        turn = jnp.where((to % width) * NOTES + to // width == of, 1.0, 0.0).astype(jnp.bfloat16)
        turned = jnp.dot(turn, notes, preferred_element_type=jnp.float32)
        row = [turned[r * width:(r + 1) * width] for r in range(NOTES)]
        quarters = wide // feats
        shifts = jnp.zeros((width, feats), jnp.float32)
        for q in range(quarters):
            parts = [row[p * quarters + q] for p in range(3)]
            mean = parts[0] + (parts[1] + parts[2])
            apart_ref[:, q * feats:(q + 1) * feats] = mean - jnp.mean(mean, 0, keepdims=True)
            terms = jnp.dot(
                jnp.concatenate(parts, 0).astype(jnp.bfloat16),
                basis_ref[q * feats:(q + 1) * feats, :],
                preferred_element_type=jnp.float32,
            )
            shifts = shifts + (terms[:width] + (terms[width:2 * width] + terms[2 * width:]))
        square = row[3 * quarters] + (row[3 * quarters + 1] + row[3 * quarters + 2])
        delta = shifts - jnp.mean(shifts, 0, keepdims=True)
        variance = jnp.sum(square + share * (delta * delta), 0, keepdims=True) / total
        scale_ref[...] = lax.rsqrt(variance + 1e-05)
        delta_ref[...] = delta
        digits = row[NOTES - 1]
        list_ref[...] = digits[:, :CAP] * 32.0 + digits[:, CAP:] - 1.0

        me = me_ref[0]
        first = me * block
        near = apart_ref[:, pl.ds(pl.multiple_of(first // LANES * LANES, LANES), LANES)]
        near = pltpu.roll(near, (LANES - first % LANES) % LANES, 1)[:, :block]
        between_ref[...] = share * lax.dot_general(
            near,
            apart_ref[...],
            (((0,), (0,)), ((), ())),
            precision=lax.Precision.HIGHEST,
            preferred_element_type=jnp.float32,
        )

    columns = jnp.transpose(list_ref[pl.ds(step * GROUP, GROUP), :])
    names = lax.broadcasted_iota(jnp.int32, (CAP, owned), 1).astype(jnp.int16)
    hits, projected, held = [], [], []
    for s in range(GROUP):
        listed = jnp.broadcast_to(columns[:, s:s + 1], (CAP, LANES))
        held.append(jnp.concatenate([listed] * (feats // LANES), 1) >= 0)
        wanted = jnp.concatenate([listed.astype(jnp.int32).astype(jnp.int16)] * (owned // LANES), 1)
        hits.append(jnp.where(wanted == names, jnp.ones((), jnp.bfloat16), jnp.zeros((), jnp.bfloat16)))
        rows = got_ref[s * SPAN:s * SPAN + CAP, :].astype(jnp.float32)
        projected.append((rows + delta_ref[pl.ds(step * GROUP + s, 1), :]) * scale_ref[...])
    centre = jnp.dot(jnp.concatenate(hits, 0), centroid_ref[...], preferred_element_type=jnp.float32)
    residual = jnp.where(jnp.concatenate(held, 0), jnp.concatenate(projected, 0) - centre, 0.0)
    out_ref[...] = jnp.dot(
        residual.astype(jnp.bfloat16), rotation_ref[...], preferred_element_type=jnp.float32
    ).astype(jnp.bfloat16)


def encode(width, total, me, got, basis, centroids, rotation):
    wide, feats = basis.shape
    owned = centroids.shape[0]
    slots = width * CAP
    whole = lambda i: (0, 0)
    return pl.pallas_call(
        functools.partial(encode_kernel, total),
        grid=(width // GROUP,),
        in_specs=[
            pl.BlockSpec(memory_space=pltpu.SMEM),
            pl.BlockSpec((GROUP * SPAN, feats), lambda i: (i, 0)),
            pl.BlockSpec((width * SPAN, feats), whole),
            pl.BlockSpec((wide, feats), whole),
            pl.BlockSpec((owned, feats), whole),
            pl.BlockSpec((feats, feats), whole),
        ],
        out_specs=[
            pl.BlockSpec((GROUP * CAP, feats), lambda i: (i, 0)),
            pl.BlockSpec((wide // width, wide), whole),
        ],
        out_shape=[
            jax.ShapeDtypeStruct((slots, feats), jnp.bfloat16),
            jax.ShapeDtypeStruct((wide // width, wide), jnp.float32),
        ],
        scratch_shapes=[
            pltpu.VMEM((width, feats), jnp.float32),
            pltpu.VMEM((1, feats), jnp.float32),
            pltpu.VMEM((width, CAP), jnp.float32),
            pltpu.VMEM((width, wide), jnp.float32),
        ],
        compiler_params=pltpu.CompilerParams(vmem_limit_bytes=VMEM_SOME),
        cost_estimate=pl.CostEstimate(
            flops=2 * slots * feats * (owned + feats), bytes_accessed=4 * slots * feats, transcendentals=0
        ),
        name="encode",
    )(me.reshape(1), got, got, basis, centroids, rotation)


def local(embeddings, basis, list_owner, list_slot, centroids, rotation):
    width = lax.axis_size("wide")
    me = lax.axis_index("wide")
    rows_here, wide = embeddings.shape
    feats = basis.shape[1]
    total = rows_here * width

    stages = halving_stages(width)
    keep, send, mean = moments(width, me, embeddings)
    came = exchange(width, stages[0], [send])
    yb, targets, lists, notes = project(width, embeddings, basis, list_owner, list_slot, mean)
    keep, *out = add_and_split(keep, came, 1 << len(stages[1]), after=[notes])
    rows = sort(yb, targets, lists, notes, out[0])
    got = lax.all_to_all(rows.reshape(width, SPAN, feats), "wide", split_axis=0, concat_axis=0, tiled=True)
    for n in range(1, len(stages)):
        came = exchange(width, stages[n], out)
        if n + 1 < len(stages):
            keep, *out = add_and_split(keep, came, 1 << len(stages[n + 1]))
    encoded, between = encode(width, total, me, got.reshape(width * SPAN, feats), basis, centroids, rotation)
    for block in came:
        keep = keep + block.astype(jnp.float32)
    covariance = (keep + between) / total
    return (encoded, covariance)


def solution(mesh):
    in_specs = (
        P(("groups", "wide"), None),
        P(),
        P(("groups", "wide")),
        P(("groups", "wide")),
        P("wide", None),
        P(),
    )
    out_specs = (P(("groups", "wide"), None), P(("groups", "wide"), None))
    return jax.shard_map(local, mesh=mesh, in_specs=in_specs, out_specs=out_specs, check_vma=False)
```

time: 67.1 us -> 67.6 us (level)
  local copies, waits for them, and re-layouts: 0.03 us -> 1.61 us
    unnamed x10 -> x16, local copies, waits for them, and re-layouts: 0.03 us -> 1.61 us
    pallas_call x3 -> x5, Pallas kernels: 15 us -> 14.5 us  [the longest x1 7.01 us: moments(): pl.pallas_call(functools.partial(moments_kernel, width), in_specs=[pl.Blo...]
  transfers between devices with their start and end apart: 6 -> 6, of which waited for: 4 -> 3; matrix products, arithmetic and copies ran while one was open for 0% -> 0% of each run, Pallas kernels for 7% -> 13%
where the time goes in v5:
time: 67.6 us; the launch traced here: 67.4 us
  waiting for transfers between devices  31.6 us (47%)
  Pallas kernels  18.9 us (28%)
  starting transfers between devices  13.7 us (20%)
  local copies, waits for them, and re-layouts  1.61 us (2%)
  between operations  0.75 us (1%)
  other arithmetic  0.74 us (1%)
    ppermute x5, waiting for transfers between devices, exchange(): came.append(lax.ppermute(out[p - 1], 'wide', partners(width, apart)))  31.6 us
    all_to_all x1, starting transfers between devices, local(): lax.all_to_all(rows.reshape(width, SPAN, feats), 'wide', split_axis=0, co...  7.08 us
    pallas_call x1, Pallas kernels, moments(): pl.pallas_call(functools.partial(moments_kernel, width), in_specs=[pl.Blo...  7.01 us
    ppermute x5, starting transfers between devices, exchange(): came.append(lax.ppermute(out[p - 1], 'wide', partners(width, apart)))  6.63 us
    pallas_call x1, Pallas kernels, encode(): pl.pallas_call(functools.partial(encode_kernel, total), grid=(width // GR...  4.43 us
    pallas_call x1, Pallas kernels, project(): pl.pallas_call(functools.partial(project_kernel, width), in_specs=[anywhe...  3.94 us
    pallas_call x1, Pallas kernels, sort(): pl.pallas_call(sort_kernel, in_specs=[vmem] * 4 + [anywhere], out_specs=a...  3.22 us
    unnamed x16, local copies, waits for them, and re-layouts  1.61 us
  transfers between devices with their start and end apart: 6, of which 3 were waited for; matrix products, arithmetic and copies ran while one was open for 0% of the time, Pallas kernels for 13%

profile of v5, /device:TPU:0, one launch (start us, length us, event | category | flops | bytes accessed | tf_op | source)
XLA Modules:
  0.0 67.4 jit_solution(1687670661718664769)
XLA Ops:
  0.6 0.0 copy-start
  0.6 0.0 copy-start.2
  0.7 0.0 copy-start.3
  0.7 0.0 copy-start.4
  0.7 7.0 %moments.1 = (bf16[512,1024]{1,0:T(8,128)(2,1)}, bf16[512,1024]{1,0:T(8,128)(2,1)}, f32[1,1024]{1,0:T(1,128)}) custom-call(s32[1]{0:T(128)} %bitcast.me_ref, bf16[2048,1024]{1,0:T(8,128)(2,1)} %e_hbm.3), custom_call_target="tpu_custom_call" | custom-call | flops 4294967296 | bytes 6291456 | tf_op jit(solution)/shard_map/moments/pallas_call | solution.py:92
  7.7 0.5 collective-permute-start
  8.2 0.0 copy-done
  8.2 0.0 copy-done.2
  8.2 0.0 copy-done.3
  8.2 0.0 copy-done.4
  8.2 0.0 copy-start.5
  8.2 0.7 %copy-done.5 = f32[1,1024]{1,0:T(1,128)S(1)} copy-done((f32[1,1024]{1,0:T(1,128)S(1)}, f32[1,1024]{1,0:T(1,128)}, u32[]{:S(2)}) %copy-start.5) | copy-done | bytes 4120
  8.9 3.9 %project.1 = (bf16[2048,256]{1,0:T(8,128)(2,1)S(1)}, s32[16,128]{1,0:T(8,128)S(1)}, f32[16,256]{1,0:T(8,128)S(1)}, f32[16,256]{1,0:T(8,128)S(1)}) custom-call(bf16[2048,1024]{1,0:T(8,128)(2,1)S(1)} %copy-done, bf16[1024,256]{1,0:T(8,128)(2,1)S(1)} %copy-done.2, s32[16,128]{1,0:T(8,128)S(1)} %bitcast.7, s32[16,128]{1,0:T(8,128)S(1)} %bitcast.8, ...), custom_call_target="tpu_custom_call" | custom-call | flops 1073741824 | bytes 5242880 | tf_op jit(solution)/shard_map/project/pallas_call | solution.py:184
  12.8 0.0 collective-permute-done.refs_0_
  12.9 0.0 copy-done.1
  12.9 0.2 add_and_split.2
  13.1 3.2 %sort.1 = bf16[2304,256]{1,0:T(8,128)(2,1)} custom-call(bf16[2048,256]{1,0:T(8,128)(2,1)S(1)} %get-tuple-element.18.yb_ref, s32[16,128]{1,0:T(8,128)S(1)} %get-tuple-element.19.target_ref, f32[16,256]{1,0:T(8,128)S(1)} %get-tuple-element.20.list_ref, f32[16,256]{1,0:T(8,128)S(1)} %get-tuple-element.21.refs_1_.notes_ref, ...), custom_call_target="tpu_custom_call" | custom-call | flops 2415919104 | bytes 2228224 | tf_op jit(solution)/shard_map/sort/pallas_call | solution.py:250
  16.3 7.1 %all-to-all-start = ((bf16[16,144,256]{2,1,0:T(8,128)(2,1)}), bf16[16,144,256]{2,1,0:T(8,128)(2,1)S(1)}, u32[]{:S(2)}, u32[]{:S(2)}) async-start(bf16[16,144,256]{2,1,0:T(8,128)(2,1)} %bitcast.3), calls=%async_computation | async-start | bytes 2359296 | tf_op jit(solution)/shard_map/all_to_all | solution.py:426
  23.4 0.0 copy-start.6
  23.4 2.0 %collective-permute-start.1 = (bf16[128,1024]{1,0:T(8,128)(2,1)S(1)}, bf16[128,1024]{1,0:T(8,128)(2,1)S(1)}, u32[]{:S(2)}, u32[]{:S(2)}) collective-permute-start(bf16[128,1024]{1,0:T(8,128)(2,1)S(1)} %get-tuple-element.24.after_hbm), channel_id=1, source_target_pairs={{0,4},{1,5},{2,6},{3,7},{4,0},{5,1},{6,2},{7,3},{8,12},{9,13},{10,... | collective-permute-start | bytes 786440 | tf_op jit(solution)/shard_map/ppermute | solution.py:304
  25.4 1.5 %collective-permute-start.2 = (bf16[128,1024]{1,0:T(8,128)(2,1)S(1)}, bf16[128,1024]{1,0:T(8,128)(2,1)S(1)}, u32[]{:S(2)}, u32[]{:S(2)}) collective-permute-start(bf16[128,1024]{1,0:T(8,128)(2,1)S(1)} %get-tuple-element.27), channel_id=1, source_target_pairs={{0,2},{1,3},{2,0},{3,1},{4,6},{5,7},{6,4},{7,5},{8,10},{9,11},{10,... | collective-permute-start | bytes 786440 | tf_op jit(solution)/shard_map/ppermute | solution.py:304
  26.9 0.1 collective-permute-start.3
  27.0 24.6 %collective-permute-done.1.refs_0_ = bf16[128,1024]{1,0:T(8,128)(2,1)S(1)} collective-permute-done((bf16[128,1024]{1,0:T(8,128)(2,1)S(1)}, bf16[128,1024]{1,0:T(8,128)(2,1)S(1)}, u32[]{:S(2)}, u32[]{:S(2)}) %collective-permute-start.1) | collective-permute-done | bytes 262176 | tf_op jit(solution)/shard_map/ppermute | solution.py:304
  51.6 0.0 collective-permute-done.2.refs_1_
  51.6 6.1 %collective-permute-done.3.refs_2_ = bf16[128,1024]{1,0:T(8,128)(2,1)S(1)} collective-permute-done((bf16[128,1024]{1,0:T(8,128)(2,1)S(1)}, bf16[128,1024]{1,0:T(8,128)(2,1)S(1)}, u32[]{:S(2)}, u32[]{:S(2)}) %collective-permute-start.3) | collective-permute-done | bytes 262176 | tf_op jit(solution)/shard_map/ppermute | solution.py:304
  57.7 0.1 add_and_split.3
  57.8 2.6 %collective-permute-start.4 = (bf16[64,1024]{1,0:T(8,128)(2,1)S(1)}, bf16[64,1024]{1,0:T(8,128)(2,1)S(1)}, u32[]{:S(2)}, u32[]{:S(2)}) collective-permute-start(bf16[64,1024]{1,0:T(8,128)(2,1)S(1)} %get-tuple-element.30), channel_id=1, source_target_pairs={{0,8},{1,9},{2,10},{3,11},{4,12},{5,13},{6,14},{7,15},{8,0},{9,1},... | collective-permute-start | bytes 393224 | tf_op jit(solution)/shard_map/ppermute | solution.py:304
  60.4 0.0 all-to-all-done
  60.4 0.9 %copy-done.7 = bf16[256,256]{1,0:T(8,128)(2,1)S(1)} copy-done((bf16[256,256]{1,0:T(8,128)(2,1)S(1)}, bf16[256,256]{1,0:T(8,128)(2,1)}, u32[]{:S(2)}) %copy-start.7) | copy-done | bytes 131096
  61.3 4.4 %encode.1 = (bf16[2048,256]{1,0:T(8,128)(2,1)}, f32[64,1024]{1,0:T(8,128)S(1)}) custom-call(s32[1]{0:T(128)} %bitcast.me_ref, bf16[2304,256]{1,0:T(8,128)(2,1)S(1)} %bitcast.5, bf16[2304,256]{1,0:T(8,128)(2,1)S(1)} %bitcast.6, bf16[1024,256]{1,0:T(8,128)(2,1)S(1)} %copy-done.2, bf16[1024,256]{1,0:T(8,128)(2,1)S(1)} %copy-done.6, bf16[256,256]{1,0:T(8,128)(2,1)S(1)} %copy-done.7), custom_call_target="tpu_custom_call" | custom-call | flops 1342177280 | bytes 2097152 | tf_op jit(solution)/shard_map/encode/pallas_call | solution.py:380
  65.7 0.9 %collective-permute-done.4 = bf16[64,1024]{1,0:T(8,128)(2,1)S(1)} collective-permute-done((bf16[64,1024]{1,0:T(8,128)(2,1)S(1)}, bf16[64,1024]{1,0:T(8,128)(2,1)S(1)}, u32[]{:S(2)}, u32[]{:S(2)}) %collective-permute-start.4) | collective-permute-done | bytes 131104 | tf_op jit(solution)/shard_map/ppermute | solution.py:304
  66.6 0.7 %add_multiply_fusion = f32[64,1024]{1,0:T(8,128)} fusion(f32[64,1024]{1,0:T(8,128)S(1)} %get-tuple-element.31, f32[64,1024]{1,0:T(8,128)S(1)} %get-tuple-element.29, bf16[64,1024]{1,0:T(8,128)(2,1)S(1)} %collective-permute-done.4), kind=kLoop, calls=%fused_computation | loop fusion | flops 262144 | bytes 917504 | tf_op jit(solution)/shard_map/div | solution.py:434
  (3 shorter events, 0.0 us)
Async XLA Ops:
  0.6 7.6 %copy-start = (bf16[2048,1024]{1,0:T(8,128)(2,1)S(1)}, bf16[2048,1024]{1,0:T(8,128)(2,1)}, u32[]{:S(2)}) copy-start(bf16[2048,1024]{1,0:T(8,128)(2,1)} %e_hbm.3) | copy-start | bytes 12582916
  0.6 7.6 %copy-start.2 = (bf16[1024,256]{1,0:T(8,128)(2,1)S(1)}, bf16[1024,256]{1,0:T(8,128)(2,1)}, u32[]{:S(2)}) copy-start(bf16[1024,256]{1,0:T(8,128)(2,1)} %basis_ref.3) | copy-start | bytes 1572868
  0.7 7.5 %copy-start.3 = (s32[2048]{0:T(1024)S(1)}, s32[2048]{0:T(1024)}, u32[]{:S(2)}) copy-start(s32[2048]{0:T(1024)} %param.8) | copy-start | bytes 24580
  0.7 7.5 %copy-start.4 = (s32[2048]{0:T(1024)S(1)}, s32[2048]{0:T(1024)}, u32[]{:S(2)}) copy-start(s32[2048]{0:T(1024)} %param.9) | copy-start | bytes 24580
  7.7 5.2 %collective-permute-start = (bf16[512,1024]{1,0:T(8,128)(2,1)}, bf16[512,1024]{1,0:T(8,128)(2,1)S(1)}, u32[]{:S(2)}, u32[]{:S(2)}) collective-permute-start(bf16[512,1024]{1,0:T(8,128)(2,1)} %get-tuple-element.23), channel_id=1, source_target_pairs={{0,1},{1,0},{2,3},{3,2},{4,5},{5,4},{6,7},{7,6},{8,9},{9,8},{10,11... | collective-permute-start | bytes 3145736 | tf_op jit(solution)/shard_map/ppermute | solution.py:304
  8.2 0.7 %copy-start.5 = (f32[1,1024]{1,0:T(1,128)S(1)}, f32[1,1024]{1,0:T(1,128)}, u32[]{:S(2)}) copy-start(f32[1,1024]{1,0:T(1,128)} %get-tuple-element.17.mean_ref) | copy-start | bytes 12292
  8.9 4.0 %copy-start.1 = (bf16[512,1024]{1,0:T(8,128)(2,1)S(1)}, bf16[512,1024]{1,0:T(8,128)(2,1)}, u32[]{:S(2)}) copy-start(bf16[512,1024]{1,0:T(8,128)(2,1)} %get-tuple-element.22.keep_ref) | copy-start | bytes 3145732
  16.3 44.0 %all-to-all-start = ((bf16[16,144,256]{2,1,0:T(8,128)(2,1)}), bf16[16,144,256]{2,1,0:T(8,128)(2,1)S(1)}, u32[]{:S(2)}, u32[]{:S(2)}) async-start(bf16[16,144,256]{2,1,0:T(8,128)(2,1)} %bitcast.3), calls=%async_computation | async-start | bytes 2359296 | tf_op jit(solution)/shard_map/all_to_all | solution.py:426
  23.4 37.0 %copy-start.6 = (bf16[1024,256]{1,0:T(8,128)(2,1)S(1)}, bf16[1024,256]{1,0:T(8,128)(2,1)}, u32[]{:S(2)}) copy-start(bf16[1024,256]{1,0:T(8,128)(2,1)} %centroid_ref.1) | copy-start | bytes 1572868
  23.4 28.2 %collective-permute-start.1 = (bf16[128,1024]{1,0:T(8,128)(2,1)S(1)}, bf16[128,1024]{1,0:T(8,128)(2,1)S(1)}, u32[]{:S(2)}, u32[]{:S(2)}) collective-permute-start(bf16[128,1024]{1,0:T(8,128)(2,1)S(1)} %get-tuple-element.24.after_hbm), channel_id=1, source_target_pairs={{0,4},{1,5},{2,6},{3,7},{4,0},{5,1},{6,2},{7,3},{8,12},{9,13},{10,... | collective-permute-start | bytes 786440 | tf_op jit(solution)/shard_map/ppermute | solution.py:304
  25.4 26.2 %collective-permute-start.2 = (bf16[128,1024]{1,0:T(8,128)(2,1)S(1)}, bf16[128,1024]{1,0:T(8,128)(2,1)S(1)}, u32[]{:S(2)}, u32[]{:S(2)}) collective-permute-start(bf16[128,1024]{1,0:T(8,128)(2,1)S(1)} %get-tuple-element.27), channel_id=1, source_target_pairs={{0,2},{1,3},{2,0},{3,1},{4,6},{5,7},{6,4},{7,5},{8,10},{9,11},{10,... | collective-permute-start | bytes 786440 | tf_op jit(solution)/shard_map/ppermute | solution.py:304
  26.9 30.8 %collective-permute-start.3 = (bf16[128,1024]{1,0:T(8,128)(2,1)S(1)}, bf16[128,1024]{1,0:T(8,128)(2,1)S(1)}, u32[]{:S(2)}, u32[]{:S(2)}) collective-permute-start(bf16[128,1024]{1,0:T(8,128)(2,1)S(1)} %get-tuple-element.28), channel_id=1, source_target_pairs={{0,6},{1,7},{2,4},{3,5},{4,2},{5,3},{6,0},{7,1},{8,14},{9,15},{10,... | collective-permute-start | bytes 786440 | tf_op jit(solution)/shard_map/ppermute | solution.py:304
  57.8 8.8 %collective-permute-start.4 = (bf16[64,1024]{1,0:T(8,128)(2,1)S(1)}, bf16[64,1024]{1,0:T(8,128)(2,1)S(1)}, u32[]{:S(2)}, u32[]{:S(2)}) collective-permute-start(bf16[64,1024]{1,0:T(8,128)(2,1)S(1)} %get-tuple-element.30), channel_id=1, source_target_pairs={{0,8},{1,9},{2,10},{3,11},{4,12},{5,13},{6,14},{7,15},{8,0},{9,1},... | collective-permute-start | bytes 393224 | tf_op jit(solution)/shard_map/ppermute | solution.py:304
  60.4 0.9 %copy-start.7 = (bf16[256,256]{1,0:T(8,128)(2,1)S(1)}, bf16[256,256]{1,0:T(8,128)(2,1)}, u32[]{:S(2)}) copy-start(bf16[256,256]{1,0:T(8,128)(2,1)} %rotation_ref.1) | copy-start | bytes 393220

commit v6 on v4

--- a/solution.py
+++ b/solution.py
@@ -16,6 +16,7 @@
 GROUP = 4
 VMEM_SOME = 24 * 1024 * 1024
 VMEM_MOST = 57 * 1024 * 1024
+VMEM_MUCH = 48 * 1024 * 1024
 
 
 def in_three(x):
@@ -25,17 +26,15 @@
     return high, middle, (rest - middle).astype(jnp.bfloat16).astype(jnp.float32)
 
 
-def first_kernel(
-    width, me_ref, e_hbm, basis_hbm, owner_ref, slot_ref,
-    rows_hbm, keep_hbm, send_hbm,
-    e_ref, basis_ref, y_ref, yb_ref, pick_ref, rows_ref, m_ref, list_ref, e_sem, basis_sem, rows_sem, block_sem,
+def rows_kernel(
+    width, e_hbm, basis_hbm, owner_ref, slot_ref,
+    rows_hbm, mean_ref,
+    e_ref, basis_ref, y_ref, yb_ref, pick_ref, rows_ref, list_ref, e_sem, basis_sem, rows_sem,
 ):
     rows_here, wide = e_ref.shape
     feats = basis_ref.shape[1]
     chunks = rows_here // LANES
     parts = rows_here // CHUNK
-    block = wide // width
-    bits = width.bit_length() - 1
 
     e_copies = []
     for c in range(parts):
@@ -112,6 +111,7 @@
         square = square + jnp.sum((centred * centred).reshape(CHUNK // 8, 8, feats), 0)
         yb_ref[at, :] = centred.astype(jnp.bfloat16)
     mean = jnp.sum(sum_e, 0, keepdims=True) / rows_here
+    mean_ref[...] = mean
     common = [part[:, q * feats:(q + 1) * feats] for part in in_three(mean) for q in range(wide // feats)]
     common = jnp.concatenate(common + list(in_three(jnp.sum(square, 0, keepdims=True))), 0)
 
@@ -122,31 +122,104 @@
             rows_ref[pl.ds(base, CAP), :] = rows[j * CAP:(j + 1) * CAP]
             notes = jnp.concatenate([common, list_ref[pl.ds(g * GROUP + j, 1), :]], 0)
             rows_ref[pl.ds(pl.multiple_of(base + CAP, 16), NOTES), :] = notes.astype(jnp.bfloat16)
+        at = pl.ds(pl.multiple_of(g * (GROUP * SPAN), 16), GROUP * SPAN)
+        return pltpu.make_async_copy(rows_ref.at[at], rows_hbm.at[at], rows_sem.at[into])
 
     if groups <= held:
+        copies = []
         for g in range(groups):
-            sort_group(g, g)
+            copies.append(sort_group(g, g))
+            copies[g].start()
+        for copy in copies:
+            copy.wait()
     else:
 
         @pl.loop(0, groups)
         def _(g):
             pick_group(g, 0)
-            sort_group(g, 0)
-
-    whole_copy = pltpu.make_async_copy(rows_ref, rows_hbm, rows_sem)
-    whole_copy.start()
-
+            copy = sort_group(g, 0)
+            copy.start()
+            copy.wait()
+
+
+def project_and_sort(width, embeddings, basis, list_owner, list_slot):
+    rows_here, wide = embeddings.shape
+    feats = basis.shape[1]
+    lanes = rows_here // LANES
+    slots = width * SPAN
+    groups = width // GROUP
+    held = groups if groups <= rows_here // CHUNK else 1
+    vmem, anywhere = pl.BlockSpec(memory_space=pltpu.VMEM), pl.BlockSpec(memory_space=pl.ANY)
+    return pl.pallas_call(
+        functools.partial(rows_kernel, width),
+        in_specs=[anywhere, anywhere, vmem, vmem],
+        out_specs=[anywhere, vmem],
+        out_shape=[jax.ShapeDtypeStruct((slots, feats), jnp.bfloat16), jax.ShapeDtypeStruct((1, wide), jnp.float32)],
+        scratch_shapes=[
+            pltpu.VMEM((rows_here, wide), jnp.bfloat16),
+            pltpu.VMEM((wide, feats), jnp.bfloat16),
+            pltpu.VMEM((rows_here, feats), jnp.float32),
+            pltpu.VMEM((rows_here, feats), jnp.bfloat16),
+            pltpu.VMEM((held, GROUP * CAP, rows_here), jnp.bfloat16),
+            pltpu.VMEM((slots, feats), jnp.bfloat16),
+            pltpu.VMEM((width, 2 * CAP), jnp.float32),
+            pltpu.SemaphoreType.DMA((rows_here // CHUNK,)),
+            pltpu.SemaphoreType.DMA,
+            pltpu.SemaphoreType.DMA((held,)),
+        ],
+        compiler_params=pltpu.CompilerParams(vmem_limit_bytes=VMEM_MOST),
+        cost_estimate=pl.CostEstimate(
+            flops=2 * rows_here * feats * (wide + slots), bytes_accessed=2 * rows_here * wide + 2 * slots * feats, transcendentals=0
+        ),
+        name="project_sort",
+    )(embeddings, basis, list_owner.reshape(lanes, LANES), list_slot.reshape(lanes, LANES))
+
+
+def moments_kernel(
+    width, me_ref, mean_hbm, e_hbm, keep_hbm, send_hbm, e_ref, mean_ref, m_ref, e_sem, mean_sem, block_sem
+):
+    rows_here, wide = e_ref.shape
+    block = wide // width
+    bits = width.bit_length() - 1
+    parts = rows_here // CHUNK
+    tiles = wide // TILE
+    e_copies = []
+    for c in range(parts):
+        at = pl.ds(c * CHUNK, CHUNK)
+        e_copies.append(pltpu.make_async_copy(e_hbm.at[at], e_ref.at[at], e_sem.at[c]))
+        e_copies[c].start()
+    mean_copy = pltpu.make_async_copy(mean_hbm, mean_ref, mean_sem)
+    mean_copy.start()
     me = me_ref[0]
     copies = []
-    for t in range(wide // TILE):
-        rows = slice(t * TILE, (t + 1) * TILE)
-        product = lax.dot_general(
-            e_ref[:, rows], e_ref[...], (((0,), (0,)), ((), ())), preferred_element_type=jnp.float32
-        )
+    for t in range(tiles):
+        rows, columns = slice(t * TILE, (t + 1) * TILE), slice(t * TILE, wide)
+        if t == 0:
+            product = jnp.zeros((TILE, wide), jnp.float32)
+            for c in range(parts):
+                e_copies[c].wait()
+                at = slice(c * CHUNK, (c + 1) * CHUNK)
+                product = product + lax.dot_general(
+                    e_ref[at, rows], e_ref[at, :], (((0,), (0,)), ((), ())), preferred_element_type=jnp.float32
+                )
+            mean_copy.wait()
+            mean = mean_ref[...]
+        else:
+            product = lax.dot_general(
+                e_ref[:, rows], e_ref[:, columns], (((0,), (0,)), ((), ())), preferred_element_type=jnp.float32
+            )
         down = jnp.transpose(jnp.broadcast_to(mean[:, rows] * rows_here, (LANES, TILE)))
-        for j in range(wide // LANES):
-            across = slice(j * LANES, (j + 1) * LANES)
-            m_ref[rows, across] = (product[:, across] - down * mean[:, across]).astype(jnp.bfloat16)
+        for u in range(t, tiles):
+            pieces = []
+            for j in range(u * TILE // LANES, (u + 1) * TILE // LANES):
+                across = slice(j * LANES, (j + 1) * LANES)
+                within = slice(j * LANES - t * TILE, (j + 1) * LANES - t * TILE)
+                pieces.append((product[:, within] - down * mean[:, across]).astype(jnp.bfloat16))
+            piece = jnp.concatenate(pieces, 1)
+            other = slice(u * TILE, (u + 1) * TILE)
+            m_ref[rows, other] = piece
+            if u > t:
+                m_ref[other, rows] = jnp.transpose(piece)
         for pair in range(TILE // block // 2):
             first = t * (TILE // block) + 2 * pair
             apart = (first ^ me) >> 1
@@ -162,48 +235,34 @@
                 copies.append(copy)
     for copy in copies:
         copy.wait()
-    whole_copy.wait()
-
-
-def first(width, me, embeddings, basis, list_owner, list_slot):
+
+
+def moments(width, me, embeddings, mean):
     rows_here, wide = embeddings.shape
-    feats = basis.shape[1]
-    lanes = rows_here // LANES
-    slots = width * SPAN
-    groups = width // GROUP
-    vmem, anywhere = pl.BlockSpec(memory_space=pltpu.VMEM), pl.BlockSpec(memory_space=pl.ANY)
+    anywhere = pl.BlockSpec(memory_space=pl.ANY)
     return pl.pallas_call(
-        functools.partial(first_kernel, width),
-        in_specs=[pl.BlockSpec(memory_space=pltpu.SMEM), anywhere, anywhere, vmem, vmem],
-        out_specs=[anywhere] * 3,
-        out_shape=[jax.ShapeDtypeStruct((slots, feats), jnp.bfloat16)]
-        + [jax.ShapeDtypeStruct((wide // 2, wide), jnp.bfloat16)] * 2,
+        functools.partial(moments_kernel, width),
+        in_specs=[pl.BlockSpec(memory_space=pltpu.SMEM), anywhere, anywhere],
+        out_specs=[anywhere] * 2,
+        out_shape=[jax.ShapeDtypeStruct((wide // 2, wide), jnp.bfloat16)] * 2,
         scratch_shapes=[
             pltpu.VMEM((rows_here, wide), jnp.bfloat16),
-            pltpu.VMEM((wide, feats), jnp.bfloat16),
-            pltpu.VMEM((rows_here, feats), jnp.float32),
-            pltpu.VMEM((rows_here, feats), jnp.bfloat16),
-            pltpu.VMEM((groups if groups <= rows_here // CHUNK else 1, GROUP * CAP, rows_here), jnp.bfloat16),
-            pltpu.VMEM((slots, feats), jnp.bfloat16),
+            pltpu.VMEM((1, wide), jnp.float32),
             pltpu.VMEM((wide, wide), jnp.bfloat16),
-            pltpu.VMEM((width, 2 * CAP), jnp.float32),
             pltpu.SemaphoreType.DMA((rows_here // CHUNK,)),
             pltpu.SemaphoreType.DMA,
-            pltpu.SemaphoreType.DMA,
             pltpu.SemaphoreType.DMA((width,)),
         ],
-        compiler_params=pltpu.CompilerParams(vmem_limit_bytes=VMEM_MOST),
+        compiler_params=pltpu.CompilerParams(vmem_limit_bytes=VMEM_MUCH),
         cost_estimate=pl.CostEstimate(
-            flops=2 * rows_here * (feats * (wide + slots) + wide * wide),
-            bytes_accessed=2 * rows_here * wide + 2 * slots * feats + 2 * wide * wide,
-            transcendentals=0,
+            flops=2 * rows_here * wide * wide, bytes_accessed=2 * rows_here * wide + 2 * wide * wide, transcendentals=0
         ),
-        name="first",
-    )(me.reshape(1), embeddings, basis, list_owner.reshape(lanes, LANES), list_slot.reshape(lanes, LANES))
-
-
-def add_kernel(pieces, keep_ref, *refs):
-    came, outs = refs[:-pieces], refs[-pieces:]
+        name="moments",
+    )(me.reshape(1), mean, embeddings)
+
+
+def add_kernel(pieces, arrived, keep_ref, *refs):
+    came, outs = refs[:arrived], refs[-pieces:]
     size = outs[0].shape[0]
     for p in range(pieces):
         at = slice(p * size, (p + 1) * size)
@@ -217,7 +276,7 @@
     rows, wide = keep.shape
     vmem = pl.BlockSpec(memory_space=pltpu.VMEM)
     return pl.pallas_call(
-        functools.partial(add_kernel, pieces),
+        functools.partial(add_kernel, pieces, len(came)),
         in_specs=[vmem] * (1 + len(came)),
         out_specs=[vmem] * pieces,
         out_shape=[
@@ -235,20 +294,15 @@
 
 def halving_stages(width):
     strides = [1 << k for k in range(width.bit_length() - 1)]
-    return [strides[:1], strides[1:3]] + [[s] for s in strides[3:]]
-
-
-def reduce_blocks(width, keep, send):
-    stages = halving_stages(width)
-    out = [send]
-    for n, stage in enumerate(stages):
-        came = []
-        for p in range(1, 1 << len(stage)):
-            apart = sum(s for k, s in enumerate(stage) if (p >> (len(stage) - 1 - k)) & 1)
-            came.append(lax.ppermute(out[p - 1], "wide", partners(width, apart)))
-        if n + 1 < len(stages):
-            keep, *out = add_and_split(keep, came, 1 << len(stages[n + 1]))
-    return keep, came
+    return [[s] for s in strides[:-2]] + [strides[-2:]]
+
+
+def exchange(width, stage, out):
+    came = []
+    for p in range(1, 1 << len(stage)):
+        apart = sum(s for k, s in enumerate(stage) if (p >> (len(stage) - 1 - k)) & 1)
+        came.append(lax.ppermute(out[p - 1], "wide", partners(width, apart)))
+    return came
 
 
 def encode_kernel(total, me_ref, got_ref, all_ref, basis_ref, centroid_ref, rotation_ref, out_ref, between_ref, delta_ref, scale_ref, list_ref, apart_ref):
@@ -363,9 +417,14 @@
     feats = basis.shape[1]
     total = rows_here * width
 
-    rows, keep, send = first(width, me, embeddings, basis, list_owner, list_slot)
+    rows, mean = project_and_sort(width, embeddings, basis, list_owner, list_slot)
     got = lax.all_to_all(rows.reshape(width, SPAN, feats), "wide", split_axis=0, concat_axis=0, tiled=True)
-    keep, came = reduce_blocks(width, keep, send)
+    stages = halving_stages(width)
+    keep, *out = moments(width, me, embeddings, mean)
+    for n, stage in enumerate(stages):
+        came = exchange(width, stage, out)
+        if n + 1 < len(stages):
+            keep, *out = add_and_split(keep, came, 1 << len(stages[n + 1]))
     encoded, between = encode(width, total, me, got.reshape(width * SPAN, feats), basis, centroids, rotation)
     for block in came:
         keep = keep + block.astype(jnp.float32)

time: 67.1 us -> 64.2 us (0.957)
  waiting for transfers between devices: 31.7 us -> 22.4 us
  Pallas kernels: 19.5 us -> 24.5 us
  starting transfers between devices: 14.1 us -> 15.6 us
    ppermute x5, waiting for transfers between devices: 31.7 us -> 22.3 us  [exchange(): came.append(lax.ppermute(out[p - 1], 'wide', partners(width, apart)))]
    pallas_call x3 -> x4, Pallas kernels: 15 us -> 20 us  [the longest x1 10.7 us: project_and_sort(): pl.pallas_call(functools.partial(rows_kernel, width), in_specs=[anywhere,...]
    ppermute x5, starting transfers between devices: 6.61 us -> 8.16 us  [exchange(): came.append(lax.ppermute(out[p - 1], 'wide', partners(width, apart)))]
  transfers between devices with their start and end apart: 6 -> 6, of which waited for: 4 -> 4; matrix products, arithmetic and copies ran while one was open for 0% -> 0% of each run, Pallas kernels for 7% -> 22%
where the time goes in v6:
time: 64.2 us; the launch traced here: 63.9 us
  Pallas kernels  24.5 us (38%)
  waiting for transfers between devices  22.4 us (35%)
  starting transfers between devices  15.6 us (24%)
  other arithmetic  0.78 us (1%)
  between operations  0.72 us (1%)
    ppermute x5, waiting for transfers between devices, exchange(): came.append(lax.ppermute(out[p - 1], 'wide', partners(width, apart)))  22.3 us
    pallas_call x1, Pallas kernels, project_and_sort(): pl.pallas_call(functools.partial(rows_kernel, width), in_specs=[anywhere,...  10.7 us
    pallas_call x1, Pallas kernels, moments(): pl.pallas_call(functools.partial(moments_kernel, width), in_specs=[pl.Blo...  8.98 us
    ppermute x5, starting transfers between devices, exchange(): came.append(lax.ppermute(out[p - 1], 'wide', partners(width, apart)))  8.16 us
    all_to_all x1, starting transfers between devices, local(): lax.all_to_all(rows.reshape(width, SPAN, feats), 'wide', split_axis=0, co...  7.39 us
    pallas_call x1, Pallas kernels, encode(): pl.pallas_call(functools.partial(encode_kernel, total), grid=(width // GR...  4.47 us
  transfers between devices with their start and end apart: 6, of which 4 were waited for; matrix products, arithmetic and copies ran while one was open for 0% of the time, Pallas kernels for 22%

profile of v6, /device:TPU:0, one launch (start us, length us, event | category | flops | bytes accessed | tf_op | source)
XLA Modules:
  0.0 63.9 jit_solution(10413393181785084745)
XLA Ops:
  0.6 10.7 %project_sort.1 = (bf16[2304,256]{1,0:T(8,128)(2,1)}, f32[1,1024]{1,0:T(1,128)}) custom-call(bf16[2048,1024]{1,0:T(8,128)(2,1)} %e_hbm.3, bf16[1024,256]{1,0:T(8,128)(2,1)} %basis_ref.1, s32[16,128]{1,0:T(8,128)} %bitcast.8, s32[16,128]{1,0:T(8,128)} %bitcast.9), custom_call_target="tpu_custom_call" | custom-call | flops 3489660928 | bytes 5373952 | tf_op jit(solution)/shard_map/project_sort/pallas_call | solution.py:153
  11.3 0.0 copy-start.3
  11.3 7.4 %all-to-all-start = ((bf16[16,144,256]{2,1,0:T(8,128)(2,1)}), bf16[16,144,256]{2,1,0:T(8,128)(2,1)S(1)}, u32[]{:S(2)}, u32[]{:S(2)}) async-start(bf16[16,144,256]{2,1,0:T(8,128)(2,1)} %bitcast.7), calls=%async_computation | async-start | bytes 2359296 | tf_op jit(solution)/shard_map/all_to_all | solution.py:421
  18.8 0.0 copy-done.3
  18.8 9.0 %moments.1 = (bf16[512,1024]{1,0:T(8,128)(2,1)S(1)}, bf16[512,1024]{1,0:T(8,128)(2,1)S(1)}) custom-call(s32[1]{0:T(128)} %bitcast.me_ref, f32[1,1024]{1,0:T(1,128)S(1)} %copy-done.3, bf16[2048,1024]{1,0:T(8,128)(2,1)} %e_hbm.3), custom_call_target="tpu_custom_call" | custom-call | flops 4294967296 | bytes 6291456 | tf_op jit(solution)/shard_map/moments/pallas_call | solution.py:243
  27.8 0.5 collective-permute-start
  28.2 2.3 %collective-permute-done.refs_0_ = bf16[512,1024]{1,0:T(8,128)(2,1)S(1)} collective-permute-done((bf16[512,1024]{1,0:T(8,128)(2,1)S(1)}, bf16[512,1024]{1,0:T(8,128)(2,1)S(1)}, u32[]{:S(2)}, u32[]{:S(2)}) %collective-permute-start) | collective-permute-done | bytes 1048608 | tf_op jit(solution)/shard_map/ppermute | solution.py:304
  30.5 0.2 add_and_split.2
  30.7 0.0 copy-start
  30.8 0.0 copy-start.1
  30.8 0.0 copy-start.2
  30.8 2.0 %collective-permute-start.1 = (bf16[256,1024]{1,0:T(8,128)(2,1)S(1)}, bf16[256,1024]{1,0:T(8,128)(2,1)S(1)}, u32[]{:S(2)}, u32[]{:S(2)}) collective-permute-start(bf16[256,1024]{1,0:T(8,128)(2,1)S(1)} %get-tuple-element.20), channel_id=1, source_target_pairs={{0,2},{1,3},{2,0},{3,1},{4,6},{5,7},{6,4},{7,5},{8,10},{9,11},{10,... | collective-permute-start | bytes 1572872 | tf_op jit(solution)/shard_map/ppermute | solution.py:304
  32.7 16.0 %collective-permute-done.1.refs_0_ = bf16[256,1024]{1,0:T(8,128)(2,1)S(1)} collective-permute-done((bf16[256,1024]{1,0:T(8,128)(2,1)S(1)}, bf16[256,1024]{1,0:T(8,128)(2,1)S(1)}, u32[]{:S(2)}, u32[]{:S(2)}) %collective-permute-start.1) | collective-permute-done | bytes 524320 | tf_op jit(solution)/shard_map/ppermute | solution.py:304
  48.7 0.1 add_and_split.3
  48.8 4.1 %collective-permute-start.2 = (bf16[64,1024]{1,0:T(8,128)(2,1)S(1)}, bf16[64,1024]{1,0:T(8,128)(2,1)S(1)}, u32[]{:S(2)}, u32[]{:S(2)}) collective-permute-start(bf16[64,1024]{1,0:T(8,128)(2,1)S(1)} %get-tuple-element.22), channel_id=1, source_target_pairs={{0,8},{1,9},{2,10},{3,11},{4,12},{5,13},{6,14},{7,15},{8,0},{9,1},... | collective-permute-start | bytes 393224 | tf_op jit(solution)/shard_map/ppermute | solution.py:304
  52.9 0.0 collective-permute-start.3
  52.9 1.7 %collective-permute-start.4 = (bf16[64,1024]{1,0:T(8,128)(2,1)S(1)}, bf16[64,1024]{1,0:T(8,128)(2,1)S(1)}, u32[]{:S(2)}, u32[]{:S(2)}) collective-permute-start(bf16[64,1024]{1,0:T(8,128)(2,1)S(1)} %get-tuple-element.24), channel_id=1, source_target_pairs={{0,12},{1,13},{2,14},{3,15},{4,8},{5,9},{6,10},{7,11},{8,4},{9,5},... | collective-permute-start | bytes 393224 | tf_op jit(solution)/shard_map/ppermute | solution.py:304
  54.5 0.0 all-to-all-done
  54.5 0.0 copy-done
  54.6 0.0 copy-done.1
  54.6 0.0 copy-done.2
  54.6 4.5 %encode.1 = (bf16[2048,256]{1,0:T(8,128)(2,1)}, f32[64,1024]{1,0:T(8,128)S(1)}) custom-call(s32[1]{0:T(128)} %bitcast.me_ref, bf16[2304,256]{1,0:T(8,128)(2,1)S(1)} %bitcast.5, bf16[2304,256]{1,0:T(8,128)(2,1)S(1)} %bitcast.6, bf16[1024,256]{1,0:T(8,128)(2,1)S(1)} %copy-done, bf16[1024,256]{1,0:T(8,128)(2,1)S(1)} %copy-done.1, bf16[256,256]{1,0:T(8,128)(2,1)S(1)} %copy-done.2), custom_call_target="tpu_custom_call" | custom-call | flops 1342177280 | bytes 2097152 | tf_op jit(solution)/shard_map/encode/pallas_call | solution.py:380
  59.0 2.3 %collective-permute-done.2 = bf16[64,1024]{1,0:T(8,128)(2,1)S(1)} collective-permute-done((bf16[64,1024]{1,0:T(8,128)(2,1)S(1)}, bf16[64,1024]{1,0:T(8,128)(2,1)S(1)}, u32[]{:S(2)}, u32[]{:S(2)}) %collective-permute-start.2) | collective-permute-done | bytes 131104 | tf_op jit(solution)/shard_map/ppermute | solution.py:304
  61.3 0.0 collective-permute-done.3
  61.3 1.8 %collective-permute-done.4 = bf16[64,1024]{1,0:T(8,128)(2,1)S(1)} collective-permute-done((bf16[64,1024]{1,0:T(8,128)(2,1)S(1)}, bf16[64,1024]{1,0:T(8,128)(2,1)S(1)}, u32[]{:S(2)}, u32[]{:S(2)}) %collective-permute-start.4) | collective-permute-done | bytes 131104 | tf_op jit(solution)/shard_map/ppermute | solution.py:304
  63.1 0.8 %add_multiply_fusion = f32[64,1024]{1,0:T(8,128)} fusion(f32[64,1024]{1,0:T(8,128)S(1)} %get-tuple-element.25, bf16[64,1024]{1,0:T(8,128)(2,1)S(1)} %collective-permute-done.4, bf16[64,1024]{1,0:T(8,128)(2,1)S(1)} %collective-permute-done.3, f32[64,1024]{1,0:T(8,128)S(1)} %get-tuple-element.21, bf16[64,1024]{1,0:T(8,128)(2,1)S(1)} %collective-permute-done.2), kind=kLoop, calls=%fused_computation | loop fusion | flops 524288 | bytes 1179648 | tf_op jit(solution)/shard_map/div | solution.py:431
Async XLA Ops:
  11.3 7.4 %copy-start.3 = (f32[1,1024]{1,0:T(1,128)S(1)}, f32[1,1024]{1,0:T(1,128)}, u32[]{:S(2)}) copy-start(f32[1,1024]{1,0:T(1,128)} %get-tuple-element.16.mean_hbm) | copy-start | bytes 12292
  11.3 43.2 %all-to-all-start = ((bf16[16,144,256]{2,1,0:T(8,128)(2,1)}), bf16[16,144,256]{2,1,0:T(8,128)(2,1)S(1)}, u32[]{:S(2)}, u32[]{:S(2)}) async-start(bf16[16,144,256]{2,1,0:T(8,128)(2,1)} %bitcast.7), calls=%async_computation | async-start | bytes 2359296 | tf_op jit(solution)/shard_map/all_to_all | solution.py:421
  27.8 2.8 %collective-permute-start = (bf16[512,1024]{1,0:T(8,128)(2,1)S(1)}, bf16[512,1024]{1,0:T(8,128)(2,1)S(1)}, u32[]{:S(2)}, u32[]{:S(2)}) collective-permute-start(bf16[512,1024]{1,0:T(8,128)(2,1)S(1)} %get-tuple-element.18), channel_id=1, source_target_pairs={{0,1},{1,0},{2,3},{3,2},{4,5},{5,4},{6,7},{7,6},{8,9},{9,8},{10,11... | collective-permute-start | bytes 3145736 | tf_op jit(solution)/shard_map/ppermute | solution.py:304
  30.7 23.8 %copy-start = (bf16[1024,256]{1,0:T(8,128)(2,1)S(1)}, bf16[1024,256]{1,0:T(8,128)(2,1)}, u32[]{:S(2)}) copy-start(bf16[1024,256]{1,0:T(8,128)(2,1)} %basis_ref.1) | copy-start | bytes 1572868
  30.8 23.8 %copy-start.1 = (bf16[1024,256]{1,0:T(8,128)(2,1)S(1)}, bf16[1024,256]{1,0:T(8,128)(2,1)}, u32[]{:S(2)}) copy-start(bf16[1024,256]{1,0:T(8,128)(2,1)} %centroid_ref.1) | copy-start | bytes 1572868
  30.8 23.8 %copy-start.2 = (bf16[256,256]{1,0:T(8,128)(2,1)S(1)}, bf16[256,256]{1,0:T(8,128)(2,1)}, u32[]{:S(2)}) copy-start(bf16[256,256]{1,0:T(8,128)(2,1)} %rotation_ref.1) | copy-start | bytes 393220
  30.8 17.9 %collective-permute-start.1 = (bf16[256,1024]{1,0:T(8,128)(2,1)S(1)}, bf16[256,1024]{1,0:T(8,128)(2,1)S(1)}, u32[]{:S(2)}, u32[]{:S(2)}) collective-permute-start(bf16[256,1024]{1,0:T(8,128)(2,1)S(1)} %get-tuple-element.20), channel_id=1, source_target_pairs={{0,2},{1,3},{2,0},{3,1},{4,6},{5,7},{6,4},{7,5},{8,10},{9,11},{10,... | collective-permute-start | bytes 1572872 | tf_op jit(solution)/shard_map/ppermute | solution.py:304
  48.8 12.5 %collective-permute-start.2 = (bf16[64,1024]{1,0:T(8,128)(2,1)S(1)}, bf16[64,1024]{1,0:T(8,128)(2,1)S(1)}, u32[]{:S(2)}, u32[]{:S(2)}) collective-permute-start(bf16[64,1024]{1,0:T(8,128)(2,1)S(1)} %get-tuple-element.22), channel_id=1, source_target_pairs={{0,8},{1,9},{2,10},{3,11},{4,12},{5,13},{6,14},{7,15},{8,0},{9,1},... | collective-permute-start | bytes 393224 | tf_op jit(solution)/shard_map/ppermute | solution.py:304
  52.9 8.4 %collective-permute-start.3 = (bf16[64,1024]{1,0:T(8,128)(2,1)S(1)}, bf16[64,1024]{1,0:T(8,128)(2,1)S(1)}, u32[]{:S(2)}, u32[]{:S(2)}) collective-permute-start(bf16[64,1024]{1,0:T(8,128)(2,1)S(1)} %get-tuple-element.23), channel_id=1, source_target_pairs={{0,4},{1,5},{2,6},{3,7},{4,0},{5,1},{6,2},{7,3},{8,12},{9,13},{10,... | collective-permute-start | bytes 393224 | tf_op jit(solution)/shard_map/ppermute | solution.py:304
  52.9 10.2 %collective-permute-start.4 = (bf16[64,1024]{1,0:T(8,128)(2,1)S(1)}, bf16[64,1024]{1,0:T(8,128)(2,1)S(1)}, u32[]{:S(2)}, u32[]{:S(2)}) collective-permute-start(bf16[64,1024]{1,0:T(8,128)(2,1)S(1)} %get-tuple-element.24), channel_id=1, source_target_pairs={{0,12},{1,13},{2,14},{3,15},{4,8},{5,9},{6,10},{7,11},{8,4},{9,5},... | collective-permute-start | bytes 393224 | tf_op jit(solution)/shard_map/ppermute | solution.py:304

commit v7 on v3

--- a/solution.py
+++ b/solution.py
@@ -14,6 +14,7 @@
 CHUNK = 512
 TILE = 256
 GROUP = 4
+SHARES = 2
 VMEM_ALL = 60 * 1024 * 1024
 VMEM_SOME = 24 * 1024 * 1024
 VMEM_MOST = 48 * 1024 * 1024
@@ -26,14 +27,24 @@
     return high, middle, (rest - middle).astype(jnp.bfloat16).astype(jnp.float32)
 
 
-def rows_kernel(width, e_ref, basis_ref, owner_ref, slot_ref, rows_ref, mean_ref, y_ref, yb_ref, sum_ref, total_ref, target_ref, list_ref):
+def rows_kernel(
+    width, e_hbm, basis_ref, owner_ref, slot_ref,
+    rows_hbm, mean_ref,
+    e_ref, rows_ref, y_ref, yb_ref, sum_ref, total_ref, target_ref, list_ref, e_sem, sem,
+):
     step = pl.program_id(0)
     rows_here, feats = y_ref.shape
     wide = e_ref.shape[1]
     chunks = rows_here // LANES
 
+    def e_copy(c):
+        at = pl.ds(pl.multiple_of(c * CHUNK, CHUNK), CHUNK)
+        return pltpu.make_async_copy(e_hbm.at[at], e_ref.at[at], e_sem.at[c])
+
     @pl.when(step == 0)
     def _():
+        for c in range(rows_here // CHUNK):
+            e_copy(c).start()
         sum_ref[...] = jnp.zeros_like(sum_ref)
         total_ref[...] = jnp.zeros_like(total_ref)
         owner = owner_ref[...]
@@ -69,10 +80,13 @@
         list_ref[:, :CAP] = found[:width]
         list_ref[:, CAP:] = found[width:]
 
-    y = jnp.dot(e_ref[...], basis_ref[...], preferred_element_type=jnp.float32)
-    y_ref[pl.ds(pl.multiple_of(step * CHUNK, CHUNK), CHUNK), :] = y
+    e_copy(step).wait()
+    here = pl.ds(pl.multiple_of(step * CHUNK, CHUNK), CHUNK)
+    rows = e_ref[here, :]
+    y = jnp.dot(rows, basis_ref[...], preferred_element_type=jnp.float32)
+    y_ref[here, :] = y
     sum_ref[...] += jnp.sum(y.reshape(CHUNK // 8, 8, feats), 0)
-    total_ref[...] += jnp.sum(e_ref[...].astype(jnp.float32).reshape(CHUNK // 8, 8, wide), 0)
+    total_ref[...] += jnp.sum(rows.astype(jnp.float32).reshape(CHUNK // 8, 8, wide), 0)
 
     @pl.when(step == pl.num_programs(0) - 1)
     def _():
@@ -91,7 +105,7 @@
 
         place = lax.broadcasted_iota(jnp.int32, (GROUP * CAP, LANES), 0).astype(jnp.int16)
 
-        def sort_group(g, _):
+        def sort_group(g):
             first = g * GROUP
             pieces = []
             for c in range(chunks):
@@ -106,14 +120,24 @@
                 rows_ref[pl.ds(base, CAP), :] = rows[j * CAP:(j + 1) * CAP]
                 notes = jnp.concatenate([common, list_ref[pl.ds(first + j, 1), :]], 0)
                 rows_ref[pl.ds(pl.multiple_of(base + CAP, 16), NOTES), :] = notes.astype(jnp.bfloat16)
-            return 0
+            at = pl.ds(pl.multiple_of(g * (GROUP * SPAN), 16), GROUP * SPAN)
+            return pltpu.make_async_copy(rows_ref.at[at], rows_hbm.at[at], sem.at[g])
 
         groups = width // GROUP
         if groups <= 4:
+            copies = []
             for g in range(groups):
-                sort_group(g, 0)
+                copies.append(sort_group(g))
+                copies[g].start()
+            for copy in copies:
+                copy.wait()
         else:
-            lax.fori_loop(0, groups, sort_group, 0)
+
+            @pl.loop(0, groups)
+            def _(g):
+                copy = sort_group(g)
+                copy.start()
+                copy.wait()
 
 
 def project_and_sort(width, embeddings, basis, list_owner, list_slot):
@@ -125,13 +149,13 @@
         functools.partial(rows_kernel, width),
         grid=(rows_here // CHUNK,),
         in_specs=[
-            pl.BlockSpec((CHUNK, wide), lambda i: (i, 0)),
+            pl.BlockSpec(memory_space=pl.ANY),
             pl.BlockSpec((wide, feats), lambda i: (0, 0)),
             pl.BlockSpec((lanes, LANES), lambda i: (0, 0)),
             pl.BlockSpec((lanes, LANES), lambda i: (0, 0)),
         ],
         out_specs=[
-            pl.BlockSpec((slots, feats), lambda i: (0, 0)),
+            pl.BlockSpec(memory_space=pl.ANY),
             pl.BlockSpec((1, wide), lambda i: (0, 0)),
         ],
         out_shape=[
@@ -139,12 +163,16 @@
             jax.ShapeDtypeStruct((1, wide), jnp.float32),
         ],
         scratch_shapes=[
+            pltpu.VMEM((rows_here, wide), jnp.bfloat16),
+            pltpu.VMEM((slots, feats), jnp.bfloat16),
             pltpu.VMEM((rows_here, feats), jnp.float32),
             pltpu.VMEM((rows_here, feats), jnp.bfloat16),
             pltpu.VMEM((8, feats), jnp.float32),
             pltpu.VMEM((8, wide), jnp.float32),
             pltpu.VMEM((lanes, LANES), jnp.int32),
             pltpu.VMEM((width, 2 * CAP), jnp.float32),
+            pltpu.SemaphoreType.DMA((rows_here // CHUNK,)),
+            pltpu.SemaphoreType.DMA((width // GROUP,)),
         ],
         compiler_params=pltpu.CompilerParams(vmem_limit_bytes=VMEM_ALL),
         cost_estimate=pl.CostEstimate(
@@ -225,56 +253,79 @@
     )(me.reshape(1), mean, embeddings)
 
 
-def add_kernel(pieces, keep_ref, *refs):
-    came, outs = refs[:-pieces], refs[-pieces:]
-    size = outs[0].shape[0]
-    for p in range(pieces):
-        at = slice(p * size, (p + 1) * size)
-        held = keep_ref[at]
-        for ref in came:
-            held = held + ref[at].astype(jnp.float32)
-        outs[p][...] = held.astype(outs[p].dtype)
-
-
-def add_and_split(keep, came, pieces):
-    rows, wide = keep.shape
+def add_kernel(shares, pieces, keep_ref, *refs):
+    outs = refs[len(refs) - shares * pieces:]
+    came = refs[:len(refs) - shares * pieces]
+    rows, columns = outs[0].shape
+    for h in range(shares):
+        across = slice(h * columns, (h + 1) * columns)
+        for p in range(pieces):
+            at = slice(p * rows, (p + 1) * rows)
+            held = keep_ref[at, across]
+            for ref in came:
+                held = held + ref[at, across].astype(jnp.float32)
+            out = outs[h * pieces + p]
+            out[...] = held.astype(out.dtype)
+
+
+def add_and_split(keep, came, shares, pieces):
+    rows, columns = keep.shape
+    vmem = pl.BlockSpec(memory_space=pltpu.VMEM)
+    shape = (rows // pieces, columns // shares)
+    kinds = [jnp.float32] + [jnp.bfloat16] * (pieces - 1)
+    outs = pl.pallas_call(
+        functools.partial(add_kernel, shares, pieces),
+        in_specs=[vmem] * (1 + len(came)),
+        out_specs=[vmem] * (shares * pieces),
+        out_shape=[jax.ShapeDtypeStruct(shape, kind) for kind in kinds * shares],
+        compiler_params=pltpu.CompilerParams(vmem_limit_bytes=VMEM_SOME),
+        cost_estimate=pl.CostEstimate(flops=2 * rows * columns, bytes_accessed=10 * rows * columns, transcendentals=0),
+        name="add_and_split",
+    )(keep, *came)
+    return [outs[h * pieces:(h + 1) * pieces] for h in range(shares)]
+
+
+def finish_kernel(total, between_ref, *refs):
+    out_ref = refs[-1]
+    each = (len(refs) - 1) // SHARES
+    columns = out_ref.shape[1] // SHARES
+    for h in range(SHARES):
+        across = slice(h * columns, (h + 1) * columns)
+        held = refs[h * each][...]
+        for ref in refs[h * each + 1:(h + 1) * each]:
+            held = held + ref[...].astype(jnp.float32)
+        out_ref[:, across] = (held + between_ref[:, across]) / total
+
+
+def finish(total, between, keeps, came):
+    parts = [part for keep, pieces in zip(keeps, came) for part in (keep, *pieces)]
     vmem = pl.BlockSpec(memory_space=pltpu.VMEM)
     return pl.pallas_call(
-        functools.partial(add_kernel, pieces),
-        in_specs=[vmem] * (1 + len(came)),
-        out_specs=[vmem] * pieces,
-        out_shape=[
-            jax.ShapeDtypeStruct((rows // pieces, wide), jnp.float32 if p == 0 else jnp.bfloat16) for p in range(pieces)
-        ],
+        functools.partial(finish_kernel, total),
+        in_specs=[vmem] * (1 + len(parts)),
+        out_specs=vmem,
+        out_shape=jax.ShapeDtypeStruct(between.shape, jnp.float32),
         compiler_params=pltpu.CompilerParams(vmem_limit_bytes=VMEM_SOME),
-        cost_estimate=pl.CostEstimate(flops=2 * rows * wide, bytes_accessed=10 * rows * wide, transcendentals=0),
-        name="add_and_split",
-    )(keep, *came)
-
-
-def partners(width, apart):
-    return [(i, i ^ apart) for i in range(width)]
+        cost_estimate=pl.CostEstimate(flops=8 * between.size, bytes_accessed=16 * between.size, transcendentals=0),
+        name="finish",
+    )(between, *parts)
 
 
 def halving_stages(width):
     strides = [1 << k for k in range(width.bit_length() - 1)]
-    return [strides[:1], strides[1:3]] + [[s] for s in strides[3:]]
-
-
-def reduce_blocks(width, keep, send):
-    stages = halving_stages(width)
-    out = [send]
-    for n, stage in enumerate(stages):
-        came = []
-        for p in range(1, 1 << len(stage)):
-            apart = sum(s for k, s in enumerate(stage) if (p >> (len(stage) - 1 - k)) & 1)
-            came.append(lax.ppermute(out[p - 1], "wide", partners(width, apart)))
-        if n + 1 < len(stages):
-            keep, *out = add_and_split(keep, came, 1 << len(stages[n + 1]))
-    return keep, came
-
-
-def encode_kernel(total, me_ref, got_ref, all_ref, basis_ref, centroid_ref, rotation_ref, out_ref, between_ref, delta_ref, scale_ref, list_ref, apart_ref):
+    return [[s] for s in strides[:-2]] + [strides[-2:]]
+
+
+def exchange(width, stage, out):
+    came = []
+    for p in range(1, 1 << len(stage)):
+        apart = sum(s for k, s in enumerate(stage) if (p >> (len(stage) - 1 - k)) & 1)
+        came.append(lax.ppermute(out[p - 1], "wide", [(i, i ^ apart) for i in range(width)]))
+    return came
+
+
+def encode_kernel(total, me_ref, got_ref, all_ref, basis_ref, centroid_ref, rotation_ref, *refs):
+    out_ref, between_ref, delta_ref, scale_ref, list_ref, apart_ref = refs[-6:]
     step = pl.program_id(0)
     width = delta_ref.shape[0]
     feats = out_ref.shape[1]
@@ -341,7 +392,7 @@
     ).astype(jnp.bfloat16)
 
 
-def encode(width, total, me, got, basis, centroids, rotation):
+def encode(width, total, me, got, basis, centroids, rotation, after):
     wide, feats = basis.shape
     owned = centroids.shape[0]
     slots = width * CAP
@@ -356,7 +407,8 @@
             pl.BlockSpec((wide, feats), whole),
             pl.BlockSpec((owned, feats), whole),
             pl.BlockSpec((feats, feats), whole),
-        ],
+        ]
+        + [pl.BlockSpec(memory_space=pl.ANY)] * len(after),
         out_specs=[
             pl.BlockSpec((GROUP * CAP, feats), lambda i: (i, 0)),
             pl.BlockSpec((wide // width, wide), whole),
@@ -376,7 +428,7 @@
             flops=2 * slots * feats * (owned + feats), bytes_accessed=4 * slots * feats, transcendentals=0
         ),
         name="encode",
-    )(me.reshape(1), got, got, basis, centroids, rotation)
+    )(me.reshape(1), got, got, basis, centroids, rotation, *after)
 
 
 def local(embeddings, basis, list_owner, list_slot, centroids, rotation):
@@ -390,11 +442,20 @@
     got = lax.all_to_all(rows.reshape(width, SPAN, feats), "wide", split_axis=0, concat_axis=0, tiled=True)
 
     keep, send = moments(width, me, embeddings, mean)
-    keep, came = reduce_blocks(width, keep, send)
-    encoded, between = encode(width, total, me, got.reshape(width * SPAN, feats), basis, centroids, rotation)
-    for block in came:
-        keep = keep + block.astype(jnp.float32)
-    covariance = (keep + between) / total
+    stages = halving_stages(width)
+    came = exchange(width, stages[0], [send])
+    shares = add_and_split(keep, came, SHARES, 1 << len(stages[1]))
+    last = []
+    for share in shares:
+        for n in range(1, len(stages) - 1):
+            came = exchange(width, stages[n], share[1:])
+            (share,) = add_and_split(share[0], came, 1, 1 << len(stages[n + 1]))
+        last.append(share)
+    came = [exchange(width, stages[-1], share[1:]) for share in last]
+    encoded, between = encode(
+        width, total, me, got.reshape(width * SPAN, feats), basis, centroids, rotation, [share[1] for share in last]
+    )
+    covariance = finish(total, between, [share[0] for share in last], came)
     return (encoded, covariance)
 
 

time: 60.6 us -> 57.8 us (0.954)
  waiting for transfers between devices: 24.6 us -> 14.4 us
  starting transfers between devices: 14.1 us -> 21.7 us
  other arithmetic: 0.74 us -> 0 us
    ppermute x5 -> x9, waiting for transfers between devices: 24.6 us -> 14.4 us  [exchange(): lax.ppermute(out[p - 1], 'wide', [(i, i ^ apart) for i in range(width)])]
    ppermute x5 -> x9, starting transfers between devices: 6.6 us -> 14.3 us  [exchange(): lax.ppermute(out[p - 1], 'wide', [(i, i ^ apart) for i in range(width)])]
    pallas_call x2 -> x4, Pallas kernels: 0.28 us -> 1.04 us  [the longest x1 0.77 us: finish(): pl.pallas_call(functools.partial(finish_kernel, total), in_specs=[vmem] *...]
    div x1 -> x0, other arithmetic: 0.74 us -> none  [local(): covariance = (keep + between) / total]
  transfers between devices with their start and end apart: 6 -> 10, of which waited for: 4 -> 4; matrix products, arithmetic and copies ran while one was open for 0% -> 0% of each run, Pallas kernels for 20% -> 21%
where the time goes in v7:
time: 57.8 us; the launch traced here: 57.5 us
  starting transfers between devices  21.7 us (38%)
  Pallas kernels  20.7 us (36%)
  waiting for transfers between devices  14.4 us (25%)
  between operations  0.73 us (1%)
    ppermute x9, waiting for transfers between devices, exchange(): lax.ppermute(out[p - 1], 'wide', [(i, i ^ apart) for i in range(width)])  14.4 us
    ppermute x9, starting transfers between devices, exchange(): lax.ppermute(out[p - 1], 'wide', [(i, i ^ apart) for i in range(width)])  14.3 us
    pallas_call x1, Pallas kernels, project_and_sort(): pl.pallas_call(functools.partial(rows_kernel, width), grid=(rows_here //...  8.06 us
    all_to_all x1, starting transfers between devices, local(): lax.all_to_all(rows.reshape(width, SPAN, feats), 'wide', split_axis=0, co...  7.39 us
    pallas_call x1, Pallas kernels, moments(): pl.pallas_call(functools.partial(moments_kernel, width), in_specs=[pl.Blo...  7.16 us
    pallas_call x1, Pallas kernels, encode(): pl.pallas_call(functools.partial(encode_kernel, total), grid=(width // GR...  4.47 us
  transfers between devices with their start and end apart: 10, of which 4 were waited for; matrix products, arithmetic and copies ran while one was open for 0% of the time, Pallas kernels for 21%

profile of v7, /device:TPU:0, one launch (start us, length us, event | category | flops | bytes accessed | tf_op | source)
XLA Modules:
  0.0 57.5 jit_solution(15427499453904939915)
XLA Ops:
  0.6 8.1 %project_sort.1 = (bf16[2304,256]{1,0:T(8,128)(2,1)}, f32[1,1024]{1,0:T(1,128)}) custom-call(bf16[2048,1024]{1,0:T(8,128)(2,1)} %e_hbm.3, bf16[1024,256]{1,0:T(8,128)(2,1)} %basis_ref.3, s32[16,128]{1,0:T(8,128)} %bitcast.8, s32[16,128]{1,0:T(8,128)} %bitcast.9), custom_call_target="tpu_custom_call" | custom-call | flops 3489660928 | bytes 5373952 | tf_op jit(solution)/shard_map/project_sort/pallas_call | solution.py:148
  8.7 0.0 copy-start.3
  8.7 7.4 %all-to-all-start = ((bf16[16,144,256]{2,1,0:T(8,128)(2,1)}), bf16[16,144,256]{2,1,0:T(8,128)(2,1)S(1)}, u32[]{:S(2)}, u32[]{:S(2)}) async-start(bf16[16,144,256]{2,1,0:T(8,128)(2,1)} %bitcast.7), calls=%async_computation | async-start | bytes 2359296 | tf_op jit(solution)/shard_map/all_to_all | solution.py:442
  16.1 0.0 copy-done.3
  16.1 7.2 %moments.1 = (f32[512,1024]{1,0:T(8,128)S(1)}, bf16[512,1024]{1,0:T(8,128)(2,1)S(1)}) custom-call(s32[1]{0:T(128)} %bitcast.me_ref, f32[1,1024]{1,0:T(1,128)S(1)} %copy-done.3, bf16[2048,1024]{1,0:T(8,128)(2,1)} %e_hbm.3), custom_call_target="tpu_custom_call" | custom-call | flops 4294967296 | bytes 7340032 | tf_op jit(solution)/shard_map/moments/pallas_call | solution.py:233
  23.3 0.5 collective-permute-start
  23.8 2.3 %collective-permute-done.refs_0_ = bf16[512,1024]{1,0:T(8,128)(2,1)S(1)} collective-permute-done((bf16[512,1024]{1,0:T(8,128)(2,1)S(1)}, bf16[512,1024]{1,0:T(8,128)(2,1)S(1)}, u32[]{:S(2)}, u32[]{:S(2)}) %collective-permute-start) | collective-permute-done | bytes 1048608 | tf_op jit(solution)/shard_map/ppermute | solution.py:323
  26.1 0.0 copy-start
  26.1 0.0 copy-start.1
  26.1 0.2 add_and_split.3
  26.2 1.9 %collective-permute-start.1 = (bf16[256,512]{1,0:T(8,128)(2,1)S(1)}, bf16[256,512]{1,0:T(8,128)(2,1)S(1)}, u32[]{:S(2)}, u32[]{:S(2)}) collective-permute-start(bf16[256,512]{1,0:T(8,128)(2,1)S(1)} %get-tuple-element.25), channel_id=1, source_target_pairs={{0,2},{1,3},{2,0},{3,1},{4,6},{5,7},{6,4},{7,5},{8,10},{9,11},{10,... | collective-permute-start | bytes 786440 | tf_op jit(solution)/shard_map/ppermute | solution.py:323
  28.2 0.2 collective-permute-start.2
  28.3 9.5 %collective-permute-done.1.refs_0_ = bf16[256,512]{1,0:T(8,128)(2,1)S(1)} collective-permute-done((bf16[256,512]{1,0:T(8,128)(2,1)S(1)}, bf16[256,512]{1,0:T(8,128)(2,1)S(1)}, u32[]{:S(2)}, u32[]{:S(2)}) %collective-permute-start.1) | collective-permute-done | bytes 262176 | tf_op jit(solution)/shard_map/ppermute | solution.py:323
  37.9 3.3 %collective-permute-start.4 = (bf16[64,512]{1,0:T(8,128)(2,1)S(1)}, bf16[64,512]{1,0:T(8,128)(2,1)S(1)}, u32[]{:S(2)}, u32[]{:S(2)}) collective-permute-start(bf16[64,512]{1,0:T(8,128)(2,1)S(1)} %get-tuple-element.33), channel_id=1, source_target_pairs={{0,4},{1,5},{2,6},{3,7},{4,0},{5,1},{6,2},{7,3},{8,12},{9,13},{10,... | collective-permute-start | bytes 196616 | tf_op jit(solution)/shard_map/ppermute | solution.py:323
  41.2 3.1 %collective-permute-start.5 = (bf16[64,512]{1,0:T(8,128)(2,1)S(1)}, bf16[64,512]{1,0:T(8,128)(2,1)S(1)}, u32[]{:S(2)}, u32[]{:S(2)}) collective-permute-start(bf16[64,512]{1,0:T(8,128)(2,1)S(1)} %get-tuple-element.34), channel_id=1, source_target_pairs={{0,12},{1,13},{2,14},{3,15},{4,8},{5,9},{6,10},{7,11},{8,4},{9,5},... | collective-permute-start | bytes 196616 | tf_op jit(solution)/shard_map/ppermute | solution.py:323
  44.3 0.0 collective-permute-start.3
  44.3 1.3 %collective-permute-done.2.refs_0_ = bf16[256,512]{1,0:T(8,128)(2,1)S(1)} collective-permute-done((bf16[256,512]{1,0:T(8,128)(2,1)S(1)}, bf16[256,512]{1,0:T(8,128)(2,1)S(1)}, u32[]{:S(2)}, u32[]{:S(2)}) %collective-permute-start.2) | collective-permute-done | bytes 262176 | tf_op jit(solution)/shard_map/ppermute | solution.py:323
  45.7 2.3 %collective-permute-start.7 = (bf16[64,512]{1,0:T(8,128)(2,1)S(1)}, bf16[64,512]{1,0:T(8,128)(2,1)S(1)}, u32[]{:S(2)}, u32[]{:S(2)}) collective-permute-start(bf16[64,512]{1,0:T(8,128)(2,1)S(1)} %get-tuple-element.36), channel_id=1, source_target_pairs={{0,4},{1,5},{2,6},{3,7},{4,0},{5,1},{6,2},{7,3},{8,12},{9,13},{10,... | collective-permute-start | bytes 196616 | tf_op jit(solution)/shard_map/ppermute | solution.py:323
  47.9 3.0 %collective-permute-start.8 = (bf16[64,512]{1,0:T(8,128)(2,1)S(1)}, bf16[64,512]{1,0:T(8,128)(2,1)S(1)}, u32[]{:S(2)}, u32[]{:S(2)}) collective-permute-start(bf16[64,512]{1,0:T(8,128)(2,1)S(1)} %get-tuple-element.37), channel_id=1, source_target_pairs={{0,12},{1,13},{2,14},{3,15},{4,8},{5,9},{6,10},{7,11},{8,4},{9,5},... | collective-permute-start | bytes 196616 | tf_op jit(solution)/shard_map/ppermute | solution.py:323
  51.0 0.0 collective-permute-done.4.refs_2_
  51.0 0.0 collective-permute-start.6
  51.0 0.0 all-to-all-done
  51.0 0.0 copy-done
  51.0 0.0 copy-done.1
  51.0 0.0 copy-done.2
  51.0 4.5 %encode.1 = (bf16[2048,256]{1,0:T(8,128)(2,1)}, f32[64,1024]{1,0:T(8,128)S(1)}) custom-call(s32[1]{0:T(128)} %bitcast.me_ref, bf16[2304,256]{1,0:T(8,128)(2,1)S(1)} %bitcast.5, bf16[2304,256]{1,0:T(8,128)(2,1)S(1)} %bitcast.6, bf16[1024,256]{1,0:T(8,128)(2,1)S(1)} %copy-done, bf16[1024,256]{1,0:T(8,128)(2,1)S(1)} %copy-done.1, ...), custom_call_target="tpu_custom_call" | custom-call | flops 1342177280 | bytes 2097152 | tf_op jit(solution)/shard_map/encode/pallas_call | solution.py:400
  55.5 0.0 collective-permute-done.5.refs_3_
  55.5 0.0 collective-permute-done.3.refs_1_
  55.5 0.0 collective-permute-done.7.refs_6_
  55.5 0.0 collective-permute-done.8.refs_7_
  55.5 1.2 %collective-permute-done.6.refs_5_ = bf16[64,512]{1,0:T(8,128)(2,1)S(1)} collective-permute-done((bf16[64,512]{1,0:T(8,128)(2,1)S(1)}, bf16[64,512]{1,0:T(8,128)(2,1)S(1)}, u32[]{:S(2)}, u32[]{:S(2)}) %collective-permute-start.6) | collective-permute-done | bytes 65568 | tf_op jit(solution)/shard_map/ppermute | solution.py:323
  56.7 0.8 %finish.1 = f32[64,1024]{1,0:T(8,128)} custom-call(f32[64,1024]{1,0:T(8,128)S(1)} %get-tuple-element.31.between_ref, f32[64,512]{1,0:T(8,128)S(1)} %get-tuple-element.32.refs_0_, bf16[64,512]{1,0:T(8,128)(2,1)S(1)} %collective-permute-done.3.refs_1_, bf16[64,512]{1,0:T(8,128)(2,1)S(1)} %collective-permute-done.4.refs_2_, ...), custom_call_target="tpu_custom_call" | custom-call | flops 524288 | bytes 1048576 | tf_op jit(solution)/shard_map/finish/pallas_call | solution.py:303
  (3 shorter events, 0.1 us)
Async XLA Ops:
  8.7 7.4 %copy-start.3 = (f32[1,1024]{1,0:T(1,128)S(1)}, f32[1,1024]{1,0:T(1,128)}, u32[]{:S(2)}) copy-start(f32[1,1024]{1,0:T(1,128)} %get-tuple-element.21.mean_hbm) | copy-start | bytes 12292
  8.7 42.3 %all-to-all-start = ((bf16[16,144,256]{2,1,0:T(8,128)(2,1)}), bf16[16,144,256]{2,1,0:T(8,128)(2,1)S(1)}, u32[]{:S(2)}, u32[]{:S(2)}) async-start(bf16[16,144,256]{2,1,0:T(8,128)(2,1)} %bitcast.7), calls=%async_computation | async-start | bytes 2359296 | tf_op jit(solution)/shard_map/all_to_all | solution.py:442
  23.3 2.8 %collective-permute-start = (bf16[512,1024]{1,0:T(8,128)(2,1)S(1)}, bf16[512,1024]{1,0:T(8,128)(2,1)S(1)}, u32[]{:S(2)}, u32[]{:S(2)}) collective-permute-start(bf16[512,1024]{1,0:T(8,128)(2,1)S(1)} %get-tuple-element.23), channel_id=1, source_target_pairs={{0,1},{1,0},{2,3},{3,2},{4,5},{5,4},{6,7},{7,6},{8,9},{9,8},{10,11... | collective-permute-start | bytes 3145736 | tf_op jit(solution)/shard_map/ppermute | solution.py:323
  26.1 24.9 %copy-start = (bf16[1024,256]{1,0:T(8,128)(2,1)S(1)}, bf16[1024,256]{1,0:T(8,128)(2,1)}, u32[]{:S(2)}) copy-start(bf16[1024,256]{1,0:T(8,128)(2,1)} %basis_ref.3) | copy-start | bytes 1572868
  26.1 24.9 %copy-start.1 = (bf16[1024,256]{1,0:T(8,128)(2,1)S(1)}, bf16[1024,256]{1,0:T(8,128)(2,1)}, u32[]{:S(2)}) copy-start(bf16[1024,256]{1,0:T(8,128)(2,1)} %centroid_ref.1) | copy-start | bytes 1572868
  26.1 24.9 %copy-start.2 = (bf16[256,256]{1,0:T(8,128)(2,1)S(1)}, bf16[256,256]{1,0:T(8,128)(2,1)}, u32[]{:S(2)}) copy-start(bf16[256,256]{1,0:T(8,128)(2,1)} %rotation_ref.1) | copy-start | bytes 393220
  26.2 11.6 %collective-permute-start.1 = (bf16[256,512]{1,0:T(8,128)(2,1)S(1)}, bf16[256,512]{1,0:T(8,128)(2,1)S(1)}, u32[]{:S(2)}, u32[]{:S(2)}) collective-permute-start(bf16[256,512]{1,0:T(8,128)(2,1)S(1)} %get-tuple-element.25), channel_id=1, source_target_pairs={{0,2},{1,3},{2,0},{3,1},{4,6},{5,7},{6,4},{7,5},{8,10},{9,11},{10,... | collective-permute-start | bytes 786440 | tf_op jit(solution)/shard_map/ppermute | solution.py:323
  28.2 17.4 %collective-permute-start.2 = (bf16[256,512]{1,0:T(8,128)(2,1)S(1)}, bf16[256,512]{1,0:T(8,128)(2,1)S(1)}, u32[]{:S(2)}, u32[]{:S(2)}) collective-permute-start(bf16[256,512]{1,0:T(8,128)(2,1)S(1)} %get-tuple-element.28), channel_id=1, source_target_pairs={{0,2},{1,3},{2,0},{3,1},{4,6},{5,7},{6,4},{7,5},{8,10},{9,11},{10,... | collective-permute-start | bytes 786440 | tf_op jit(solution)/shard_map/ppermute | solution.py:323
  37.9 13.1 %collective-permute-start.4 = (bf16[64,512]{1,0:T(8,128)(2,1)S(1)}, bf16[64,512]{1,0:T(8,128)(2,1)S(1)}, u32[]{:S(2)}, u32[]{:S(2)}) collective-permute-start(bf16[64,512]{1,0:T(8,128)(2,1)S(1)} %get-tuple-element.33), channel_id=1, source_target_pairs={{0,4},{1,5},{2,6},{3,7},{4,0},{5,1},{6,2},{7,3},{8,12},{9,13},{10,... | collective-permute-start | bytes 196616 | tf_op jit(solution)/shard_map/ppermute | solution.py:323
  41.2 14.3 %collective-permute-start.5 = (bf16[64,512]{1,0:T(8,128)(2,1)S(1)}, bf16[64,512]{1,0:T(8,128)(2,1)S(1)}, u32[]{:S(2)}, u32[]{:S(2)}) collective-permute-start(bf16[64,512]{1,0:T(8,128)(2,1)S(1)} %get-tuple-element.34), channel_id=1, source_target_pairs={{0,12},{1,13},{2,14},{3,15},{4,8},{5,9},{6,10},{7,11},{8,4},{9,5},... | collective-permute-start | bytes 196616 | tf_op jit(solution)/shard_map/ppermute | solution.py:323
  44.3 11.2 %collective-permute-start.3 = (bf16[64,512]{1,0:T(8,128)(2,1)S(1)}, bf16[64,512]{1,0:T(8,128)(2,1)S(1)}, u32[]{:S(2)}, u32[]{:S(2)}) collective-permute-start(bf16[64,512]{1,0:T(8,128)(2,1)S(1)} %get-tuple-element.26.refs_0_), channel_id=1, source_target_pairs={{0,8},{1,9},{2,10},{3,11},{4,12},{5,13},{6,14},{7,15},{8,0},{9,1},... | collective-permute-start | bytes 196616 | tf_op jit(solution)/shard_map/ppermute | solution.py:323
  45.7 9.8 %collective-permute-start.7 = (bf16[64,512]{1,0:T(8,128)(2,1)S(1)}, bf16[64,512]{1,0:T(8,128)(2,1)S(1)}, u32[]{:S(2)}, u32[]{:S(2)}) collective-permute-start(bf16[64,512]{1,0:T(8,128)(2,1)S(1)} %get-tuple-element.36), channel_id=1, source_target_pairs={{0,4},{1,5},{2,6},{3,7},{4,0},{5,1},{6,2},{7,3},{8,12},{9,13},{10,... | collective-permute-start | bytes 196616 | tf_op jit(solution)/shard_map/ppermute | solution.py:323
  47.9 7.6 %collective-permute-start.8 = (bf16[64,512]{1,0:T(8,128)(2,1)S(1)}, bf16[64,512]{1,0:T(8,128)(2,1)S(1)}, u32[]{:S(2)}, u32[]{:S(2)}) collective-permute-start(bf16[64,512]{1,0:T(8,128)(2,1)S(1)} %get-tuple-element.37), channel_id=1, source_target_pairs={{0,12},{1,13},{2,14},{3,15},{4,8},{5,9},{6,10},{7,11},{8,4},{9,5},... | collective-permute-start | bytes 196616 | tf_op jit(solution)/shard_map/ppermute | solution.py:323
  51.0 5.8 %collective-permute-start.6 = (bf16[64,512]{1,0:T(8,128)(2,1)S(1)}, bf16[64,512]{1,0:T(8,128)(2,1)S(1)}, u32[]{:S(2)}, u32[]{:S(2)}) collective-permute-start(bf16[64,512]{1,0:T(8,128)(2,1)S(1)} %get-tuple-element.29.refs_1_), channel_id=1, source_target_pairs={{0,8},{1,9},{2,10},{3,11},{4,12},{5,13},{6,14},{7,15},{8,0},{9,1},... | collective-permute-start | bytes 196616 | tf_op jit(solution)/shard_map/ppermute | solution.py:323

commit v8 on v7

--- a/solution.py
+++ b/solution.py
@@ -28,9 +28,9 @@
 
 
 def rows_kernel(
-    width, e_hbm, basis_ref, owner_ref, slot_ref,
-    rows_hbm, mean_ref,
-    e_ref, rows_ref, y_ref, yb_ref, sum_ref, total_ref, target_ref, list_ref, e_sem, sem,
+    width, e_hbm, basis_hbm, owner_hbm, slot_hbm,
+    rows_hbm, mean_hbm,
+    owner_ref, slot_ref, mean_ref, basis_ref, e_ref, rows_ref, y_ref, yb_ref, sum_ref, total_ref, target_ref, list_ref, e_sem, small_sem, sem,
 ):
     step = pl.program_id(0)
     rows_here, feats = y_ref.shape
@@ -43,8 +43,16 @@
 
     @pl.when(step == 0)
     def _():
-        for c in range(rows_here // CHUNK):
+        owner_copy = pltpu.make_async_copy(owner_hbm, owner_ref, small_sem.at[0])
+        slot_copy = pltpu.make_async_copy(slot_hbm, slot_ref, small_sem.at[1])
+        basis_copy = pltpu.make_async_copy(basis_hbm, basis_ref, small_sem.at[2])
+        owner_copy.start()
+        e_copy(0).start()
+        slot_copy.start()
+        basis_copy.start()
+        for c in range(1, rows_here // CHUNK):
             e_copy(c).start()
+        owner_copy.wait()
         sum_ref[...] = jnp.zeros_like(sum_ref)
         total_ref[...] = jnp.zeros_like(total_ref)
         owner = owner_ref[...]
@@ -65,6 +73,7 @@
             carry = carry + counts[at]
             target_ref[c:c + 1, :] = owner[c:c + 1, :] * CAP + ranks[c]
 
+        slot_copy.wait()
         slot = slot_ref[...] + 1
         high, low = (slot >> 5).astype(jnp.float32), (slot & 31).astype(jnp.float32)
         spots = lax.broadcasted_iota(jnp.int32, (CAP, LANES), 0)
@@ -79,6 +88,7 @@
         found = lax.dot_general(digits, placed, (((1,), (1,)), ((), ())), preferred_element_type=jnp.float32)
         list_ref[:, :CAP] = found[:width]
         list_ref[:, CAP:] = found[width:]
+        basis_copy.wait()
 
     e_copy(step).wait()
     here = pl.ds(pl.multiple_of(step * CHUNK, CHUNK), CHUNK)
@@ -99,6 +109,8 @@
             yb_ref[at, :] = centred.astype(jnp.bfloat16)
         mean = jnp.sum(total_ref[...], 0, keepdims=True) / rows_here
         mean_ref[...] = mean
+        mean_copy = pltpu.make_async_copy(mean_ref, mean_hbm, small_sem.at[3])
+        mean_copy.start()
         parts = in_three(mean)
         common = [part[:, q * feats:(q + 1) * feats] for part in parts for q in range(wide // feats)]
         common = jnp.concatenate(common + list(in_three(jnp.sum(square, 0, keepdims=True))), 0)
@@ -139,6 +151,8 @@
                 copy.start()
                 copy.wait()
 
+        mean_copy.wait()
+
 
 def project_and_sort(width, embeddings, basis, list_owner, list_slot):
     rows_here, wide = embeddings.shape
@@ -148,21 +162,17 @@
     return pl.pallas_call(
         functools.partial(rows_kernel, width),
         grid=(rows_here // CHUNK,),
-        in_specs=[
-            pl.BlockSpec(memory_space=pl.ANY),
-            pl.BlockSpec((wide, feats), lambda i: (0, 0)),
-            pl.BlockSpec((lanes, LANES), lambda i: (0, 0)),
-            pl.BlockSpec((lanes, LANES), lambda i: (0, 0)),
-        ],
-        out_specs=[
-            pl.BlockSpec(memory_space=pl.ANY),
-            pl.BlockSpec((1, wide), lambda i: (0, 0)),
-        ],
+        in_specs=[pl.BlockSpec(memory_space=pl.ANY)] * 4,
+        out_specs=[pl.BlockSpec(memory_space=pl.ANY)] * 2,
         out_shape=[
             jax.ShapeDtypeStruct((slots, feats), jnp.bfloat16),
             jax.ShapeDtypeStruct((1, wide), jnp.float32),
         ],
         scratch_shapes=[
+            pltpu.VMEM((lanes, LANES), jnp.int32),
+            pltpu.VMEM((lanes, LANES), jnp.int32),
+            pltpu.VMEM((1, wide), jnp.float32),
+            pltpu.VMEM((wide, feats), jnp.bfloat16),
             pltpu.VMEM((rows_here, wide), jnp.bfloat16),
             pltpu.VMEM((slots, feats), jnp.bfloat16),
             pltpu.VMEM((rows_here, feats), jnp.float32),
@@ -172,6 +182,7 @@
             pltpu.VMEM((lanes, LANES), jnp.int32),
             pltpu.VMEM((width, 2 * CAP), jnp.float32),
             pltpu.SemaphoreType.DMA((rows_here // CHUNK,)),
+            pltpu.SemaphoreType.DMA((4,)),
             pltpu.SemaphoreType.DMA((width // GROUP,)),
         ],
         compiler_params=pltpu.CompilerParams(vmem_limit_bytes=VMEM_ALL),
@@ -324,9 +335,8 @@
     return came
 
 
-def encode_kernel(total, me_ref, got_ref, all_ref, basis_ref, centroid_ref, rotation_ref, *refs):
-    out_ref, between_ref, delta_ref, scale_ref, list_ref, apart_ref = refs[-6:]
-    step = pl.program_id(0)
+def encode_kernel(total, me_ref, got_ref, basis_ref, centroid_ref, rotation_ref, *refs):
+    out_hbm, between_ref, out_ref, delta_ref, list_ref, apart_ref, sem = refs[-7:]
     width = delta_ref.shape[0]
     feats = out_ref.shape[1]
     owned = centroid_ref.shape[0]
@@ -334,101 +344,108 @@
     block = wide // width
     share = total // width
 
-    @pl.when(step == 0)
-    def _():
-        notes = jnp.concatenate([all_ref[s * SPAN + CAP:(s + 1) * SPAN, :] for s in range(width)], 0)
-        size = width * NOTES
-        to = lax.broadcasted_iota(jnp.int32, (size, size), 0)
-        of = lax.broadcasted_iota(jnp.int32, (size, size), 1)
-        turn = jnp.where((to % width) * NOTES + to // width == of, 1.0, 0.0).astype(jnp.bfloat16)
-        turned = jnp.dot(turn, notes, preferred_element_type=jnp.float32)
-        row = [turned[r * width:(r + 1) * width] for r in range(NOTES)]
-        quarters = wide // feats
-        shifts = jnp.zeros((width, feats), jnp.float32)
-        for q in range(quarters):
-            parts = [row[p * quarters + q] for p in range(3)]
-            mean = parts[0] + (parts[1] + parts[2])
-            apart_ref[:, q * feats:(q + 1) * feats] = mean - jnp.mean(mean, 0, keepdims=True)
-            terms = jnp.dot(
-                jnp.concatenate(parts, 0).astype(jnp.bfloat16),
-                basis_ref[q * feats:(q + 1) * feats, :],
-                preferred_element_type=jnp.float32,
-            )
-            shifts = shifts + (terms[:width] + (terms[width:2 * width] + terms[2 * width:]))
-        square = row[3 * quarters] + (row[3 * quarters + 1] + row[3 * quarters + 2])
-        delta = shifts - jnp.mean(shifts, 0, keepdims=True)
-        variance = jnp.sum(square + share * (delta * delta), 0, keepdims=True) / total
-        scale_ref[...] = lax.rsqrt(variance + 1e-05)
-        delta_ref[...] = delta
-        digits = row[NOTES - 1]
-        list_ref[...] = digits[:, :CAP] * 32.0 + digits[:, CAP:] - 1.0
-
-        me = me_ref[0]
-        first = me * block
-        near = apart_ref[:, pl.ds(pl.multiple_of(first // LANES * LANES, LANES), LANES)]
-        near = pltpu.roll(near, (LANES - first % LANES) % LANES, 1)[:, :block]
-        between_ref[...] = share * lax.dot_general(
-            near,
-            apart_ref[...],
-            (((0,), (0,)), ((), ())),
-            precision=lax.Precision.HIGHEST,
+    notes = jnp.concatenate([got_ref[s * SPAN + CAP:(s + 1) * SPAN, :] for s in range(width)], 0)
+    size = width * NOTES
+    to = lax.broadcasted_iota(jnp.int32, (size, size), 0)
+    of = lax.broadcasted_iota(jnp.int32, (size, size), 1)
+    turn = jnp.where((to % width) * NOTES + to // width == of, 1.0, 0.0).astype(jnp.bfloat16)
+    turned = jnp.dot(turn, notes, preferred_element_type=jnp.float32)
+    row = [turned[r * width:(r + 1) * width] for r in range(NOTES)]
+    digits = row[NOTES - 1]
+    list_ref[...] = digits[:, :CAP] * 32.0 + digits[:, CAP:] - 1.0
+    quarters = wide // feats
+    shifts = jnp.zeros((width, feats), jnp.float32)
+    for q in range(quarters):
+        parts = [row[p * quarters + q] for p in range(3)]
+        mean = parts[0] + (parts[1] + parts[2])
+        apart_ref[:, q * feats:(q + 1) * feats] = mean - jnp.mean(mean, 0, keepdims=True)
+        terms = jnp.dot(
+            jnp.concatenate(parts, 0).astype(jnp.bfloat16),
+            basis_ref[q * feats:(q + 1) * feats, :],
             preferred_element_type=jnp.float32,
         )
-
-    columns = jnp.transpose(list_ref[pl.ds(step * GROUP, GROUP), :])
+        shifts = shifts + (terms[:width] + (terms[width:2 * width] + terms[2 * width:]))
+    square = row[3 * quarters] + (row[3 * quarters + 1] + row[3 * quarters + 2])
+    delta = shifts - jnp.mean(shifts, 0, keepdims=True)
+    variance = jnp.sum(square + share * (delta * delta), 0, keepdims=True) / total
+    scale = lax.rsqrt(variance + 1e-05)
+    delta_ref[...] = delta
+
     names = lax.broadcasted_iota(jnp.int32, (CAP, owned), 1).astype(jnp.int16)
-    hits, projected, held = [], [], []
-    for s in range(GROUP):
-        listed = jnp.broadcast_to(columns[:, s:s + 1], (CAP, LANES))
-        held.append(jnp.concatenate([listed] * (feats // LANES), 1) >= 0)
-        wanted = jnp.concatenate([listed.astype(jnp.int32).astype(jnp.int16)] * (owned // LANES), 1)
-        hits.append(jnp.where(wanted == names, jnp.ones((), jnp.bfloat16), jnp.zeros((), jnp.bfloat16)))
-        rows = got_ref[s * SPAN:s * SPAN + CAP, :].astype(jnp.float32)
-        projected.append((rows + delta_ref[pl.ds(step * GROUP + s, 1), :]) * scale_ref[...])
-    centre = jnp.dot(jnp.concatenate(hits, 0), centroid_ref[...], preferred_element_type=jnp.float32)
-    residual = jnp.where(jnp.concatenate(held, 0), jnp.concatenate(projected, 0) - centre, 0.0)
-    out_ref[...] = jnp.dot(
-        residual.astype(jnp.bfloat16), rotation_ref[...], preferred_element_type=jnp.float32
-    ).astype(jnp.bfloat16)
+
+    def encode_group(g):
+        columns = jnp.transpose(list_ref[pl.ds(g * GROUP, GROUP), :])
+        hits, projected, held = [], [], []
+        for s in range(GROUP):
+            listed = jnp.broadcast_to(columns[:, s:s + 1], (CAP, LANES))
+            held.append(jnp.concatenate([listed] * (feats // LANES), 1) >= 0)
+            wanted = jnp.concatenate([listed.astype(jnp.int32).astype(jnp.int16)] * (owned // LANES), 1)
+            hits.append(jnp.where(wanted == names, jnp.ones((), jnp.bfloat16), jnp.zeros((), jnp.bfloat16)))
+            base = pl.multiple_of((g * GROUP + s) * SPAN, 16)
+            rows = got_ref[pl.ds(base, CAP), :].astype(jnp.float32)
+            projected.append((rows + delta_ref[pl.ds(g * GROUP + s, 1), :]) * scale)
+        centre = jnp.dot(jnp.concatenate(hits, 0), centroid_ref[...], preferred_element_type=jnp.float32)
+        residual = jnp.where(jnp.concatenate(held, 0), jnp.concatenate(projected, 0) - centre, 0.0)
+        at = pl.ds(pl.multiple_of(g * (GROUP * CAP), GROUP * CAP), GROUP * CAP)
+        out_ref[at, :] = jnp.dot(
+            residual.astype(jnp.bfloat16), rotation_ref[...], preferred_element_type=jnp.float32
+        ).astype(jnp.bfloat16)
+        return pltpu.make_async_copy(out_ref.at[at], out_hbm.at[at], sem.at[g])
+
+    groups = width // GROUP
+    copies = []
+    if groups <= 4:
+        for g in range(groups):
+            copies.append(encode_group(g))
+            copies[g].start()
+    else:
+
+        @pl.loop(0, groups)
+        def _(g):
+            copy = encode_group(g)
+            copy.start()
+            copy.wait()
+
+    first = me_ref[0] * block
+    near = apart_ref[:, pl.ds(pl.multiple_of(first // LANES * LANES, LANES), LANES)]
+    near = pltpu.roll(near, (LANES - first % LANES) % LANES, 1)[:, :block]
+    between_ref[...] = share * lax.dot_general(
+        near,
+        apart_ref[...],
+        (((0,), (0,)), ((), ())),
+        precision=lax.Precision.HIGHEST,
+        preferred_element_type=jnp.float32,
+    )
+    for copy in copies:
+        copy.wait()
 
 
 def encode(width, total, me, got, basis, centroids, rotation, after):
     wide, feats = basis.shape
     owned = centroids.shape[0]
     slots = width * CAP
-    whole = lambda i: (0, 0)
+    vmem, anywhere = pl.BlockSpec(memory_space=pltpu.VMEM), pl.BlockSpec(memory_space=pl.ANY)
     return pl.pallas_call(
         functools.partial(encode_kernel, total),
-        grid=(width // GROUP,),
-        in_specs=[
-            pl.BlockSpec(memory_space=pltpu.SMEM),
-            pl.BlockSpec((GROUP * SPAN, feats), lambda i: (i, 0)),
-            pl.BlockSpec((width * SPAN, feats), whole),
-            pl.BlockSpec((wide, feats), whole),
-            pl.BlockSpec((owned, feats), whole),
-            pl.BlockSpec((feats, feats), whole),
-        ]
-        + [pl.BlockSpec(memory_space=pl.ANY)] * len(after),
-        out_specs=[
-            pl.BlockSpec((GROUP * CAP, feats), lambda i: (i, 0)),
-            pl.BlockSpec((wide // width, wide), whole),
-        ],
+        in_specs=[pl.BlockSpec(memory_space=pltpu.SMEM)] + [vmem] * 4 + [anywhere] * len(after),
+        out_specs=[anywhere, vmem],
         out_shape=[
             jax.ShapeDtypeStruct((slots, feats), jnp.bfloat16),
             jax.ShapeDtypeStruct((wide // width, wide), jnp.float32),
         ],
         scratch_shapes=[
+            pltpu.VMEM((slots, feats), jnp.bfloat16),
             pltpu.VMEM((width, feats), jnp.float32),
-            pltpu.VMEM((1, feats), jnp.float32),
             pltpu.VMEM((width, CAP), jnp.float32),
             pltpu.VMEM((width, wide), jnp.float32),
+            pltpu.SemaphoreType.DMA((width // GROUP,)),
         ],
         compiler_params=pltpu.CompilerParams(vmem_limit_bytes=VMEM_SOME),
         cost_estimate=pl.CostEstimate(
             flops=2 * slots * feats * (owned + feats), bytes_accessed=4 * slots * feats, transcendentals=0
         ),
         name="encode",
-    )(me.reshape(1), got, got, basis, centroids, rotation, *after)
+    )(me.reshape(1), got, basis, centroids, rotation, *after)
 
 
 def local(embeddings, basis, list_owner, list_slot, centroids, rotation):

time: 57.8 us -> 57 us (0.986)
  Pallas kernels: 20.7 us -> 19.5 us
    pallas_call x1, Pallas kernels: 8.06 us -> 7.27 us  [project_and_sort(): pl.pallas_call(functools.partial(rows_kernel, width), grid=(rows_here //...]
  transfers between devices with their start and end apart: 10 -> 10, of which waited for: 4 -> 4; matrix products, arithmetic and copies ran while one was open for 0% -> 0% of each run, Pallas kernels for 21% -> 20%
where the time goes in v8:
time: 57 us; the launch traced here: 56.7 us
  starting transfers between devices  21.7 us (38%)
  Pallas kernels  19.5 us (34%)
  waiting for transfers between devices  14.8 us (26%)
  between operations  0.76 us (1%)
    ppermute x9, waiting for transfers between devices, exchange(): lax.ppermute(out[p - 1], 'wide', [(i, i ^ apart) for i in range(width)])  14.8 us
    ppermute x9, starting transfers between devices, exchange(): lax.ppermute(out[p - 1], 'wide', [(i, i ^ apart) for i in range(width)])  14.3 us
    all_to_all x1, starting transfers between devices, local(): lax.all_to_all(rows.reshape(width, SPAN, feats), 'wide', split_axis=0, co...  7.4 us
    pallas_call x1, Pallas kernels, project_and_sort(): pl.pallas_call(functools.partial(rows_kernel, width), grid=(rows_here //...  7.27 us
    pallas_call x1, Pallas kernels, moments(): pl.pallas_call(functools.partial(moments_kernel, width), in_specs=[pl.Blo...  7.16 us
    pallas_call x1, Pallas kernels, encode(): pl.pallas_call(functools.partial(encode_kernel, total), in_specs=[pl.Bloc...  4 us
  transfers between devices with their start and end apart: 10, of which 4 were waited for; matrix products, arithmetic and copies ran while one was open for 0% of the time, Pallas kernels for 20%

profile of v8, /device:TPU:0, one launch (start us, length us, event | category | flops | bytes accessed | tf_op | source)
XLA Modules:
  0.0 56.7 jit_solution(2943341183493867295)
XLA Ops:
  0.6 7.3 %project_sort.1 = (bf16[2304,256]{1,0:T(8,128)(2,1)}, f32[1,1024]{1,0:T(1,128)}) custom-call(bf16[2048,1024]{1,0:T(8,128)(2,1)} %e_hbm.3, bf16[1024,256]{1,0:T(8,128)(2,1)} %basis_ref.1, s32[16,128]{1,0:T(8,128)} %bitcast.7, s32[16,128]{1,0:T(8,128)} %bitcast.8), custom_call_target="tpu_custom_call" | custom-call | flops 3489660928 | bytes 5373952 | tf_op jit(solution)/shard_map/project_sort/pallas_call | solution.py:162
  7.9 0.0 copy-start.3
  7.9 7.4 %all-to-all-start = ((bf16[16,144,256]{2,1,0:T(8,128)(2,1)}), bf16[16,144,256]{2,1,0:T(8,128)(2,1)S(1)}, u32[]{:S(2)}, u32[]{:S(2)}) async-start(bf16[16,144,256]{2,1,0:T(8,128)(2,1)} %bitcast.6), calls=%async_computation | async-start | bytes 2359296 | tf_op jit(solution)/shard_map/all_to_all | solution.py:459
  15.3 0.0 copy-done.3
  15.3 7.2 %moments.1 = (f32[512,1024]{1,0:T(8,128)S(1)}, bf16[512,1024]{1,0:T(8,128)(2,1)S(1)}) custom-call(s32[1]{0:T(128)} %bitcast.me_ref, f32[1,1024]{1,0:T(1,128)S(1)} %copy-done.3, bf16[2048,1024]{1,0:T(8,128)(2,1)} %e_hbm.3), custom_call_target="tpu_custom_call" | custom-call | flops 4294967296 | bytes 7340032 | tf_op jit(solution)/shard_map/moments/pallas_call | solution.py:244
  22.5 0.5 collective-permute-start
  23.0 2.3 %collective-permute-done.refs_0_ = bf16[512,1024]{1,0:T(8,128)(2,1)S(1)} collective-permute-done((bf16[512,1024]{1,0:T(8,128)(2,1)S(1)}, bf16[512,1024]{1,0:T(8,128)(2,1)S(1)}, u32[]{:S(2)}, u32[]{:S(2)}) %collective-permute-start) | collective-permute-done | bytes 1048608 | tf_op jit(solution)/shard_map/ppermute | solution.py:334
  25.3 0.0 copy-start
  25.3 0.0 copy-start.1
  25.3 0.2 add_and_split.3
  25.5 1.9 %collective-permute-start.1 = (bf16[256,512]{1,0:T(8,128)(2,1)S(1)}, bf16[256,512]{1,0:T(8,128)(2,1)S(1)}, u32[]{:S(2)}, u32[]{:S(2)}) collective-permute-start(bf16[256,512]{1,0:T(8,128)(2,1)S(1)} %get-tuple-element.25), channel_id=1, source_target_pairs={{0,2},{1,3},{2,0},{3,1},{4,6},{5,7},{6,4},{7,5},{8,10},{9,11},{10,... | collective-permute-start | bytes 786440 | tf_op jit(solution)/shard_map/ppermute | solution.py:334
  27.4 0.2 collective-permute-start.2
  27.6 9.5 %collective-permute-done.1.refs_0_ = bf16[256,512]{1,0:T(8,128)(2,1)S(1)} collective-permute-done((bf16[256,512]{1,0:T(8,128)(2,1)S(1)}, bf16[256,512]{1,0:T(8,128)(2,1)S(1)}, u32[]{:S(2)}, u32[]{:S(2)}) %collective-permute-start.1) | collective-permute-done | bytes 262176 | tf_op jit(solution)/shard_map/ppermute | solution.py:334
  37.1 3.3 %collective-permute-start.4 = (bf16[64,512]{1,0:T(8,128)(2,1)S(1)}, bf16[64,512]{1,0:T(8,128)(2,1)S(1)}, u32[]{:S(2)}, u32[]{:S(2)}) collective-permute-start(bf16[64,512]{1,0:T(8,128)(2,1)S(1)} %get-tuple-element.33), channel_id=1, source_target_pairs={{0,4},{1,5},{2,6},{3,7},{4,0},{5,1},{6,2},{7,3},{8,12},{9,13},{10,... | collective-permute-start | bytes 196616 | tf_op jit(solution)/shard_map/ppermute | solution.py:334
  40.4 3.1 %collective-permute-start.5 = (bf16[64,512]{1,0:T(8,128)(2,1)S(1)}, bf16[64,512]{1,0:T(8,128)(2,1)S(1)}, u32[]{:S(2)}, u32[]{:S(2)}) collective-permute-start(bf16[64,512]{1,0:T(8,128)(2,1)S(1)} %get-tuple-element.34), channel_id=1, source_target_pairs={{0,12},{1,13},{2,14},{3,15},{4,8},{5,9},{6,10},{7,11},{8,4},{9,5},... | collective-permute-start | bytes 196616 | tf_op jit(solution)/shard_map/ppermute | solution.py:334
  43.5 0.0 collective-permute-start.3
  43.5 1.3 %collective-permute-done.2.refs_0_ = bf16[256,512]{1,0:T(8,128)(2,1)S(1)} collective-permute-done((bf16[256,512]{1,0:T(8,128)(2,1)S(1)}, bf16[256,512]{1,0:T(8,128)(2,1)S(1)}, u32[]{:S(2)}, u32[]{:S(2)}) %collective-permute-start.2) | collective-permute-done | bytes 262176 | tf_op jit(solution)/shard_map/ppermute | solution.py:334
  44.9 2.3 %collective-permute-start.7 = (bf16[64,512]{1,0:T(8,128)(2,1)S(1)}, bf16[64,512]{1,0:T(8,128)(2,1)S(1)}, u32[]{:S(2)}, u32[]{:S(2)}) collective-permute-start(bf16[64,512]{1,0:T(8,128)(2,1)S(1)} %get-tuple-element.36), channel_id=1, source_target_pairs={{0,4},{1,5},{2,6},{3,7},{4,0},{5,1},{6,2},{7,3},{8,12},{9,13},{10,... | collective-permute-start | bytes 196616 | tf_op jit(solution)/shard_map/ppermute | solution.py:334
  47.2 3.0 %collective-permute-start.8 = (bf16[64,512]{1,0:T(8,128)(2,1)S(1)}, bf16[64,512]{1,0:T(8,128)(2,1)S(1)}, u32[]{:S(2)}, u32[]{:S(2)}) collective-permute-start(bf16[64,512]{1,0:T(8,128)(2,1)S(1)} %get-tuple-element.37), channel_id=1, source_target_pairs={{0,12},{1,13},{2,14},{3,15},{4,8},{5,9},{6,10},{7,11},{8,4},{9,5},... | collective-permute-start | bytes 196616 | tf_op jit(solution)/shard_map/ppermute | solution.py:334
  50.2 0.0 collective-permute-done.4.refs_2_
  50.2 0.0 collective-permute-start.6
  50.2 0.0 all-to-all-done
  50.2 0.0 copy-done
  50.2 0.0 copy-done.1
  50.2 0.0 copy-done.2
  50.2 4.0 %encode.1 = (bf16[2048,256]{1,0:T(8,128)(2,1)}, f32[64,1024]{1,0:T(8,128)S(1)}) custom-call(s32[1]{0:T(128)} %bitcast.me_ref, bf16[2304,256]{1,0:T(8,128)(2,1)S(1)} %bitcast.5, bf16[1024,256]{1,0:T(8,128)(2,1)S(1)} %copy-done, bf16[1024,256]{1,0:T(8,128)(2,1)S(1)} %copy-done.1, bf16[256,256]{1,0:T(8,128)(2,1)S(1)} %copy-done.2, ...), custom_call_target="tpu_custom_call" | custom-call | flops 1342177280 | bytes 2097152 | tf_op jit(solution)/shard_map/encode/pallas_call | solution.py:428
  54.2 0.0 collective-permute-done.5.refs_3_
  54.2 0.0 collective-permute-done.3.refs_1_
  54.3 0.0 collective-permute-done.7.refs_6_
  54.3 0.0 collective-permute-done.8.refs_7_
  54.3 1.7 %collective-permute-done.6.refs_5_ = bf16[64,512]{1,0:T(8,128)(2,1)S(1)} collective-permute-done((bf16[64,512]{1,0:T(8,128)(2,1)S(1)}, bf16[64,512]{1,0:T(8,128)(2,1)S(1)}, u32[]{:S(2)}, u32[]{:S(2)}) %collective-permute-start.6) | collective-permute-done | bytes 65568 | tf_op jit(solution)/shard_map/ppermute | solution.py:334
  56.0 0.8 %finish.1 = f32[64,1024]{1,0:T(8,128)} custom-call(f32[64,1024]{1,0:T(8,128)S(1)} %get-tuple-element.31.between_ref, f32[64,512]{1,0:T(8,128)S(1)} %get-tuple-element.32.refs_0_, bf16[64,512]{1,0:T(8,128)(2,1)S(1)} %collective-permute-done.3.refs_1_, bf16[64,512]{1,0:T(8,128)(2,1)S(1)} %collective-permute-done.4.refs_2_, ...), custom_call_target="tpu_custom_call" | custom-call | flops 524288 | bytes 1048576 | tf_op jit(solution)/shard_map/finish/pallas_call | solution.py:314
  (3 shorter events, 0.1 us)
Async XLA Ops:
  7.9 7.4 %copy-start.3 = (f32[1,1024]{1,0:T(1,128)S(1)}, f32[1,1024]{1,0:T(1,128)}, u32[]{:S(2)}) copy-start(f32[1,1024]{1,0:T(1,128)} %get-tuple-element.21.mean_hbm) | copy-start | bytes 12292
  7.9 42.3 %all-to-all-start = ((bf16[16,144,256]{2,1,0:T(8,128)(2,1)}), bf16[16,144,256]{2,1,0:T(8,128)(2,1)S(1)}, u32[]{:S(2)}, u32[]{:S(2)}) async-start(bf16[16,144,256]{2,1,0:T(8,128)(2,1)} %bitcast.6), calls=%async_computation | async-start | bytes 2359296 | tf_op jit(solution)/shard_map/all_to_all | solution.py:459
  22.5 2.8 %collective-permute-start = (bf16[512,1024]{1,0:T(8,128)(2,1)S(1)}, bf16[512,1024]{1,0:T(8,128)(2,1)S(1)}, u32[]{:S(2)}, u32[]{:S(2)}) collective-permute-start(bf16[512,1024]{1,0:T(8,128)(2,1)S(1)} %get-tuple-element.23), channel_id=1, source_target_pairs={{0,1},{1,0},{2,3},{3,2},{4,5},{5,4},{6,7},{7,6},{8,9},{9,8},{10,11... | collective-permute-start | bytes 3145736 | tf_op jit(solution)/shard_map/ppermute | solution.py:334
  25.3 24.9 %copy-start = (bf16[1024,256]{1,0:T(8,128)(2,1)S(1)}, bf16[1024,256]{1,0:T(8,128)(2,1)}, u32[]{:S(2)}) copy-start(bf16[1024,256]{1,0:T(8,128)(2,1)} %basis_ref.1) | copy-start | bytes 1572868
  25.3 24.9 %copy-start.1 = (bf16[1024,256]{1,0:T(8,128)(2,1)S(1)}, bf16[1024,256]{1,0:T(8,128)(2,1)}, u32[]{:S(2)}) copy-start(bf16[1024,256]{1,0:T(8,128)(2,1)} %centroid_ref.1) | copy-start | bytes 1572868
  25.3 24.9 %copy-start.2 = (bf16[256,256]{1,0:T(8,128)(2,1)S(1)}, bf16[256,256]{1,0:T(8,128)(2,1)}, u32[]{:S(2)}) copy-start(bf16[256,256]{1,0:T(8,128)(2,1)} %rotation_ref.1) | copy-start | bytes 393220
  25.5 11.6 %collective-permute-start.1 = (bf16[256,512]{1,0:T(8,128)(2,1)S(1)}, bf16[256,512]{1,0:T(8,128)(2,1)S(1)}, u32[]{:S(2)}, u32[]{:S(2)}) collective-permute-start(bf16[256,512]{1,0:T(8,128)(2,1)S(1)} %get-tuple-element.25), channel_id=1, source_target_pairs={{0,2},{1,3},{2,0},{3,1},{4,6},{5,7},{6,4},{7,5},{8,10},{9,11},{10,... | collective-permute-start | bytes 786440 | tf_op jit(solution)/shard_map/ppermute | solution.py:334
  27.4 17.4 %collective-permute-start.2 = (bf16[256,512]{1,0:T(8,128)(2,1)S(1)}, bf16[256,512]{1,0:T(8,128)(2,1)S(1)}, u32[]{:S(2)}, u32[]{:S(2)}) collective-permute-start(bf16[256,512]{1,0:T(8,128)(2,1)S(1)} %get-tuple-element.28), channel_id=1, source_target_pairs={{0,2},{1,3},{2,0},{3,1},{4,6},{5,7},{6,4},{7,5},{8,10},{9,11},{10,... | collective-permute-start | bytes 786440 | tf_op jit(solution)/shard_map/ppermute | solution.py:334
  37.1 13.1 %collective-permute-start.4 = (bf16[64,512]{1,0:T(8,128)(2,1)S(1)}, bf16[64,512]{1,0:T(8,128)(2,1)S(1)}, u32[]{:S(2)}, u32[]{:S(2)}) collective-permute-start(bf16[64,512]{1,0:T(8,128)(2,1)S(1)} %get-tuple-element.33), channel_id=1, source_target_pairs={{0,4},{1,5},{2,6},{3,7},{4,0},{5,1},{6,2},{7,3},{8,12},{9,13},{10,... | collective-permute-start | bytes 196616 | tf_op jit(solution)/shard_map/ppermute | solution.py:334
  40.4 13.8 %collective-permute-start.5 = (bf16[64,512]{1,0:T(8,128)(2,1)S(1)}, bf16[64,512]{1,0:T(8,128)(2,1)S(1)}, u32[]{:S(2)}, u32[]{:S(2)}) collective-permute-start(bf16[64,512]{1,0:T(8,128)(2,1)S(1)} %get-tuple-element.34), channel_id=1, source_target_pairs={{0,12},{1,13},{2,14},{3,15},{4,8},{5,9},{6,10},{7,11},{8,4},{9,5},... | collective-permute-start | bytes 196616 | tf_op jit(solution)/shard_map/ppermute | solution.py:334
  43.5 10.8 %collective-permute-start.3 = (bf16[64,512]{1,0:T(8,128)(2,1)S(1)}, bf16[64,512]{1,0:T(8,128)(2,1)S(1)}, u32[]{:S(2)}, u32[]{:S(2)}) collective-permute-start(bf16[64,512]{1,0:T(8,128)(2,1)S(1)} %get-tuple-element.26.refs_0_), channel_id=1, source_target_pairs={{0,8},{1,9},{2,10},{3,11},{4,12},{5,13},{6,14},{7,15},{8,0},{9,1},... | collective-permute-start | bytes 196616 | tf_op jit(solution)/shard_map/ppermute | solution.py:334
  44.9 9.4 %collective-permute-start.7 = (bf16[64,512]{1,0:T(8,128)(2,1)S(1)}, bf16[64,512]{1,0:T(8,128)(2,1)S(1)}, u32[]{:S(2)}, u32[]{:S(2)}) collective-permute-start(bf16[64,512]{1,0:T(8,128)(2,1)S(1)} %get-tuple-element.36), channel_id=1, source_target_pairs={{0,4},{1,5},{2,6},{3,7},{4,0},{5,1},{6,2},{7,3},{8,12},{9,13},{10,... | collective-permute-start | bytes 196616 | tf_op jit(solution)/shard_map/ppermute | solution.py:334
  47.2 7.1 %collective-permute-start.8 = (bf16[64,512]{1,0:T(8,128)(2,1)S(1)}, bf16[64,512]{1,0:T(8,128)(2,1)S(1)}, u32[]{:S(2)}, u32[]{:S(2)}) collective-permute-start(bf16[64,512]{1,0:T(8,128)(2,1)S(1)} %get-tuple-element.37), channel_id=1, source_target_pairs={{0,12},{1,13},{2,14},{3,15},{4,8},{5,9},{6,10},{7,11},{8,4},{9,5},... | collective-permute-start | bytes 196616 | tf_op jit(solution)/shard_map/ppermute | solution.py:334
  50.2 5.8 %collective-permute-start.6 = (bf16[64,512]{1,0:T(8,128)(2,1)S(1)}, bf16[64,512]{1,0:T(8,128)(2,1)S(1)}, u32[]{:S(2)}, u32[]{:S(2)}) collective-permute-start(bf16[64,512]{1,0:T(8,128)(2,1)S(1)} %get-tuple-element.29.refs_1_), channel_id=1, source_target_pairs={{0,8},{1,9},{2,10},{3,11},{4,12},{5,13},{6,14},{7,15},{8,0},{9,1},... | collective-permute-start | bytes 196616 | tf_op jit(solution)/shard_map/ppermute | solution.py:334

commit v9 on v8

--- a/solution.py
+++ b/solution.py
@@ -14,27 +14,26 @@
 CHUNK = 512
 TILE = 256
 GROUP = 4
-SHARES = 2
+SHARES = (5, 3)
 VMEM_ALL = 60 * 1024 * 1024
 VMEM_SOME = 24 * 1024 * 1024
 VMEM_MOST = 48 * 1024 * 1024
 
 
-def in_three(x):
+def in_two(x):
     high = x.astype(jnp.bfloat16).astype(jnp.float32)
-    rest = x - high
-    middle = rest.astype(jnp.bfloat16).astype(jnp.float32)
-    return high, middle, (rest - middle).astype(jnp.bfloat16).astype(jnp.float32)
+    return [high, (x - high).astype(jnp.bfloat16).astype(jnp.float32)]
 
 
 def rows_kernel(
     width, e_hbm, basis_hbm, owner_hbm, slot_hbm,
     rows_hbm, mean_hbm,
-    owner_ref, slot_ref, mean_ref, basis_ref, e_ref, rows_ref, y_ref, yb_ref, sum_ref, total_ref, target_ref, list_ref, e_sem, small_sem, sem,
+    owner_ref, slot_ref, mean_ref, basis_ref, e_ref, rows_ref, sorted_ref, centre_ref, sum_ref, square_ref, total_ref, target_ref, list_ref, e_sem, small_sem, sem,
 ):
     step = pl.program_id(0)
-    rows_here, feats = y_ref.shape
-    wide = e_ref.shape[1]
+    rows_here, wide = e_ref.shape
+    feats = basis_ref.shape[1]
+    groups = width // GROUP
     chunks = rows_here // LANES
 
     def e_copy(c):
@@ -53,7 +52,9 @@
         for c in range(1, rows_here // CHUNK):
             e_copy(c).start()
         owner_copy.wait()
+        sorted_ref[...] = jnp.zeros_like(sorted_ref)
         sum_ref[...] = jnp.zeros_like(sum_ref)
+        square_ref[...] = jnp.zeros_like(square_ref)
         total_ref[...] = jnp.zeros_like(total_ref)
         owner = owner_ref[...]
         wanted = lax.broadcasted_iota(jnp.int32, (width, LANES), 0)
@@ -94,63 +95,77 @@
     here = pl.ds(pl.multiple_of(step * CHUNK, CHUNK), CHUNK)
     rows = e_ref[here, :]
     y = jnp.dot(rows, basis_ref[...], preferred_element_type=jnp.float32)
-    y_ref[here, :] = y
+
+    @pl.when(step == 0)
+    def _():
+        high, low = in_two(jnp.mean(y, 0, keepdims=True))
+        centre_ref[0:1, :] = high
+        centre_ref[1:2, :] = low
+
+    y = y - (centre_ref[0:1, :] + centre_ref[1:2, :])
     sum_ref[...] += jnp.sum(y.reshape(CHUNK // 8, 8, feats), 0)
+    square_ref[...] += jnp.sum((y * y).reshape(CHUNK // 8, 8, feats), 0)
     total_ref[...] += jnp.sum(rows.astype(jnp.float32).reshape(CHUNK // 8, 8, wide), 0)
+    y = y.astype(jnp.bfloat16)
+
+    place = lax.broadcasted_iota(jnp.int32, (GROUP * CAP, LANES), 0).astype(jnp.int16)
+
+    def sort_group(g):
+        pieces = []
+        for c in range(CHUNK // LANES):
+            aim = target_ref[pl.ds(step * (CHUNK // LANES) + c, 1), :] - g * (GROUP * CAP)
+            aim = jnp.broadcast_to(aim, (16, LANES)).astype(jnp.int16)
+            aim = jnp.concatenate([aim] * (GROUP * CAP // 16), 0)
+            pieces.append(jnp.where(aim == place, jnp.ones((), jnp.bfloat16), jnp.zeros((), jnp.bfloat16)))
+        at = pl.ds(pl.multiple_of(g * (GROUP * CAP), GROUP * CAP), GROUP * CAP)
+        sorted_ref[at, :] += jnp.dot(jnp.concatenate(pieces, 1), y, preferred_element_type=jnp.float32)
+
+    if groups <= 4:
+        for g in range(groups):
+            sort_group(g)
+    else:
+
+        @pl.loop(0, groups)
+        def _(g):
+            sort_group(g)
 
     @pl.when(step == pl.num_programs(0) - 1)
     def _():
-        mean_y = jnp.sum(sum_ref[...], 0, keepdims=True) / rows_here
-        square = jnp.zeros((8, feats), jnp.float32)
-        for c in range(rows_here // CHUNK):
-            at = slice(c * CHUNK, (c + 1) * CHUNK)
-            centred = y_ref[at, :] - mean_y
-            square = square + jnp.sum((centred * centred).reshape(CHUNK // 8, 8, feats), 0)
-            yb_ref[at, :] = centred.astype(jnp.bfloat16)
         mean = jnp.sum(total_ref[...], 0, keepdims=True) / rows_here
         mean_ref[...] = mean
         mean_copy = pltpu.make_async_copy(mean_ref, mean_hbm, small_sem.at[3])
         mean_copy.start()
-        parts = in_three(mean)
-        common = [part[:, q * feats:(q + 1) * feats] for part in parts for q in range(wide // feats)]
-        common = jnp.concatenate(common + list(in_three(jnp.sum(square, 0, keepdims=True))), 0)
-
-        place = lax.broadcasted_iota(jnp.int32, (GROUP * CAP, LANES), 0).astype(jnp.int16)
-
-        def sort_group(g):
-            first = g * GROUP
-            pieces = []
-            for c in range(chunks):
-                wanted = (target_ref[c:c + 1, :] - first * CAP).astype(jnp.int32)
-                wanted = jnp.broadcast_to(wanted, (16, LANES)).astype(jnp.int16)
-                wanted = jnp.concatenate([wanted] * (GROUP * CAP // 16), 0)
-                pieces.append(jnp.where(wanted == place, jnp.ones((), jnp.bfloat16), jnp.zeros((), jnp.bfloat16)))
-            pick = jnp.concatenate(pieces, 1)
-            rows = jnp.dot(pick, yb_ref[...], preferred_element_type=jnp.float32).astype(jnp.bfloat16)
-            for j in range(GROUP):
-                base = pl.multiple_of((first + j) * SPAN, 16)
-                rows_ref[pl.ds(base, CAP), :] = rows[j * CAP:(j + 1) * CAP]
-                notes = jnp.concatenate([common, list_ref[pl.ds(first + j, 1), :]], 0)
-                rows_ref[pl.ds(pl.multiple_of(base + CAP, 16), NOTES), :] = notes.astype(jnp.bfloat16)
+        offset = jnp.sum(sum_ref[...], 0, keepdims=True) / rows_here
+        square = jnp.sum(square_ref[...], 0, keepdims=True) - rows_here * (offset * offset)
+        common = [part[:, q * feats:(q + 1) * feats] for part in in_two(mean) for q in range(wide // feats)]
+        common = common + [centre_ref[0:1, :], centre_ref[1:2, :]] + in_two(offset) + in_two(square)
+        common = common + [jnp.zeros((1, feats), jnp.float32)] * (NOTES - 1 - len(common))
+        common = jnp.concatenate(common, 0)
+
+        def rows_copy(g):
             at = pl.ds(pl.multiple_of(g * (GROUP * SPAN), 16), GROUP * SPAN)
             return pltpu.make_async_copy(rows_ref.at[at], rows_hbm.at[at], sem.at[g])
 
-        groups = width // GROUP
+        def place_group(g):
+            for j in range(GROUP):
+                base = pl.multiple_of((g * GROUP + j) * SPAN, 16)
+                from_here = pl.ds(pl.multiple_of((g * GROUP + j) * CAP, CAP), CAP)
+                rows_ref[pl.ds(base, CAP), :] = sorted_ref[from_here, :].astype(jnp.bfloat16)
+                notes = jnp.concatenate([common, list_ref[pl.ds(g * GROUP + j, 1), :]], 0)
+                rows_ref[pl.ds(pl.multiple_of(base + CAP, 16), NOTES), :] = notes.astype(jnp.bfloat16)
+            rows_copy(g).start()
+
         if groups <= 4:
-            copies = []
             for g in range(groups):
-                copies.append(sort_group(g))
-                copies[g].start()
-            for copy in copies:
-                copy.wait()
+                place_group(g)
         else:
 
             @pl.loop(0, groups)
             def _(g):
-                copy = sort_group(g)
-                copy.start()
-                copy.wait()
-
+                place_group(g)
+
+        for g in range(groups):
+            rows_copy(g).wait()
         mean_copy.wait()
 
 
@@ -175,8 +190,9 @@
             pltpu.VMEM((wide, feats), jnp.bfloat16),
             pltpu.VMEM((rows_here, wide), jnp.bfloat16),
             pltpu.VMEM((slots, feats), jnp.bfloat16),
-            pltpu.VMEM((rows_here, feats), jnp.float32),
-            pltpu.VMEM((rows_here, feats), jnp.bfloat16),
+            pltpu.VMEM((width * CAP, feats), jnp.float32),
+            pltpu.VMEM((2, feats), jnp.float32),
+            pltpu.VMEM((8, feats), jnp.float32),
             pltpu.VMEM((8, feats), jnp.float32),
             pltpu.VMEM((8, wide), jnp.float32),
             pltpu.VMEM((lanes, LANES), jnp.int32),
@@ -264,48 +280,51 @@
     )(me.reshape(1), mean, embeddings)
 
 
+def cuts(columns, shares):
+    unit = columns // sum(shares)
+    ends = [unit * sum(shares[:h + 1]) for h in range(len(shares))]
+    return list(zip([0] + ends[:-1], ends))
+
+
 def add_kernel(shares, pieces, keep_ref, *refs):
-    outs = refs[len(refs) - shares * pieces:]
-    came = refs[:len(refs) - shares * pieces]
-    rows, columns = outs[0].shape
-    for h in range(shares):
-        across = slice(h * columns, (h + 1) * columns)
+    count = len(shares) * pieces
+    came, outs = refs[:-count], refs[-count:]
+    for h, (first, end) in enumerate(cuts(keep_ref.shape[1], shares)):
         for p in range(pieces):
-            at = slice(p * rows, (p + 1) * rows)
-            held = keep_ref[at, across]
+            out = outs[h * pieces + p]
+            at = slice(p * out.shape[0], (p + 1) * out.shape[0])
+            held = keep_ref[at, first:end].astype(jnp.float32)
             for ref in came:
-                held = held + ref[at, across].astype(jnp.float32)
-            out = outs[h * pieces + p]
+                held = held + ref[at, first:end].astype(jnp.float32)
             out[...] = held.astype(out.dtype)
 
 
 def add_and_split(keep, came, shares, pieces):
     rows, columns = keep.shape
     vmem = pl.BlockSpec(memory_space=pltpu.VMEM)
-    shape = (rows // pieces, columns // shares)
     kinds = [jnp.float32] + [jnp.bfloat16] * (pieces - 1)
     outs = pl.pallas_call(
         functools.partial(add_kernel, shares, pieces),
         in_specs=[vmem] * (1 + len(came)),
-        out_specs=[vmem] * (shares * pieces),
-        out_shape=[jax.ShapeDtypeStruct(shape, kind) for kind in kinds * shares],
+        out_specs=[vmem] * (len(shares) * pieces),
+        out_shape=[
+            jax.ShapeDtypeStruct((rows // pieces, end - first), kind) for first, end in cuts(columns, shares) for kind in kinds
+        ],
         compiler_params=pltpu.CompilerParams(vmem_limit_bytes=VMEM_SOME),
         cost_estimate=pl.CostEstimate(flops=2 * rows * columns, bytes_accessed=10 * rows * columns, transcendentals=0),
         name="add_and_split",
     )(keep, *came)
-    return [outs[h * pieces:(h + 1) * pieces] for h in range(shares)]
+    return [outs[h * pieces:(h + 1) * pieces] for h in range(len(shares))]
 
 
 def finish_kernel(total, between_ref, *refs):
     out_ref = refs[-1]
-    each = (len(refs) - 1) // SHARES
-    columns = out_ref.shape[1] // SHARES
-    for h in range(SHARES):
-        across = slice(h * columns, (h + 1) * columns)
+    each = (len(refs) - 1) // len(SHARES)
+    for h, (first, end) in enumerate(cuts(out_ref.shape[1], SHARES)):
         held = refs[h * each][...]
         for ref in refs[h * each + 1:(h + 1) * each]:
             held = held + ref[...].astype(jnp.float32)
-        out_ref[:, across] = (held + between_ref[:, across]) / total
+        out_ref[:, first:end] = (held + between_ref[:, first:end]) / total
 
 
 def finish(total, between, keeps, came):
@@ -335,12 +354,12 @@
     return came
 
 
-def encode_kernel(total, me_ref, got_ref, basis_ref, centroid_ref, rotation_ref, *refs):
+def encode_kernel(total, me_ref, got_ref, centroid_ref, rotation_ref, *refs):
     out_hbm, between_ref, out_ref, delta_ref, list_ref, apart_ref, sem = refs[-7:]
     width = delta_ref.shape[0]
     feats = out_ref.shape[1]
     owned = centroid_ref.shape[0]
-    wide = basis_ref.shape[0]
+    wide = apart_ref.shape[1]
     block = wide // width
     share = total // width
 
@@ -354,20 +373,12 @@
     digits = row[NOTES - 1]
     list_ref[...] = digits[:, :CAP] * 32.0 + digits[:, CAP:] - 1.0
     quarters = wide // feats
-    shifts = jnp.zeros((width, feats), jnp.float32)
     for q in range(quarters):
-        parts = [row[p * quarters + q] for p in range(3)]
-        mean = parts[0] + (parts[1] + parts[2])
+        mean = row[q] + row[quarters + q]
         apart_ref[:, q * feats:(q + 1) * feats] = mean - jnp.mean(mean, 0, keepdims=True)
-        terms = jnp.dot(
-            jnp.concatenate(parts, 0).astype(jnp.bfloat16),
-            basis_ref[q * feats:(q + 1) * feats, :],
-            preferred_element_type=jnp.float32,
-        )
-        shifts = shifts + (terms[:width] + (terms[width:2 * width] + terms[2 * width:]))
-    square = row[3 * quarters] + (row[3 * quarters + 1] + row[3 * quarters + 2])
-    delta = shifts - jnp.mean(shifts, 0, keepdims=True)
-    variance = jnp.sum(square + share * (delta * delta), 0, keepdims=True) / total
+    centre, offset, square = [row[n] + row[n + 1] for n in range(2 * quarters, 2 * quarters + 6, 2)]
+    delta = centre - jnp.mean(centre, 0, keepdims=True) - jnp.mean(offset, 0, keepdims=True)
+    variance = jnp.sum(square + share * ((delta + offset) * (delta + offset)), 0, keepdims=True) / total
     scale = lax.rsqrt(variance + 1e-05)
     delta_ref[...] = delta
 
@@ -384,8 +395,8 @@
             base = pl.multiple_of((g * GROUP + s) * SPAN, 16)
             rows = got_ref[pl.ds(base, CAP), :].astype(jnp.float32)
             projected.append((rows + delta_ref[pl.ds(g * GROUP + s, 1), :]) * scale)
-        centre = jnp.dot(jnp.concatenate(hits, 0), centroid_ref[...], preferred_element_type=jnp.float32)
-        residual = jnp.where(jnp.concatenate(held, 0), jnp.concatenate(projected, 0) - centre, 0.0)
+        centroid = jnp.dot(jnp.concatenate(hits, 0), centroid_ref[...], preferred_element_type=jnp.float32)
+        residual = jnp.where(jnp.concatenate(held, 0), jnp.concatenate(projected, 0) - centroid, 0.0)
         at = pl.ds(pl.multiple_of(g * (GROUP * CAP), GROUP * CAP), GROUP * CAP)
         out_ref[at, :] = jnp.dot(
             residual.astype(jnp.bfloat16), rotation_ref[...], preferred_element_type=jnp.float32
@@ -420,14 +431,13 @@
         copy.wait()
 
 
-def encode(width, total, me, got, basis, centroids, rotation, after):
-    wide, feats = basis.shape
-    owned = centroids.shape[0]
+def encode(width, total, me, wide, got, centroids, rotation, after):
+    owned, feats = centroids.shape
     slots = width * CAP
     vmem, anywhere = pl.BlockSpec(memory_space=pltpu.VMEM), pl.BlockSpec(memory_space=pl.ANY)
     return pl.pallas_call(
         functools.partial(encode_kernel, total),
-        in_specs=[pl.BlockSpec(memory_space=pltpu.SMEM)] + [vmem] * 4 + [anywhere] * len(after),
+        in_specs=[pl.BlockSpec(memory_space=pltpu.SMEM)] + [vmem] * 3 + [anywhere] * len(after),
         out_specs=[anywhere, vmem],
         out_shape=[
             jax.ShapeDtypeStruct((slots, feats), jnp.bfloat16),
@@ -445,7 +455,7 @@
             flops=2 * slots * feats * (owned + feats), bytes_accessed=4 * slots * feats, transcendentals=0
         ),
         name="encode",
-    )(me.reshape(1), got, basis, centroids, rotation, *after)
+    )(me.reshape(1), got, centroids, rotation, *after)
 
 
 def local(embeddings, basis, list_owner, list_slot, centroids, rotation):
@@ -466,11 +476,11 @@
     for share in shares:
         for n in range(1, len(stages) - 1):
             came = exchange(width, stages[n], share[1:])
-            (share,) = add_and_split(share[0], came, 1, 1 << len(stages[n + 1]))
+            (share,) = add_and_split(share[0], came, (1,), 1 << len(stages[n + 1]))
         last.append(share)
     came = [exchange(width, stages[-1], share[1:]) for share in last]
     encoded, between = encode(
-        width, total, me, got.reshape(width * SPAN, feats), basis, centroids, rotation, [share[1] for share in last]
+        width, total, me, wide, got.reshape(width * SPAN, feats), centroids, rotation, [share[1] for share in last]
     )
     covariance = finish(total, between, [share[0] for share in last], came)
     return (encoded, covariance)

time: 57 us -> 66.1 us (1.16)
  waiting for transfers between devices: 14.8 us -> 22.6 us
  Pallas kernels: 19.5 us -> 22.7 us
  starting transfers between devices: 21.7 us -> 19.7 us
    ppermute x9, waiting for transfers between devices: 14.8 us -> 22.6 us  [exchange(): lax.ppermute(out[p - 1], 'wide', [(i, i ^ apart) for i in range(width)])]
    pallas_call x1, Pallas kernels: 7.27 us -> 10.5 us  [project_and_sort(): pl.pallas_call(functools.partial(rows_kernel, width), grid=(rows_here //...]
    ppermute x9, starting transfers between devices: 14.3 us -> 12.3 us  [exchange(): lax.ppermute(out[p - 1], 'wide', [(i, i ^ apart) for i in range(width)])]
  transfers between devices with their start and end apart: 10 -> 10, of which waited for: 4 -> 3; matrix products, arithmetic and copies ran while one was open for 0% -> 0% of each run, Pallas kernels for 20% -> 17%
where the time goes in v9:
time: 66.1 us; the launch traced here: 65.8 us
  Pallas kernels  22.7 us (34%)
  waiting for transfers between devices  22.6 us (34%)
  starting transfers between devices  19.7 us (30%)
  between operations  0.75 us (1%)
    ppermute x9, waiting for transfers between devices, exchange(): lax.ppermute(out[p - 1], 'wide', [(i, i ^ apart) for i in range(width)])  22.6 us
    ppermute x9, starting transfers between devices, exchange(): lax.ppermute(out[p - 1], 'wide', [(i, i ^ apart) for i in range(width)])  12.3 us
    pallas_call x1, Pallas kernels, project_and_sort(): pl.pallas_call(functools.partial(rows_kernel, width), grid=(rows_here //...  10.5 us
    all_to_all x1, starting transfers between devices, local(): lax.all_to_all(rows.reshape(width, SPAN, feats), 'wide', split_axis=0, co...  7.4 us
    pallas_call x1, Pallas kernels, moments(): pl.pallas_call(functools.partial(moments_kernel, width), in_specs=[pl.Blo...  7.17 us
    pallas_call x1, Pallas kernels, encode(): pl.pallas_call(functools.partial(encode_kernel, total), in_specs=[pl.Bloc...  3.96 us
  transfers between devices with their start and end apart: 10, of which 3 were waited for; matrix products, arithmetic and copies ran while one was open for 0% of the time, Pallas kernels for 17%

profile of v9, /device:TPU:0, one launch (start us, length us, event | category | flops | bytes accessed | tf_op | source)
XLA Modules:
  0.0 65.8 jit_solution(7101603997592569945)
XLA Ops:
  0.6 10.5 %project_sort.1 = (bf16[2304,256]{1,0:T(8,128)(2,1)}, f32[1,1024]{1,0:T(1,128)}) custom-call(bf16[2048,1024]{1,0:T(8,128)(2,1)} %e_hbm.3, bf16[1024,256]{1,0:T(8,128)(2,1)} %basis_hbm.1, s32[16,128]{1,0:T(8,128)} %bitcast.7, s32[16,128]{1,0:T(8,128)} %bitcast.8), custom_call_target="tpu_custom_call" | custom-call | flops 3489660928 | bytes 5373952 | tf_op jit(solution)/shard_map/project_sort/pallas_call | solution.py:177
  11.2 0.0 copy-start.2
  11.2 7.4 %all-to-all-start = ((bf16[16,144,256]{2,1,0:T(8,128)(2,1)}), bf16[16,144,256]{2,1,0:T(8,128)(2,1)S(1)}, u32[]{:S(2)}, u32[]{:S(2)}) async-start(bf16[16,144,256]{2,1,0:T(8,128)(2,1)} %bitcast.6), calls=%async_computation | async-start | bytes 2359296 | tf_op jit(solution)/shard_map/all_to_all | solution.py:469
  18.6 0.0 copy-done.2
  18.6 7.2 %moments.1 = (f32[512,1024]{1,0:T(8,128)S(1)}, bf16[512,1024]{1,0:T(8,128)(2,1)S(1)}) custom-call(s32[1]{0:T(128)} %bitcast.me_ref, f32[1,1024]{1,0:T(1,128)S(1)} %copy-done.2, bf16[2048,1024]{1,0:T(8,128)(2,1)} %e_hbm.3), custom_call_target="tpu_custom_call" | custom-call | flops 4294967296 | bytes 7340032 | tf_op jit(solution)/shard_map/moments/pallas_call | solution.py:260
  25.8 0.5 collective-permute-start
  26.3 2.3 %collective-permute-done.refs_0_ = bf16[512,1024]{1,0:T(8,128)(2,1)S(1)} collective-permute-done((bf16[512,1024]{1,0:T(8,128)(2,1)S(1)}, bf16[512,1024]{1,0:T(8,128)(2,1)S(1)}, u32[]{:S(2)}, u32[]{:S(2)}) %collective-permute-start) | collective-permute-done | bytes 1048608 | tf_op jit(solution)/shard_map/ppermute | solution.py:353
  28.5 0.0 copy-start
  28.5 0.0 copy-start.1
  28.5 0.2 add_and_split.3
  28.7 1.9 %collective-permute-start.1 = (bf16[256,640]{1,0:T(8,128)(2,1)S(1)}, bf16[256,640]{1,0:T(8,128)(2,1)S(1)}, u32[]{:S(2)}, u32[]{:S(2)}) collective-permute-start(bf16[256,640]{1,0:T(8,128)(2,1)S(1)} %get-tuple-element.25), channel_id=1, source_target_pairs={{0,2},{1,3},{2,0},{3,1},{4,6},{5,7},{6,4},{7,5},{8,10},{9,11},{10,... | collective-permute-start | bytes 983048 | tf_op jit(solution)/shard_map/ppermute | solution.py:353
  30.7 0.2 collective-permute-start.2
  30.8 17.3 %collective-permute-done.2.refs_0_ = bf16[256,384]{1,0:T(8,128)(2,1)S(1)} collective-permute-done((bf16[256,384]{1,0:T(8,128)(2,1)S(1)}, bf16[256,384]{1,0:T(8,128)(2,1)S(1)}, u32[]{:S(2)}, u32[]{:S(2)}) %collective-permute-start.2) | collective-permute-done | bytes 196640 | tf_op jit(solution)/shard_map/ppermute | solution.py:353
  48.1 2.3 %collective-permute-start.7 = (bf16[64,384]{1,0:T(8,128)(2,1)S(1)}, bf16[64,384]{1,0:T(8,128)(2,1)S(1)}, u32[]{:S(2)}, u32[]{:S(2)}) collective-permute-start(bf16[64,384]{1,0:T(8,128)(2,1)S(1)} %get-tuple-element.36), channel_id=1, source_target_pairs={{0,4},{1,5},{2,6},{3,7},{4,0},{5,1},{6,2},{7,3},{8,12},{9,13},{10,... | collective-permute-start | bytes 147464 | tf_op jit(solution)/shard_map/ppermute | solution.py:353
  50.4 3.0 %collective-permute-start.8 = (bf16[64,384]{1,0:T(8,128)(2,1)S(1)}, bf16[64,384]{1,0:T(8,128)(2,1)S(1)}, u32[]{:S(2)}, u32[]{:S(2)}) collective-permute-start(bf16[64,384]{1,0:T(8,128)(2,1)S(1)} %get-tuple-element.37), channel_id=1, source_target_pairs={{0,12},{1,13},{2,14},{3,15},{4,8},{5,9},{6,10},{7,11},{8,4},{9,5},... | collective-permute-start | bytes 147464 | tf_op jit(solution)/shard_map/ppermute | solution.py:353
  53.4 0.0 collective-permute-start.6
  53.4 0.0 collective-permute-done.1.refs_0_
  53.5 0.1 add_and_split.4
  53.5 1.4 %collective-permute-start.4 = (bf16[64,640]{1,0:T(8,128)(2,1)S(1)}, bf16[64,640]{1,0:T(8,128)(2,1)S(1)}, u32[]{:S(2)}, u32[]{:S(2)}) collective-permute-start(bf16[64,640]{1,0:T(8,128)(2,1)S(1)} %get-tuple-element.33), channel_id=1, source_target_pairs={{0,4},{1,5},{2,6},{3,7},{4,0},{5,1},{6,2},{7,3},{8,12},{9,13},{10,... | collective-permute-start | bytes 245768 | tf_op jit(solution)/shard_map/ppermute | solution.py:353
  54.9 3.0 %collective-permute-start.5 = (bf16[64,640]{1,0:T(8,128)(2,1)S(1)}, bf16[64,640]{1,0:T(8,128)(2,1)S(1)}, u32[]{:S(2)}, u32[]{:S(2)}) collective-permute-start(bf16[64,640]{1,0:T(8,128)(2,1)S(1)} %get-tuple-element.34), channel_id=1, source_target_pairs={{0,12},{1,13},{2,14},{3,15},{4,8},{5,9},{6,10},{7,11},{8,4},{9,5},... | collective-permute-start | bytes 245768 | tf_op jit(solution)/shard_map/ppermute | solution.py:353
  58.0 0.0 collective-permute-done.7.refs_6_
  58.0 0.0 collective-permute-start.3
  58.0 0.0 all-to-all-done
  58.0 0.0 copy-done
  58.0 0.0 copy-done.1
  58.0 4.0 %encode.1 = (bf16[2048,256]{1,0:T(8,128)(2,1)}, f32[64,1024]{1,0:T(8,128)S(1)}) custom-call(s32[1]{0:T(128)} %bitcast.me_ref, bf16[2304,256]{1,0:T(8,128)(2,1)S(1)} %bitcast.5, bf16[1024,256]{1,0:T(8,128)(2,1)S(1)} %copy-done, bf16[256,256]{1,0:T(8,128)(2,1)S(1)} %copy-done.1, bf16[64,640]{1,0:T(8,128)(2,1)S(1)} %get-tuple-element.26.refs_0_, ...), custom_call_target="tpu_custom_call" | custom-call | flops 1342177280 | bytes 2097152 | tf_op jit(solution)/shard_map/encode/pallas_call | solution.py:438
  62.0 0.0 collective-permute-done.8.refs_7_
  62.0 0.0 collective-permute-done.6.refs_5_
  62.0 0.0 collective-permute-done.4.refs_2_
  62.0 0.0 collective-permute-done.5.refs_3_
  62.0 3.0 %collective-permute-done.3.refs_1_ = bf16[64,640]{1,0:T(8,128)(2,1)S(1)} collective-permute-done((bf16[64,640]{1,0:T(8,128)(2,1)S(1)}, bf16[64,640]{1,0:T(8,128)(2,1)S(1)}, u32[]{:S(2)}, u32[]{:S(2)}) %collective-permute-start.3) | collective-permute-done | bytes 81952 | tf_op jit(solution)/shard_map/ppermute | solution.py:353
  65.1 0.8 %finish.1 = f32[64,1024]{1,0:T(8,128)} custom-call(f32[64,1024]{1,0:T(8,128)S(1)} %get-tuple-element.31.between_ref, f32[64,640]{1,0:T(8,128)S(1)} %get-tuple-element.32.refs_0_, bf16[64,640]{1,0:T(8,128)(2,1)S(1)} %collective-permute-done.3.refs_1_, bf16[64,640]{1,0:T(8,128)(2,1)S(1)} %collective-permute-done.4.refs_2_, ...), custom_call_target="tpu_custom_call" | custom-call | flops 524288 | bytes 1048576 | tf_op jit(solution)/shard_map/finish/pallas_call | solution.py:333
  (1 shorter events, 0.0 us)
Async XLA Ops:
  11.2 7.4 %copy-start.2 = (f32[1,1024]{1,0:T(1,128)S(1)}, f32[1,1024]{1,0:T(1,128)}, u32[]{:S(2)}) copy-start(f32[1,1024]{1,0:T(1,128)} %get-tuple-element.21.mean_hbm) | copy-start | bytes 12292
  11.2 46.8 %all-to-all-start = ((bf16[16,144,256]{2,1,0:T(8,128)(2,1)}), bf16[16,144,256]{2,1,0:T(8,128)(2,1)S(1)}, u32[]{:S(2)}, u32[]{:S(2)}) async-start(bf16[16,144,256]{2,1,0:T(8,128)(2,1)} %bitcast.6), calls=%async_computation | async-start | bytes 2359296 | tf_op jit(solution)/shard_map/all_to_all | solution.py:469
  25.8 2.8 %collective-permute-start = (bf16[512,1024]{1,0:T(8,128)(2,1)S(1)}, bf16[512,1024]{1,0:T(8,128)(2,1)S(1)}, u32[]{:S(2)}, u32[]{:S(2)}) collective-permute-start(bf16[512,1024]{1,0:T(8,128)(2,1)S(1)} %get-tuple-element.23), channel_id=1, source_target_pairs={{0,1},{1,0},{2,3},{3,2},{4,5},{5,4},{6,7},{7,6},{8,9},{9,8},{10,11... | collective-permute-start | bytes 3145736 | tf_op jit(solution)/shard_map/ppermute | solution.py:353
  28.5 29.4 %copy-start = (bf16[1024,256]{1,0:T(8,128)(2,1)S(1)}, bf16[1024,256]{1,0:T(8,128)(2,1)}, u32[]{:S(2)}) copy-start(bf16[1024,256]{1,0:T(8,128)(2,1)} %centroid_ref.1) | copy-start | bytes 1572868
  28.5 29.4 %copy-start.1 = (bf16[256,256]{1,0:T(8,128)(2,1)S(1)}, bf16[256,256]{1,0:T(8,128)(2,1)}, u32[]{:S(2)}) copy-start(bf16[256,256]{1,0:T(8,128)(2,1)} %rotation_ref.1) | copy-start | bytes 393220
  28.7 24.7 %collective-permute-start.1 = (bf16[256,640]{1,0:T(8,128)(2,1)S(1)}, bf16[256,640]{1,0:T(8,128)(2,1)S(1)}, u32[]{:S(2)}, u32[]{:S(2)}) collective-permute-start(bf16[256,640]{1,0:T(8,128)(2,1)S(1)} %get-tuple-element.25), channel_id=1, source_target_pairs={{0,2},{1,3},{2,0},{3,1},{4,6},{5,7},{6,4},{7,5},{8,10},{9,11},{10,... | collective-permute-start | bytes 983048 | tf_op jit(solution)/shard_map/ppermute | solution.py:353
  30.7 17.4 %collective-permute-start.2 = (bf16[256,384]{1,0:T(8,128)(2,1)S(1)}, bf16[256,384]{1,0:T(8,128)(2,1)S(1)}, u32[]{:S(2)}, u32[]{:S(2)}) collective-permute-start(bf16[256,384]{1,0:T(8,128)(2,1)S(1)} %get-tuple-element.28), channel_id=1, source_target_pairs={{0,2},{1,3},{2,0},{3,1},{4,6},{5,7},{6,4},{7,5},{8,10},{9,11},{10,... | collective-permute-start | bytes 589832 | tf_op jit(solution)/shard_map/ppermute | solution.py:353
  48.1 9.8 %collective-permute-start.7 = (bf16[64,384]{1,0:T(8,128)(2,1)S(1)}, bf16[64,384]{1,0:T(8,128)(2,1)S(1)}, u32[]{:S(2)}, u32[]{:S(2)}) collective-permute-start(bf16[64,384]{1,0:T(8,128)(2,1)S(1)} %get-tuple-element.36), channel_id=1, source_target_pairs={{0,4},{1,5},{2,6},{3,7},{4,0},{5,1},{6,2},{7,3},{8,12},{9,13},{10,... | collective-permute-start | bytes 147464 | tf_op jit(solution)/shard_map/ppermute | solution.py:353
  50.4 11.5 %collective-permute-start.8 = (bf16[64,384]{1,0:T(8,128)(2,1)S(1)}, bf16[64,384]{1,0:T(8,128)(2,1)S(1)}, u32[]{:S(2)}, u32[]{:S(2)}) collective-permute-start(bf16[64,384]{1,0:T(8,128)(2,1)S(1)} %get-tuple-element.37), channel_id=1, source_target_pairs={{0,12},{1,13},{2,14},{3,15},{4,8},{5,9},{6,10},{7,11},{8,4},{9,5},... | collective-permute-start | bytes 147464 | tf_op jit(solution)/shard_map/ppermute | solution.py:353
  53.4 8.5 %collective-permute-start.6 = (bf16[64,384]{1,0:T(8,128)(2,1)S(1)}, bf16[64,384]{1,0:T(8,128)(2,1)S(1)}, u32[]{:S(2)}, u32[]{:S(2)}) collective-permute-start(bf16[64,384]{1,0:T(8,128)(2,1)S(1)} %get-tuple-element.29.refs_1_), channel_id=1, source_target_pairs={{0,8},{1,9},{2,10},{3,11},{4,12},{5,13},{6,14},{7,15},{8,0},{9,1},... | collective-permute-start | bytes 147464 | tf_op jit(solution)/shard_map/ppermute | solution.py:353
  53.5 8.5 %collective-permute-start.4 = (bf16[64,640]{1,0:T(8,128)(2,1)S(1)}, bf16[64,640]{1,0:T(8,128)(2,1)S(1)}, u32[]{:S(2)}, u32[]{:S(2)}) collective-permute-start(bf16[64,640]{1,0:T(8,128)(2,1)S(1)} %get-tuple-element.33), channel_id=1, source_target_pairs={{0,4},{1,5},{2,6},{3,7},{4,0},{5,1},{6,2},{7,3},{8,12},{9,13},{10,... | collective-permute-start | bytes 245768 | tf_op jit(solution)/shard_map/ppermute | solution.py:353
  54.9 7.1 %collective-permute-start.5 = (bf16[64,640]{1,0:T(8,128)(2,1)S(1)}, bf16[64,640]{1,0:T(8,128)(2,1)S(1)}, u32[]{:S(2)}, u32[]{:S(2)}) collective-permute-start(bf16[64,640]{1,0:T(8,128)(2,1)S(1)} %get-tuple-element.34), channel_id=1, source_target_pairs={{0,12},{1,13},{2,14},{3,15},{4,8},{5,9},{6,10},{7,11},{8,4},{9,5},... | collective-permute-start | bytes 245768 | tf_op jit(solution)/shard_map/ppermute | solution.py:353
  58.0 7.1 %collective-permute-start.3 = (bf16[64,640]{1,0:T(8,128)(2,1)S(1)}, bf16[64,640]{1,0:T(8,128)(2,1)S(1)}, u32[]{:S(2)}, u32[]{:S(2)}) collective-permute-start(bf16[64,640]{1,0:T(8,128)(2,1)S(1)} %get-tuple-element.26.refs_0_), channel_id=1, source_target_pairs={{0,8},{1,9},{2,10},{3,11},{4,12},{5,13},{6,14},{7,15},{8,0},{9,1},... | collective-permute-start | bytes 245768 | tf_op jit(solution)/shard_map/ppermute | solution.py:353

commit v10 on v9

--- a/solution.py
+++ b/solution.py
@@ -28,7 +28,7 @@
 def rows_kernel(
     width, e_hbm, basis_hbm, owner_hbm, slot_hbm,
     rows_hbm, mean_hbm,
-    owner_ref, slot_ref, mean_ref, basis_ref, e_ref, rows_ref, sorted_ref, centre_ref, sum_ref, square_ref, total_ref, target_ref, list_ref, e_sem, small_sem, sem,
+    owner_ref, slot_ref, mean_ref, basis_ref, e_ref, rows_ref, yb_ref, centre_ref, sum_ref, square_ref, total_ref, target_ref, list_ref, e_sem, small_sem, sem,
 ):
     step = pl.program_id(0)
     rows_here, wide = e_ref.shape
@@ -52,7 +52,6 @@
         for c in range(1, rows_here // CHUNK):
             e_copy(c).start()
         owner_copy.wait()
-        sorted_ref[...] = jnp.zeros_like(sorted_ref)
         sum_ref[...] = jnp.zeros_like(sum_ref)
         square_ref[...] = jnp.zeros_like(square_ref)
         total_ref[...] = jnp.zeros_like(total_ref)
@@ -106,28 +105,7 @@
     sum_ref[...] += jnp.sum(y.reshape(CHUNK // 8, 8, feats), 0)
     square_ref[...] += jnp.sum((y * y).reshape(CHUNK // 8, 8, feats), 0)
     total_ref[...] += jnp.sum(rows.astype(jnp.float32).reshape(CHUNK // 8, 8, wide), 0)
-    y = y.astype(jnp.bfloat16)
-
-    place = lax.broadcasted_iota(jnp.int32, (GROUP * CAP, LANES), 0).astype(jnp.int16)
-
-    def sort_group(g):
-        pieces = []
-        for c in range(CHUNK // LANES):
-            aim = target_ref[pl.ds(step * (CHUNK // LANES) + c, 1), :] - g * (GROUP * CAP)
-            aim = jnp.broadcast_to(aim, (16, LANES)).astype(jnp.int16)
-            aim = jnp.concatenate([aim] * (GROUP * CAP // 16), 0)
-            pieces.append(jnp.where(aim == place, jnp.ones((), jnp.bfloat16), jnp.zeros((), jnp.bfloat16)))
-        at = pl.ds(pl.multiple_of(g * (GROUP * CAP), GROUP * CAP), GROUP * CAP)
-        sorted_ref[at, :] += jnp.dot(jnp.concatenate(pieces, 1), y, preferred_element_type=jnp.float32)
-
-    if groups <= 4:
-        for g in range(groups):
-            sort_group(g)
-    else:
-
-        @pl.loop(0, groups)
-        def _(g):
-            sort_group(g)
+    yb_ref[here, :] = y.astype(jnp.bfloat16)
 
     @pl.when(step == pl.num_programs(0) - 1)
     def _():
@@ -142,30 +120,41 @@
         common = common + [jnp.zeros((1, feats), jnp.float32)] * (NOTES - 1 - len(common))
         common = jnp.concatenate(common, 0)
 
-        def rows_copy(g):
+        place = lax.broadcasted_iota(jnp.int32, (GROUP * CAP, LANES), 0).astype(jnp.int16)
+
+        def sort_group(g):
+            first = g * GROUP
+            pieces = []
+            for c in range(chunks):
+                aim = target_ref[c:c + 1, :] - first * CAP
+                aim = jnp.broadcast_to(aim, (16, LANES)).astype(jnp.int16)
+                aim = jnp.concatenate([aim] * (GROUP * CAP // 16), 0)
+                pieces.append(jnp.where(aim == place, jnp.ones((), jnp.bfloat16), jnp.zeros((), jnp.bfloat16)))
+            pick = jnp.concatenate(pieces, 1)
+            rows = jnp.dot(pick, yb_ref[...], preferred_element_type=jnp.float32).astype(jnp.bfloat16)
+            for j in range(GROUP):
+                base = pl.multiple_of((first + j) * SPAN, 16)
+                rows_ref[pl.ds(base, CAP), :] = rows[j * CAP:(j + 1) * CAP]
+                notes = jnp.concatenate([common, list_ref[pl.ds(first + j, 1), :]], 0)
+                rows_ref[pl.ds(pl.multiple_of(base + CAP, 16), NOTES), :] = notes.astype(jnp.bfloat16)
             at = pl.ds(pl.multiple_of(g * (GROUP * SPAN), 16), GROUP * SPAN)
             return pltpu.make_async_copy(rows_ref.at[at], rows_hbm.at[at], sem.at[g])
 
-        def place_group(g):
-            for j in range(GROUP):
-                base = pl.multiple_of((g * GROUP + j) * SPAN, 16)
-                from_here = pl.ds(pl.multiple_of((g * GROUP + j) * CAP, CAP), CAP)
-                rows_ref[pl.ds(base, CAP), :] = sorted_ref[from_here, :].astype(jnp.bfloat16)
-                notes = jnp.concatenate([common, list_ref[pl.ds(g * GROUP + j, 1), :]], 0)
-                rows_ref[pl.ds(pl.multiple_of(base + CAP, 16), NOTES), :] = notes.astype(jnp.bfloat16)
-            rows_copy(g).start()
-
         if groups <= 4:
+            copies = []
             for g in range(groups):
-                place_group(g)
+                copies.append(sort_group(g))
+                copies[g].start()
+            for copy in copies:
+                copy.wait()
         else:
 
             @pl.loop(0, groups)
             def _(g):
-                place_group(g)
-
-        for g in range(groups):
-            rows_copy(g).wait()
+                copy = sort_group(g)
+                copy.start()
+                copy.wait()
+
         mean_copy.wait()
 
 
@@ -190,7 +179,7 @@
             pltpu.VMEM((wide, feats), jnp.bfloat16),
             pltpu.VMEM((rows_here, wide), jnp.bfloat16),
             pltpu.VMEM((slots, feats), jnp.bfloat16),
-            pltpu.VMEM((width * CAP, feats), jnp.float32),
+            pltpu.VMEM((rows_here, feats), jnp.bfloat16),
             pltpu.VMEM((2, feats), jnp.float32),
             pltpu.VMEM((8, feats), jnp.float32),
             pltpu.VMEM((8, feats), jnp.float32),
@@ -286,9 +275,9 @@
     return list(zip([0] + ends[:-1], ends))
 
 
-def add_kernel(shares, pieces, keep_ref, *refs):
+def add_kernel(shares, pieces, arrived, keep_ref, *refs):
     count = len(shares) * pieces
-    came, outs = refs[:-count], refs[-count:]
+    came, outs = refs[:arrived], refs[-count:]
     for h, (first, end) in enumerate(cuts(keep_ref.shape[1], shares)):
         for p in range(pieces):
             out = outs[h * pieces + p]
@@ -299,13 +288,13 @@
             out[...] = held.astype(out.dtype)
 
 
-def add_and_split(keep, came, shares, pieces):
+def add_and_split(keep, came, shares, pieces, after=()):
     rows, columns = keep.shape
     vmem = pl.BlockSpec(memory_space=pltpu.VMEM)
     kinds = [jnp.float32] + [jnp.bfloat16] * (pieces - 1)
     outs = pl.pallas_call(
-        functools.partial(add_kernel, shares, pieces),
-        in_specs=[vmem] * (1 + len(came)),
+        functools.partial(add_kernel, shares, pieces, len(came)),
+        in_specs=[vmem] * (1 + len(came)) + [pl.BlockSpec(memory_space=pl.ANY)] * len(after),
         out_specs=[vmem] * (len(shares) * pieces),
         out_shape=[
             jax.ShapeDtypeStruct((rows // pieces, end - first), kind) for first, end in cuts(columns, shares) for kind in kinds
@@ -313,7 +302,7 @@
         compiler_params=pltpu.CompilerParams(vmem_limit_bytes=VMEM_SOME),
         cost_estimate=pl.CostEstimate(flops=2 * rows * columns, bytes_accessed=10 * rows * columns, transcendentals=0),
         name="add_and_split",
-    )(keep, *came)
+    )(keep, *came, *after)
     return [outs[h * pieces:(h + 1) * pieces] for h in range(len(shares))]
 
 
@@ -476,7 +465,7 @@
     for share in shares:
         for n in range(1, len(stages) - 1):
             came = exchange(width, stages[n], share[1:])
-            (share,) = add_and_split(share[0], came, (1,), 1 << len(stages[n + 1]))
+            (share,) = add_and_split(share[0], came, (1,), 1 << len(stages[n + 1]), [held[1] for held in last[-1:]])
         last.append(share)
     came = [exchange(width, stages[-1], share[1:]) for share in last]
     encoded, between = encode(

time: 66.1 us -> 62.3 us (0.943)
  Pallas kernels: 22.7 us -> 20.4 us
  waiting for transfers between devices: 22.6 us -> 21.2 us
    pallas_call x1, Pallas kernels: 10.5 us -> 8.27 us  [project_and_sort(): pl.pallas_call(functools.partial(rows_kernel, width), grid=(rows_here //...]
    ppermute x9, waiting for transfers between devices: 22.6 us -> 21.2 us  [exchange(): lax.ppermute(out[p - 1], 'wide', [(i, i ^ apart) for i in range(width)])]
  transfers between devices with their start and end apart: 10 -> 10, of which waited for: 3 -> 4; matrix products, arithmetic and copies ran while one was open for 0% -> 0% of each run, Pallas kernels for 17% -> 18%
where the time goes in v10:
time: 62.3 us; the launch traced here: 62.1 us
  waiting for transfers between devices  21.2 us (34%)
  Pallas kernels  20.4 us (33%)
  starting transfers between devices  19.7 us (32%)
  between operations  0.72 us (1%)
    ppermute x9, waiting for transfers between devices, exchange(): lax.ppermute(out[p - 1], 'wide', [(i, i ^ apart) for i in range(width)])  21.2 us
    ppermute x9, starting transfers between devices, exchange(): lax.ppermute(out[p - 1], 'wide', [(i, i ^ apart) for i in range(width)])  12.3 us
    pallas_call x1, Pallas kernels, project_and_sort(): pl.pallas_call(functools.partial(rows_kernel, width), grid=(rows_here //...  8.27 us
    all_to_all x1, starting transfers between devices, local(): lax.all_to_all(rows.reshape(width, SPAN, feats), 'wide', split_axis=0, co...  7.4 us
    pallas_call x1, Pallas kernels, moments(): pl.pallas_call(functools.partial(moments_kernel, width), in_specs=[pl.Blo...  7.16 us
    pallas_call x1, Pallas kernels, encode(): pl.pallas_call(functools.partial(encode_kernel, total), in_specs=[pl.Bloc...  3.96 us
  transfers between devices with their start and end apart: 10, of which 4 were waited for; matrix products, arithmetic and copies ran while one was open for 0% of the time, Pallas kernels for 18%

profile of v10, /device:TPU:0, one launch (start us, length us, event | category | flops | bytes accessed | tf_op | source)
XLA Modules:
  0.0 62.1 jit_solution(10928694292259865971)
XLA Ops:
  0.6 8.3 %project_sort.1 = (bf16[2304,256]{1,0:T(8,128)(2,1)}, f32[1,1024]{1,0:T(1,128)}) custom-call(bf16[2048,1024]{1,0:T(8,128)(2,1)} %e_hbm.3, bf16[1024,256]{1,0:T(8,128)(2,1)} %basis_hbm.1, s32[16,128]{1,0:T(8,128)} %bitcast.7, s32[16,128]{1,0:T(8,128)} %bitcast.8), custom_call_target="tpu_custom_call" | custom-call | flops 3489660928 | bytes 5373952 | tf_op jit(solution)/shard_map/project_sort/pallas_call | solution.py:166
  8.9 0.0 copy-start.2
  8.9 7.4 %all-to-all-start = ((bf16[16,144,256]{2,1,0:T(8,128)(2,1)}), bf16[16,144,256]{2,1,0:T(8,128)(2,1)S(1)}, u32[]{:S(2)}, u32[]{:S(2)}) async-start(bf16[16,144,256]{2,1,0:T(8,128)(2,1)} %bitcast.6), calls=%async_computation | async-start | bytes 2359296 | tf_op jit(solution)/shard_map/all_to_all | solution.py:458
  16.3 0.0 copy-done.2
  16.3 7.2 %moments.1 = (f32[512,1024]{1,0:T(8,128)S(1)}, bf16[512,1024]{1,0:T(8,128)(2,1)S(1)}) custom-call(s32[1]{0:T(128)} %bitcast.me_ref, f32[1,1024]{1,0:T(1,128)S(1)} %copy-done.2, bf16[2048,1024]{1,0:T(8,128)(2,1)} %e_hbm.3), custom_call_target="tpu_custom_call" | custom-call | flops 4294967296 | bytes 7340032 | tf_op jit(solution)/shard_map/moments/pallas_call | solution.py:249
  23.5 0.5 collective-permute-start
  24.0 2.3 %collective-permute-done.refs_0_ = bf16[512,1024]{1,0:T(8,128)(2,1)S(1)} collective-permute-done((bf16[512,1024]{1,0:T(8,128)(2,1)S(1)}, bf16[512,1024]{1,0:T(8,128)(2,1)S(1)}, u32[]{:S(2)}, u32[]{:S(2)}) %collective-permute-start) | collective-permute-done | bytes 1048608 | tf_op jit(solution)/shard_map/ppermute | solution.py:342
  26.3 0.0 copy-start
  26.3 0.0 copy-start.1
  26.3 0.2 add_and_split.3
  26.5 1.9 %collective-permute-start.1 = (bf16[256,640]{1,0:T(8,128)(2,1)S(1)}, bf16[256,640]{1,0:T(8,128)(2,1)S(1)}, u32[]{:S(2)}, u32[]{:S(2)}) collective-permute-start(bf16[256,640]{1,0:T(8,128)(2,1)S(1)} %get-tuple-element.25), channel_id=1, source_target_pairs={{0,2},{1,3},{2,0},{3,1},{4,6},{5,7},{6,4},{7,5},{8,10},{9,11},{10,... | collective-permute-start | bytes 983048 | tf_op jit(solution)/shard_map/ppermute | solution.py:342
  28.4 0.2 collective-permute-start.2
  28.6 10.9 %collective-permute-done.1.refs_0_ = bf16[256,640]{1,0:T(8,128)(2,1)S(1)} collective-permute-done((bf16[256,640]{1,0:T(8,128)(2,1)S(1)}, bf16[256,640]{1,0:T(8,128)(2,1)S(1)}, u32[]{:S(2)}, u32[]{:S(2)}) %collective-permute-start.1) | collective-permute-done | bytes 327712 | tf_op jit(solution)/shard_map/ppermute | solution.py:342
  39.5 0.1 add_and_split.4
  39.5 6.3 %collective-permute-done.2.refs_0_ = bf16[256,384]{1,0:T(8,128)(2,1)S(1)} collective-permute-done((bf16[256,384]{1,0:T(8,128)(2,1)S(1)}, bf16[256,384]{1,0:T(8,128)(2,1)S(1)}, u32[]{:S(2)}, u32[]{:S(2)}) %collective-permute-start.2) | collective-permute-done | bytes 196640 | tf_op jit(solution)/shard_map/ppermute | solution.py:342
  45.9 2.3 %collective-permute-start.7 = (bf16[64,384]{1,0:T(8,128)(2,1)S(1)}, bf16[64,384]{1,0:T(8,128)(2,1)S(1)}, u32[]{:S(2)}, u32[]{:S(2)}) collective-permute-start(bf16[64,384]{1,0:T(8,128)(2,1)S(1)} %get-tuple-element.36), channel_id=1, source_target_pairs={{0,4},{1,5},{2,6},{3,7},{4,0},{5,1},{6,2},{7,3},{8,12},{9,13},{10,... | collective-permute-start | bytes 147464 | tf_op jit(solution)/shard_map/ppermute | solution.py:342
  48.1 1.7 %collective-permute-start.3 = (bf16[64,640]{1,0:T(8,128)(2,1)S(1)}, bf16[64,640]{1,0:T(8,128)(2,1)S(1)}, u32[]{:S(2)}, u32[]{:S(2)}) collective-permute-start(bf16[64,640]{1,0:T(8,128)(2,1)S(1)} %get-tuple-element.26.refs_1_.refs_0_), channel_id=1, source_target_pairs={{0,8},{1,9},{2,10},{3,11},{4,12},{5,13},{6,14},{7,15},{8,0},{9,1},... | collective-permute-start | bytes 245768 | tf_op jit(solution)/shard_map/ppermute | solution.py:342
  49.8 1.4 %collective-permute-start.8 = (bf16[64,384]{1,0:T(8,128)(2,1)S(1)}, bf16[64,384]{1,0:T(8,128)(2,1)S(1)}, u32[]{:S(2)}, u32[]{:S(2)}) collective-permute-start(bf16[64,384]{1,0:T(8,128)(2,1)S(1)} %get-tuple-element.37), channel_id=1, source_target_pairs={{0,12},{1,13},{2,14},{3,15},{4,8},{5,9},{6,10},{7,11},{8,4},{9,5},... | collective-permute-start | bytes 147464 | tf_op jit(solution)/shard_map/ppermute | solution.py:342
  51.2 2.0 %collective-permute-start.6 = (bf16[64,384]{1,0:T(8,128)(2,1)S(1)}, bf16[64,384]{1,0:T(8,128)(2,1)S(1)}, u32[]{:S(2)}, u32[]{:S(2)}) collective-permute-start(bf16[64,384]{1,0:T(8,128)(2,1)S(1)} %get-tuple-element.29.refs_1_), channel_id=1, source_target_pairs={{0,8},{1,9},{2,10},{3,11},{4,12},{5,13},{6,14},{7,15},{8,0},{9,1},... | collective-permute-start | bytes 147464 | tf_op jit(solution)/shard_map/ppermute | solution.py:342
  53.2 1.0 %collective-permute-start.4 = (bf16[64,640]{1,0:T(8,128)(2,1)S(1)}, bf16[64,640]{1,0:T(8,128)(2,1)S(1)}, u32[]{:S(2)}, u32[]{:S(2)}) collective-permute-start(bf16[64,640]{1,0:T(8,128)(2,1)S(1)} %get-tuple-element.33), channel_id=1, source_target_pairs={{0,4},{1,5},{2,6},{3,7},{4,0},{5,1},{6,2},{7,3},{8,12},{9,13},{10,... | collective-permute-start | bytes 245768 | tf_op jit(solution)/shard_map/ppermute | solution.py:342
  54.2 0.0 collective-permute-done.7.refs_6_
  54.2 1.4 %collective-permute-start.5 = (bf16[64,640]{1,0:T(8,128)(2,1)S(1)}, bf16[64,640]{1,0:T(8,128)(2,1)S(1)}, u32[]{:S(2)}, u32[]{:S(2)}) collective-permute-start(bf16[64,640]{1,0:T(8,128)(2,1)S(1)} %get-tuple-element.34), channel_id=1, source_target_pairs={{0,12},{1,13},{2,14},{3,15},{4,8},{5,9},{6,10},{7,11},{8,4},{9,5},... | collective-permute-start | bytes 245768 | tf_op jit(solution)/shard_map/ppermute | solution.py:342
  55.6 0.0 all-to-all-done
  55.6 0.0 copy-done
  55.6 0.0 copy-done.1
  55.6 4.0 %encode.1 = (bf16[2048,256]{1,0:T(8,128)(2,1)}, f32[64,1024]{1,0:T(8,128)S(1)}) custom-call(s32[1]{0:T(128)} %bitcast.me_ref, bf16[2304,256]{1,0:T(8,128)(2,1)S(1)} %bitcast.5, bf16[1024,256]{1,0:T(8,128)(2,1)S(1)} %copy-done, bf16[256,256]{1,0:T(8,128)(2,1)S(1)} %copy-done.1, bf16[64,640]{1,0:T(8,128)(2,1)S(1)} %get-tuple-element.26.refs_1_.refs_0_, ...), custom_call_target="tpu_custom_call" | custom-call | flops 1342177280 | bytes 2097152 | tf_op jit(solution)/shard_map/encode/pallas_call | solution.py:427
  59.6 0.0 collective-permute-done.8.refs_7_
  59.6 1.7 %collective-permute-done.6.refs_5_ = bf16[64,384]{1,0:T(8,128)(2,1)S(1)} collective-permute-done((bf16[64,384]{1,0:T(8,128)(2,1)S(1)}, bf16[64,384]{1,0:T(8,128)(2,1)S(1)}, u32[]{:S(2)}, u32[]{:S(2)}) %collective-permute-start.6) | collective-permute-done | bytes 49184 | tf_op jit(solution)/shard_map/ppermute | solution.py:342
  61.3 0.0 collective-permute-done.4.refs_2_
  61.3 0.0 collective-permute-done.5.refs_3_
  61.3 0.0 collective-permute-done.3.refs_1_
  61.3 0.8 %finish.1 = f32[64,1024]{1,0:T(8,128)} custom-call(f32[64,1024]{1,0:T(8,128)S(1)} %get-tuple-element.31.between_ref, f32[64,640]{1,0:T(8,128)S(1)} %get-tuple-element.32.refs_0_, bf16[64,640]{1,0:T(8,128)(2,1)S(1)} %collective-permute-done.3.refs_1_, bf16[64,640]{1,0:T(8,128)(2,1)S(1)} %collective-permute-done.4.refs_2_, ...), custom_call_target="tpu_custom_call" | custom-call | flops 524288 | bytes 1048576 | tf_op jit(solution)/shard_map/finish/pallas_call | solution.py:322
  (1 shorter events, 0.0 us)
Async XLA Ops:
  8.9 7.4 %copy-start.2 = (f32[1,1024]{1,0:T(1,128)S(1)}, f32[1,1024]{1,0:T(1,128)}, u32[]{:S(2)}) copy-start(f32[1,1024]{1,0:T(1,128)} %get-tuple-element.21.mean_hbm) | copy-start | bytes 12292
  8.9 46.7 %all-to-all-start = ((bf16[16,144,256]{2,1,0:T(8,128)(2,1)}), bf16[16,144,256]{2,1,0:T(8,128)(2,1)S(1)}, u32[]{:S(2)}, u32[]{:S(2)}) async-start(bf16[16,144,256]{2,1,0:T(8,128)(2,1)} %bitcast.6), calls=%async_computation | async-start | bytes 2359296 | tf_op jit(solution)/shard_map/all_to_all | solution.py:458
  23.5 2.8 %collective-permute-start = (bf16[512,1024]{1,0:T(8,128)(2,1)S(1)}, bf16[512,1024]{1,0:T(8,128)(2,1)S(1)}, u32[]{:S(2)}, u32[]{:S(2)}) collective-permute-start(bf16[512,1024]{1,0:T(8,128)(2,1)S(1)} %get-tuple-element.23), channel_id=1, source_target_pairs={{0,1},{1,0},{2,3},{3,2},{4,5},{5,4},{6,7},{7,6},{8,9},{9,8},{10,11... | collective-permute-start | bytes 3145736 | tf_op jit(solution)/shard_map/ppermute | solution.py:342
  26.3 29.3 %copy-start = (bf16[1024,256]{1,0:T(8,128)(2,1)S(1)}, bf16[1024,256]{1,0:T(8,128)(2,1)}, u32[]{:S(2)}) copy-start(bf16[1024,256]{1,0:T(8,128)(2,1)} %centroid_ref.1) | copy-start | bytes 1572868
  26.3 29.3 %copy-start.1 = (bf16[256,256]{1,0:T(8,128)(2,1)S(1)}, bf16[256,256]{1,0:T(8,128)(2,1)}, u32[]{:S(2)}) copy-start(bf16[256,256]{1,0:T(8,128)(2,1)} %rotation_ref.1) | copy-start | bytes 393220
  26.5 13.0 %collective-permute-start.1 = (bf16[256,640]{1,0:T(8,128)(2,1)S(1)}, bf16[256,640]{1,0:T(8,128)(2,1)S(1)}, u32[]{:S(2)}, u32[]{:S(2)}) collective-permute-start(bf16[256,640]{1,0:T(8,128)(2,1)S(1)} %get-tuple-element.25), channel_id=1, source_target_pairs={{0,2},{1,3},{2,0},{3,1},{4,6},{5,7},{6,4},{7,5},{8,10},{9,11},{10,... | collective-permute-start | bytes 983048 | tf_op jit(solution)/shard_map/ppermute | solution.py:342
  28.4 17.4 %collective-permute-start.2 = (bf16[256,384]{1,0:T(8,128)(2,1)S(1)}, bf16[256,384]{1,0:T(8,128)(2,1)S(1)}, u32[]{:S(2)}, u32[]{:S(2)}) collective-permute-start(bf16[256,384]{1,0:T(8,128)(2,1)S(1)} %get-tuple-element.28), channel_id=1, source_target_pairs={{0,2},{1,3},{2,0},{3,1},{4,6},{5,7},{6,4},{7,5},{8,10},{9,11},{10,... | collective-permute-start | bytes 589832 | tf_op jit(solution)/shard_map/ppermute | solution.py:342
  45.9 8.3 %collective-permute-start.7 = (bf16[64,384]{1,0:T(8,128)(2,1)S(1)}, bf16[64,384]{1,0:T(8,128)(2,1)S(1)}, u32[]{:S(2)}, u32[]{:S(2)}) collective-permute-start(bf16[64,384]{1,0:T(8,128)(2,1)S(1)} %get-tuple-element.36), channel_id=1, source_target_pairs={{0,4},{1,5},{2,6},{3,7},{4,0},{5,1},{6,2},{7,3},{8,12},{9,13},{10,... | collective-permute-start | bytes 147464 | tf_op jit(solution)/shard_map/ppermute | solution.py:342
  48.1 13.2 %collective-permute-start.3 = (bf16[64,640]{1,0:T(8,128)(2,1)S(1)}, bf16[64,640]{1,0:T(8,128)(2,1)S(1)}, u32[]{:S(2)}, u32[]{:S(2)}) collective-permute-start(bf16[64,640]{1,0:T(8,128)(2,1)S(1)} %get-tuple-element.26.refs_1_.refs_0_), channel_id=1, source_target_pairs={{0,8},{1,9},{2,10},{3,11},{4,12},{5,13},{6,14},{7,15},{8,0},{9,1},... | collective-permute-start | bytes 245768 | tf_op jit(solution)/shard_map/ppermute | solution.py:342
  49.8 9.8 %collective-permute-start.8 = (bf16[64,384]{1,0:T(8,128)(2,1)S(1)}, bf16[64,384]{1,0:T(8,128)(2,1)S(1)}, u32[]{:S(2)}, u32[]{:S(2)}) collective-permute-start(bf16[64,384]{1,0:T(8,128)(2,1)S(1)} %get-tuple-element.37), channel_id=1, source_target_pairs={{0,12},{1,13},{2,14},{3,15},{4,8},{5,9},{6,10},{7,11},{8,4},{9,5},... | collective-permute-start | bytes 147464 | tf_op jit(solution)/shard_map/ppermute | solution.py:342
  51.2 10.1 %collective-permute-start.6 = (bf16[64,384]{1,0:T(8,128)(2,1)S(1)}, bf16[64,384]{1,0:T(8,128)(2,1)S(1)}, u32[]{:S(2)}, u32[]{:S(2)}) collective-permute-start(bf16[64,384]{1,0:T(8,128)(2,1)S(1)} %get-tuple-element.29.refs_1_), channel_id=1, source_target_pairs={{0,8},{1,9},{2,10},{3,11},{4,12},{5,13},{6,14},{7,15},{8,0},{9,1},... | collective-permute-start | bytes 147464 | tf_op jit(solution)/shard_map/ppermute | solution.py:342
  53.2 8.1 %collective-permute-start.4 = (bf16[64,640]{1,0:T(8,128)(2,1)S(1)}, bf16[64,640]{1,0:T(8,128)(2,1)S(1)}, u32[]{:S(2)}, u32[]{:S(2)}) collective-permute-start(bf16[64,640]{1,0:T(8,128)(2,1)S(1)} %get-tuple-element.33), channel_id=1, source_target_pairs={{0,4},{1,5},{2,6},{3,7},{4,0},{5,1},{6,2},{7,3},{8,12},{9,13},{10,... | collective-permute-start | bytes 245768 | tf_op jit(solution)/shard_map/ppermute | solution.py:342
  54.2 7.1 %collective-permute-start.5 = (bf16[64,640]{1,0:T(8,128)(2,1)S(1)}, bf16[64,640]{1,0:T(8,128)(2,1)S(1)}, u32[]{:S(2)}, u32[]{:S(2)}) collective-permute-start(bf16[64,640]{1,0:T(8,128)(2,1)S(1)} %get-tuple-element.34), channel_id=1, source_target_pairs={{0,12},{1,13},{2,14},{3,15},{4,8},{5,9},{6,10},{7,11},{8,4},{9,5},... | collective-permute-start | bytes 245768 | tf_op jit(solution)/shard_map/ppermute | solution.py:342

commit v11 on v8

--- a/solution.py
+++ b/solution.py
@@ -14,7 +14,7 @@
 CHUNK = 512
 TILE = 256
 GROUP = 4
-SHARES = 2
+SHARES = (5, 3)
 VMEM_ALL = 60 * 1024 * 1024
 VMEM_SOME = 24 * 1024 * 1024
 VMEM_MOST = 48 * 1024 * 1024
@@ -264,52 +264,55 @@
     )(me.reshape(1), mean, embeddings)
 
 
-def add_kernel(shares, pieces, keep_ref, *refs):
-    outs = refs[len(refs) - shares * pieces:]
-    came = refs[:len(refs) - shares * pieces]
-    rows, columns = outs[0].shape
-    for h in range(shares):
-        across = slice(h * columns, (h + 1) * columns)
+def cuts(columns, shares):
+    unit = columns // sum(shares)
+    ends = [unit * sum(shares[:h + 1]) for h in range(len(shares))]
+    return list(zip([0] + ends[:-1], ends))
+
+
+def add_kernel(shares, pieces, arrived, keep_ref, *refs):
+    count = len(shares) * pieces
+    came, outs = refs[:arrived], refs[-count:]
+    for h, (first, end) in enumerate(cuts(keep_ref.shape[1], shares)):
         for p in range(pieces):
-            at = slice(p * rows, (p + 1) * rows)
-            held = keep_ref[at, across]
+            out = outs[h * pieces + p]
+            at = slice(p * out.shape[0], (p + 1) * out.shape[0])
+            held = keep_ref[at, first:end].astype(jnp.float32)
             for ref in came:
-                held = held + ref[at, across].astype(jnp.float32)
-            out = outs[h * pieces + p]
+                held = held + ref[at, first:end].astype(jnp.float32)
             out[...] = held.astype(out.dtype)
 
 
-def add_and_split(keep, came, shares, pieces):
+def add_and_split(keep, came, shares, pieces, after=()):
     rows, columns = keep.shape
     vmem = pl.BlockSpec(memory_space=pltpu.VMEM)
-    shape = (rows // pieces, columns // shares)
     kinds = [jnp.float32] + [jnp.bfloat16] * (pieces - 1)
     outs = pl.pallas_call(
-        functools.partial(add_kernel, shares, pieces),
-        in_specs=[vmem] * (1 + len(came)),
-        out_specs=[vmem] * (shares * pieces),
-        out_shape=[jax.ShapeDtypeStruct(shape, kind) for kind in kinds * shares],
+        functools.partial(add_kernel, shares, pieces, len(came)),
+        in_specs=[vmem] * (1 + len(came)) + [pl.BlockSpec(memory_space=pl.ANY)] * len(after),
+        out_specs=[vmem] * (len(shares) * pieces),
+        out_shape=[
+            jax.ShapeDtypeStruct((rows // pieces, end - first), kind) for first, end in cuts(columns, shares) for kind in kinds
+        ],
         compiler_params=pltpu.CompilerParams(vmem_limit_bytes=VMEM_SOME),
         cost_estimate=pl.CostEstimate(flops=2 * rows * columns, bytes_accessed=10 * rows * columns, transcendentals=0),
         name="add_and_split",
-    )(keep, *came)
-    return [outs[h * pieces:(h + 1) * pieces] for h in range(shares)]
+    )(keep, *came, *after)
+    return [outs[h * pieces:(h + 1) * pieces] for h in range(len(shares))]
 
 
 def finish_kernel(total, between_ref, *refs):
     out_ref = refs[-1]
-    each = (len(refs) - 1) // SHARES
-    columns = out_ref.shape[1] // SHARES
-    for h in range(SHARES):
-        across = slice(h * columns, (h + 1) * columns)
+    each = (len(refs) - 1) // len(SHARES)
+    for h, (first, end) in enumerate(cuts(out_ref.shape[1], SHARES)):
         held = refs[h * each][...]
         for ref in refs[h * each + 1:(h + 1) * each]:
             held = held + ref[...].astype(jnp.float32)
-        out_ref[:, across] = (held + between_ref[:, across]) / total
-
-
-def finish(total, between, keeps, came):
-    parts = [part for keep, pieces in zip(keeps, came) for part in (keep, *pieces)]
+        out_ref[:, first:end] = (held + between_ref[:, first:end]) / total
+
+
+def finish(total, between, ends):
+    parts = [part for end in ends for part in end]
     vmem = pl.BlockSpec(memory_space=pltpu.VMEM)
     return pl.pallas_call(
         functools.partial(finish_kernel, total),
@@ -322,17 +325,8 @@
     )(between, *parts)
 
 
-def halving_stages(width):
-    strides = [1 << k for k in range(width.bit_length() - 1)]
-    return [[s] for s in strides[:-2]] + [strides[-2:]]
-
-
-def exchange(width, stage, out):
-    came = []
-    for p in range(1, 1 << len(stage)):
-        apart = sum(s for k, s in enumerate(stage) if (p >> (len(stage) - 1 - k)) & 1)
-        came.append(lax.ppermute(out[p - 1], "wide", [(i, i ^ apart) for i in range(width)]))
-    return came
+def exchange(width, stride, out):
+    return lax.ppermute(out, "wide", [(i, i ^ stride) for i in range(width)])
 
 
 def encode_kernel(total, me_ref, got_ref, basis_ref, centroid_ref, rotation_ref, *refs):
@@ -459,20 +453,24 @@
     got = lax.all_to_all(rows.reshape(width, SPAN, feats), "wide", split_axis=0, concat_axis=0, tiled=True)
 
     keep, send = moments(width, me, embeddings, mean)
-    stages = halving_stages(width)
-    came = exchange(width, stages[0], [send])
-    shares = add_and_split(keep, came, SHARES, 1 << len(stages[1]))
-    last = []
-    for share in shares:
-        for n in range(1, len(stages) - 1):
-            came = exchange(width, stages[n], share[1:])
-            (share,) = add_and_split(share[0], came, 1, 1 << len(stages[n + 1]))
-        last.append(share)
-    came = [exchange(width, stages[-1], share[1:]) for share in last]
-    encoded, between = encode(
-        width, total, me, got.reshape(width * SPAN, feats), basis, centroids, rotation, [share[1] for share in last]
-    )
-    covariance = finish(total, between, [share[0] for share in last], came)
+    came = exchange(width, 1, send)
+    shares = add_and_split(keep, [came], SHARES, 2)
+    encoded, ends, after = None, [], []
+    for keep, send in shares:
+        stride = 2
+        while stride < width:
+            came = exchange(width, stride, send)
+            stride *= 2
+            if stride < width:
+                ((keep, send),) = add_and_split(keep, [came], (1,), 2, after)
+                after = []
+            if encoded is None:
+                encoded, between = encode(
+                    width, total, me, got.reshape(width * SPAN, feats), basis, centroids, rotation, [send]
+                )
+        ends.append([keep, came])
+        after = [between]
+    covariance = finish(total, between, ends)
     return (encoded, covariance)
 
 

time: 57 us -> 59.6 us (1.046)
  waiting for transfers between devices: 14.8 us -> 16.8 us
  starting transfers between devices: 21.7 us -> 20.7 us
  local copies, waits for them, and re-layouts: 0.02 us -> 0.92 us
  Pallas kernels: 19.5 us -> 20.1 us
    ppermute x9 -> x7, waiting for transfers between devices: 14.8 us -> 16.8 us  [exchange(): return lax.ppermute(out, 'wide', [(i, i ^ stride) for i in range(width)])]
    ppermute x9 -> x7, starting transfers between devices: 14.3 us -> 13.3 us  [exchange(): return lax.ppermute(out, 'wide', [(i, i ^ stride) for i in range(width)])]
    unnamed x8, local copies, waits for them, and re-layouts: 0.02 us -> 0.92 us
    pallas_call x3 -> x5, Pallas kernels: 0.26 us -> 0.98 us  [add_and_split(): pl.pallas_call(functools.partial(add_kernel, shares, pieces, len(came)),...]
  transfers between devices with their start and end apart: 10 -> 8, of which waited for: 4 -> 5; matrix products, arithmetic and copies ran while one was open for 0% -> 0% of each run, Pallas kernels for 20% -> 20%
where the time goes in v11:
time: 59.6 us; the launch traced here: 59.3 us
  starting transfers between devices  20.7 us (35%)
  Pallas kernels  20.1 us (34%)
  waiting for transfers between devices  16.8 us (28%)
  local copies, waits for them, and re-layouts  0.92 us (2%)
  between operations  0.74 us (1%)
    ppermute x7, waiting for transfers between devices, exchange(): return lax.ppermute(out, 'wide', [(i, i ^ stride) for i in range(width)])  16.8 us
    ppermute x7, starting transfers between devices, exchange(): return lax.ppermute(out, 'wide', [(i, i ^ stride) for i in range(width)])  13.3 us
    all_to_all x1, starting transfers between devices, local(): lax.all_to_all(rows.reshape(width, SPAN, feats), 'wide', split_axis=0, co...  7.4 us
    pallas_call x1, Pallas kernels, project_and_sort(): pl.pallas_call(functools.partial(rows_kernel, width), grid=(rows_here //...  7.27 us
    pallas_call x1, Pallas kernels, moments(): pl.pallas_call(functools.partial(moments_kernel, width), in_specs=[pl.Blo...  7.16 us
    pallas_call x1, Pallas kernels, encode(): pl.pallas_call(functools.partial(encode_kernel, total), in_specs=[pl.Bloc...  3.99 us
  transfers between devices with their start and end apart: 8, of which 5 were waited for; matrix products, arithmetic and copies ran while one was open for 0% of the time, Pallas kernels for 20%

profile of v11, /device:TPU:0, one launch (start us, length us, event | category | flops | bytes accessed | tf_op | source)
XLA Modules:
  0.0 59.3 jit_solution(18368587715993033110)
XLA Ops:
  0.6 7.3 %project_sort.1 = (bf16[2304,256]{1,0:T(8,128)(2,1)}, f32[1,1024]{1,0:T(1,128)}) custom-call(bf16[2048,1024]{1,0:T(8,128)(2,1)} %e_hbm.3, bf16[1024,256]{1,0:T(8,128)(2,1)} %basis_ref.1, s32[16,128]{1,0:T(8,128)} %bitcast.7, s32[16,128]{1,0:T(8,128)} %bitcast.8), custom_call_target="tpu_custom_call" | custom-call | flops 3489660928 | bytes 5373952 | tf_op jit(solution)/shard_map/project_sort/pallas_call | solution.py:162
  7.9 0.0 copy-start.3
  7.9 7.4 %all-to-all-start = ((bf16[16,144,256]{2,1,0:T(8,128)(2,1)}), bf16[16,144,256]{2,1,0:T(8,128)(2,1)S(1)}, u32[]{:S(2)}, u32[]{:S(2)}) async-start(bf16[16,144,256]{2,1,0:T(8,128)(2,1)} %bitcast.6), calls=%async_computation | async-start | bytes 2359296 | tf_op jit(solution)/shard_map/all_to_all | solution.py:453
  15.3 0.0 copy-done.3
  15.3 7.2 %moments.1 = (f32[512,1024]{1,0:T(8,128)S(1)}, bf16[512,1024]{1,0:T(8,128)(2,1)S(1)}) custom-call(s32[1]{0:T(128)} %bitcast.me_ref, f32[1,1024]{1,0:T(1,128)S(1)} %copy-done.3, bf16[2048,1024]{1,0:T(8,128)(2,1)} %e_hbm.3), custom_call_target="tpu_custom_call" | custom-call | flops 4294967296 | bytes 7340032 | tf_op jit(solution)/shard_map/moments/pallas_call | solution.py:244
  22.5 0.0 copy-start
  22.5 0.0 copy-start.1
  22.5 0.5 collective-permute-start
  23.0 2.3 %collective-permute-done.refs_0_ = bf16[512,1024]{1,0:T(8,128)(2,1)S(1)} collective-permute-done((bf16[512,1024]{1,0:T(8,128)(2,1)S(1)}, bf16[512,1024]{1,0:T(8,128)(2,1)S(1)}, u32[]{:S(2)}, u32[]{:S(2)}) %collective-permute-start) | collective-permute-done | bytes 1048608 | tf_op jit(solution)/shard_map/ppermute | solution.py:329
  25.3 0.2 add_and_split.5
  25.5 1.9 %collective-permute-start.1 = (bf16[256,640]{1,0:T(8,128)(2,1)S(1)}, bf16[256,640]{1,0:T(8,128)(2,1)S(1)}, u32[]{:S(2)}, u32[]{:S(2)}) collective-permute-start(bf16[256,640]{1,0:T(8,128)(2,1)S(1)} %get-tuple-element.25), channel_id=1, source_target_pairs={{0,2},{1,3},{2,0},{3,1},{4,6},{5,7},{6,4},{7,5},{8,10},{9,11},{10,... | collective-permute-start | bytes 983048 | tf_op jit(solution)/shard_map/ppermute | solution.py:329
  27.4 0.2 collective-permute-start.4
  27.6 10.9 %collective-permute-done.1.refs_0_ = bf16[256,640]{1,0:T(8,128)(2,1)S(1)} collective-permute-done((bf16[256,640]{1,0:T(8,128)(2,1)S(1)}, bf16[256,640]{1,0:T(8,128)(2,1)S(1)}, u32[]{:S(2)}, u32[]{:S(2)}) %collective-permute-start.1) | collective-permute-done | bytes 327712 | tf_op jit(solution)/shard_map/ppermute | solution.py:329
  38.5 0.7 %add_and_split.6 = (f32[128,640]{1,0:T(8,128)S(1)}, bf16[128,640]{1,0:T(8,128)(2,1)}) custom-call(f32[256,640]{1,0:T(8,128)S(1)} %get-tuple-element.24.keep_ref, bf16[256,640]{1,0:T(8,128)(2,1)S(1)} %collective-permute-done.1.refs_0_), custom_call_target="tpu_custom_call" | custom-call | flops 327680 | bytes 1638400 | tf_op jit(solution)/shard_map/add_and_split/pallas_call | solution.py:290
  39.2 3.2 %collective-permute-start.2 = (bf16[128,640]{1,0:T(8,128)(2,1)}, bf16[128,640]{1,0:T(8,128)(2,1)S(1)}, u32[]{:S(2)}, u32[]{:S(2)}) collective-permute-start(bf16[128,640]{1,0:T(8,128)(2,1)} %get-tuple-element.26.refs_0_), channel_id=1, source_target_pairs={{0,4},{1,5},{2,6},{3,7},{4,0},{5,1},{6,2},{7,3},{8,12},{9,13},{10,... | collective-permute-start | bytes 491528 | tf_op jit(solution)/shard_map/ppermute | solution.py:329
  42.4 0.0 all-to-all-done
  42.4 0.0 copy-done
  42.4 0.0 copy-done.1
  42.4 0.0 copy-start.2
  42.5 0.9 %copy-done.2 = bf16[256,256]{1,0:T(8,128)(2,1)S(1)} copy-done((bf16[256,256]{1,0:T(8,128)(2,1)S(1)}, bf16[256,256]{1,0:T(8,128)(2,1)}, u32[]{:S(2)}) %copy-start.2) | copy-done | bytes 131096
  43.4 4.0 %encode.1 = (bf16[2048,256]{1,0:T(8,128)(2,1)}, f32[64,1024]{1,0:T(8,128)S(1)}) custom-call(s32[1]{0:T(128)} %bitcast.me_ref, bf16[2304,256]{1,0:T(8,128)(2,1)S(1)} %bitcast.5, bf16[1024,256]{1,0:T(8,128)(2,1)S(1)} %copy-done, bf16[1024,256]{1,0:T(8,128)(2,1)S(1)} %copy-done.1, bf16[256,256]{1,0:T(8,128)(2,1)S(1)} %copy-done.2, ...), custom_call_target="tpu_custom_call" | custom-call | flops 1342177280 | bytes 2097152 | tf_op jit(solution)/shard_map/encode/pallas_call | solution.py:422
  47.4 0.0 collective-permute-done.4.refs_0_
  47.4 1.9 %collective-permute-start.5 = (bf16[128,384]{1,0:T(8,128)(2,1)S(1)}, bf16[128,384]{1,0:T(8,128)(2,1)S(1)}, u32[]{:S(2)}, u32[]{:S(2)}) collective-permute-start(bf16[128,384]{1,0:T(8,128)(2,1)S(1)} %get-tuple-element.35), channel_id=1, source_target_pairs={{0,4},{1,5},{2,6},{3,7},{4,0},{5,1},{6,2},{7,3},{8,12},{9,13},{10,... | collective-permute-start | bytes 294920 | tf_op jit(solution)/shard_map/ppermute | solution.py:329
  49.3 0.0 collective-permute-done.2.refs_0_
  49.4 2.1 %collective-permute-start.3 = (bf16[64,640]{1,0:T(8,128)(2,1)S(1)}, bf16[64,640]{1,0:T(8,128)(2,1)S(1)}, u32[]{:S(2)}, u32[]{:S(2)}) collective-permute-start(bf16[64,640]{1,0:T(8,128)(2,1)S(1)} %get-tuple-element.31), channel_id=1, source_target_pairs={{0,8},{1,9},{2,10},{3,11},{4,12},{5,13},{6,14},{7,15},{8,0},{9,1},... | collective-permute-start | bytes 245768 | tf_op jit(solution)/shard_map/ppermute | solution.py:329
  51.4 1.5 %collective-permute-done.5.refs_0_ = bf16[128,384]{1,0:T(8,128)(2,1)S(1)} collective-permute-done((bf16[128,384]{1,0:T(8,128)(2,1)S(1)}, bf16[128,384]{1,0:T(8,128)(2,1)S(1)}, u32[]{:S(2)}, u32[]{:S(2)}) %collective-permute-start.5) | collective-permute-done | bytes 98336 | tf_op jit(solution)/shard_map/ppermute | solution.py:329
  53.0 3.5 %collective-permute-start.6 = (bf16[64,384]{1,0:T(8,128)(2,1)S(1)}, bf16[64,384]{1,0:T(8,128)(2,1)S(1)}, u32[]{:S(2)}, u32[]{:S(2)}) collective-permute-start(bf16[64,384]{1,0:T(8,128)(2,1)S(1)} %get-tuple-element.37), channel_id=1, source_target_pairs={{0,8},{1,9},{2,10},{3,11},{4,12},{5,13},{6,14},{7,15},{8,0},{9,1},... | collective-permute-start | bytes 147464 | tf_op jit(solution)/shard_map/ppermute | solution.py:329
  56.5 0.3 collective-permute-done.3.refs_1_
  56.8 1.8 %collective-permute-done.6.refs_3_ = bf16[64,384]{1,0:T(8,128)(2,1)S(1)} collective-permute-done((bf16[64,384]{1,0:T(8,128)(2,1)S(1)}, bf16[64,384]{1,0:T(8,128)(2,1)S(1)}, u32[]{:S(2)}, u32[]{:S(2)}) %collective-permute-start.6) | collective-permute-done | bytes 49184 | tf_op jit(solution)/shard_map/ppermute | solution.py:329
  58.6 0.7 %finish.1 = f32[64,1024]{1,0:T(8,128)} custom-call(f32[64,1024]{1,0:T(8,128)S(1)} %get-tuple-element.28.refs_1_.between_ref, f32[64,640]{1,0:T(8,128)S(1)} %get-tuple-element.30.refs_0_, bf16[64,640]{1,0:T(8,128)(2,1)S(1)} %collective-permute-done.3.refs_1_, f32[64,384]{1,0:T(8,128)S(1)} %get-tuple-element.36.refs_2_, ...), custom_call_target="tpu_custom_call" | custom-call | flops 524288 | bytes 1048576 | tf_op jit(solution)/shard_map/finish/pallas_call | solution.py:317
  (3 shorter events, 0.1 us)
Async XLA Ops:
  7.9 7.4 %copy-start.3 = (f32[1,1024]{1,0:T(1,128)S(1)}, f32[1,1024]{1,0:T(1,128)}, u32[]{:S(2)}) copy-start(f32[1,1024]{1,0:T(1,128)} %get-tuple-element.21.mean_hbm) | copy-start | bytes 12292
  7.9 34.5 %all-to-all-start = ((bf16[16,144,256]{2,1,0:T(8,128)(2,1)}), bf16[16,144,256]{2,1,0:T(8,128)(2,1)S(1)}, u32[]{:S(2)}, u32[]{:S(2)}) async-start(bf16[16,144,256]{2,1,0:T(8,128)(2,1)} %bitcast.6), calls=%async_computation | async-start | bytes 2359296 | tf_op jit(solution)/shard_map/all_to_all | solution.py:453
  22.5 19.9 %copy-start = (bf16[1024,256]{1,0:T(8,128)(2,1)S(1)}, bf16[1024,256]{1,0:T(8,128)(2,1)}, u32[]{:S(2)}) copy-start(bf16[1024,256]{1,0:T(8,128)(2,1)} %basis_ref.1) | copy-start | bytes 1572868
  22.5 19.9 %copy-start.1 = (bf16[1024,256]{1,0:T(8,128)(2,1)S(1)}, bf16[1024,256]{1,0:T(8,128)(2,1)}, u32[]{:S(2)}) copy-start(bf16[1024,256]{1,0:T(8,128)(2,1)} %centroid_ref.1) | copy-start | bytes 1572868
  22.5 2.8 %collective-permute-start = (bf16[512,1024]{1,0:T(8,128)(2,1)S(1)}, bf16[512,1024]{1,0:T(8,128)(2,1)S(1)}, u32[]{:S(2)}, u32[]{:S(2)}) collective-permute-start(bf16[512,1024]{1,0:T(8,128)(2,1)S(1)} %get-tuple-element.23), channel_id=1, source_target_pairs={{0,1},{1,0},{2,3},{3,2},{4,5},{5,4},{6,7},{7,6},{8,9},{9,8},{10,11... | collective-permute-start | bytes 3145736 | tf_op jit(solution)/shard_map/ppermute | solution.py:329
  25.5 13.0 %collective-permute-start.1 = (bf16[256,640]{1,0:T(8,128)(2,1)S(1)}, bf16[256,640]{1,0:T(8,128)(2,1)S(1)}, u32[]{:S(2)}, u32[]{:S(2)}) collective-permute-start(bf16[256,640]{1,0:T(8,128)(2,1)S(1)} %get-tuple-element.25), channel_id=1, source_target_pairs={{0,2},{1,3},{2,0},{3,1},{4,6},{5,7},{6,4},{7,5},{8,10},{9,11},{10,... | collective-permute-start | bytes 983048 | tf_op jit(solution)/shard_map/ppermute | solution.py:329
  27.4 19.9 %collective-permute-start.4 = (bf16[256,384]{1,0:T(8,128)(2,1)S(1)}, bf16[256,384]{1,0:T(8,128)(2,1)S(1)}, u32[]{:S(2)}, u32[]{:S(2)}) collective-permute-start(bf16[256,384]{1,0:T(8,128)(2,1)S(1)} %get-tuple-element.33), channel_id=1, source_target_pairs={{0,2},{1,3},{2,0},{3,1},{4,6},{5,7},{6,4},{7,5},{8,10},{9,11},{10,... | collective-permute-start | bytes 589832 | tf_op jit(solution)/shard_map/ppermute | solution.py:329
  39.2 10.1 %collective-permute-start.2 = (bf16[128,640]{1,0:T(8,128)(2,1)}, bf16[128,640]{1,0:T(8,128)(2,1)S(1)}, u32[]{:S(2)}, u32[]{:S(2)}) collective-permute-start(bf16[128,640]{1,0:T(8,128)(2,1)} %get-tuple-element.26.refs_0_), channel_id=1, source_target_pairs={{0,4},{1,5},{2,6},{3,7},{4,0},{5,1},{6,2},{7,3},{8,12},{9,13},{10,... | collective-permute-start | bytes 491528 | tf_op jit(solution)/shard_map/ppermute | solution.py:329
  42.4 0.9 %copy-start.2 = (bf16[256,256]{1,0:T(8,128)(2,1)S(1)}, bf16[256,256]{1,0:T(8,128)(2,1)}, u32[]{:S(2)}) copy-start(bf16[256,256]{1,0:T(8,128)(2,1)} %rotation_ref.1) | copy-start | bytes 393220
  47.4 5.5 %collective-permute-start.5 = (bf16[128,384]{1,0:T(8,128)(2,1)S(1)}, bf16[128,384]{1,0:T(8,128)(2,1)S(1)}, u32[]{:S(2)}, u32[]{:S(2)}) collective-permute-start(bf16[128,384]{1,0:T(8,128)(2,1)S(1)} %get-tuple-element.35), channel_id=1, source_target_pairs={{0,4},{1,5},{2,6},{3,7},{4,0},{5,1},{6,2},{7,3},{8,12},{9,13},{10,... | collective-permute-start | bytes 294920 | tf_op jit(solution)/shard_map/ppermute | solution.py:329
  49.4 7.5 %collective-permute-start.3 = (bf16[64,640]{1,0:T(8,128)(2,1)S(1)}, bf16[64,640]{1,0:T(8,128)(2,1)S(1)}, u32[]{:S(2)}, u32[]{:S(2)}) collective-permute-start(bf16[64,640]{1,0:T(8,128)(2,1)S(1)} %get-tuple-element.31), channel_id=1, source_target_pairs={{0,8},{1,9},{2,10},{3,11},{4,12},{5,13},{6,14},{7,15},{8,0},{9,1},... | collective-permute-start | bytes 245768 | tf_op jit(solution)/shard_map/ppermute | solution.py:329
  53.0 5.6 %collective-permute-start.6 = (bf16[64,384]{1,0:T(8,128)(2,1)S(1)}, bf16[64,384]{1,0:T(8,128)(2,1)S(1)}, u32[]{:S(2)}, u32[]{:S(2)}) collective-permute-start(bf16[64,384]{1,0:T(8,128)(2,1)S(1)} %get-tuple-element.37), channel_id=1, source_target_pairs={{0,8},{1,9},{2,10},{3,11},{4,12},{5,13},{6,14},{7,15},{8,0},{9,1},... | collective-permute-start | bytes 147464 | tf_op jit(solution)/shard_map/ppermute | solution.py:329

commit v12 on v8

--- a/solution.py
+++ b/solution.py
@@ -296,30 +296,54 @@
     return [outs[h * pieces:(h + 1) * pieces] for h in range(shares)]
 
 
-def finish_kernel(total, between_ref, *refs):
-    out_ref = refs[-1]
-    each = (len(refs) - 1) // SHARES
-    columns = out_ref.shape[1] // SHARES
-    for h in range(SHARES):
-        across = slice(h * columns, (h + 1) * columns)
-        held = refs[h * each][...]
-        for ref in refs[h * each + 1:(h + 1) * each]:
-            held = held + ref[...].astype(jnp.float32)
-        out_ref[:, across] = (held + between_ref[:, across]) / total
-
-
-def finish(total, between, keeps, came):
-    parts = [part for keep, pieces in zip(keeps, came) for part in (keep, *pieces)]
+def gather_kernel(strides, me_ref, keep_ref, came_ref, out_ref):
+    pieces = 1 << len(strides)
+    size = out_ref.shape[0] // pieces
+    here = me_ref[0] // strides[0]
+    for p in range(pieces):
+        at = slice(p * size, (p + 1) * size)
+        there = here ^ sum(((p >> (len(strides) - 1 - k)) & 1) << k for k in range(len(strides)))
+        held = keep_ref[at] + came_ref[at].astype(jnp.float32)
+        out_ref[pl.ds(pl.multiple_of(there * size, size), size), :] = held.astype(jnp.bfloat16)
+
+
+def add_and_gather(strides, me, keep, came):
+    vmem = pl.BlockSpec(memory_space=pltpu.VMEM)
+    return pl.pallas_call(
+        functools.partial(gather_kernel, strides),
+        in_specs=[pl.BlockSpec(memory_space=pltpu.SMEM), vmem, vmem],
+        out_specs=vmem,
+        out_shape=jax.ShapeDtypeStruct(keep.shape, jnp.bfloat16),
+        compiler_params=pltpu.CompilerParams(vmem_limit_bytes=VMEM_SOME),
+        cost_estimate=pl.CostEstimate(flops=2 * keep.size, bytes_accessed=8 * keep.size, transcendentals=0),
+        name="add_and_gather",
+    )(me.reshape(1), keep, came)
+
+
+def finish_kernel(total, between_ref, first_ref, *refs):
+    *came, second_ref, out_ref = refs
+    rows, columns = first_ref.shape
+    held = first_ref[...]
+    for ref in came:
+        held = held + ref[...].astype(jnp.float32)
+    out_ref[:, :columns] = (held + between_ref[:, :columns]) / total
+    held = between_ref[:, columns:]
+    for p in range(second_ref.shape[0] // rows):
+        held = held + second_ref[p * rows:(p + 1) * rows, :].astype(jnp.float32)
+    out_ref[:, columns:] = held / total
+
+
+def finish(total, between, first, came, second):
     vmem = pl.BlockSpec(memory_space=pltpu.VMEM)
     return pl.pallas_call(
         functools.partial(finish_kernel, total),
-        in_specs=[vmem] * (1 + len(parts)),
+        in_specs=[vmem] * (3 + len(came)),
         out_specs=vmem,
         out_shape=jax.ShapeDtypeStruct(between.shape, jnp.float32),
         compiler_params=pltpu.CompilerParams(vmem_limit_bytes=VMEM_SOME),
         cost_estimate=pl.CostEstimate(flops=8 * between.size, bytes_accessed=16 * between.size, transcendentals=0),
         name="finish",
-    )(between, *parts)
+    )(between, first, *came, second)
 
 
 def halving_stages(width):
@@ -462,17 +486,25 @@
     stages = halving_stages(width)
     came = exchange(width, stages[0], [send])
     shares = add_and_split(keep, came, SHARES, 1 << len(stages[1]))
-    last = []
-    for share in shares:
-        for n in range(1, len(stages) - 1):
-            came = exchange(width, stages[n], share[1:])
-            (share,) = add_and_split(share[0], came, 1, 1 << len(stages[n + 1]))
-        last.append(share)
-    came = [exchange(width, stages[-1], share[1:]) for share in last]
+    first, second = shares
+    for n in range(1, len(stages) - 2):
+        came = exchange(width, stages[n], first[1:])
+        (first,) = add_and_split(first[0], came, 1, 2)
+        came = exchange(width, stages[n], second[1:])
+        (second,) = add_and_split(second[0], came, 1, 2)
+    came = exchange(width, stages[-2], first[1:])
+    (first,) = add_and_split(first[0], came, 1, 1 << len(stages[-1]))
+    came = exchange(width, stages[-1], first[1:])
+    (last,) = exchange(width, stages[-2], second[1:])
+    second = add_and_gather(stages[-1], me, second[0], last)
+    stride = stages[-1][0]
+    lines = [list(range(i, width, stride)) for i in range(stride)]
+    blocks = second.reshape(width // stride, second.shape[0] * stride // width, -1)
+    gathered = lax.all_to_all(blocks, "wide", split_axis=0, concat_axis=0, tiled=True, axis_index_groups=lines)
     encoded, between = encode(
-        width, total, me, got.reshape(width * SPAN, feats), basis, centroids, rotation, [share[1] for share in last]
+        width, total, me, got.reshape(width * SPAN, feats), basis, centroids, rotation, [first[1], second]
     )
-    covariance = finish(total, between, [share[0] for share in last], came)
+    covariance = finish(total, between, first[0], came, gathered.reshape(second.shape))
     return (encoded, covariance)
 
 

time: 57 us -> 66.1 us (1.16)
  waiting for transfers between devices: 14.8 us -> 23 us
    all_to_all x0 -> x1, starting transfers between devices: none -> 6.95 us  [local(): lax.all_to_all(blocks, 'wide', split_axis=0, concat_axis=0, tiled=True, a...]
    ppermute x9 -> x6, starting transfers between devices: 14.3 us -> 7.57 us  [exchange(): lax.ppermute(out[p - 1], 'wide', [(i, i ^ apart) for i in range(width)])]
    ppermute x9 -> x6, waiting for transfers between devices: 14.8 us -> 20.1 us  [exchange(): lax.ppermute(out[p - 1], 'wide', [(i, i ^ apart) for i in range(width)])]
    all_to_all x1, waiting for transfers between devices: 0.01 us -> 2.91 us  [local(): lax.all_to_all(rows.reshape(width, SPAN, feats), 'wide', split_axis=0, co...]
    pallas_call x0 -> x1, Pallas kernels: none -> 0.75 us  [add_and_gather(): pl.pallas_call(functools.partial(gather_kernel, strides), in_specs=[pl.Bl...]
  transfers between devices with their start and end apart: 10 -> 8, of which waited for: 4 -> 5; matrix products, arithmetic and copies ran while one was open for 0% -> 0% of each run, Pallas kernels for 20% -> 18%
where the time goes in v12:
time: 66.1 us; the launch traced here: 65.8 us
  waiting for transfers between devices  23 us (35%)
  starting transfers between devices  21.9 us (33%)
  Pallas kernels  20.1 us (30%)
  between operations  0.72 us (1%)
    ppermute x6, waiting for transfers between devices, exchange(): lax.ppermute(out[p - 1], 'wide', [(i, i ^ apart) for i in range(width)])  20.1 us
    ppermute x6, starting transfers between devices, exchange(): lax.ppermute(out[p - 1], 'wide', [(i, i ^ apart) for i in range(width)])  7.57 us
    all_to_all x1, starting transfers between devices, local(): lax.all_to_all(rows.reshape(width, SPAN, feats), 'wide', split_axis=0, co...  7.4 us
    pallas_call x1, Pallas kernels, project_and_sort(): pl.pallas_call(functools.partial(rows_kernel, width), grid=(rows_here //...  7.25 us
    pallas_call x1, Pallas kernels, moments(): pl.pallas_call(functools.partial(moments_kernel, width), in_specs=[pl.Blo...  7.16 us
    all_to_all x1, starting transfers between devices, local(): lax.all_to_all(blocks, 'wide', split_axis=0, concat_axis=0, tiled=True, a...  6.95 us
    pallas_call x1, Pallas kernels, encode(): pl.pallas_call(functools.partial(encode_kernel, total), in_specs=[pl.Bloc...  4 us
    all_to_all x1, waiting for transfers between devices, local(): lax.all_to_all(rows.reshape(width, SPAN, feats), 'wide', split_axis=0, co...  2.91 us
  transfers between devices with their start and end apart: 8, of which 5 were waited for; matrix products, arithmetic and copies ran while one was open for 0% of the time, Pallas kernels for 18%

profile of v12, /device:TPU:0, one launch (start us, length us, event | category | flops | bytes accessed | tf_op | source)
XLA Modules:
  0.0 65.8 jit_solution(18243899564196876324)
XLA Ops:
  0.6 7.2 %project_sort.1 = (bf16[2304,256]{1,0:T(8,128)(2,1)}, f32[1,1024]{1,0:T(1,128)}) custom-call(bf16[2048,1024]{1,0:T(8,128)(2,1)} %e_hbm.3, bf16[1024,256]{1,0:T(8,128)(2,1)} %basis_ref.1, s32[16,128]{1,0:T(8,128)} %bitcast.10, s32[16,128]{1,0:T(8,128)} %bitcast.11), custom_call_target="tpu_custom_call" | custom-call | flops 3489660928 | bytes 5373952 | tf_op jit(solution)/shard_map/project_sort/pallas_call | solution.py:162
  7.9 0.0 copy-start.3
  7.9 7.4 %all-to-all-start = ((bf16[16,144,256]{2,1,0:T(8,128)(2,1)}), bf16[16,144,256]{2,1,0:T(8,128)(2,1)S(1)}, u32[]{:S(2)}, u32[]{:S(2)}) async-start(bf16[16,144,256]{2,1,0:T(8,128)(2,1)} %bitcast.9), calls=%async_computation | async-start | bytes 2359296 | tf_op jit(solution)/shard_map/all_to_all | solution.py:483
  15.3 0.0 copy-done.3
  15.3 7.2 %moments.1 = (f32[512,1024]{1,0:T(8,128)S(1)}, bf16[512,1024]{1,0:T(8,128)(2,1)S(1)}) custom-call(s32[1]{0:T(128)} %bitcast.me_ref, f32[1,1024]{1,0:T(1,128)S(1)} %copy-done.3, bf16[2048,1024]{1,0:T(8,128)(2,1)} %e_hbm.3), custom_call_target="tpu_custom_call" | custom-call | flops 4294967296 | bytes 7340032 | tf_op jit(solution)/shard_map/moments/pallas_call | solution.py:244
  22.5 0.5 collective-permute-start
  23.0 2.3 %collective-permute-done.refs_0_ = bf16[512,1024]{1,0:T(8,128)(2,1)S(1)} collective-permute-done((bf16[512,1024]{1,0:T(8,128)(2,1)S(1)}, bf16[512,1024]{1,0:T(8,128)(2,1)S(1)}, u32[]{:S(2)}, u32[]{:S(2)}) %collective-permute-start) | collective-permute-done | bytes 1048608 | tf_op jit(solution)/shard_map/ppermute | solution.py:358
  25.2 0.0 copy-start
  25.2 0.0 copy-start.1
  25.2 0.0 copy-start.2
  25.2 0.2 add_and_split.2
  25.4 1.9 %collective-permute-start.2 = (bf16[256,512]{1,0:T(8,128)(2,1)S(1)}, bf16[256,512]{1,0:T(8,128)(2,1)S(1)}, u32[]{:S(2)}, u32[]{:S(2)}) collective-permute-start(bf16[256,512]{1,0:T(8,128)(2,1)S(1)} %get-tuple-element.24), channel_id=1, source_target_pairs={{0,2},{1,3},{2,0},{3,1},{4,6},{5,7},{6,4},{7,5},{8,10},{9,11},{10,... | collective-permute-start | bytes 786440 | tf_op jit(solution)/shard_map/ppermute | solution.py:358
  27.4 9.4 %collective-permute-done.2.came_ref = bf16[256,512]{1,0:T(8,128)(2,1)S(1)} collective-permute-done((bf16[256,512]{1,0:T(8,128)(2,1)S(1)}, bf16[256,512]{1,0:T(8,128)(2,1)S(1)}, u32[]{:S(2)}, u32[]{:S(2)}) %collective-permute-start.2) | collective-permute-done | bytes 262176 | tf_op jit(solution)/shard_map/ppermute | solution.py:358
  36.8 0.7 %add_and_gather.1.refs_1_ = bf16[256,512]{1,0:T(8,128)(2,1)} custom-call(s32[1]{0:T(128)} %bitcast.me_ref, f32[256,512]{1,0:T(8,128)S(1)} %get-tuple-element.23.keep_ref, bf16[256,512]{1,0:T(8,128)(2,1)S(1)} %collective-permute-done.2.came_ref), custom_call_target="tpu_custom_call" | custom-call | flops 262144 | bytes 1048576 | tf_op jit(solution)/shard_map/add_and_gather/pallas_call | solution.py:312
  37.5 2.9 %all-to-all-done = bf16[16,144,256]{2,1,0:T(8,128)(2,1)S(1)} async-done(((bf16[16,144,256]{2,1,0:T(8,128)(2,1)}), bf16[16,144,256]{2,1,0:T(8,128)(2,1)S(1)}, u32[]{:S(2)}, u32[]{:S(2)}) %all-to-all-start) | async-done | bytes 1179680 | tf_op jit(solution)/shard_map/all_to_all | solution.py:483
  40.4 7.0 %all-to-all-start.1 = ((bf16[4,64,512]{2,1,0:T(8,128)(2,1)}), bf16[4,64,512]{2,1,0:T(8,128)(2,1)S(1)}, u32[]{:S(2)}, u32[]{:S(2)}) async-start(bf16[4,64,512]{2,1,0:T(8,128)(2,1)} %bitcast.5), calls=%async_computation.1 | async-start | bytes 524288 | tf_op jit(solution)/shard_map/all_to_all | solution.py:503
  47.4 1.0 %collective-permute-start.1 = (bf16[256,512]{1,0:T(8,128)(2,1)S(1)}, bf16[256,512]{1,0:T(8,128)(2,1)S(1)}, u32[]{:S(2)}, u32[]{:S(2)}) collective-permute-start(bf16[256,512]{1,0:T(8,128)(2,1)S(1)} %get-tuple-element.21), channel_id=1, source_target_pairs={{0,2},{1,3},{2,0},{3,1},{4,6},{5,7},{6,4},{7,5},{8,10},{9,11},{10,... | collective-permute-start | bytes 786440 | tf_op jit(solution)/shard_map/ppermute | solution.py:358
  48.4 6.6 %collective-permute-done.1.refs_0_ = bf16[256,512]{1,0:T(8,128)(2,1)S(1)} collective-permute-done((bf16[256,512]{1,0:T(8,128)(2,1)S(1)}, bf16[256,512]{1,0:T(8,128)(2,1)S(1)}, u32[]{:S(2)}, u32[]{:S(2)}) %collective-permute-start.1) | collective-permute-done | bytes 262176 | tf_op jit(solution)/shard_map/ppermute | solution.py:358
  55.0 1.8 %collective-permute-start.4 = (bf16[64,512]{1,0:T(8,128)(2,1)S(1)}, bf16[64,512]{1,0:T(8,128)(2,1)S(1)}, u32[]{:S(2)}, u32[]{:S(2)}) collective-permute-start(bf16[64,512]{1,0:T(8,128)(2,1)S(1)} %get-tuple-element.28), channel_id=1, source_target_pairs={{0,4},{1,5},{2,6},{3,7},{4,0},{5,1},{6,2},{7,3},{8,12},{9,13},{10,... | collective-permute-start | bytes 196616 | tf_op jit(solution)/shard_map/ppermute | solution.py:358
  56.8 2.4 %collective-permute-start.5 = (bf16[64,512]{1,0:T(8,128)(2,1)S(1)}, bf16[64,512]{1,0:T(8,128)(2,1)S(1)}, u32[]{:S(2)}, u32[]{:S(2)}) collective-permute-start(bf16[64,512]{1,0:T(8,128)(2,1)S(1)} %get-tuple-element.29), channel_id=1, source_target_pairs={{0,12},{1,13},{2,14},{3,15},{4,8},{5,9},{6,10},{7,11},{8,4},{9,5},... | collective-permute-start | bytes 196616 | tf_op jit(solution)/shard_map/ppermute | solution.py:358
  59.2 0.0 collective-permute-start.3
  59.2 0.0 copy-done
  59.2 0.0 copy-done.1
  59.2 0.0 copy-done.2
  59.2 4.0 %encode.1 = (bf16[2048,256]{1,0:T(8,128)(2,1)}, f32[64,1024]{1,0:T(8,128)S(1)}) custom-call(s32[1]{0:T(128)} %bitcast.me_ref, bf16[2304,256]{1,0:T(8,128)(2,1)S(1)} %bitcast.7, bf16[1024,256]{1,0:T(8,128)(2,1)S(1)} %copy-done, bf16[1024,256]{1,0:T(8,128)(2,1)S(1)} %copy-done.1, bf16[256,256]{1,0:T(8,128)(2,1)S(1)} %copy-done.2, ...), custom_call_target="tpu_custom_call" | custom-call | flops 1342177280 | bytes 2097152 | tf_op jit(solution)/shard_map/encode/pallas_call | solution.py:452
  63.2 0.0 collective-permute-done.4.refs_1_
  63.2 0.0 collective-permute-done.5.refs_2_
  63.2 1.8 %collective-permute-done.3.refs_0_ = bf16[64,512]{1,0:T(8,128)(2,1)S(1)} collective-permute-done((bf16[64,512]{1,0:T(8,128)(2,1)S(1)}, bf16[64,512]{1,0:T(8,128)(2,1)S(1)}, u32[]{:S(2)}, u32[]{:S(2)}) %collective-permute-start.3) | collective-permute-done | bytes 65568 | tf_op jit(solution)/shard_map/ppermute | solution.py:358
  65.0 0.0 all-to-all-done.1
  65.0 0.8 %finish.1 = f32[64,1024]{1,0:T(8,128)} custom-call(f32[64,1024]{1,0:T(8,128)S(1)} %get-tuple-element.26.between_ref, f32[64,512]{1,0:T(8,128)S(1)} %get-tuple-element.27.first_ref, bf16[64,512]{1,0:T(8,128)(2,1)S(1)} %collective-permute-done.3.refs_0_, bf16[64,512]{1,0:T(8,128)(2,1)S(1)} %collective-permute-done.4.refs_1_, ...), custom_call_target="tpu_custom_call" | custom-call | flops 524288 | bytes 1048576 | tf_op jit(solution)/shard_map/finish/pallas_call | solution.py:338
  (1 shorter events, 0.0 us)
Async XLA Ops:
  7.9 7.4 %copy-start.3 = (f32[1,1024]{1,0:T(1,128)S(1)}, f32[1,1024]{1,0:T(1,128)}, u32[]{:S(2)}) copy-start(f32[1,1024]{1,0:T(1,128)} %get-tuple-element.17.mean_hbm) | copy-start | bytes 12292
  7.9 32.5 %all-to-all-start = ((bf16[16,144,256]{2,1,0:T(8,128)(2,1)}), bf16[16,144,256]{2,1,0:T(8,128)(2,1)S(1)}, u32[]{:S(2)}, u32[]{:S(2)}) async-start(bf16[16,144,256]{2,1,0:T(8,128)(2,1)} %bitcast.9), calls=%async_computation | async-start | bytes 2359296 | tf_op jit(solution)/shard_map/all_to_all | solution.py:483
  22.5 2.8 %collective-permute-start = (bf16[512,1024]{1,0:T(8,128)(2,1)S(1)}, bf16[512,1024]{1,0:T(8,128)(2,1)S(1)}, u32[]{:S(2)}, u32[]{:S(2)}) collective-permute-start(bf16[512,1024]{1,0:T(8,128)(2,1)S(1)} %get-tuple-element.19), channel_id=1, source_target_pairs={{0,1},{1,0},{2,3},{3,2},{4,5},{5,4},{6,7},{7,6},{8,9},{9,8},{10,11... | collective-permute-start | bytes 3145736 | tf_op jit(solution)/shard_map/ppermute | solution.py:358
  25.2 33.9 %copy-start = (bf16[1024,256]{1,0:T(8,128)(2,1)S(1)}, bf16[1024,256]{1,0:T(8,128)(2,1)}, u32[]{:S(2)}) copy-start(bf16[1024,256]{1,0:T(8,128)(2,1)} %basis_ref.1) | copy-start | bytes 1572868
  25.2 33.9 %copy-start.1 = (bf16[1024,256]{1,0:T(8,128)(2,1)S(1)}, bf16[1024,256]{1,0:T(8,128)(2,1)}, u32[]{:S(2)}) copy-start(bf16[1024,256]{1,0:T(8,128)(2,1)} %centroid_ref.1) | copy-start | bytes 1572868
  25.2 33.9 %copy-start.2 = (bf16[256,256]{1,0:T(8,128)(2,1)S(1)}, bf16[256,256]{1,0:T(8,128)(2,1)}, u32[]{:S(2)}) copy-start(bf16[256,256]{1,0:T(8,128)(2,1)} %rotation_ref.1) | copy-start | bytes 393220
  25.4 11.4 %collective-permute-start.2 = (bf16[256,512]{1,0:T(8,128)(2,1)S(1)}, bf16[256,512]{1,0:T(8,128)(2,1)S(1)}, u32[]{:S(2)}, u32[]{:S(2)}) collective-permute-start(bf16[256,512]{1,0:T(8,128)(2,1)S(1)} %get-tuple-element.24), channel_id=1, source_target_pairs={{0,2},{1,3},{2,0},{3,1},{4,6},{5,7},{6,4},{7,5},{8,10},{9,11},{10,... | collective-permute-start | bytes 786440 | tf_op jit(solution)/shard_map/ppermute | solution.py:358
  40.4 24.6 %all-to-all-start.1 = ((bf16[4,64,512]{2,1,0:T(8,128)(2,1)}), bf16[4,64,512]{2,1,0:T(8,128)(2,1)S(1)}, u32[]{:S(2)}, u32[]{:S(2)}) async-start(bf16[4,64,512]{2,1,0:T(8,128)(2,1)} %bitcast.5), calls=%async_computation.1 | async-start | bytes 524288 | tf_op jit(solution)/shard_map/all_to_all | solution.py:503
  47.4 7.6 %collective-permute-start.1 = (bf16[256,512]{1,0:T(8,128)(2,1)S(1)}, bf16[256,512]{1,0:T(8,128)(2,1)S(1)}, u32[]{:S(2)}, u32[]{:S(2)}) collective-permute-start(bf16[256,512]{1,0:T(8,128)(2,1)S(1)} %get-tuple-element.21), channel_id=1, source_target_pairs={{0,2},{1,3},{2,0},{3,1},{4,6},{5,7},{6,4},{7,5},{8,10},{9,11},{10,... | collective-permute-start | bytes 786440 | tf_op jit(solution)/shard_map/ppermute | solution.py:358
  55.0 8.2 %collective-permute-start.4 = (bf16[64,512]{1,0:T(8,128)(2,1)S(1)}, bf16[64,512]{1,0:T(8,128)(2,1)S(1)}, u32[]{:S(2)}, u32[]{:S(2)}) collective-permute-start(bf16[64,512]{1,0:T(8,128)(2,1)S(1)} %get-tuple-element.28), channel_id=1, source_target_pairs={{0,4},{1,5},{2,6},{3,7},{4,0},{5,1},{6,2},{7,3},{8,12},{9,13},{10,... | collective-permute-start | bytes 196616 | tf_op jit(solution)/shard_map/ppermute | solution.py:358
  56.8 6.4 %collective-permute-start.5 = (bf16[64,512]{1,0:T(8,128)(2,1)S(1)}, bf16[64,512]{1,0:T(8,128)(2,1)S(1)}, u32[]{:S(2)}, u32[]{:S(2)}) collective-permute-start(bf16[64,512]{1,0:T(8,128)(2,1)S(1)} %get-tuple-element.29), channel_id=1, source_target_pairs={{0,12},{1,13},{2,14},{3,15},{4,8},{5,9},{6,10},{7,11},{8,4},{9,5},... | collective-permute-start | bytes 196616 | tf_op jit(solution)/shard_map/ppermute | solution.py:358
  59.2 5.9 %collective-permute-start.3 = (bf16[64,512]{1,0:T(8,128)(2,1)S(1)}, bf16[64,512]{1,0:T(8,128)(2,1)S(1)}, u32[]{:S(2)}, u32[]{:S(2)}) collective-permute-start(bf16[64,512]{1,0:T(8,128)(2,1)S(1)} %get-tuple-element.22.refs_0_), channel_id=1, source_target_pairs={{0,8},{1,9},{2,10},{3,11},{4,12},{5,13},{6,14},{7,15},{8,0},{9,1},... | collective-permute-start | bytes 196616 | tf_op jit(solution)/shard_map/ppermute | solution.py:358

commit v13 on v8

--- a/solution.py
+++ b/solution.py
@@ -12,8 +12,8 @@
 NOTES = 16
 SPAN = CAP + NOTES
 CHUNK = 512
-TILE = 256
-GROUP = 4
+TILE = 512
+GROUP = 8
 SHARES = 2
 VMEM_ALL = 60 * 1024 * 1024
 VMEM_SOME = 24 * 1024 * 1024
@@ -264,9 +264,9 @@
     )(me.reshape(1), mean, embeddings)
 
 
-def add_kernel(shares, pieces, keep_ref, *refs):
+def add_kernel(shares, pieces, arrived, keep_ref, *refs):
     outs = refs[len(refs) - shares * pieces:]
-    came = refs[:len(refs) - shares * pieces]
+    came = refs[:arrived]
     rows, columns = outs[0].shape
     for h in range(shares):
         across = slice(h * columns, (h + 1) * columns)
@@ -279,20 +279,20 @@
             out[...] = held.astype(out.dtype)
 
 
-def add_and_split(keep, came, shares, pieces):
+def add_and_split(keep, came, shares, pieces, after=()):
     rows, columns = keep.shape
     vmem = pl.BlockSpec(memory_space=pltpu.VMEM)
     shape = (rows // pieces, columns // shares)
     kinds = [jnp.float32] + [jnp.bfloat16] * (pieces - 1)
     outs = pl.pallas_call(
-        functools.partial(add_kernel, shares, pieces),
-        in_specs=[vmem] * (1 + len(came)),
+        functools.partial(add_kernel, shares, pieces, len(came)),
+        in_specs=[vmem] * (1 + len(came)) + [pl.BlockSpec(memory_space=pl.ANY)] * len(after),
         out_specs=[vmem] * (shares * pieces),
         out_shape=[jax.ShapeDtypeStruct(shape, kind) for kind in kinds * shares],
         compiler_params=pltpu.CompilerParams(vmem_limit_bytes=VMEM_SOME),
         cost_estimate=pl.CostEstimate(flops=2 * rows * columns, bytes_accessed=10 * rows * columns, transcendentals=0),
         name="add_and_split",
-    )(keep, *came)
+    )(keep, *came, *after)
     return [outs[h * pieces:(h + 1) * pieces] for h in range(shares)]
 
 
@@ -462,17 +462,19 @@
     stages = halving_stages(width)
     came = exchange(width, stages[0], [send])
     shares = add_and_split(keep, came, SHARES, 1 << len(stages[1]))
-    last = []
+    keeps, ends, after = [], [], []
     for share in shares:
         for n in range(1, len(stages) - 1):
             came = exchange(width, stages[n], share[1:])
-            (share,) = add_and_split(share[0], came, 1, 1 << len(stages[n + 1]))
-        last.append(share)
-    came = [exchange(width, stages[-1], share[1:]) for share in last]
-    encoded, between = encode(
-        width, total, me, got.reshape(width * SPAN, feats), basis, centroids, rotation, [share[1] for share in last]
-    )
-    covariance = finish(total, between, [share[0] for share in last], came)
+            (share,) = add_and_split(share[0], came, 1, 1 << len(stages[n + 1]), after if n == 1 else [])
+        keeps.append(share[0])
+        ends.append(exchange(width, stages[-1], share[1:]))
+        if not after:
+            encoded, between = encode(
+                width, total, me, got.reshape(width * SPAN, feats), basis, centroids, rotation, [share[1]]
+            )
+            after = [between, *ends[0]]
+    covariance = finish(total, between, keeps, ends)
     return (encoded, covariance)
 
 

time: 57 us -> 59.9 us (1.051)
  waiting for transfers between devices: 14.8 us -> 17.9 us
  starting transfers between devices: 21.7 us -> 20.5 us
  Pallas kernels: 19.5 us -> 20.4 us
    ppermute x9, waiting for transfers between devices: 14.8 us -> 17.9 us  [exchange(): lax.ppermute(out[p - 1], 'wide', [(i, i ^ apart) for i in range(width)])]
    pallas_call x3, Pallas kernels: 0.26 us -> 1.57 us  [add_and_split(): pl.pallas_call(functools.partial(add_kernel, shares, pieces, len(came)),...]
    ppermute x9, starting transfers between devices: 14.3 us -> 13.1 us  [exchange(): lax.ppermute(out[p - 1], 'wide', [(i, i ^ apart) for i in range(width)])]
  transfers between devices with their start and end apart: 10 -> 10, of which waited for: 4 -> 7; matrix products, arithmetic and copies ran while one was open for 0% -> 0% of each run, Pallas kernels for 20% -> 20%
where the time goes in v13:
time: 59.9 us; the launch traced here: 59.6 us
  starting transfers between devices  20.5 us (34%)
  Pallas kernels  20.4 us (34%)
  waiting for transfers between devices  17.9 us (30%)
  between operations  0.75 us (1%)
    ppermute x9, waiting for transfers between devices, exchange(): lax.ppermute(out[p - 1], 'wide', [(i, i ^ apart) for i in range(width)])  17.9 us
    ppermute x9, starting transfers between devices, exchange(): lax.ppermute(out[p - 1], 'wide', [(i, i ^ apart) for i in range(width)])  13.1 us
    pallas_call x1, Pallas kernels, project_and_sort(): pl.pallas_call(functools.partial(rows_kernel, width), grid=(rows_here //...  7.41 us
    all_to_all x1, starting transfers between devices, local(): lax.all_to_all(rows.reshape(width, SPAN, feats), 'wide', split_axis=0, co...  7.4 us
    pallas_call x1, Pallas kernels, moments(): pl.pallas_call(functools.partial(moments_kernel, width), in_specs=[pl.Blo...  6.91 us
    pallas_call x1, Pallas kernels, encode(): pl.pallas_call(functools.partial(encode_kernel, total), in_specs=[pl.Bloc...  3.77 us
    pallas_call x3, Pallas kernels, add_and_split(): pl.pallas_call(functools.partial(add_kernel, shares, pieces, len(came)),...  1.57 us
  transfers between devices with their start and end apart: 10, of which 7 were waited for; matrix products, arithmetic and copies ran while one was open for 0% of the time, Pallas kernels for 20%

profile of v13, /device:TPU:0, one launch (start us, length us, event | category | flops | bytes accessed | tf_op | source)
XLA Modules:
  0.0 59.6 jit_solution(8460564375007567348)
XLA Ops:
  0.6 7.4 %project_sort.1 = (bf16[2304,256]{1,0:T(8,128)(2,1)}, f32[1,1024]{1,0:T(1,128)}) custom-call(bf16[2048,1024]{1,0:T(8,128)(2,1)} %e_hbm.3, bf16[1024,256]{1,0:T(8,128)(2,1)} %basis_ref.1, s32[16,128]{1,0:T(8,128)} %bitcast.7, s32[16,128]{1,0:T(8,128)} %bitcast.8), custom_call_target="tpu_custom_call" | custom-call | flops 3489660928 | bytes 5373952 | tf_op jit(solution)/shard_map/project_sort/pallas_call | solution.py:162
  8.1 0.0 copy-start.3
  8.1 7.4 %all-to-all-start = ((bf16[16,144,256]{2,1,0:T(8,128)(2,1)}), bf16[16,144,256]{2,1,0:T(8,128)(2,1)S(1)}, u32[]{:S(2)}, u32[]{:S(2)}) async-start(bf16[16,144,256]{2,1,0:T(8,128)(2,1)} %bitcast.6), calls=%async_computation | async-start | bytes 2359296 | tf_op jit(solution)/shard_map/all_to_all | solution.py:459
  15.5 6.9 %moments.1 = (f32[512,1024]{1,0:T(8,128)S(1)}, bf16[512,1024]{1,0:T(8,128)(2,1)S(1)}) custom-call(s32[1]{0:T(128)} %bitcast.me_ref, f32[1,1024]{1,0:T(1,128)S(1)} %copy-done.3, bf16[2048,1024]{1,0:T(8,128)(2,1)} %e_hbm.3), custom_call_target="tpu_custom_call" | custom-call | flops 4294967296 | bytes 7340032 | tf_op jit(solution)/shard_map/moments/pallas_call | solution.py:244
  22.4 0.0 copy-start
  22.4 0.0 copy-start.1
  22.4 0.0 copy-start.2
  22.4 0.5 collective-permute-start
  22.9 2.3 %collective-permute-done.refs_0_ = bf16[512,1024]{1,0:T(8,128)(2,1)S(1)} collective-permute-done((bf16[512,1024]{1,0:T(8,128)(2,1)S(1)}, bf16[512,1024]{1,0:T(8,128)(2,1)S(1)}, u32[]{:S(2)}, u32[]{:S(2)}) %collective-permute-start) | collective-permute-done | bytes 1048608 | tf_op jit(solution)/shard_map/ppermute | solution.py:334
  25.2 0.8 %add_and_split.3 = (f32[256,512]{1,0:T(8,128)S(1)}, bf16[256,512]{1,0:T(8,128)(2,1)S(1)}, f32[256,512]{1,0:T(8,128)S(1)}, bf16[256,512]{1,0:T(8,128)(2,1)}) custom-call(f32[512,1024]{1,0:T(8,128)S(1)} %get-tuple-element.22.keep_ref, bf16[512,1024]{1,0:T(8,128)(2,1)S(1)} %collective-permute-done.refs_0_), custom_call_target="tpu_custom_call" | custom-call | flops 1048576 | bytes 5242880 | tf_op jit(solution)/shard_map/add_and_split/pallas_call | solution.py:287
  26.1 1.9 %collective-permute-start.1 = (bf16[256,512]{1,0:T(8,128)(2,1)S(1)}, bf16[256,512]{1,0:T(8,128)(2,1)S(1)}, u32[]{:S(2)}, u32[]{:S(2)}) collective-permute-start(bf16[256,512]{1,0:T(8,128)(2,1)S(1)} %get-tuple-element.25), channel_id=1, source_target_pairs={{0,2},{1,3},{2,0},{3,1},{4,6},{5,7},{6,4},{7,5},{8,10},{9,11},{10,... | collective-permute-start | bytes 786440 | tf_op jit(solution)/shard_map/ppermute | solution.py:334
  27.9 0.1 collective-permute-start.5
  28.1 9.4 %collective-permute-done.1.refs_0_ = bf16[256,512]{1,0:T(8,128)(2,1)S(1)} collective-permute-done((bf16[256,512]{1,0:T(8,128)(2,1)S(1)}, bf16[256,512]{1,0:T(8,128)(2,1)S(1)}, u32[]{:S(2)}, u32[]{:S(2)}) %collective-permute-start.1) | collective-permute-done | bytes 262176 | tf_op jit(solution)/shard_map/ppermute | solution.py:334
  37.5 0.7 %add_and_split.4 = (f32[64,512]{1,0:T(8,128)S(1)}, bf16[64,512]{1,0:T(8,128)(2,1)S(1)}, bf16[64,512]{1,0:T(8,128)(2,1)}, bf16[64,512]{1,0:T(8,128)(2,1)}) custom-call(f32[256,512]{1,0:T(8,128)S(1)} %get-tuple-element.24.keep_ref, bf16[256,512]{1,0:T(8,128)(2,1)S(1)} %collective-permute-done.1.refs_0_), custom_call_target="tpu_custom_call" | custom-call | flops 262144 | bytes 1310720 | tf_op jit(solution)/shard_map/add_and_split/pallas_call | solution.py:287
  38.2 3.4 %collective-permute-start.3 = (bf16[64,512]{1,0:T(8,128)(2,1)}, bf16[64,512]{1,0:T(8,128)(2,1)S(1)}, u32[]{:S(2)}, u32[]{:S(2)}) collective-permute-start(bf16[64,512]{1,0:T(8,128)(2,1)} %get-tuple-element.30), channel_id=1, source_target_pairs={{0,4},{1,5},{2,6},{3,7},{4,0},{5,1},{6,2},{7,3},{8,12},{9,13},{10,... | collective-permute-start | bytes 196616 | tf_op jit(solution)/shard_map/ppermute | solution.py:334
  41.5 2.8 %collective-permute-start.4 = (bf16[64,512]{1,0:T(8,128)(2,1)}, bf16[64,512]{1,0:T(8,128)(2,1)S(1)}, u32[]{:S(2)}, u32[]{:S(2)}) collective-permute-start(bf16[64,512]{1,0:T(8,128)(2,1)} %get-tuple-element.31), channel_id=1, source_target_pairs={{0,12},{1,13},{2,14},{3,15},{4,8},{5,9},{6,10},{7,11},{8,4},{9,5},... | collective-permute-start | bytes 196616 | tf_op jit(solution)/shard_map/ppermute | solution.py:334
  44.3 0.0 collective-permute-start.2
  44.3 0.0 all-to-all-done
  44.3 0.0 copy-done.1
  44.3 0.0 copy-done.2
  44.3 3.8 %encode.1 = (bf16[2048,256]{1,0:T(8,128)(2,1)}, f32[64,1024]{1,0:T(8,128)S(1)}) custom-call(s32[1]{0:T(128)} %bitcast.me_ref, bf16[2304,256]{1,0:T(8,128)(2,1)S(1)} %bitcast.5, bf16[1024,256]{1,0:T(8,128)(2,1)S(1)} %copy-done, bf16[1024,256]{1,0:T(8,128)(2,1)S(1)} %copy-done.1, bf16[256,256]{1,0:T(8,128)(2,1)S(1)} %copy-done.2, ...), custom_call_target="tpu_custom_call" | custom-call | flops 1342177280 | bytes 2097152 | tf_op jit(solution)/shard_map/encode/pallas_call | solution.py:428
  48.1 0.0 collective-permute-done.5.refs_0_
  48.1 0.0 collective-permute-done.3.refs_3_.refs_2_
  48.1 0.2 collective-permute-done.4.refs_4_.refs_3_
  48.3 2.2 %collective-permute-done.2.refs_2_.refs_1_ = bf16[64,512]{1,0:T(8,128)(2,1)S(1)} collective-permute-done((bf16[64,512]{1,0:T(8,128)(2,1)S(1)}, bf16[64,512]{1,0:T(8,128)(2,1)S(1)}, u32[]{:S(2)}, u32[]{:S(2)}) %collective-permute-start.2) | collective-permute-done | bytes 65568 | tf_op jit(solution)/shard_map/ppermute | solution.py:334
  50.5 0.7 %collective-permute-start.6 = (bf16[64,512]{1,0:T(8,128)(2,1)S(1)}, bf16[64,512]{1,0:T(8,128)(2,1)S(1)}, u32[]{:S(2)}, u32[]{:S(2)}) collective-permute-start(bf16[64,512]{1,0:T(8,128)(2,1)S(1)} %get-tuple-element.35), channel_id=1, source_target_pairs={{0,8},{1,9},{2,10},{3,11},{4,12},{5,13},{6,14},{7,15},{8,0},{9,1},... | collective-permute-start | bytes 196616 | tf_op jit(solution)/shard_map/ppermute | solution.py:334
  51.2 1.6 %collective-permute-start.7 = (bf16[64,512]{1,0:T(8,128)(2,1)S(1)}, bf16[64,512]{1,0:T(8,128)(2,1)S(1)}, u32[]{:S(2)}, u32[]{:S(2)}) collective-permute-start(bf16[64,512]{1,0:T(8,128)(2,1)S(1)} %get-tuple-element.36), channel_id=1, source_target_pairs={{0,4},{1,5},{2,6},{3,7},{4,0},{5,1},{6,2},{7,3},{8,12},{9,13},{10,... | collective-permute-start | bytes 196616 | tf_op jit(solution)/shard_map/ppermute | solution.py:334
  52.8 2.2 %collective-permute-start.8 = (bf16[64,512]{1,0:T(8,128)(2,1)S(1)}, bf16[64,512]{1,0:T(8,128)(2,1)S(1)}, u32[]{:S(2)}, u32[]{:S(2)}) collective-permute-start(bf16[64,512]{1,0:T(8,128)(2,1)S(1)} %get-tuple-element.37), channel_id=1, source_target_pairs={{0,12},{1,13},{2,14},{3,15},{4,8},{5,9},{6,10},{7,11},{8,4},{9,5},... | collective-permute-start | bytes 196616 | tf_op jit(solution)/shard_map/ppermute | solution.py:334
  55.0 2.2 %collective-permute-done.6.refs_5_ = bf16[64,512]{1,0:T(8,128)(2,1)S(1)} collective-permute-done((bf16[64,512]{1,0:T(8,128)(2,1)S(1)}, bf16[64,512]{1,0:T(8,128)(2,1)S(1)}, u32[]{:S(2)}, u32[]{:S(2)}) %collective-permute-start.6) | collective-permute-done | bytes 65568 | tf_op jit(solution)/shard_map/ppermute | solution.py:334
  57.2 0.2 collective-permute-done.7.refs_6_
  57.4 1.5 %collective-permute-done.8.refs_7_ = bf16[64,512]{1,0:T(8,128)(2,1)S(1)} collective-permute-done((bf16[64,512]{1,0:T(8,128)(2,1)S(1)}, bf16[64,512]{1,0:T(8,128)(2,1)S(1)}, u32[]{:S(2)}, u32[]{:S(2)}) %collective-permute-start.8) | collective-permute-done | bytes 65568 | tf_op jit(solution)/shard_map/ppermute | solution.py:334
  58.9 0.8 %finish.1 = f32[64,1024]{1,0:T(8,128)} custom-call(f32[64,1024]{1,0:T(8,128)S(1)} %get-tuple-element.28.refs_1_.between_ref, f32[64,512]{1,0:T(8,128)S(1)} %get-tuple-element.29.refs_0_, bf16[64,512]{1,0:T(8,128)(2,1)S(1)} %collective-permute-done.2.refs_2_.refs_1_, bf16[64,512]{1,0:T(8,128)(2,1)S(1)} %collective-permute-done.3.refs_3_.refs_2_, ...), custom_call_target="tpu_custom_call" | custom-call | flops 524288 | bytes 1048576 | tf_op jit(solution)/shard_map/finish/pallas_call | solution.py:314
  (3 shorter events, 0.1 us)
Async XLA Ops:
  8.1 7.4 %copy-start.3 = (f32[1,1024]{1,0:T(1,128)S(1)}, f32[1,1024]{1,0:T(1,128)}, u32[]{:S(2)}) copy-start(f32[1,1024]{1,0:T(1,128)} %get-tuple-element.21.mean_hbm) | copy-start | bytes 12292
  8.1 36.2 %all-to-all-start = ((bf16[16,144,256]{2,1,0:T(8,128)(2,1)}), bf16[16,144,256]{2,1,0:T(8,128)(2,1)S(1)}, u32[]{:S(2)}, u32[]{:S(2)}) async-start(bf16[16,144,256]{2,1,0:T(8,128)(2,1)} %bitcast.6), calls=%async_computation | async-start | bytes 2359296 | tf_op jit(solution)/shard_map/all_to_all | solution.py:459
  22.4 21.9 %copy-start = (bf16[1024,256]{1,0:T(8,128)(2,1)S(1)}, bf16[1024,256]{1,0:T(8,128)(2,1)}, u32[]{:S(2)}) copy-start(bf16[1024,256]{1,0:T(8,128)(2,1)} %basis_ref.1) | copy-start | bytes 1572868
  22.4 21.9 %copy-start.1 = (bf16[1024,256]{1,0:T(8,128)(2,1)S(1)}, bf16[1024,256]{1,0:T(8,128)(2,1)}, u32[]{:S(2)}) copy-start(bf16[1024,256]{1,0:T(8,128)(2,1)} %centroid_ref.1) | copy-start | bytes 1572868
  22.4 21.9 %copy-start.2 = (bf16[256,256]{1,0:T(8,128)(2,1)S(1)}, bf16[256,256]{1,0:T(8,128)(2,1)}, u32[]{:S(2)}) copy-start(bf16[256,256]{1,0:T(8,128)(2,1)} %rotation_ref.1) | copy-start | bytes 393220
  22.4 2.8 %collective-permute-start = (bf16[512,1024]{1,0:T(8,128)(2,1)S(1)}, bf16[512,1024]{1,0:T(8,128)(2,1)S(1)}, u32[]{:S(2)}, u32[]{:S(2)}) collective-permute-start(bf16[512,1024]{1,0:T(8,128)(2,1)S(1)} %get-tuple-element.23), channel_id=1, source_target_pairs={{0,1},{1,0},{2,3},{3,2},{4,5},{5,4},{6,7},{7,6},{8,9},{9,8},{10,11... | collective-permute-start | bytes 3145736 | tf_op jit(solution)/shard_map/ppermute | solution.py:334
  26.1 11.4 %collective-permute-start.1 = (bf16[256,512]{1,0:T(8,128)(2,1)S(1)}, bf16[256,512]{1,0:T(8,128)(2,1)S(1)}, u32[]{:S(2)}, u32[]{:S(2)}) collective-permute-start(bf16[256,512]{1,0:T(8,128)(2,1)S(1)} %get-tuple-element.25), channel_id=1, source_target_pairs={{0,2},{1,3},{2,0},{3,1},{4,6},{5,7},{6,4},{7,5},{8,10},{9,11},{10,... | collective-permute-start | bytes 786440 | tf_op jit(solution)/shard_map/ppermute | solution.py:334
  27.9 20.2 %collective-permute-start.5 = (bf16[256,512]{1,0:T(8,128)(2,1)}, bf16[256,512]{1,0:T(8,128)(2,1)S(1)}, u32[]{:S(2)}, u32[]{:S(2)}) collective-permute-start(bf16[256,512]{1,0:T(8,128)(2,1)} %get-tuple-element.33), channel_id=1, source_target_pairs={{0,2},{1,3},{2,0},{3,1},{4,6},{5,7},{6,4},{7,5},{8,10},{9,11},{10,... | collective-permute-start | bytes 786440 | tf_op jit(solution)/shard_map/ppermute | solution.py:334
  38.2 10.0 %collective-permute-start.3 = (bf16[64,512]{1,0:T(8,128)(2,1)}, bf16[64,512]{1,0:T(8,128)(2,1)S(1)}, u32[]{:S(2)}, u32[]{:S(2)}) collective-permute-start(bf16[64,512]{1,0:T(8,128)(2,1)} %get-tuple-element.30), channel_id=1, source_target_pairs={{0,4},{1,5},{2,6},{3,7},{4,0},{5,1},{6,2},{7,3},{8,12},{9,13},{10,... | collective-permute-start | bytes 196616 | tf_op jit(solution)/shard_map/ppermute | solution.py:334
  41.5 6.8 %collective-permute-start.4 = (bf16[64,512]{1,0:T(8,128)(2,1)}, bf16[64,512]{1,0:T(8,128)(2,1)S(1)}, u32[]{:S(2)}, u32[]{:S(2)}) collective-permute-start(bf16[64,512]{1,0:T(8,128)(2,1)} %get-tuple-element.31), channel_id=1, source_target_pairs={{0,12},{1,13},{2,14},{3,15},{4,8},{5,9},{6,10},{7,11},{8,4},{9,5},... | collective-permute-start | bytes 196616 | tf_op jit(solution)/shard_map/ppermute | solution.py:334
  44.3 6.2 %collective-permute-start.2 = (bf16[64,512]{1,0:T(8,128)(2,1)S(1)}, bf16[64,512]{1,0:T(8,128)(2,1)S(1)}, u32[]{:S(2)}, u32[]{:S(2)}) collective-permute-start(bf16[64,512]{1,0:T(8,128)(2,1)S(1)} %get-tuple-element.26.refs_0_), channel_id=1, source_target_pairs={{0,8},{1,9},{2,10},{3,11},{4,12},{5,13},{6,14},{7,15},{8,0},{9,1},... | collective-permute-start | bytes 196616 | tf_op jit(solution)/shard_map/ppermute | solution.py:334
  50.5 6.7 %collective-permute-start.6 = (bf16[64,512]{1,0:T(8,128)(2,1)S(1)}, bf16[64,512]{1,0:T(8,128)(2,1)S(1)}, u32[]{:S(2)}, u32[]{:S(2)}) collective-permute-start(bf16[64,512]{1,0:T(8,128)(2,1)S(1)} %get-tuple-element.35), channel_id=1, source_target_pairs={{0,8},{1,9},{2,10},{3,11},{4,12},{5,13},{6,14},{7,15},{8,0},{9,1},... | collective-permute-start | bytes 196616 | tf_op jit(solution)/shard_map/ppermute | solution.py:334
  51.2 6.2 %collective-permute-start.7 = (bf16[64,512]{1,0:T(8,128)(2,1)S(1)}, bf16[64,512]{1,0:T(8,128)(2,1)S(1)}, u32[]{:S(2)}, u32[]{:S(2)}) collective-permute-start(bf16[64,512]{1,0:T(8,128)(2,1)S(1)} %get-tuple-element.36), channel_id=1, source_target_pairs={{0,4},{1,5},{2,6},{3,7},{4,0},{5,1},{6,2},{7,3},{8,12},{9,13},{10,... | collective-permute-start | bytes 196616 | tf_op jit(solution)/shard_map/ppermute | solution.py:334
  52.8 6.1 %collective-permute-start.8 = (bf16[64,512]{1,0:T(8,128)(2,1)S(1)}, bf16[64,512]{1,0:T(8,128)(2,1)S(1)}, u32[]{:S(2)}, u32[]{:S(2)}) collective-permute-start(bf16[64,512]{1,0:T(8,128)(2,1)S(1)} %get-tuple-element.37), channel_id=1, source_target_pairs={{0,12},{1,13},{2,14},{3,15},{4,8},{5,9},{6,10},{7,11},{8,4},{9,5},... | collective-permute-start | bytes 196616 | tf_op jit(solution)/shard_map/ppermute | solution.py:334

commit v14 on v8

--- a/solution.py
+++ b/solution.py
@@ -14,7 +14,7 @@
 CHUNK = 512
 TILE = 256
 GROUP = 4
-SHARES = 2
+SHARES = (5, 3)
 VMEM_ALL = 60 * 1024 * 1024
 VMEM_SOME = 24 * 1024 * 1024
 VMEM_MOST = 48 * 1024 * 1024
@@ -264,48 +264,47 @@
     )(me.reshape(1), mean, embeddings)
 
 
-def add_kernel(shares, pieces, keep_ref, *refs):
-    outs = refs[len(refs) - shares * pieces:]
-    came = refs[:len(refs) - shares * pieces]
+def cuts(columns):
+    ends = [columns * sum(SHARES[:h + 1]) // sum(SHARES) for h in range(len(SHARES))]
+    return list(zip([0] + ends[:-1], ends))
+
+
+def add_kernel(first, arrived, pieces, keep_ref, *refs):
+    came, outs = refs[:arrived], refs[-pieces:]
     rows, columns = outs[0].shape
-    for h in range(shares):
-        across = slice(h * columns, (h + 1) * columns)
-        for p in range(pieces):
-            at = slice(p * rows, (p + 1) * rows)
-            held = keep_ref[at, across]
-            for ref in came:
-                held = held + ref[at, across].astype(jnp.float32)
-            out = outs[h * pieces + p]
-            out[...] = held.astype(out.dtype)
-
-
-def add_and_split(keep, came, shares, pieces):
+    across = slice(first, first + columns)
+    for p in range(pieces):
+        at = slice(p * rows, (p + 1) * rows)
+        held = keep_ref[at, across]
+        for ref in came:
+            held = held + ref[at, across].astype(jnp.float32)
+        outs[p][...] = held.astype(outs[p].dtype)
+
+
+def add_and_split(keep, came, pieces, share=None, after=()):
     rows, columns = keep.shape
+    first, end = share or (0, columns)
     vmem = pl.BlockSpec(memory_space=pltpu.VMEM)
-    shape = (rows // pieces, columns // shares)
-    kinds = [jnp.float32] + [jnp.bfloat16] * (pieces - 1)
-    outs = pl.pallas_call(
-        functools.partial(add_kernel, shares, pieces),
-        in_specs=[vmem] * (1 + len(came)),
-        out_specs=[vmem] * (shares * pieces),
-        out_shape=[jax.ShapeDtypeStruct(shape, kind) for kind in kinds * shares],
+    shape = (rows // pieces, end - first)
+    return pl.pallas_call(
+        functools.partial(add_kernel, first, len(came), pieces),
+        in_specs=[vmem] * (1 + len(came)) + [pl.BlockSpec(memory_space=pl.ANY)] * len(after),
+        out_specs=[vmem] * pieces,
+        out_shape=[jax.ShapeDtypeStruct(shape, jnp.float32 if p == 0 else jnp.bfloat16) for p in range(pieces)],
         compiler_params=pltpu.CompilerParams(vmem_limit_bytes=VMEM_SOME),
-        cost_estimate=pl.CostEstimate(flops=2 * rows * columns, bytes_accessed=10 * rows * columns, transcendentals=0),
+        cost_estimate=pl.CostEstimate(flops=2 * rows * (end - first), bytes_accessed=10 * rows * (end - first), transcendentals=0),
         name="add_and_split",
-    )(keep, *came)
-    return [outs[h * pieces:(h + 1) * pieces] for h in range(shares)]
+    )(keep, *came, *after)
 
 
 def finish_kernel(total, between_ref, *refs):
     out_ref = refs[-1]
-    each = (len(refs) - 1) // SHARES
-    columns = out_ref.shape[1] // SHARES
-    for h in range(SHARES):
-        across = slice(h * columns, (h + 1) * columns)
+    each = (len(refs) - 1) // len(SHARES)
+    for h, (first, end) in enumerate(cuts(out_ref.shape[1])):
         held = refs[h * each][...]
         for ref in refs[h * each + 1:(h + 1) * each]:
             held = held + ref[...].astype(jnp.float32)
-        out_ref[:, across] = (held + between_ref[:, across]) / total
+        out_ref[:, first:end] = (held + between_ref[:, first:end]) / total
 
 
 def finish(total, between, keeps, came):
@@ -461,12 +460,14 @@
     keep, send = moments(width, me, embeddings, mean)
     stages = halving_stages(width)
     came = exchange(width, stages[0], [send])
-    shares = add_and_split(keep, came, SHARES, 1 << len(stages[1]))
-    last = []
-    for share in shares:
+    last, after = [], []
+    for cut in cuts(wide):
+        share = add_and_split(keep, came, 1 << len(stages[1]), cut, after)
         for n in range(1, len(stages) - 1):
-            came = exchange(width, stages[n], share[1:])
-            (share,) = add_and_split(share[0], came, 1, 1 << len(stages[n + 1]))
+            moved = exchange(width, stages[n], share[1:])
+            share = add_and_split(share[0], moved, 1 << len(stages[n + 1]))
+            if n == 1:
+                after = [share[1]]
         last.append(share)
     came = [exchange(width, stages[-1], share[1:]) for share in last]
     encoded, between = encode(

time: 57 us -> 58.2 us (1.021)
  starting transfers between devices: 21.7 us -> 23.3 us
    ppermute x9, starting transfers between devices: 14.3 us -> 15.9 us  [exchange(): lax.ppermute(out[p - 1], 'wide', [(i, i ^ apart) for i in range(width)])]
  transfers between devices with their start and end apart: 10 -> 10, of which waited for: 4 -> 3; matrix products, arithmetic and copies ran while one was open for 0% -> 0% of each run, Pallas kernels for 20% -> 20%
where the time goes in v14:
time: 58.2 us; the launch traced here: 58 us
  starting transfers between devices  23.3 us (40%)
  Pallas kernels  19.5 us (34%)
  waiting for transfers between devices  14.4 us (25%)
  between operations  0.79 us (1%)
    ppermute x9, starting transfers between devices, exchange(): lax.ppermute(out[p - 1], 'wide', [(i, i ^ apart) for i in range(width)])  15.9 us
    ppermute x9, waiting for transfers between devices, exchange(): lax.ppermute(out[p - 1], 'wide', [(i, i ^ apart) for i in range(width)])  14.4 us
    all_to_all x1, starting transfers between devices, local(): lax.all_to_all(rows.reshape(width, SPAN, feats), 'wide', split_axis=0, co...  7.4 us
    pallas_call x1, Pallas kernels, project_and_sort(): pl.pallas_call(functools.partial(rows_kernel, width), grid=(rows_here //...  7.25 us
    pallas_call x1, Pallas kernels, moments(): pl.pallas_call(functools.partial(moments_kernel, width), in_specs=[pl.Blo...  7.16 us
    pallas_call x1, Pallas kernels, encode(): pl.pallas_call(functools.partial(encode_kernel, total), in_specs=[pl.Bloc...  4 us
  transfers between devices with their start and end apart: 10, of which 3 were waited for; matrix products, arithmetic and copies ran while one was open for 0% of the time, Pallas kernels for 20%

profile of v14, /device:TPU:0, one launch (start us, length us, event | category | flops | bytes accessed | tf_op | source)
XLA Modules:
  0.0 58.0 jit_solution(18314895183800478495)
XLA Ops:
  0.6 7.3 %project_sort.1 = (bf16[2304,256]{1,0:T(8,128)(2,1)}, f32[1,1024]{1,0:T(1,128)}) custom-call(bf16[2048,1024]{1,0:T(8,128)(2,1)} %e_hbm.3, bf16[1024,256]{1,0:T(8,128)(2,1)} %basis_ref.1, s32[16,128]{1,0:T(8,128)} %bitcast.7, s32[16,128]{1,0:T(8,128)} %bitcast.8), custom_call_target="tpu_custom_call" | custom-call | flops 3489660928 | bytes 5373952 | tf_op jit(solution)/shard_map/project_sort/pallas_call | solution.py:162
  7.9 0.0 copy-start.3
  7.9 7.4 %all-to-all-start = ((bf16[16,144,256]{2,1,0:T(8,128)(2,1)}), bf16[16,144,256]{2,1,0:T(8,128)(2,1)S(1)}, u32[]{:S(2)}, u32[]{:S(2)}) async-start(bf16[16,144,256]{2,1,0:T(8,128)(2,1)} %bitcast.6), calls=%async_computation | async-start | bytes 2359296 | tf_op jit(solution)/shard_map/all_to_all | solution.py:458
  15.3 0.0 copy-done.3
  15.3 7.2 %moments.1 = (f32[512,1024]{1,0:T(8,128)S(1)}, bf16[512,1024]{1,0:T(8,128)(2,1)S(1)}) custom-call(s32[1]{0:T(128)} %bitcast.me_ref, f32[1,1024]{1,0:T(1,128)S(1)} %copy-done.3, bf16[2048,1024]{1,0:T(8,128)(2,1)} %e_hbm.3), custom_call_target="tpu_custom_call" | custom-call | flops 4294967296 | bytes 7340032 | tf_op jit(solution)/shard_map/moments/pallas_call | solution.py:244
  22.5 0.5 collective-permute-start
  23.0 2.3 %collective-permute-done.refs_0_ = bf16[512,1024]{1,0:T(8,128)(2,1)S(1)} collective-permute-done((bf16[512,1024]{1,0:T(8,128)(2,1)S(1)}, bf16[512,1024]{1,0:T(8,128)(2,1)S(1)}, u32[]{:S(2)}, u32[]{:S(2)}) %collective-permute-start) | collective-permute-done | bytes 1048608 | tf_op jit(solution)/shard_map/ppermute | solution.py:333
  25.2 0.1 add_and_split.4
  25.4 2.0 %collective-permute-start.1 = (bf16[256,640]{1,0:T(8,128)(2,1)S(1)}, bf16[256,640]{1,0:T(8,128)(2,1)S(1)}, u32[]{:S(2)}, u32[]{:S(2)}) collective-permute-start(bf16[256,640]{1,0:T(8,128)(2,1)S(1)} %get-tuple-element.25), channel_id=1, source_target_pairs={{0,2},{1,3},{2,0},{3,1},{4,6},{5,7},{6,4},{7,5},{8,10},{9,11},{10,... | collective-permute-start | bytes 983048 | tf_op jit(solution)/shard_map/ppermute | solution.py:333
  27.3 10.8 %collective-permute-done.1.refs_0_ = bf16[256,640]{1,0:T(8,128)(2,1)S(1)} collective-permute-done((bf16[256,640]{1,0:T(8,128)(2,1)S(1)}, bf16[256,640]{1,0:T(8,128)(2,1)S(1)}, u32[]{:S(2)}, u32[]{:S(2)}) %collective-permute-start.1) | collective-permute-done | bytes 327712 | tf_op jit(solution)/shard_map/ppermute | solution.py:333
  38.2 0.1 add_and_split.5
  38.2 0.0 copy-start
  38.2 0.0 copy-start.1
  38.2 0.0 copy-start.2
  38.3 0.1 add_and_split.6
  38.3 2.5 %collective-permute-start.2 = (bf16[256,384]{1,0:T(8,128)(2,1)S(1)}, bf16[256,384]{1,0:T(8,128)(2,1)S(1)}, u32[]{:S(2)}, u32[]{:S(2)}) collective-permute-start(bf16[256,384]{1,0:T(8,128)(2,1)S(1)} %get-tuple-element.28), channel_id=1, source_target_pairs={{0,2},{1,3},{2,0},{3,1},{4,6},{5,7},{6,4},{7,5},{8,10},{9,11},{10,... | collective-permute-start | bytes 589832 | tf_op jit(solution)/shard_map/ppermute | solution.py:333
  40.9 2.5 %collective-permute-start.4 = (bf16[64,640]{1,0:T(8,128)(2,1)S(1)}, bf16[64,640]{1,0:T(8,128)(2,1)S(1)}, u32[]{:S(2)}, u32[]{:S(2)}) collective-permute-start(bf16[64,640]{1,0:T(8,128)(2,1)S(1)} %get-tuple-element.33), channel_id=1, source_target_pairs={{0,4},{1,5},{2,6},{3,7},{4,0},{5,1},{6,2},{7,3},{8,12},{9,13},{10,... | collective-permute-start | bytes 245768 | tf_op jit(solution)/shard_map/ppermute | solution.py:333
  43.4 1.0 %collective-permute-start.3 = (bf16[64,640]{1,0:T(8,128)(2,1)S(1)}, bf16[64,640]{1,0:T(8,128)(2,1)S(1)}, u32[]{:S(2)}, u32[]{:S(2)}) collective-permute-start(bf16[64,640]{1,0:T(8,128)(2,1)S(1)} %get-tuple-element.26.refs_1_.refs_0_), channel_id=1, source_target_pairs={{0,8},{1,9},{2,10},{3,11},{4,12},{5,13},{6,14},{7,15},{8,0},{9,1},... | collective-permute-start | bytes 245768 | tf_op jit(solution)/shard_map/ppermute | solution.py:333
  44.4 1.5 %collective-permute-start.5 = (bf16[64,640]{1,0:T(8,128)(2,1)S(1)}, bf16[64,640]{1,0:T(8,128)(2,1)S(1)}, u32[]{:S(2)}, u32[]{:S(2)}) collective-permute-start(bf16[64,640]{1,0:T(8,128)(2,1)S(1)} %get-tuple-element.34), channel_id=1, source_target_pairs={{0,12},{1,13},{2,14},{3,15},{4,8},{5,9},{6,10},{7,11},{8,4},{9,5},... | collective-permute-start | bytes 245768 | tf_op jit(solution)/shard_map/ppermute | solution.py:333
  45.9 0.0 collective-permute-done.2.refs_0_
  46.0 3.0 %collective-permute-start.7 = (bf16[64,384]{1,0:T(8,128)(2,1)S(1)}, bf16[64,384]{1,0:T(8,128)(2,1)S(1)}, u32[]{:S(2)}, u32[]{:S(2)}) collective-permute-start(bf16[64,384]{1,0:T(8,128)(2,1)S(1)} %get-tuple-element.36), channel_id=1, source_target_pairs={{0,4},{1,5},{2,6},{3,7},{4,0},{5,1},{6,2},{7,3},{8,12},{9,13},{10,... | collective-permute-start | bytes 147464 | tf_op jit(solution)/shard_map/ppermute | solution.py:333
  49.0 2.9 %collective-permute-start.8 = (bf16[64,384]{1,0:T(8,128)(2,1)S(1)}, bf16[64,384]{1,0:T(8,128)(2,1)S(1)}, u32[]{:S(2)}, u32[]{:S(2)}) collective-permute-start(bf16[64,384]{1,0:T(8,128)(2,1)S(1)} %get-tuple-element.37), channel_id=1, source_target_pairs={{0,12},{1,13},{2,14},{3,15},{4,8},{5,9},{6,10},{7,11},{8,4},{9,5},... | collective-permute-start | bytes 147464 | tf_op jit(solution)/shard_map/ppermute | solution.py:333
  51.9 0.0 collective-permute-done.4.refs_2_
  51.9 0.0 collective-permute-start.6
  51.9 0.0 all-to-all-done
  51.9 4.0 %encode.1 = (bf16[2048,256]{1,0:T(8,128)(2,1)}, f32[64,1024]{1,0:T(8,128)S(1)}) custom-call(s32[1]{0:T(128)} %bitcast.me_ref, bf16[2304,256]{1,0:T(8,128)(2,1)S(1)} %bitcast.5, bf16[1024,256]{1,0:T(8,128)(2,1)S(1)} %copy-done, bf16[1024,256]{1,0:T(8,128)(2,1)S(1)} %copy-done.1, bf16[256,256]{1,0:T(8,128)(2,1)S(1)} %copy-done.2, ...), custom_call_target="tpu_custom_call" | custom-call | flops 1342177280 | bytes 2097152 | tf_op jit(solution)/shard_map/encode/pallas_call | solution.py:427
  55.9 0.0 collective-permute-done.5.refs_3_
  56.0 0.0 collective-permute-done.3.refs_1_
  56.0 0.0 collective-permute-done.7.refs_6_
  56.0 0.0 collective-permute-done.8.refs_7_
  56.0 1.3 %collective-permute-done.6.refs_5_ = bf16[64,384]{1,0:T(8,128)(2,1)S(1)} collective-permute-done((bf16[64,384]{1,0:T(8,128)(2,1)S(1)}, bf16[64,384]{1,0:T(8,128)(2,1)S(1)}, u32[]{:S(2)}, u32[]{:S(2)}) %collective-permute-start.6) | collective-permute-done | bytes 49184 | tf_op jit(solution)/shard_map/ppermute | solution.py:333
  57.2 0.8 %finish.1 = f32[64,1024]{1,0:T(8,128)} custom-call(f32[64,1024]{1,0:T(8,128)S(1)} %get-tuple-element.31.between_ref, f32[64,640]{1,0:T(8,128)S(1)} %get-tuple-element.32.refs_0_, bf16[64,640]{1,0:T(8,128)(2,1)S(1)} %collective-permute-done.3.refs_1_, bf16[64,640]{1,0:T(8,128)(2,1)S(1)} %collective-permute-done.4.refs_2_, ...), custom_call_target="tpu_custom_call" | custom-call | flops 524288 | bytes 1048576 | tf_op jit(solution)/shard_map/finish/pallas_call | solution.py:313
  (4 shorter events, 0.0 us)
Async XLA Ops:
  7.9 7.4 %copy-start.3 = (f32[1,1024]{1,0:T(1,128)S(1)}, f32[1,1024]{1,0:T(1,128)}, u32[]{:S(2)}) copy-start(f32[1,1024]{1,0:T(1,128)} %get-tuple-element.21.mean_hbm) | copy-start | bytes 12292
  7.9 44.0 %all-to-all-start = ((bf16[16,144,256]{2,1,0:T(8,128)(2,1)}), bf16[16,144,256]{2,1,0:T(8,128)(2,1)S(1)}, u32[]{:S(2)}, u32[]{:S(2)}) async-start(bf16[16,144,256]{2,1,0:T(8,128)(2,1)} %bitcast.6), calls=%async_computation | async-start | bytes 2359296 | tf_op jit(solution)/shard_map/all_to_all | solution.py:458
  22.5 2.7 %collective-permute-start = (bf16[512,1024]{1,0:T(8,128)(2,1)S(1)}, bf16[512,1024]{1,0:T(8,128)(2,1)S(1)}, u32[]{:S(2)}, u32[]{:S(2)}) collective-permute-start(bf16[512,1024]{1,0:T(8,128)(2,1)S(1)} %get-tuple-element.23), channel_id=1, source_target_pairs={{0,1},{1,0},{2,3},{3,2},{4,5},{5,4},{6,7},{7,6},{8,9},{9,8},{10,11... | collective-permute-start | bytes 3145736 | tf_op jit(solution)/shard_map/ppermute | solution.py:333
  25.4 12.8 %collective-permute-start.1 = (bf16[256,640]{1,0:T(8,128)(2,1)S(1)}, bf16[256,640]{1,0:T(8,128)(2,1)S(1)}, u32[]{:S(2)}, u32[]{:S(2)}) collective-permute-start(bf16[256,640]{1,0:T(8,128)(2,1)S(1)} %get-tuple-element.25), channel_id=1, source_target_pairs={{0,2},{1,3},{2,0},{3,1},{4,6},{5,7},{6,4},{7,5},{8,10},{9,11},{10,... | collective-permute-start | bytes 983048 | tf_op jit(solution)/shard_map/ppermute | solution.py:333
  38.2 13.7 %copy-start = (bf16[1024,256]{1,0:T(8,128)(2,1)S(1)}, bf16[1024,256]{1,0:T(8,128)(2,1)}, u32[]{:S(2)}) copy-start(bf16[1024,256]{1,0:T(8,128)(2,1)} %basis_ref.1) | copy-start | bytes 1572868
  38.2 13.7 %copy-start.1 = (bf16[1024,256]{1,0:T(8,128)(2,1)S(1)}, bf16[1024,256]{1,0:T(8,128)(2,1)}, u32[]{:S(2)}) copy-start(bf16[1024,256]{1,0:T(8,128)(2,1)} %centroid_ref.1) | copy-start | bytes 1572868
  38.2 13.7 %copy-start.2 = (bf16[256,256]{1,0:T(8,128)(2,1)S(1)}, bf16[256,256]{1,0:T(8,128)(2,1)}, u32[]{:S(2)}) copy-start(bf16[256,256]{1,0:T(8,128)(2,1)} %rotation_ref.1) | copy-start | bytes 393220
  38.3 7.6 %collective-permute-start.2 = (bf16[256,384]{1,0:T(8,128)(2,1)S(1)}, bf16[256,384]{1,0:T(8,128)(2,1)S(1)}, u32[]{:S(2)}, u32[]{:S(2)}) collective-permute-start(bf16[256,384]{1,0:T(8,128)(2,1)S(1)} %get-tuple-element.28), channel_id=1, source_target_pairs={{0,2},{1,3},{2,0},{3,1},{4,6},{5,7},{6,4},{7,5},{8,10},{9,11},{10,... | collective-permute-start | bytes 589832 | tf_op jit(solution)/shard_map/ppermute | solution.py:333
  40.9 11.0 %collective-permute-start.4 = (bf16[64,640]{1,0:T(8,128)(2,1)S(1)}, bf16[64,640]{1,0:T(8,128)(2,1)S(1)}, u32[]{:S(2)}, u32[]{:S(2)}) collective-permute-start(bf16[64,640]{1,0:T(8,128)(2,1)S(1)} %get-tuple-element.33), channel_id=1, source_target_pairs={{0,4},{1,5},{2,6},{3,7},{4,0},{5,1},{6,2},{7,3},{8,12},{9,13},{10,... | collective-permute-start | bytes 245768 | tf_op jit(solution)/shard_map/ppermute | solution.py:333
  43.4 12.6 %collective-permute-start.3 = (bf16[64,640]{1,0:T(8,128)(2,1)S(1)}, bf16[64,640]{1,0:T(8,128)(2,1)S(1)}, u32[]{:S(2)}, u32[]{:S(2)}) collective-permute-start(bf16[64,640]{1,0:T(8,128)(2,1)S(1)} %get-tuple-element.26.refs_1_.refs_0_), channel_id=1, source_target_pairs={{0,8},{1,9},{2,10},{3,11},{4,12},{5,13},{6,14},{7,15},{8,0},{9,1},... | collective-permute-start | bytes 245768 | tf_op jit(solution)/shard_map/ppermute | solution.py:333
  44.4 11.5 %collective-permute-start.5 = (bf16[64,640]{1,0:T(8,128)(2,1)S(1)}, bf16[64,640]{1,0:T(8,128)(2,1)S(1)}, u32[]{:S(2)}, u32[]{:S(2)}) collective-permute-start(bf16[64,640]{1,0:T(8,128)(2,1)S(1)} %get-tuple-element.34), channel_id=1, source_target_pairs={{0,12},{1,13},{2,14},{3,15},{4,8},{5,9},{6,10},{7,11},{8,4},{9,5},... | collective-permute-start | bytes 245768 | tf_op jit(solution)/shard_map/ppermute | solution.py:333
  46.0 10.0 %collective-permute-start.7 = (bf16[64,384]{1,0:T(8,128)(2,1)S(1)}, bf16[64,384]{1,0:T(8,128)(2,1)S(1)}, u32[]{:S(2)}, u32[]{:S(2)}) collective-permute-start(bf16[64,384]{1,0:T(8,128)(2,1)S(1)} %get-tuple-element.36), channel_id=1, source_target_pairs={{0,4},{1,5},{2,6},{3,7},{4,0},{5,1},{6,2},{7,3},{8,12},{9,13},{10,... | collective-permute-start | bytes 147464 | tf_op jit(solution)/shard_map/ppermute | solution.py:333
  49.0 7.0 %collective-permute-start.8 = (bf16[64,384]{1,0:T(8,128)(2,1)S(1)}, bf16[64,384]{1,0:T(8,128)(2,1)S(1)}, u32[]{:S(2)}, u32[]{:S(2)}) collective-permute-start(bf16[64,384]{1,0:T(8,128)(2,1)S(1)} %get-tuple-element.37), channel_id=1, source_target_pairs={{0,12},{1,13},{2,14},{3,15},{4,8},{5,9},{6,10},{7,11},{8,4},{9,5},... | collective-permute-start | bytes 147464 | tf_op jit(solution)/shard_map/ppermute | solution.py:333
  51.9 5.3 %collective-permute-start.6 = (bf16[64,384]{1,0:T(8,128)(2,1)S(1)}, bf16[64,384]{1,0:T(8,128)(2,1)S(1)}, u32[]{:S(2)}, u32[]{:S(2)}) collective-permute-start(bf16[64,384]{1,0:T(8,128)(2,1)S(1)} %get-tuple-element.29.refs_1_), channel_id=1, source_target_pairs={{0,8},{1,9},{2,10},{3,11},{4,12},{5,13},{6,14},{7,15},{8,0},{9,1},... | collective-permute-start | bytes 147464 | tf_op jit(solution)/shard_map/ppermute | solution.py:333

commit v15 on v8

--- a/solution.py
+++ b/solution.py
@@ -52,9 +52,26 @@
         basis_copy.start()
         for c in range(1, rows_here // CHUNK):
             e_copy(c).start()
-        owner_copy.wait()
         sum_ref[...] = jnp.zeros_like(sum_ref)
         total_ref[...] = jnp.zeros_like(total_ref)
+        basis_copy.wait()
+
+    def project():
+        e_copy(step).wait()
+        here = pl.ds(pl.multiple_of(step * CHUNK, CHUNK), CHUNK)
+        rows = e_ref[here, :]
+        y = jnp.dot(rows, basis_ref[...], preferred_element_type=jnp.float32)
+        y_ref[here, :] = y
+        sum_ref[...] += jnp.sum(y.reshape(CHUNK // 8, 8, feats), 0)
+        total_ref[...] += jnp.sum(rows.astype(jnp.float32).reshape(CHUNK // 8, 8, wide), 0)
+
+    @pl.when(step != 1)
+    def _():
+        project()
+
+    @pl.when(step == 1)
+    def _():
+        pltpu.make_async_copy(owner_hbm, owner_ref, small_sem.at[0]).wait()
         owner = owner_ref[...]
         wanted = lax.broadcasted_iota(jnp.int32, (width, LANES), 0)
         hits = [jnp.where(owner[c:c + 1, :] == wanted, 1.0, 0.0) for c in range(chunks)]
@@ -72,31 +89,7 @@
             ranks.append(jnp.sum(hits[c] * (within[at] + carry), 0, keepdims=True).astype(jnp.int32))
             carry = carry + counts[at]
             target_ref[c:c + 1, :] = owner[c:c + 1, :] * CAP + ranks[c]
-
-        slot_copy.wait()
-        slot = slot_ref[...] + 1
-        high, low = (slot >> 5).astype(jnp.float32), (slot & 31).astype(jnp.float32)
-        spots = lax.broadcasted_iota(jnp.int32, (CAP, LANES), 0)
-        placed = jnp.concatenate([jnp.where(ranks[c] == spots, 1.0, 0.0) for c in range(chunks)], 1).astype(jnp.bfloat16)
-        digits = jnp.concatenate(
-            [
-                jnp.concatenate([hits[c] * high[c:c + 1, :] for c in range(chunks)], 1),
-                jnp.concatenate([hits[c] * low[c:c + 1, :] for c in range(chunks)], 1),
-            ],
-            0,
-        ).astype(jnp.bfloat16)
-        found = lax.dot_general(digits, placed, (((1,), (1,)), ((), ())), preferred_element_type=jnp.float32)
-        list_ref[:, :CAP] = found[:width]
-        list_ref[:, CAP:] = found[width:]
-        basis_copy.wait()
-
-    e_copy(step).wait()
-    here = pl.ds(pl.multiple_of(step * CHUNK, CHUNK), CHUNK)
-    rows = e_ref[here, :]
-    y = jnp.dot(rows, basis_ref[...], preferred_element_type=jnp.float32)
-    y_ref[here, :] = y
-    sum_ref[...] += jnp.sum(y.reshape(CHUNK // 8, 8, feats), 0)
-    total_ref[...] += jnp.sum(rows.astype(jnp.float32).reshape(CHUNK // 8, 8, wide), 0)
+        project()
 
     @pl.when(step == pl.num_programs(0) - 1)
     def _():
@@ -114,6 +107,27 @@
         parts = in_three(mean)
         common = [part[:, q * feats:(q + 1) * feats] for part in parts for q in range(wide // feats)]
         common = jnp.concatenate(common + list(in_three(jnp.sum(square, 0, keepdims=True))), 0)
+
+        pltpu.make_async_copy(slot_hbm, slot_ref, small_sem.at[1]).wait()
+        owner = owner_ref[...]
+        wanted = lax.broadcasted_iota(jnp.int32, (width, LANES), 0)
+        hits = [jnp.where(owner[c:c + 1, :] == wanted, 1.0, 0.0) for c in range(chunks)]
+        ranks = [target_ref[c:c + 1, :] - owner[c:c + 1, :] * CAP for c in range(chunks)]
+        slot = slot_ref[...] + 1
+        high, low = (slot >> 5).astype(jnp.float32), (slot & 31).astype(jnp.float32)
+        spots = lax.broadcasted_iota(jnp.int32, (CAP, LANES), 0)
+        placed = jnp.concatenate([jnp.where(ranks[c] == spots, 1.0, 0.0) for c in range(chunks)], 1).astype(jnp.bfloat16)
+        digits = jnp.concatenate(
+            [
+                jnp.concatenate([hits[c] * high[c:c + 1, :] for c in range(chunks)], 1),
+                jnp.concatenate([hits[c] * low[c:c + 1, :] for c in range(chunks)], 1),
+            ],
+            0,
+        ).astype(jnp.bfloat16)
+        found = lax.dot_general(digits, placed, (((1,), (1,)), ((), ())), preferred_element_type=jnp.float32)
+        list_ref[:, :CAP] = found[:width]
+        list_ref[:, CAP:] = found[width:]
+
 
         place = lax.broadcasted_iota(jnp.int32, (GROUP * CAP, LANES), 0).astype(jnp.int16)
 
@@ -197,6 +211,7 @@
     rows_here, wide = e_ref.shape
     block = wide // width
     bits = width.bit_length() - 1
+    tiles = wide // TILE
     mean_copy = pltpu.make_async_copy(mean_hbm, mean_ref, mean_sem)
     mean_copy.start()
     copies = []
@@ -205,10 +220,11 @@
         copies.append(pltpu.make_async_copy(e_hbm.at[at], e_ref.at[at], sem.at[c]))
         copies[c].start()
     me = me_ref[0]
+    odd = (me & 1) == 1
     mean_copy.wait()
     mean = mean_ref[...]
-    for t in range(wide // TILE):
-        rows = slice(t * TILE, (t + 1) * TILE)
+    for t in range(tiles):
+        rows, columns = slice(t * TILE, (t + 1) * TILE), slice(t * TILE, wide)
         if t == 0:
             product = jnp.zeros((TILE, wide), jnp.float32)
             for c in range(rows_here // CHUNK):
@@ -219,12 +235,20 @@
                 )
         else:
             product = lax.dot_general(
-                e_ref[:, rows], e_ref[...], (((0,), (0,)), ((), ())), preferred_element_type=jnp.float32
+                e_ref[:, rows], e_ref[:, columns], (((0,), (0,)), ((), ())), preferred_element_type=jnp.float32
             )
         down = jnp.transpose(jnp.broadcast_to(mean[:, rows] * rows_here, (LANES, TILE)))
-        for j in range(wide // LANES):
-            across = slice(j * LANES, (j + 1) * LANES)
-            m_ref[rows, across] = product[:, across] - down * mean[:, across]
+        for u in range(t, tiles):
+            pieces = []
+            for j in range(u * TILE // LANES, (u + 1) * TILE // LANES):
+                across = slice(j * LANES, (j + 1) * LANES)
+                within = slice(j * LANES - t * TILE, (j + 1) * LANES - t * TILE)
+                pieces.append((product[:, within] - down * mean[:, across]).astype(jnp.bfloat16))
+            piece = jnp.concatenate(pieces, 1)
+            other = slice(u * TILE, (u + 1) * TILE)
+            m_ref[rows, other] = piece
+            if u > t:
+                m_ref[other, rows] = jnp.transpose(piece)
         for pair in range(TILE // block // 2):
             first = t * (TILE // block) + 2 * pair
             apart = (first ^ me) >> 1
@@ -232,10 +256,10 @@
             for k in range(bits - 1):
                 place = place + (((apart >> k) & 1) << (bits - 2 - k))
             to = pl.ds(pl.multiple_of(place * block, block), block)
-            kept = pl.multiple_of((first + (me & 1)) * block, block)
-            sent = pl.multiple_of((first + 1 - (me & 1)) * block, block)
-            keep_ref[to, :] = m_ref[pl.ds(kept, block), :]
-            send_ref[to, :] = m_ref[pl.ds(sent, block), :].astype(jnp.bfloat16)
+            even_rows = m_ref[first * block:(first + 1) * block, :]
+            odd_rows = m_ref[(first + 1) * block:(first + 2) * block, :]
+            keep_ref[to, :] = jnp.where(odd, odd_rows, even_rows)
+            send_ref[to, :] = jnp.where(odd, even_rows, odd_rows)
 
 
 def moments(width, me, embeddings, mean):
@@ -246,13 +270,13 @@
         in_specs=[pl.BlockSpec(memory_space=pltpu.SMEM)] + [pl.BlockSpec(memory_space=pl.ANY)] * 2,
         out_specs=[vmem] * 2,
         out_shape=[
-            jax.ShapeDtypeStruct((wide // 2, wide), jnp.float32),
+            jax.ShapeDtypeStruct((wide // 2, wide), jnp.bfloat16),
             jax.ShapeDtypeStruct((wide // 2, wide), jnp.bfloat16),
         ],
         scratch_shapes=[
             pltpu.VMEM((rows_here, wide), jnp.bfloat16),
             pltpu.VMEM((1, wide), jnp.float32),
-            pltpu.VMEM((wide, wide), jnp.float32),
+            pltpu.VMEM((wide, wide), jnp.bfloat16),
             pltpu.SemaphoreType.DMA((rows_here // CHUNK,)),
             pltpu.SemaphoreType.DMA,
         ],
@@ -272,7 +296,7 @@
         across = slice(h * columns, (h + 1) * columns)
         for p in range(pieces):
             at = slice(p * rows, (p + 1) * rows)
-            held = keep_ref[at, across]
+            held = keep_ref[at, across].astype(jnp.float32)
             for ref in came:
                 held = held + ref[at, across].astype(jnp.float32)
             out = outs[h * pieces + p]

time: 57 us -> 57.6 us (1.011)
  waiting for transfers between devices: 14.8 us -> 18.9 us
  starting transfers between devices: 21.7 us -> 19.8 us
  Pallas kernels: 19.5 us -> 17.9 us
    ppermute x9, waiting for transfers between devices: 14.8 us -> 18.9 us  [exchange(): lax.ppermute(out[p - 1], 'wide', [(i, i ^ apart) for i in range(width)])]
    pallas_call x1, Pallas kernels: 7.16 us -> 4.92 us  [moments(): pl.pallas_call(functools.partial(moments_kernel, width), in_specs=[pl.Blo...]
    ppermute x9, starting transfers between devices: 14.3 us -> 12.4 us  [exchange(): lax.ppermute(out[p - 1], 'wide', [(i, i ^ apart) for i in range(width)])]
    pallas_call x1, Pallas kernels: 7.27 us -> 7.93 us  [project_and_sort(): pl.pallas_call(functools.partial(rows_kernel, width), grid=(rows_here //...]
  transfers between devices with their start and end apart: 10 -> 10, of which waited for: 4 -> 5; matrix products, arithmetic and copies ran while one was open for 0% -> 0% of each run, Pallas kernels for 20% -> 16%
where the time goes in v15:
time: 57.6 us; the launch traced here: 57.4 us
  starting transfers between devices  19.8 us (34%)
  waiting for transfers between devices  18.9 us (33%)
  Pallas kernels  17.9 us (31%)
  between operations  0.74 us (1%)
    ppermute x9, waiting for transfers between devices, exchange(): lax.ppermute(out[p - 1], 'wide', [(i, i ^ apart) for i in range(width)])  18.9 us
    ppermute x9, starting transfers between devices, exchange(): lax.ppermute(out[p - 1], 'wide', [(i, i ^ apart) for i in range(width)])  12.4 us
    pallas_call x1, Pallas kernels, project_and_sort(): pl.pallas_call(functools.partial(rows_kernel, width), grid=(rows_here //...  7.93 us
    all_to_all x1, starting transfers between devices, local(): lax.all_to_all(rows.reshape(width, SPAN, feats), 'wide', split_axis=0, co...  7.4 us
    pallas_call x1, Pallas kernels, moments(): pl.pallas_call(functools.partial(moments_kernel, width), in_specs=[pl.Blo...  4.92 us
    pallas_call x1, Pallas kernels, encode(): pl.pallas_call(functools.partial(encode_kernel, total), in_specs=[pl.Bloc...  4 us
  transfers between devices with their start and end apart: 10, of which 5 were waited for; matrix products, arithmetic and copies ran while one was open for 0% of the time, Pallas kernels for 16%

profile of v15, /device:TPU:0, one launch (start us, length us, event | category | flops | bytes accessed | tf_op | source)
XLA Modules:
  0.0 57.4 jit_solution(14901934028851462175)
XLA Ops:
  0.6 7.9 %project_sort.1 = (bf16[2304,256]{1,0:T(8,128)(2,1)}, f32[1,1024]{1,0:T(1,128)}) custom-call(bf16[2048,1024]{1,0:T(8,128)(2,1)} %e_hbm.3, bf16[1024,256]{1,0:T(8,128)(2,1)} %basis_ref.1, s32[16,128]{1,0:T(8,128)} %bitcast.7, s32[16,128]{1,0:T(8,128)} %bitcast.8), custom_call_target="tpu_custom_call" | custom-call | flops 3489660928 | bytes 5373952 | tf_op jit(solution)/shard_map/project_sort/pallas_call | solution.py:176
  8.6 0.0 copy-start.3
  8.6 7.4 %all-to-all-start = ((bf16[16,144,256]{2,1,0:T(8,128)(2,1)}), bf16[16,144,256]{2,1,0:T(8,128)(2,1)S(1)}, u32[]{:S(2)}, u32[]{:S(2)}) async-start(bf16[16,144,256]{2,1,0:T(8,128)(2,1)} %bitcast.6), calls=%async_computation | async-start | bytes 2359296 | tf_op jit(solution)/shard_map/all_to_all | solution.py:483
  16.0 0.0 copy-done.3
  16.0 4.9 %moments.1 = (bf16[512,1024]{1,0:T(8,128)(2,1)S(1)}, bf16[512,1024]{1,0:T(8,128)(2,1)S(1)}) custom-call(s32[1]{0:T(128)} %bitcast.me_ref, f32[1,1024]{1,0:T(1,128)S(1)} %copy-done.3, bf16[2048,1024]{1,0:T(8,128)(2,1)} %e_hbm.3), custom_call_target="tpu_custom_call" | custom-call | flops 4294967296 | bytes 7340032 | tf_op jit(solution)/shard_map/moments/pallas_call | solution.py:268
  20.9 0.5 collective-permute-start
  21.4 2.3 %collective-permute-done.refs_0_ = bf16[512,1024]{1,0:T(8,128)(2,1)S(1)} collective-permute-done((bf16[512,1024]{1,0:T(8,128)(2,1)S(1)}, bf16[512,1024]{1,0:T(8,128)(2,1)S(1)}, u32[]{:S(2)}, u32[]{:S(2)}) %collective-permute-start) | collective-permute-done | bytes 1048608 | tf_op jit(solution)/shard_map/ppermute | solution.py:358
  23.7 0.2 add_and_split.3
  23.9 0.0 copy-start
  23.9 0.0 copy-start.1
  23.9 0.0 copy-start.2
  24.0 2.0 %collective-permute-start.1 = (bf16[256,512]{1,0:T(8,128)(2,1)S(1)}, bf16[256,512]{1,0:T(8,128)(2,1)S(1)}, u32[]{:S(2)}, u32[]{:S(2)}) collective-permute-start(bf16[256,512]{1,0:T(8,128)(2,1)S(1)} %get-tuple-element.25), channel_id=1, source_target_pairs={{0,2},{1,3},{2,0},{3,1},{4,6},{5,7},{6,4},{7,5},{8,10},{9,11},{10,... | collective-permute-start | bytes 786440 | tf_op jit(solution)/shard_map/ppermute | solution.py:358
  25.9 0.2 collective-permute-start.2
  26.1 11.0 %collective-permute-done.1.refs_0_ = bf16[256,512]{1,0:T(8,128)(2,1)S(1)} collective-permute-done((bf16[256,512]{1,0:T(8,128)(2,1)S(1)}, bf16[256,512]{1,0:T(8,128)(2,1)S(1)}, u32[]{:S(2)}, u32[]{:S(2)}) %collective-permute-start.1) | collective-permute-done | bytes 262176 | tf_op jit(solution)/shard_map/ppermute | solution.py:358
  37.2 3.6 %collective-permute-start.4 = (bf16[64,512]{1,0:T(8,128)(2,1)S(1)}, bf16[64,512]{1,0:T(8,128)(2,1)S(1)}, u32[]{:S(2)}, u32[]{:S(2)}) collective-permute-start(bf16[64,512]{1,0:T(8,128)(2,1)S(1)} %get-tuple-element.33), channel_id=1, source_target_pairs={{0,4},{1,5},{2,6},{3,7},{4,0},{5,1},{6,2},{7,3},{8,12},{9,13},{10,... | collective-permute-start | bytes 196616 | tf_op jit(solution)/shard_map/ppermute | solution.py:358
  40.7 1.3 %collective-permute-start.5 = (bf16[64,512]{1,0:T(8,128)(2,1)S(1)}, bf16[64,512]{1,0:T(8,128)(2,1)S(1)}, u32[]{:S(2)}, u32[]{:S(2)}) collective-permute-start(bf16[64,512]{1,0:T(8,128)(2,1)S(1)} %get-tuple-element.34), channel_id=1, source_target_pairs={{0,12},{1,13},{2,14},{3,15},{4,8},{5,9},{6,10},{7,11},{8,4},{9,5},... | collective-permute-start | bytes 196616 | tf_op jit(solution)/shard_map/ppermute | solution.py:358
  42.0 0.2 collective-permute-start.3
  42.3 1.8 %collective-permute-done.2.refs_0_ = bf16[256,512]{1,0:T(8,128)(2,1)S(1)} collective-permute-done((bf16[256,512]{1,0:T(8,128)(2,1)S(1)}, bf16[256,512]{1,0:T(8,128)(2,1)S(1)}, u32[]{:S(2)}, u32[]{:S(2)}) %collective-permute-start.2) | collective-permute-done | bytes 262176 | tf_op jit(solution)/shard_map/ppermute | solution.py:358
  44.1 3.1 %collective-permute-start.7 = (bf16[64,512]{1,0:T(8,128)(2,1)S(1)}, bf16[64,512]{1,0:T(8,128)(2,1)S(1)}, u32[]{:S(2)}, u32[]{:S(2)}) collective-permute-start(bf16[64,512]{1,0:T(8,128)(2,1)S(1)} %get-tuple-element.36), channel_id=1, source_target_pairs={{0,4},{1,5},{2,6},{3,7},{4,0},{5,1},{6,2},{7,3},{8,12},{9,13},{10,... | collective-permute-start | bytes 196616 | tf_op jit(solution)/shard_map/ppermute | solution.py:358
  47.2 0.4 collective-permute-start.8
  47.7 0.0 collective-permute-done.4.refs_2_
  47.7 1.1 %collective-permute-start.6 = (bf16[64,512]{1,0:T(8,128)(2,1)S(1)}, bf16[64,512]{1,0:T(8,128)(2,1)S(1)}, u32[]{:S(2)}, u32[]{:S(2)}) collective-permute-start(bf16[64,512]{1,0:T(8,128)(2,1)S(1)} %get-tuple-element.29.refs_1_), channel_id=1, source_target_pairs={{0,8},{1,9},{2,10},{3,11},{4,12},{5,13},{6,14},{7,15},{8,0},{9,1},... | collective-permute-start | bytes 196616 | tf_op jit(solution)/shard_map/ppermute | solution.py:358
  48.8 0.0 all-to-all-done
  48.8 0.0 copy-done
  48.8 0.0 copy-done.1
  48.8 4.0 %encode.1 = (bf16[2048,256]{1,0:T(8,128)(2,1)}, f32[64,1024]{1,0:T(8,128)S(1)}) custom-call(s32[1]{0:T(128)} %bitcast.me_ref, bf16[2304,256]{1,0:T(8,128)(2,1)S(1)} %bitcast.5, bf16[1024,256]{1,0:T(8,128)(2,1)S(1)} %copy-done, bf16[1024,256]{1,0:T(8,128)(2,1)S(1)} %copy-done.1, bf16[256,256]{1,0:T(8,128)(2,1)S(1)} %copy-done.2, ...), custom_call_target="tpu_custom_call" | custom-call | flops 1342177280 | bytes 2097152 | tf_op jit(solution)/shard_map/encode/pallas_call | solution.py:452
  52.8 0.0 collective-permute-done.5.refs_3_
  52.8 1.5 %collective-permute-done.3.refs_1_ = bf16[64,512]{1,0:T(8,128)(2,1)S(1)} collective-permute-done((bf16[64,512]{1,0:T(8,128)(2,1)S(1)}, bf16[64,512]{1,0:T(8,128)(2,1)S(1)}, u32[]{:S(2)}, u32[]{:S(2)}) %collective-permute-start.3) | collective-permute-done | bytes 65568 | tf_op jit(solution)/shard_map/ppermute | solution.py:358
  54.3 0.0 collective-permute-done.7.refs_6_
  54.3 0.0 collective-permute-done.8.refs_7_
  54.3 2.3 %collective-permute-done.6.refs_5_ = bf16[64,512]{1,0:T(8,128)(2,1)S(1)} collective-permute-done((bf16[64,512]{1,0:T(8,128)(2,1)S(1)}, bf16[64,512]{1,0:T(8,128)(2,1)S(1)}, u32[]{:S(2)}, u32[]{:S(2)}) %collective-permute-start.6) | collective-permute-done | bytes 65568 | tf_op jit(solution)/shard_map/ppermute | solution.py:358
  56.6 0.8 %finish.1 = f32[64,1024]{1,0:T(8,128)} custom-call(f32[64,1024]{1,0:T(8,128)S(1)} %get-tuple-element.31.between_ref, f32[64,512]{1,0:T(8,128)S(1)} %get-tuple-element.32.refs_0_, bf16[64,512]{1,0:T(8,128)(2,1)S(1)} %collective-permute-done.3.refs_1_, bf16[64,512]{1,0:T(8,128)(2,1)S(1)} %collective-permute-done.4.refs_2_, ...), custom_call_target="tpu_custom_call" | custom-call | flops 524288 | bytes 1048576 | tf_op jit(solution)/shard_map/finish/pallas_call | solution.py:338
  (3 shorter events, 0.1 us)
Async XLA Ops:
  8.6 7.4 %copy-start.3 = (f32[1,1024]{1,0:T(1,128)S(1)}, f32[1,1024]{1,0:T(1,128)}, u32[]{:S(2)}) copy-start(f32[1,1024]{1,0:T(1,128)} %get-tuple-element.21.mean_hbm) | copy-start | bytes 12292
  8.6 40.2 %all-to-all-start = ((bf16[16,144,256]{2,1,0:T(8,128)(2,1)}), bf16[16,144,256]{2,1,0:T(8,128)(2,1)S(1)}, u32[]{:S(2)}, u32[]{:S(2)}) async-start(bf16[16,144,256]{2,1,0:T(8,128)(2,1)} %bitcast.6), calls=%async_computation | async-start | bytes 2359296 | tf_op jit(solution)/shard_map/all_to_all | solution.py:483
  20.9 2.8 %collective-permute-start = (bf16[512,1024]{1,0:T(8,128)(2,1)S(1)}, bf16[512,1024]{1,0:T(8,128)(2,1)S(1)}, u32[]{:S(2)}, u32[]{:S(2)}) collective-permute-start(bf16[512,1024]{1,0:T(8,128)(2,1)S(1)} %get-tuple-element.23), channel_id=1, source_target_pairs={{0,1},{1,0},{2,3},{3,2},{4,5},{5,4},{6,7},{7,6},{8,9},{9,8},{10,11... | collective-permute-start | bytes 3145736 | tf_op jit(solution)/shard_map/ppermute | solution.py:358
  23.9 24.9 %copy-start = (bf16[1024,256]{1,0:T(8,128)(2,1)S(1)}, bf16[1024,256]{1,0:T(8,128)(2,1)}, u32[]{:S(2)}) copy-start(bf16[1024,256]{1,0:T(8,128)(2,1)} %basis_ref.1) | copy-start | bytes 1572868
  23.9 24.9 %copy-start.1 = (bf16[1024,256]{1,0:T(8,128)(2,1)S(1)}, bf16[1024,256]{1,0:T(8,128)(2,1)}, u32[]{:S(2)}) copy-start(bf16[1024,256]{1,0:T(8,128)(2,1)} %centroid_ref.1) | copy-start | bytes 1572868
  23.9 24.9 %copy-start.2 = (bf16[256,256]{1,0:T(8,128)(2,1)S(1)}, bf16[256,256]{1,0:T(8,128)(2,1)}, u32[]{:S(2)}) copy-start(bf16[256,256]{1,0:T(8,128)(2,1)} %rotation_ref.1) | copy-start | bytes 393220
  24.0 13.2 %collective-permute-start.1 = (bf16[256,512]{1,0:T(8,128)(2,1)S(1)}, bf16[256,512]{1,0:T(8,128)(2,1)S(1)}, u32[]{:S(2)}, u32[]{:S(2)}) collective-permute-start(bf16[256,512]{1,0:T(8,128)(2,1)S(1)} %get-tuple-element.25), channel_id=1, source_target_pairs={{0,2},{1,3},{2,0},{3,1},{4,6},{5,7},{6,4},{7,5},{8,10},{9,11},{10,... | collective-permute-start | bytes 786440 | tf_op jit(solution)/shard_map/ppermute | solution.py:358
  25.9 18.1 %collective-permute-start.2 = (bf16[256,512]{1,0:T(8,128)(2,1)S(1)}, bf16[256,512]{1,0:T(8,128)(2,1)S(1)}, u32[]{:S(2)}, u32[]{:S(2)}) collective-permute-start(bf16[256,512]{1,0:T(8,128)(2,1)S(1)} %get-tuple-element.28), channel_id=1, source_target_pairs={{0,2},{1,3},{2,0},{3,1},{4,6},{5,7},{6,4},{7,5},{8,10},{9,11},{10,... | collective-permute-start | bytes 786440 | tf_op jit(solution)/shard_map/ppermute | solution.py:358
  37.2 10.5 %collective-permute-start.4 = (bf16[64,512]{1,0:T(8,128)(2,1)S(1)}, bf16[64,512]{1,0:T(8,128)(2,1)S(1)}, u32[]{:S(2)}, u32[]{:S(2)}) collective-permute-start(bf16[64,512]{1,0:T(8,128)(2,1)S(1)} %get-tuple-element.33), channel_id=1, source_target_pairs={{0,4},{1,5},{2,6},{3,7},{4,0},{5,1},{6,2},{7,3},{8,12},{9,13},{10,... | collective-permute-start | bytes 196616 | tf_op jit(solution)/shard_map/ppermute | solution.py:358
  40.7 12.1 %collective-permute-start.5 = (bf16[64,512]{1,0:T(8,128)(2,1)S(1)}, bf16[64,512]{1,0:T(8,128)(2,1)S(1)}, u32[]{:S(2)}, u32[]{:S(2)}) collective-permute-start(bf16[64,512]{1,0:T(8,128)(2,1)S(1)} %get-tuple-element.34), channel_id=1, source_target_pairs={{0,12},{1,13},{2,14},{3,15},{4,8},{5,9},{6,10},{7,11},{8,4},{9,5},... | collective-permute-start | bytes 196616 | tf_op jit(solution)/shard_map/ppermute | solution.py:358
  42.0 12.3 %collective-permute-start.3 = (bf16[64,512]{1,0:T(8,128)(2,1)S(1)}, bf16[64,512]{1,0:T(8,128)(2,1)S(1)}, u32[]{:S(2)}, u32[]{:S(2)}) collective-permute-start(bf16[64,512]{1,0:T(8,128)(2,1)S(1)} %get-tuple-element.26.refs_0_), channel_id=1, source_target_pairs={{0,8},{1,9},{2,10},{3,11},{4,12},{5,13},{6,14},{7,15},{8,0},{9,1},... | collective-permute-start | bytes 196616 | tf_op jit(solution)/shard_map/ppermute | solution.py:358
  44.1 10.2 %collective-permute-start.7 = (bf16[64,512]{1,0:T(8,128)(2,1)S(1)}, bf16[64,512]{1,0:T(8,128)(2,1)S(1)}, u32[]{:S(2)}, u32[]{:S(2)}) collective-permute-start(bf16[64,512]{1,0:T(8,128)(2,1)S(1)} %get-tuple-element.36), channel_id=1, source_target_pairs={{0,4},{1,5},{2,6},{3,7},{4,0},{5,1},{6,2},{7,3},{8,12},{9,13},{10,... | collective-permute-start | bytes 196616 | tf_op jit(solution)/shard_map/ppermute | solution.py:358
  47.2 7.1 %collective-permute-start.8 = (bf16[64,512]{1,0:T(8,128)(2,1)S(1)}, bf16[64,512]{1,0:T(8,128)(2,1)S(1)}, u32[]{:S(2)}, u32[]{:S(2)}) collective-permute-start(bf16[64,512]{1,0:T(8,128)(2,1)S(1)} %get-tuple-element.37), channel_id=1, source_target_pairs={{0,12},{1,13},{2,14},{3,15},{4,8},{5,9},{6,10},{7,11},{8,4},{9,5},... | collective-permute-start | bytes 196616 | tf_op jit(solution)/shard_map/ppermute | solution.py:358
  47.7 9.0 %collective-permute-start.6 = (bf16[64,512]{1,0:T(8,128)(2,1)S(1)}, bf16[64,512]{1,0:T(8,128)(2,1)S(1)}, u32[]{:S(2)}, u32[]{:S(2)}) collective-permute-start(bf16[64,512]{1,0:T(8,128)(2,1)S(1)} %get-tuple-element.29.refs_1_), channel_id=1, source_target_pairs={{0,8},{1,9},{2,10},{3,11},{4,12},{5,13},{6,14},{7,15},{8,0},{9,1},... | collective-permute-start | bytes 196616 | tf_op jit(solution)/shard_map/ppermute | solution.py:358

commit v16 on v8

--- a/solution.py
+++ b/solution.py
@@ -28,8 +28,8 @@
 
 
 def rows_kernel(
-    width, e_hbm, basis_hbm, owner_hbm, slot_hbm,
-    rows_hbm, mean_hbm,
+    width, me_ref, e_hbm, basis_hbm, owner_hbm, slot_hbm,
+    near_hbm, far_hbm, mean_hbm,
     owner_ref, slot_ref, mean_ref, basis_ref, e_ref, rows_ref, y_ref, yb_ref, sum_ref, total_ref, target_ref, list_ref, e_sem, small_sem, sem,
 ):
     step = pl.program_id(0)
@@ -117,44 +117,51 @@
 
         place = lax.broadcasted_iota(jnp.int32, (GROUP * CAP, LANES), 0).astype(jnp.int16)
 
-        def sort_group(g):
-            first = g * GROUP
+        half = me_ref[0] // (width // 2)
+        each = width // GROUP // 2
+
+        def sort_group(apart, q):
+            first = ((half ^ apart) * each + q) * GROUP
             pieces = []
             for c in range(chunks):
-                wanted = (target_ref[c:c + 1, :] - first * CAP).astype(jnp.int32)
+                wanted = target_ref[c:c + 1, :] - first * CAP
                 wanted = jnp.broadcast_to(wanted, (16, LANES)).astype(jnp.int16)
                 wanted = jnp.concatenate([wanted] * (GROUP * CAP // 16), 0)
                 pieces.append(jnp.where(wanted == place, jnp.ones((), jnp.bfloat16), jnp.zeros((), jnp.bfloat16)))
             pick = jnp.concatenate(pieces, 1)
             rows = jnp.dot(pick, yb_ref[...], preferred_element_type=jnp.float32).astype(jnp.bfloat16)
+            start = (apart * each + q) * (GROUP * SPAN)
             for j in range(GROUP):
-                base = pl.multiple_of((first + j) * SPAN, 16)
+                base = pl.multiple_of(start + j * SPAN, 16)
                 rows_ref[pl.ds(base, CAP), :] = rows[j * CAP:(j + 1) * CAP]
                 notes = jnp.concatenate([common, list_ref[pl.ds(first + j, 1), :]], 0)
                 rows_ref[pl.ds(pl.multiple_of(base + CAP, 16), NOTES), :] = notes.astype(jnp.bfloat16)
-            at = pl.ds(pl.multiple_of(g * (GROUP * SPAN), 16), GROUP * SPAN)
-            return pltpu.make_async_copy(rows_ref.at[at], rows_hbm.at[at], sem.at[g])
-
-        groups = width // GROUP
-        if groups <= 4:
-            copies = []
-            for g in range(groups):
-                copies.append(sort_group(g))
-                copies[g].start()
-            for copy in copies:
-                copy.wait()
-        else:
-
-            @pl.loop(0, groups)
-            def _(g):
-                copy = sort_group(g)
-                copy.start()
-                copy.wait()
-
+            here = pl.ds(pl.multiple_of(start, 16), GROUP * SPAN)
+            there = pl.ds(pl.multiple_of(q * (GROUP * SPAN), 16), GROUP * SPAN)
+            return pltpu.make_async_copy(
+                rows_ref.at[here], (near_hbm, far_hbm)[apart].at[there], sem.at[apart * each + q]
+            )
+
+        copies = []
+        for apart in (1, 0):
+            if each <= 2:
+                for q in range(each):
+                    copies.append(sort_group(apart, q))
+                    copies[-1].start()
+            else:
+
+                @pl.loop(0, each)
+                def _(q):
+                    copy = sort_group(apart, q)
+                    copy.start()
+                    copy.wait()
+
+        for copy in copies:
+            copy.wait()
         mean_copy.wait()
 
 
-def project_and_sort(width, embeddings, basis, list_owner, list_slot):
+def project_and_sort(width, me, embeddings, basis, list_owner, list_slot):
     rows_here, wide = embeddings.shape
     feats = basis.shape[1]
     lanes = rows_here // LANES
@@ -162,12 +169,10 @@
     return pl.pallas_call(
         functools.partial(rows_kernel, width),
         grid=(rows_here // CHUNK,),
-        in_specs=[pl.BlockSpec(memory_space=pl.ANY)] * 4,
-        out_specs=[pl.BlockSpec(memory_space=pl.ANY)] * 2,
-        out_shape=[
-            jax.ShapeDtypeStruct((slots, feats), jnp.bfloat16),
-            jax.ShapeDtypeStruct((1, wide), jnp.float32),
-        ],
+        in_specs=[pl.BlockSpec(memory_space=pltpu.SMEM)] + [pl.BlockSpec(memory_space=pl.ANY)] * 4,
+        out_specs=[pl.BlockSpec(memory_space=pl.ANY)] * 3,
+        out_shape=[jax.ShapeDtypeStruct((slots // 2, feats), jnp.bfloat16)] * 2
+        + [jax.ShapeDtypeStruct((1, wide), jnp.float32)],
         scratch_shapes=[
             pltpu.VMEM((lanes, LANES), jnp.int32),
             pltpu.VMEM((lanes, LANES), jnp.int32),
@@ -190,13 +195,14 @@
             flops=2 * rows_here * feats * (wide + slots), bytes_accessed=2 * rows_here * wide + 2 * slots * feats, transcendentals=0
         ),
         name="project_sort",
-    )(embeddings, basis, list_owner.reshape(lanes, LANES), list_slot.reshape(lanes, LANES))
+    )(me.reshape(1), embeddings, basis, list_owner.reshape(lanes, LANES), list_slot.reshape(lanes, LANES))
 
 
 def moments_kernel(width, me_ref, mean_hbm, e_hbm, keep_ref, send_ref, e_ref, mean_ref, m_ref, sem, mean_sem):
     rows_here, wide = e_ref.shape
     block = wide // width
     bits = width.bit_length() - 1
+    tiles = wide // TILE
     mean_copy = pltpu.make_async_copy(mean_hbm, mean_ref, mean_sem)
     mean_copy.start()
     copies = []
@@ -205,10 +211,11 @@
         copies.append(pltpu.make_async_copy(e_hbm.at[at], e_ref.at[at], sem.at[c]))
         copies[c].start()
     me = me_ref[0]
+    odd = (me & 1) == 1
     mean_copy.wait()
     mean = mean_ref[...]
-    for t in range(wide // TILE):
-        rows = slice(t * TILE, (t + 1) * TILE)
+    for t in range(tiles):
+        rows, columns = slice(t * TILE, (t + 1) * TILE), slice(t * TILE, wide)
         if t == 0:
             product = jnp.zeros((TILE, wide), jnp.float32)
             for c in range(rows_here // CHUNK):
@@ -219,12 +226,20 @@
                 )
         else:
             product = lax.dot_general(
-                e_ref[:, rows], e_ref[...], (((0,), (0,)), ((), ())), preferred_element_type=jnp.float32
+                e_ref[:, rows], e_ref[:, columns], (((0,), (0,)), ((), ())), preferred_element_type=jnp.float32
             )
         down = jnp.transpose(jnp.broadcast_to(mean[:, rows] * rows_here, (LANES, TILE)))
-        for j in range(wide // LANES):
-            across = slice(j * LANES, (j + 1) * LANES)
-            m_ref[rows, across] = product[:, across] - down * mean[:, across]
+        for u in range(t, tiles):
+            pieces = []
+            for j in range(u * TILE // LANES, (u + 1) * TILE // LANES):
+                across = slice(j * LANES, (j + 1) * LANES)
+                within = slice(j * LANES - t * TILE, (j + 1) * LANES - t * TILE)
+                pieces.append((product[:, within] - down * mean[:, across]).astype(jnp.bfloat16))
+            piece = jnp.concatenate(pieces, 1)
+            other = slice(u * TILE, (u + 1) * TILE)
+            m_ref[rows, other] = piece
+            if u > t:
+                m_ref[other, rows] = jnp.transpose(piece)
         for pair in range(TILE // block // 2):
             first = t * (TILE // block) + 2 * pair
             apart = (first ^ me) >> 1
@@ -232,10 +247,10 @@
             for k in range(bits - 1):
                 place = place + (((apart >> k) & 1) << (bits - 2 - k))
             to = pl.ds(pl.multiple_of(place * block, block), block)
-            kept = pl.multiple_of((first + (me & 1)) * block, block)
-            sent = pl.multiple_of((first + 1 - (me & 1)) * block, block)
-            keep_ref[to, :] = m_ref[pl.ds(kept, block), :]
-            send_ref[to, :] = m_ref[pl.ds(sent, block), :].astype(jnp.bfloat16)
+            even_rows = m_ref[first * block:(first + 1) * block, :]
+            odd_rows = m_ref[(first + 1) * block:(first + 2) * block, :]
+            keep_ref[to, :] = jnp.where(odd, odd_rows, even_rows)
+            send_ref[to, :] = jnp.where(odd, even_rows, odd_rows)
 
 
 def moments(width, me, embeddings, mean):
@@ -246,13 +261,13 @@
         in_specs=[pl.BlockSpec(memory_space=pltpu.SMEM)] + [pl.BlockSpec(memory_space=pl.ANY)] * 2,
         out_specs=[vmem] * 2,
         out_shape=[
-            jax.ShapeDtypeStruct((wide // 2, wide), jnp.float32),
+            jax.ShapeDtypeStruct((wide // 2, wide), jnp.bfloat16),
             jax.ShapeDtypeStruct((wide // 2, wide), jnp.bfloat16),
         ],
         scratch_shapes=[
             pltpu.VMEM((rows_here, wide), jnp.bfloat16),
             pltpu.VMEM((1, wide), jnp.float32),
-            pltpu.VMEM((wide, wide), jnp.float32),
+            pltpu.VMEM((wide, wide), jnp.bfloat16),
             pltpu.SemaphoreType.DMA((rows_here // CHUNK,)),
             pltpu.SemaphoreType.DMA,
         ],
@@ -272,7 +287,7 @@
         across = slice(h * columns, (h + 1) * columns)
         for p in range(pieces):
             at = slice(p * rows, (p + 1) * rows)
-            held = keep_ref[at, across]
+            held = keep_ref[at, across].astype(jnp.float32)
             for ref in came:
                 held = held + ref[at, across].astype(jnp.float32)
             out = outs[h * pieces + p]
@@ -335,7 +350,7 @@
     return came
 
 
-def encode_kernel(total, me_ref, got_ref, basis_ref, centroid_ref, rotation_ref, *refs):
+def encode_kernel(total, me_ref, near_ref, far_ref, basis_ref, centroid_ref, rotation_ref, *refs):
     out_hbm, between_ref, out_ref, delta_ref, list_ref, apart_ref, sem = refs[-7:]
     width = delta_ref.shape[0]
     feats = out_ref.shape[1]
@@ -344,7 +359,9 @@
     block = wide // width
     share = total // width
 
-    notes = jnp.concatenate([got_ref[s * SPAN + CAP:(s + 1) * SPAN, :] for s in range(width)], 0)
+    notes = jnp.concatenate(
+        [ref[s * SPAN + CAP:(s + 1) * SPAN, :] for ref in (near_ref, far_ref) for s in range(width // 2)], 0
+    )
     size = width * NOTES
     to = lax.broadcasted_iota(jnp.int32, (size, size), 0)
     of = lax.broadcasted_iota(jnp.int32, (size, size), 1)
@@ -373,38 +390,43 @@
 
     names = lax.broadcasted_iota(jnp.int32, (CAP, owned), 1).astype(jnp.int16)
 
-    def encode_group(g):
-        columns = jnp.transpose(list_ref[pl.ds(g * GROUP, GROUP), :])
+    half = me_ref[0] // (width // 2)
+    each = width // GROUP // 2
+
+    def encode_group(apart, q):
+        start = (apart * each + q) * GROUP
+        columns = jnp.transpose(list_ref[pl.ds(start, GROUP), :])
         hits, projected, held = [], [], []
         for s in range(GROUP):
             listed = jnp.broadcast_to(columns[:, s:s + 1], (CAP, LANES))
             held.append(jnp.concatenate([listed] * (feats // LANES), 1) >= 0)
             wanted = jnp.concatenate([listed.astype(jnp.int32).astype(jnp.int16)] * (owned // LANES), 1)
             hits.append(jnp.where(wanted == names, jnp.ones((), jnp.bfloat16), jnp.zeros((), jnp.bfloat16)))
-            base = pl.multiple_of((g * GROUP + s) * SPAN, 16)
-            rows = got_ref[pl.ds(base, CAP), :].astype(jnp.float32)
-            projected.append((rows + delta_ref[pl.ds(g * GROUP + s, 1), :]) * scale)
+            base = pl.multiple_of((q * GROUP + s) * SPAN, 16)
+            rows = (near_ref, far_ref)[apart][pl.ds(base, CAP), :].astype(jnp.float32)
+            projected.append((rows + delta_ref[pl.ds(start + s, 1), :]) * scale)
         centre = jnp.dot(jnp.concatenate(hits, 0), centroid_ref[...], preferred_element_type=jnp.float32)
         residual = jnp.where(jnp.concatenate(held, 0), jnp.concatenate(projected, 0) - centre, 0.0)
-        at = pl.ds(pl.multiple_of(g * (GROUP * CAP), GROUP * CAP), GROUP * CAP)
-        out_ref[at, :] = jnp.dot(
+        here = pl.ds(pl.multiple_of(start * CAP, GROUP * CAP), GROUP * CAP)
+        there = pl.ds(pl.multiple_of(((half ^ apart) * each + q) * (GROUP * CAP), GROUP * CAP), GROUP * CAP)
+        out_ref[here, :] = jnp.dot(
             residual.astype(jnp.bfloat16), rotation_ref[...], preferred_element_type=jnp.float32
         ).astype(jnp.bfloat16)
-        return pltpu.make_async_copy(out_ref.at[at], out_hbm.at[at], sem.at[g])
-
-    groups = width // GROUP
+        return pltpu.make_async_copy(out_ref.at[here], out_hbm.at[there], sem.at[apart * each + q])
+
     copies = []
-    if groups <= 4:
-        for g in range(groups):
-            copies.append(encode_group(g))
-            copies[g].start()
-    else:
-
-        @pl.loop(0, groups)
-        def _(g):
-            copy = encode_group(g)
-            copy.start()
-            copy.wait()
+    for apart in (0, 1):
+        if each <= 2:
+            for q in range(each):
+                copies.append(encode_group(apart, q))
+                copies[-1].start()
+        else:
+
+            @pl.loop(0, each)
+            def _(q):
+                copy = encode_group(apart, q)
+                copy.start()
+                copy.wait()
 
     first = me_ref[0] * block
     near = apart_ref[:, pl.ds(pl.multiple_of(first // LANES * LANES, LANES), LANES)]
@@ -420,14 +442,14 @@
         copy.wait()
 
 
-def encode(width, total, me, got, basis, centroids, rotation, after):
+def encode(width, total, me, near, far, basis, centroids, rotation, after):
     wide, feats = basis.shape
     owned = centroids.shape[0]
     slots = width * CAP
     vmem, anywhere = pl.BlockSpec(memory_space=pltpu.VMEM), pl.BlockSpec(memory_space=pl.ANY)
     return pl.pallas_call(
         functools.partial(encode_kernel, total),
-        in_specs=[pl.BlockSpec(memory_space=pltpu.SMEM)] + [vmem] * 4 + [anywhere] * len(after),
+        in_specs=[pl.BlockSpec(memory_space=pltpu.SMEM)] + [vmem] * 5 + [anywhere] * len(after),
         out_specs=[anywhere, vmem],
         out_shape=[
             jax.ShapeDtypeStruct((slots, feats), jnp.bfloat16),
@@ -445,7 +467,7 @@
             flops=2 * slots * feats * (owned + feats), bytes_accessed=4 * slots * feats, transcendentals=0
         ),
         name="encode",
-    )(me.reshape(1), got, basis, centroids, rotation, *after)
+    )(me.reshape(1), near, far, basis, centroids, rotation, *after)
 
 
 def local(embeddings, basis, list_owner, list_slot, centroids, rotation):
@@ -455,9 +477,19 @@
     feats = basis.shape[1]
     total = rows_here * width
 
-    rows, mean = project_and_sort(width, embeddings, basis, list_owner, list_slot)
-    got = lax.all_to_all(rows.reshape(width, SPAN, feats), "wide", split_axis=0, concat_axis=0, tiled=True)
-
+    near, far, mean = project_and_sort(width, me, embeddings, basis, list_owner, list_slot)
+    half = width // 2
+    halves = [list(range(half)), list(range(half, width))]
+
+    def spread(blocks):
+        blocks = lax.all_to_all(
+            blocks.reshape(half, SPAN, feats), "wide", split_axis=0, concat_axis=0, tiled=True, axis_index_groups=halves
+        )
+        return blocks.reshape(half * SPAN, feats)
+
+    far = lax.ppermute(far, "wide", [(i, i ^ half) for i in range(width)])
+    near = spread(near)
+    far = spread(far)
     keep, send = moments(width, me, embeddings, mean)
     stages = halving_stages(width)
     came = exchange(width, stages[0], [send])
@@ -470,7 +502,7 @@
         last.append(share)
     came = [exchange(width, stages[-1], share[1:]) for share in last]
     encoded, between = encode(
-        width, total, me, got.reshape(width * SPAN, feats), basis, centroids, rotation, [share[1] for share in last]
+        width, total, me, near, far, basis, centroids, rotation, [share[1] for share in last]
     )
     covariance = finish(total, between, [share[0] for share in last], came)
     return (encoded, covariance)

time: 57 us -> 79.8 us (1.40)
  waiting for transfers between devices: 14.8 us -> 34.1 us
  local copies, waits for them, and re-layouts: 0.02 us -> 3.6 us
  Pallas kernels: 19.5 us -> 18.2 us
  starting transfers between devices: 21.7 us -> 22.8 us
    ppermute x0 -> x1, waiting for transfers between devices: none -> 20.1 us  [local(): far = lax.ppermute(far, 'wide', [(i, i ^ half) for i in range(width)])]
    unnamed x8 -> x10, local copies, waits for them, and re-layouts: 0.02 us -> 3.6 us
    ppermute x9, starting transfers between devices: 14.3 us -> 11.4 us  [exchange(): lax.ppermute(out[p - 1], 'wide', [(i, i ^ apart) for i in range(width)])]
    ppermute x0 -> x1, starting transfers between devices: none -> 2.58 us  [local(): far = lax.ppermute(far, 'wide', [(i, i ^ half) for i in range(width)])]
    all_to_all x1 -> x2, starting transfers between devices: 7.4 us -> 8.81 us  [spread(): lax.all_to_all(blocks.reshape(half, SPAN, feats), 'wide', split_axis=0, c...]
    pallas_call x1, Pallas kernels: 7.16 us -> 5.84 us  [moments(): pl.pallas_call(functools.partial(moments_kernel, width), in_specs=[pl.Blo...]
    ppermute x9, waiting for transfers between devices: 14.8 us -> 14 us  [exchange(): lax.ppermute(out[p - 1], 'wide', [(i, i ^ apart) for i in range(width)])]
  transfers between devices with their start and end apart: 10 -> 12, of which waited for: 4 -> 4; matrix products, arithmetic and copies ran while one was open for 0% -> 0% of each run, Pallas kernels for 20% -> 13%
where the time goes in v16:
time: 79.8 us; the launch traced here: 79.4 us
  waiting for transfers between devices  34.1 us (43%)
  starting transfers between devices  22.8 us (29%)
  Pallas kernels  18.2 us (23%)
  local copies, waits for them, and re-layouts  3.6 us (5%)
    ppermute x1, waiting for transfers between devices, local(): far = lax.ppermute(far, 'wide', [(i, i ^ half) for i in range(width)])  20.1 us
    ppermute x9, waiting for transfers between devices, exchange(): lax.ppermute(out[p - 1], 'wide', [(i, i ^ apart) for i in range(width)])  14 us
    ppermute x9, starting transfers between devices, exchange(): lax.ppermute(out[p - 1], 'wide', [(i, i ^ apart) for i in range(width)])  11.4 us
    all_to_all x2, starting transfers between devices, spread(): lax.all_to_all(blocks.reshape(half, SPAN, feats), 'wide', split_axis=0, c...  8.81 us
    pallas_call x1, Pallas kernels, project_and_sort(): pl.pallas_call(functools.partial(rows_kernel, width), grid=(rows_here //...  7.25 us
    pallas_call x1, Pallas kernels, moments(): pl.pallas_call(functools.partial(moments_kernel, width), in_specs=[pl.Blo...  5.84 us
    pallas_call x1, Pallas kernels, encode(): pl.pallas_call(functools.partial(encode_kernel, total), in_specs=[pl.Bloc...  3.99 us
    unnamed x10, local copies, waits for them, and re-layouts  3.6 us
  transfers between devices with their start and end apart: 12, of which 4 were waited for; matrix products, arithmetic and copies ran while one was open for 0% of the time, Pallas kernels for 13%

profile of v16, /device:TPU:0, one launch (start us, length us, event | category | flops | bytes accessed | tf_op | source)
XLA Modules:
  0.0 79.4 jit_solution(13006767253741876428)
XLA Ops:
  0.6 7.3 %project_sort.1 = (bf16[1152,256]{1,0:T(8,128)(2,1)}, bf16[1152,256]{1,0:T(8,128)(2,1)}, f32[1,1024]{1,0:T(1,128)}) custom-call(s32[1]{0:T(128)} %bitcast.me_ref, bf16[2048,1024]{1,0:T(8,128)(2,1)} %e_hbm.3, bf16[1024,256]{1,0:T(8,128)(2,1)} %basis_ref.1, s32[16,128]{1,0:T(8,128)} %bitcast.11, s32[16,128]{1,0:T(8,128)} %bitcast.12), custom_call_target="tpu_custom_call" | custom-call | flops 3489660928 | bytes 5373952 | tf_op jit(solution)/shard_map/project_sort/pallas_call | solution.py:169
  7.9 5.3 %all-to-all-start = ((bf16[8,144,256]{2,1,0:T(8,128)(2,1)}), bf16[8,144,256]{2,1,0:T(8,128)(2,1)S(1)}, u32[]{:S(2)}, u32[]{:S(2)}) async-start(bf16[8,144,256]{2,1,0:T(8,128)(2,1)} %bitcast.10), calls=%async_computation | async-start | bytes 1179648 | tf_op jit(solution)/shard_map/all_to_all | solution.py:485
  13.2 2.6 %collective-permute-start = (bf16[1152,256]{1,0:T(8,128)(2,1)}, bf16[1152,256]{1,0:T(8,128)(2,1)S(1)}, u32[]{:S(2)}, u32[]{:S(2)}) collective-permute-start(bf16[1152,256]{1,0:T(8,128)(2,1)} %get-tuple-element.22), channel_id=1, source_target_pairs={{0,8},{1,9},{2,10},{3,11},{4,12},{5,13},{6,14},{7,15},{8,0},{9,1},... | collective-permute-start | bytes 1769480 | tf_op jit(solution)/shard_map/ppermute | solution.py:490
  15.7 0.7 copy-done.3
  16.4 5.8 %moments.1 = (bf16[512,1024]{1,0:T(8,128)(2,1)S(1)}, bf16[512,1024]{1,0:T(8,128)(2,1)}) custom-call(s32[1]{0:T(128)} %bitcast.me_ref, f32[1,1024]{1,0:T(1,128)S(1)} %copy-done.3, bf16[2048,1024]{1,0:T(8,128)(2,1)} %e_hbm.3), custom_call_target="tpu_custom_call" | custom-call | flops 4294967296 | bytes 7340032 | tf_op jit(solution)/shard_map/moments/pallas_call | solution.py:259
  22.3 0.0 copy-start.2
  22.3 0.3 collective-permute-start.1
  22.6 20.1 %collective-permute-done = bf16[1152,256]{1,0:T(8,128)(2,1)S(1)} collective-permute-done((bf16[1152,256]{1,0:T(8,128)(2,1)}, bf16[1152,256]{1,0:T(8,128)(2,1)S(1)}, u32[]{:S(2)}, u32[]{:S(2)}) %collective-permute-start) | collective-permute-done | bytes 589856 | tf_op jit(solution)/shard_map/ppermute | solution.py:490
  42.7 0.8 %copy-done.4 = bf16[1152,256]{1,0:T(8,128)(2,1)} copy-done((bf16[1152,256]{1,0:T(8,128)(2,1)}, bf16[1152,256]{1,0:T(8,128)(2,1)S(1)}, u32[]{:S(2)}) %copy-start.4) | copy-done | bytes 589848
  43.5 3.5 %all-to-all-start.1 = ((bf16[8,144,256]{2,1,0:T(8,128)(2,1)}), bf16[8,144,256]{2,1,0:T(8,128)(2,1)S(1)}, u32[]{:S(2)}, u32[]{:S(2)}) async-start(bf16[8,144,256]{2,1,0:T(8,128)(2,1)} %bitcast.9), calls=%async_computation.1 | async-start | bytes 1179648 | tf_op jit(solution)/shard_map/all_to_all | solution.py:485
  47.1 0.0 collective-permute-done.1.refs_0_
  47.1 0.2 add_and_split.3
  47.3 2.0 %collective-permute-start.2 = (bf16[256,512]{1,0:T(8,128)(2,1)S(1)}, bf16[256,512]{1,0:T(8,128)(2,1)S(1)}, u32[]{:S(2)}, u32[]{:S(2)}) collective-permute-start(bf16[256,512]{1,0:T(8,128)(2,1)S(1)} %get-tuple-element.27), channel_id=1, source_target_pairs={{0,2},{1,3},{2,0},{3,1},{4,6},{5,7},{6,4},{7,5},{8,10},{9,11},{10,... | collective-permute-start | bytes 786440 | tf_op jit(solution)/shard_map/ppermute | solution.py:349
  49.3 0.1 collective-permute-start.3
  49.4 13.2 %collective-permute-done.2.refs_0_ = bf16[256,512]{1,0:T(8,128)(2,1)S(1)} collective-permute-done((bf16[256,512]{1,0:T(8,128)(2,1)S(1)}, bf16[256,512]{1,0:T(8,128)(2,1)S(1)}, u32[]{:S(2)}, u32[]{:S(2)}) %collective-permute-start.2) | collective-permute-done | bytes 262176 | tf_op jit(solution)/shard_map/ppermute | solution.py:349
  62.7 1.5 %collective-permute-start.5 = (bf16[64,512]{1,0:T(8,128)(2,1)S(1)}, bf16[64,512]{1,0:T(8,128)(2,1)S(1)}, u32[]{:S(2)}, u32[]{:S(2)}) collective-permute-start(bf16[64,512]{1,0:T(8,128)(2,1)S(1)} %get-tuple-element.35), channel_id=1, source_target_pairs={{0,4},{1,5},{2,6},{3,7},{4,0},{5,1},{6,2},{7,3},{8,12},{9,13},{10,... | collective-permute-start | bytes 196616 | tf_op jit(solution)/shard_map/ppermute | solution.py:349
  64.2 3.0 %collective-permute-start.6 = (bf16[64,512]{1,0:T(8,128)(2,1)S(1)}, bf16[64,512]{1,0:T(8,128)(2,1)S(1)}, u32[]{:S(2)}, u32[]{:S(2)}) collective-permute-start(bf16[64,512]{1,0:T(8,128)(2,1)S(1)} %get-tuple-element.36), channel_id=1, source_target_pairs={{0,12},{1,13},{2,14},{3,15},{4,8},{5,9},{6,10},{7,11},{8,4},{9,5},... | collective-permute-start | bytes 196616 | tf_op jit(solution)/shard_map/ppermute | solution.py:349
  67.2 0.0 collective-permute-start.4
  67.2 0.6 collective-permute-done.3.refs_0_
  67.8 1.6 %collective-permute-start.8 = (bf16[64,512]{1,0:T(8,128)(2,1)S(1)}, bf16[64,512]{1,0:T(8,128)(2,1)S(1)}, u32[]{:S(2)}, u32[]{:S(2)}) collective-permute-start(bf16[64,512]{1,0:T(8,128)(2,1)S(1)} %get-tuple-element.38), channel_id=1, source_target_pairs={{0,4},{1,5},{2,6},{3,7},{4,0},{5,1},{6,2},{7,3},{8,12},{9,13},{10,... | collective-permute-start | bytes 196616 | tf_op jit(solution)/shard_map/ppermute | solution.py:349
  69.4 2.9 %collective-permute-start.9 = (bf16[64,512]{1,0:T(8,128)(2,1)S(1)}, bf16[64,512]{1,0:T(8,128)(2,1)S(1)}, u32[]{:S(2)}, u32[]{:S(2)}) collective-permute-start(bf16[64,512]{1,0:T(8,128)(2,1)S(1)} %get-tuple-element.39), channel_id=1, source_target_pairs={{0,12},{1,13},{2,14},{3,15},{4,8},{5,9},{6,10},{7,11},{8,4},{9,5},... | collective-permute-start | bytes 196616 | tf_op jit(solution)/shard_map/ppermute | solution.py:349
  72.3 0.0 collective-permute-done.5.refs_2_
  72.3 0.0 collective-permute-start.7
  72.3 0.0 all-to-all-done.1
  72.3 0.0 copy-start
  72.3 1.0 %copy-done = bf16[1024,256]{1,0:T(8,128)(2,1)S(1)} copy-done((bf16[1024,256]{1,0:T(8,128)(2,1)S(1)}, bf16[1024,256]{1,0:T(8,128)(2,1)}, u32[]{:S(2)}) %copy-start) | copy-done | bytes 524312
  73.4 1.0 %copy-done.1 = bf16[1024,256]{1,0:T(8,128)(2,1)S(1)} copy-done((bf16[1024,256]{1,0:T(8,128)(2,1)S(1)}, bf16[1024,256]{1,0:T(8,128)(2,1)}, u32[]{:S(2)}) %copy-start.1) | copy-done | bytes 524312
  74.4 4.0 %encode.1 = (bf16[2048,256]{1,0:T(8,128)(2,1)}, f32[64,1024]{1,0:T(8,128)S(1)}) custom-call(s32[1]{0:T(128)} %bitcast.me_ref, bf16[1152,256]{1,0:T(8,128)(2,1)S(1)} %bitcast.7, bf16[1152,256]{1,0:T(8,128)(2,1)S(1)} %bitcast.8, bf16[1024,256]{1,0:T(8,128)(2,1)S(1)} %copy-done, bf16[1024,256]{1,0:T(8,128)(2,1)S(1)} %copy-done.1, ...), custom_call_target="tpu_custom_call" | custom-call | flops 1342177280 | bytes 2097152 | tf_op jit(solution)/shard_map/encode/pallas_call | solution.py:450
  78.4 0.0 collective-permute-done.6.refs_3_
  78.4 0.0 collective-permute-done.4.refs_1_
  78.5 0.2 collective-permute-done.7.refs_5_
  78.7 0.8 finish.1
  (9 shorter events, 0.1 us)
Async XLA Ops:
  7.9 34.8 %all-to-all-start = ((bf16[8,144,256]{2,1,0:T(8,128)(2,1)}), bf16[8,144,256]{2,1,0:T(8,128)(2,1)S(1)}, u32[]{:S(2)}, u32[]{:S(2)}) async-start(bf16[8,144,256]{2,1,0:T(8,128)(2,1)} %bitcast.10), calls=%async_computation | async-start | bytes 1179648 | tf_op jit(solution)/shard_map/all_to_all | solution.py:485
  13.2 29.5 %collective-permute-start = (bf16[1152,256]{1,0:T(8,128)(2,1)}, bf16[1152,256]{1,0:T(8,128)(2,1)S(1)}, u32[]{:S(2)}, u32[]{:S(2)}) collective-permute-start(bf16[1152,256]{1,0:T(8,128)(2,1)} %get-tuple-element.22), channel_id=1, source_target_pairs={{0,8},{1,9},{2,10},{3,11},{4,12},{5,13},{6,14},{7,15},{8,0},{9,1},... | collective-permute-start | bytes 1769480 | tf_op jit(solution)/shard_map/ppermute | solution.py:490
  15.7 0.7 copy-start.3
  22.3 50.1 %copy-start.2 = (bf16[256,256]{1,0:T(8,128)(2,1)S(1)}, bf16[256,256]{1,0:T(8,128)(2,1)}, u32[]{:S(2)}) copy-start(bf16[256,256]{1,0:T(8,128)(2,1)} %rotation_ref.1) | copy-start | bytes 393220
  22.3 24.8 %collective-permute-start.1 = (bf16[512,1024]{1,0:T(8,128)(2,1)}, bf16[512,1024]{1,0:T(8,128)(2,1)S(1)}, u32[]{:S(2)}, u32[]{:S(2)}) collective-permute-start(bf16[512,1024]{1,0:T(8,128)(2,1)} %get-tuple-element.25), channel_id=1, source_target_pairs={{0,1},{1,0},{2,3},{3,2},{4,5},{5,4},{6,7},{7,6},{8,9},{9,8},{10,11... | collective-permute-start | bytes 3145736 | tf_op jit(solution)/shard_map/ppermute | solution.py:349
  42.7 0.8 %copy-start.4 = (bf16[1152,256]{1,0:T(8,128)(2,1)}, bf16[1152,256]{1,0:T(8,128)(2,1)S(1)}, u32[]{:S(2)}) copy-start(bf16[1152,256]{1,0:T(8,128)(2,1)S(1)} %collective-permute-done) | copy-start | bytes 1769476
  43.5 28.8 %all-to-all-start.1 = ((bf16[8,144,256]{2,1,0:T(8,128)(2,1)}), bf16[8,144,256]{2,1,0:T(8,128)(2,1)S(1)}, u32[]{:S(2)}, u32[]{:S(2)}) async-start(bf16[8,144,256]{2,1,0:T(8,128)(2,1)} %bitcast.9), calls=%async_computation.1 | async-start | bytes 1179648 | tf_op jit(solution)/shard_map/all_to_all | solution.py:485
  47.3 15.3 %collective-permute-start.2 = (bf16[256,512]{1,0:T(8,128)(2,1)S(1)}, bf16[256,512]{1,0:T(8,128)(2,1)S(1)}, u32[]{:S(2)}, u32[]{:S(2)}) collective-permute-start(bf16[256,512]{1,0:T(8,128)(2,1)S(1)} %get-tuple-element.27), channel_id=1, source_target_pairs={{0,2},{1,3},{2,0},{3,1},{4,6},{5,7},{6,4},{7,5},{8,10},{9,11},{10,... | collective-permute-start | bytes 786440 | tf_op jit(solution)/shard_map/ppermute | solution.py:349
  49.3 18.5 %collective-permute-start.3 = (bf16[256,512]{1,0:T(8,128)(2,1)S(1)}, bf16[256,512]{1,0:T(8,128)(2,1)S(1)}, u32[]{:S(2)}, u32[]{:S(2)}) collective-permute-start(bf16[256,512]{1,0:T(8,128)(2,1)S(1)} %get-tuple-element.30), channel_id=1, source_target_pairs={{0,2},{1,3},{2,0},{3,1},{4,6},{5,7},{6,4},{7,5},{8,10},{9,11},{10,... | collective-permute-start | bytes 786440 | tf_op jit(solution)/shard_map/ppermute | solution.py:349
  62.7 9.7 %collective-permute-start.5 = (bf16[64,512]{1,0:T(8,128)(2,1)S(1)}, bf16[64,512]{1,0:T(8,128)(2,1)S(1)}, u32[]{:S(2)}, u32[]{:S(2)}) collective-permute-start(bf16[64,512]{1,0:T(8,128)(2,1)S(1)} %get-tuple-element.35), channel_id=1, source_target_pairs={{0,4},{1,5},{2,6},{3,7},{4,0},{5,1},{6,2},{7,3},{8,12},{9,13},{10,... | collective-permute-start | bytes 196616 | tf_op jit(solution)/shard_map/ppermute | solution.py:349
  64.2 14.2 %collective-permute-start.6 = (bf16[64,512]{1,0:T(8,128)(2,1)S(1)}, bf16[64,512]{1,0:T(8,128)(2,1)S(1)}, u32[]{:S(2)}, u32[]{:S(2)}) collective-permute-start(bf16[64,512]{1,0:T(8,128)(2,1)S(1)} %get-tuple-element.36), channel_id=1, source_target_pairs={{0,12},{1,13},{2,14},{3,15},{4,8},{5,9},{6,10},{7,11},{8,4},{9,5},... | collective-permute-start | bytes 196616 | tf_op jit(solution)/shard_map/ppermute | solution.py:349
  67.2 11.3 %collective-permute-start.4 = (bf16[64,512]{1,0:T(8,128)(2,1)S(1)}, bf16[64,512]{1,0:T(8,128)(2,1)S(1)}, u32[]{:S(2)}, u32[]{:S(2)}) collective-permute-start(bf16[64,512]{1,0:T(8,128)(2,1)S(1)} %get-tuple-element.28.refs_0_), channel_id=1, source_target_pairs={{0,8},{1,9},{2,10},{3,11},{4,12},{5,13},{6,14},{7,15},{8,0},{9,1},... | collective-permute-start | bytes 196616 | tf_op jit(solution)/shard_map/ppermute | solution.py:349
  67.8 10.6 %collective-permute-start.8 = (bf16[64,512]{1,0:T(8,128)(2,1)S(1)}, bf16[64,512]{1,0:T(8,128)(2,1)S(1)}, u32[]{:S(2)}, u32[]{:S(2)}) collective-permute-start(bf16[64,512]{1,0:T(8,128)(2,1)S(1)} %get-tuple-element.38), channel_id=1, source_target_pairs={{0,4},{1,5},{2,6},{3,7},{4,0},{5,1},{6,2},{7,3},{8,12},{9,13},{10,... | collective-permute-start | bytes 196616 | tf_op jit(solution)/shard_map/ppermute | solution.py:349
  69.4 9.1 %collective-permute-start.9 = (bf16[64,512]{1,0:T(8,128)(2,1)S(1)}, bf16[64,512]{1,0:T(8,128)(2,1)S(1)}, u32[]{:S(2)}, u32[]{:S(2)}) collective-permute-start(bf16[64,512]{1,0:T(8,128)(2,1)S(1)} %get-tuple-element.39), channel_id=1, source_target_pairs={{0,12},{1,13},{2,14},{3,15},{4,8},{5,9},{6,10},{7,11},{8,4},{9,5},... | collective-permute-start | bytes 196616 | tf_op jit(solution)/shard_map/ppermute | solution.py:349
  72.3 6.3 %collective-permute-start.7 = (bf16[64,512]{1,0:T(8,128)(2,1)S(1)}, bf16[64,512]{1,0:T(8,128)(2,1)S(1)}, u32[]{:S(2)}, u32[]{:S(2)}) collective-permute-start(bf16[64,512]{1,0:T(8,128)(2,1)S(1)} %get-tuple-element.31.refs_1_), channel_id=1, source_target_pairs={{0,8},{1,9},{2,10},{3,11},{4,12},{5,13},{6,14},{7,15},{8,0},{9,1},... | collective-permute-start | bytes 196616 | tf_op jit(solution)/shard_map/ppermute | solution.py:349
  72.3 1.0 %copy-start = (bf16[1024,256]{1,0:T(8,128)(2,1)S(1)}, bf16[1024,256]{1,0:T(8,128)(2,1)}, u32[]{:S(2)}) copy-start(bf16[1024,256]{1,0:T(8,128)(2,1)} %basis_ref.1) | copy-start | bytes 1572868
  73.4 1.0 %copy-start.1 = (bf16[1024,256]{1,0:T(8,128)(2,1)S(1)}, bf16[1024,256]{1,0:T(8,128)(2,1)}, u32[]{:S(2)}) copy-start(bf16[1024,256]{1,0:T(8,128)(2,1)} %centroid_ref.1) | copy-start | bytes 1572868

commit v17 on v16

--- a/solution.py
+++ b/solution.py
@@ -27,10 +27,89 @@
     return high, middle, (rest - middle).astype(jnp.bfloat16).astype(jnp.float32)
 
 
+def sort_half(half, yb_ref, target_ref, list_ref, notes_ref, rows_ref, rows_hbm, sem):
+    chunks = target_ref.shape[0]
+    groups = rows_ref.shape[0] // (GROUP * SPAN)
+    place = lax.broadcasted_iota(jnp.int32, (GROUP * CAP, LANES), 0).astype(jnp.int16)
+
+    def sort_group(g):
+        first = (half * groups + g) * GROUP
+        pieces = []
+        for c in range(chunks):
+            wanted = target_ref[c:c + 1, :] - first * CAP
+            wanted = jnp.broadcast_to(wanted, (16, LANES)).astype(jnp.int16)
+            wanted = jnp.concatenate([wanted] * (GROUP * CAP // 16), 0)
+            pieces.append(jnp.where(wanted == place, jnp.ones((), jnp.bfloat16), jnp.zeros((), jnp.bfloat16)))
+        pick = jnp.concatenate(pieces, 1)
+        rows = jnp.dot(pick, yb_ref[...], preferred_element_type=jnp.float32).astype(jnp.bfloat16)
+        for j in range(GROUP):
+            base = pl.multiple_of((g * GROUP + j) * SPAN, 16)
+            rows_ref[pl.ds(base, CAP), :] = rows[j * CAP:(j + 1) * CAP]
+            notes = jnp.concatenate([notes_ref[:NOTES - 1, :], list_ref[pl.ds(first + j, 1), :]], 0)
+            rows_ref[pl.ds(pl.multiple_of(base + CAP, 16), NOTES), :] = notes.astype(jnp.bfloat16)
+        at = pl.ds(pl.multiple_of(g * (GROUP * SPAN), 16), GROUP * SPAN)
+        return pltpu.make_async_copy(rows_ref.at[at], rows_hbm.at[at], sem.at[g])
+
+    if groups <= 4:
+        copies = []
+        for g in range(groups):
+            copies.append(sort_group(g))
+            copies[g].start()
+        for copy in copies:
+            copy.wait()
+    else:
+
+        @pl.loop(0, groups)
+        def _(g):
+            copy = sort_group(g)
+            copy.start()
+            copy.wait()
+
+
+def near_kernel(me_ref, yb_ref, target_ref, list_ref, notes_ref, near_hbm, sorted_ref, rows_ref, sem):
+    sorted_ref[...] = jnp.zeros_like(sorted_ref)
+    half = me_ref[0] // (list_ref.shape[0] // 2)
+    sort_half(half, yb_ref, target_ref, list_ref, notes_ref, rows_ref, near_hbm, sem)
+
+
+def sort_near(me, yb, targets, lists, notes):
+    rows_here, feats = yb.shape
+    slots = lists.shape[0] // 2 * SPAN
+    vmem, anywhere = pl.BlockSpec(memory_space=pltpu.VMEM), pl.BlockSpec(memory_space=pl.ANY)
+    return pl.pallas_call(
+        near_kernel,
+        in_specs=[pl.BlockSpec(memory_space=pltpu.SMEM)] + [vmem] * 4,
+        out_specs=[anywhere, vmem],
+        out_shape=[jax.ShapeDtypeStruct((slots, feats), jnp.bfloat16), jax.ShapeDtypeStruct((8, LANES), jnp.float32)],
+        scratch_shapes=[pltpu.VMEM((slots, feats), jnp.bfloat16), pltpu.SemaphoreType.DMA((slots // (GROUP * SPAN),))],
+        compiler_params=pltpu.CompilerParams(vmem_limit_bytes=VMEM_ALL),
+        cost_estimate=pl.CostEstimate(
+            flops=2 * rows_here * feats * slots, bytes_accessed=2 * (rows_here + slots) * feats, transcendentals=0
+        ),
+        name="sort_near",
+    )(me.reshape(1), yb, targets, lists, notes)
+
+
+def tie_kernel(*refs):
+    pass
+
+
+def tie(x, after):
+    anywhere = pl.BlockSpec(memory_space=pl.ANY)
+    return pl.pallas_call(
+        tie_kernel,
+        in_specs=[anywhere] * (1 + len(after)),
+        out_specs=anywhere,
+        out_shape=jax.ShapeDtypeStruct(x.shape, x.dtype),
+        input_output_aliases={0: 0},
+        name="tie",
+    )(x, *after)
+
+
 def rows_kernel(
     width, me_ref, e_hbm, basis_hbm, owner_hbm, slot_hbm,
-    near_hbm, far_hbm, mean_hbm,
-    owner_ref, slot_ref, mean_ref, basis_ref, e_ref, rows_ref, y_ref, yb_ref, sum_ref, total_ref, target_ref, list_ref, e_sem, small_sem, sem,
+    far_hbm, mean_hbm, yb_hbm, target_hbm, list_hbm, notes_hbm,
+    owner_ref, slot_ref, mean_ref, basis_ref, e_ref, rows_ref, y_ref, yb_ref, sum_ref, total_ref, target_ref, list_ref, notes_ref, e_sem, small_sem, sem,
 ):
     step = pl.program_id(0)
     rows_here, feats = y_ref.shape
@@ -113,55 +192,22 @@
         mean_copy.start()
         parts = in_three(mean)
         common = [part[:, q * feats:(q + 1) * feats] for part in parts for q in range(wide // feats)]
-        common = jnp.concatenate(common + list(in_three(jnp.sum(square, 0, keepdims=True))), 0)
-
-        place = lax.broadcasted_iota(jnp.int32, (GROUP * CAP, LANES), 0).astype(jnp.int16)
-
-        half = me_ref[0] // (width // 2)
-        each = width // GROUP // 2
-
-        def sort_group(apart, q):
-            first = ((half ^ apart) * each + q) * GROUP
-            pieces = []
-            for c in range(chunks):
-                wanted = target_ref[c:c + 1, :] - first * CAP
-                wanted = jnp.broadcast_to(wanted, (16, LANES)).astype(jnp.int16)
-                wanted = jnp.concatenate([wanted] * (GROUP * CAP // 16), 0)
-                pieces.append(jnp.where(wanted == place, jnp.ones((), jnp.bfloat16), jnp.zeros((), jnp.bfloat16)))
-            pick = jnp.concatenate(pieces, 1)
-            rows = jnp.dot(pick, yb_ref[...], preferred_element_type=jnp.float32).astype(jnp.bfloat16)
-            start = (apart * each + q) * (GROUP * SPAN)
-            for j in range(GROUP):
-                base = pl.multiple_of(start + j * SPAN, 16)
-                rows_ref[pl.ds(base, CAP), :] = rows[j * CAP:(j + 1) * CAP]
-                notes = jnp.concatenate([common, list_ref[pl.ds(first + j, 1), :]], 0)
-                rows_ref[pl.ds(pl.multiple_of(base + CAP, 16), NOTES), :] = notes.astype(jnp.bfloat16)
-            here = pl.ds(pl.multiple_of(start, 16), GROUP * SPAN)
-            there = pl.ds(pl.multiple_of(q * (GROUP * SPAN), 16), GROUP * SPAN)
-            return pltpu.make_async_copy(
-                rows_ref.at[here], (near_hbm, far_hbm)[apart].at[there], sem.at[apart * each + q]
-            )
-
-        copies = []
-        for apart in (1, 0):
-            if each <= 2:
-                for q in range(each):
-                    copies.append(sort_group(apart, q))
-                    copies[-1].start()
-            else:
-
-                @pl.loop(0, each)
-                def _(q):
-                    copy = sort_group(apart, q)
-                    copy.start()
-                    copy.wait()
-
+        common = common + list(in_three(jnp.sum(square, 0, keepdims=True)))
+        notes_ref[:NOTES - 1, :] = jnp.concatenate(common, 0)
+        notes_ref[NOTES - 1:, :] = jnp.zeros((1, feats), jnp.float32)
+        copies = [mean_copy]
+        for n, (ref, hbm) in enumerate(
+            ((yb_ref, yb_hbm), (target_ref, target_hbm), (list_ref, list_hbm), (notes_ref, notes_hbm))
+        ):
+            copies.append(pltpu.make_async_copy(ref, hbm, small_sem.at[4 + n]))
+            copies[-1].start()
+        other = 1 - me_ref[0] // (width // 2)
+        sort_half(other, yb_ref, target_ref, list_ref, notes_ref, rows_ref, far_hbm, sem)
         for copy in copies:
             copy.wait()
-        mean_copy.wait()
-
-
-def project_and_sort(width, me, embeddings, basis, list_owner, list_slot):
+
+
+def project_and_sort_far(width, me, embeddings, basis, list_owner, list_slot):
     rows_here, wide = embeddings.shape
     feats = basis.shape[1]
     lanes = rows_here // LANES
@@ -170,25 +216,32 @@
         functools.partial(rows_kernel, width),
         grid=(rows_here // CHUNK,),
         in_specs=[pl.BlockSpec(memory_space=pltpu.SMEM)] + [pl.BlockSpec(memory_space=pl.ANY)] * 4,
-        out_specs=[pl.BlockSpec(memory_space=pl.ANY)] * 3,
-        out_shape=[jax.ShapeDtypeStruct((slots // 2, feats), jnp.bfloat16)] * 2
-        + [jax.ShapeDtypeStruct((1, wide), jnp.float32)],
+        out_specs=[pl.BlockSpec(memory_space=pl.ANY)] * 6,
+        out_shape=[
+            jax.ShapeDtypeStruct((slots // 2, feats), jnp.bfloat16),
+            jax.ShapeDtypeStruct((1, wide), jnp.float32),
+            jax.ShapeDtypeStruct((rows_here, feats), jnp.bfloat16),
+            jax.ShapeDtypeStruct((lanes, LANES), jnp.int32),
+            jax.ShapeDtypeStruct((width, 2 * CAP), jnp.float32),
+            jax.ShapeDtypeStruct((NOTES, feats), jnp.float32),
+        ],
         scratch_shapes=[
             pltpu.VMEM((lanes, LANES), jnp.int32),
             pltpu.VMEM((lanes, LANES), jnp.int32),
             pltpu.VMEM((1, wide), jnp.float32),
             pltpu.VMEM((wide, feats), jnp.bfloat16),
             pltpu.VMEM((rows_here, wide), jnp.bfloat16),
-            pltpu.VMEM((slots, feats), jnp.bfloat16),
+            pltpu.VMEM((slots // 2, feats), jnp.bfloat16),
             pltpu.VMEM((rows_here, feats), jnp.float32),
             pltpu.VMEM((rows_here, feats), jnp.bfloat16),
             pltpu.VMEM((8, feats), jnp.float32),
             pltpu.VMEM((8, wide), jnp.float32),
             pltpu.VMEM((lanes, LANES), jnp.int32),
             pltpu.VMEM((width, 2 * CAP), jnp.float32),
+            pltpu.VMEM((NOTES, feats), jnp.float32),
             pltpu.SemaphoreType.DMA((rows_here // CHUNK,)),
-            pltpu.SemaphoreType.DMA((4,)),
-            pltpu.SemaphoreType.DMA((width // GROUP,)),
+            pltpu.SemaphoreType.DMA((8,)),
+            pltpu.SemaphoreType.DMA((width // GROUP // 2,)),
         ],
         compiler_params=pltpu.CompilerParams(vmem_limit_bytes=VMEM_ALL),
         cost_estimate=pl.CostEstimate(
@@ -198,7 +251,7 @@
     )(me.reshape(1), embeddings, basis, list_owner.reshape(lanes, LANES), list_slot.reshape(lanes, LANES))
 
 
-def moments_kernel(width, me_ref, mean_hbm, e_hbm, keep_ref, send_ref, e_ref, mean_ref, m_ref, sem, mean_sem):
+def moments_kernel(width, me_ref, mean_hbm, e_hbm, after_hbm, keep_ref, send_ref, e_ref, mean_ref, m_ref, sem, mean_sem):
     rows_here, wide = e_ref.shape
     block = wide // width
     bits = width.bit_length() - 1
@@ -253,12 +306,12 @@
             send_ref[to, :] = jnp.where(odd, even_rows, odd_rows)
 
 
-def moments(width, me, embeddings, mean):
+def moments(width, me, embeddings, mean, after):
     rows_here, wide = embeddings.shape
     vmem = pl.BlockSpec(memory_space=pltpu.VMEM)
     return pl.pallas_call(
         functools.partial(moments_kernel, width),
-        in_specs=[pl.BlockSpec(memory_space=pltpu.SMEM)] + [pl.BlockSpec(memory_space=pl.ANY)] * 2,
+        in_specs=[pl.BlockSpec(memory_space=pltpu.SMEM)] + [pl.BlockSpec(memory_space=pl.ANY)] * 3,
         out_specs=[vmem] * 2,
         out_shape=[
             jax.ShapeDtypeStruct((wide // 2, wide), jnp.bfloat16),
@@ -276,12 +329,12 @@
             flops=2 * rows_here * wide * wide, bytes_accessed=2 * rows_here * wide + 3 * wide * wide, transcendentals=0
         ),
         name="moments",
-    )(me.reshape(1), mean, embeddings)
-
-
-def add_kernel(shares, pieces, keep_ref, *refs):
+    )(me.reshape(1), mean, embeddings, after)
+
+
+def add_kernel(shares, pieces, arrived, keep_ref, *refs):
     outs = refs[len(refs) - shares * pieces:]
-    came = refs[:len(refs) - shares * pieces]
+    came = refs[:arrived]
     rows, columns = outs[0].shape
     for h in range(shares):
         across = slice(h * columns, (h + 1) * columns)
@@ -294,20 +347,20 @@
             out[...] = held.astype(out.dtype)
 
 
-def add_and_split(keep, came, shares, pieces):
+def add_and_split(keep, came, shares, pieces, after=()):
     rows, columns = keep.shape
     vmem = pl.BlockSpec(memory_space=pltpu.VMEM)
     shape = (rows // pieces, columns // shares)
     kinds = [jnp.float32] + [jnp.bfloat16] * (pieces - 1)
     outs = pl.pallas_call(
-        functools.partial(add_kernel, shares, pieces),
-        in_specs=[vmem] * (1 + len(came)),
+        functools.partial(add_kernel, shares, pieces, len(came)),
+        in_specs=[vmem] * (1 + len(came)) + [pl.BlockSpec(memory_space=pl.ANY)] * len(after),
         out_specs=[vmem] * (shares * pieces),
         out_shape=[jax.ShapeDtypeStruct(shape, kind) for kind in kinds * shares],
         compiler_params=pltpu.CompilerParams(vmem_limit_bytes=VMEM_SOME),
         cost_estimate=pl.CostEstimate(flops=2 * rows * columns, bytes_accessed=10 * rows * columns, transcendentals=0),
         name="add_and_split",
-    )(keep, *came)
+    )(keep, *came, *after)
     return [outs[h * pieces:(h + 1) * pieces] for h in range(shares)]
 
 
@@ -477,7 +530,7 @@
     feats = basis.shape[1]
     total = rows_here * width
 
-    near, far, mean = project_and_sort(width, me, embeddings, basis, list_owner, list_slot)
+    far, mean, *rest = project_and_sort_far(width, me, embeddings, basis, list_owner, list_slot)
     half = width // 2
     halves = [list(range(half)), list(range(half, width))]
 
@@ -488,18 +541,22 @@
         return blocks.reshape(half * SPAN, feats)
 
     far = lax.ppermute(far, "wide", [(i, i ^ half) for i in range(width)])
+    near, near_sorted = sort_near(me, *rest)
     near = spread(near)
-    far = spread(far)
-    keep, send = moments(width, me, embeddings, mean)
+    keep, send = moments(width, me, embeddings, mean, near_sorted)
     stages = halving_stages(width)
     came = exchange(width, stages[0], [send])
     shares = add_and_split(keep, came, SHARES, 1 << len(stages[1]))
-    last = []
+    last, after = [], []
     for share in shares:
         for n in range(1, len(stages) - 1):
             came = exchange(width, stages[n], share[1:])
-            (share,) = add_and_split(share[0], came, 1, 1 << len(stages[n + 1]))
+            (share,) = add_and_split(share[0], came, 1, 1 << len(stages[n + 1]), after)
         last.append(share)
+        if not after:
+            far = tie(far, [share[1]])
+            after = [far]
+    far = spread(far)
     came = [exchange(width, stages[-1], share[1:]) for share in last]
     encoded, between = encode(
         width, total, me, near, far, basis, centroids, rotation, [share[1] for share in last]

time: 79.8 us -> 87.9 us (1.10)
  local copies, waits for them, and re-layouts: 3.6 us -> 8.82 us
  Pallas kernels: 18.2 us -> 21.3 us
  waiting for transfers between devices: 34.1 us -> 31.9 us
  starting transfers between devices: 22.8 us -> 24.5 us
    ppermute x1, waiting for transfers between devices: 20.1 us -> 14.7 us  [local(): far = lax.ppermute(far, 'wide', [(i, i ^ half) for i in range(width)])]
    unnamed x10 -> x22, local copies, waits for them, and re-layouts: 3.6 us -> 8.82 us
    ppermute x9, waiting for transfers between devices: 14 us -> 17.2 us  [exchange(): lax.ppermute(out[p - 1], 'wide', [(i, i ^ apart) for i in range(width)])]
    pallas_call x4 -> x6, Pallas kernels: 7.57 us -> 10.7 us  [the longest x1 6.45 us: project_and_sort_far(): pl.pallas_call(functools.partial(rows_kernel, width), grid=(rows_here //...]
    ppermute x9, starting transfers between devices: 11.4 us -> 13.5 us  [exchange(): lax.ppermute(out[p - 1], 'wide', [(i, i ^ apart) for i in range(width)])]
  transfers between devices with their start and end apart: 12 -> 12, of which waited for: 4 -> 3; matrix products, arithmetic and copies ran while one was open for 0% -> 0% of each run, Pallas kernels for 13% -> 5%
where the time goes in v17:
time: 87.9 us; the launch traced here: 87.3 us
  waiting for transfers between devices  31.9 us (36%)
  starting transfers between devices  24.5 us (28%)
  Pallas kernels  21.3 us (24%)
  local copies, waits for them, and re-layouts  8.82 us (10%)
    ppermute x9, waiting for transfers between devices, exchange(): lax.ppermute(out[p - 1], 'wide', [(i, i ^ apart) for i in range(width)])  17.2 us
    ppermute x1, waiting for transfers between devices, local(): far = lax.ppermute(far, 'wide', [(i, i ^ half) for i in range(width)])  14.7 us
    ppermute x9, starting transfers between devices, exchange(): lax.ppermute(out[p - 1], 'wide', [(i, i ^ apart) for i in range(width)])  13.5 us
    unnamed x22, local copies, waits for them, and re-layouts  8.82 us
    all_to_all x2, starting transfers between devices, spread(): lax.all_to_all(blocks.reshape(half, SPAN, feats), 'wide', split_axis=0, c...  8.43 us
    pallas_call x1, Pallas kernels, project_and_sort_far(): pl.pallas_call(functools.partial(rows_kernel, width), grid=(rows_here //...  6.45 us
    pallas_call x1, Pallas kernels, moments(): pl.pallas_call(functools.partial(moments_kernel, width), in_specs=[pl.Blo...  5.85 us
    pallas_call x1, Pallas kernels, encode(): pl.pallas_call(functools.partial(encode_kernel, total), in_specs=[pl.Bloc...  3.99 us
  transfers between devices with their start and end apart: 12, of which 3 were waited for; matrix products, arithmetic and copies ran while one was open for 0% of the time, Pallas kernels for 5%

profile of v17, /device:TPU:0, one launch (start us, length us, event | category | flops | bytes accessed | tf_op | source)
XLA Modules:
  0.0 87.3 jit_solution(15417821958990472609)
XLA Ops:
  0.6 6.4 %project_sort.1 = (bf16[1152,256]{1,0:T(8,128)(2,1)}, f32[1,1024]{1,0:T(1,128)}, bf16[2048,256]{1,0:T(8,128)(2,1)}, s32[16,128]{1,0:T(8,128)}, f32[16,256]{1,0:T(8,128)}, /*index=5*/f32[16,256]{1,0:T(8,128)}) custom-call(s32[1]{0:T(128)} %bitcast.me_ref, bf16[2048,1024]{1,0:T(8,128)(2,1)} %e_hbm.3, bf16[1024,256]{1,0:T(8,128)(2,1)} %basis_ref.1, ...), custom_call_target="tpu_custom_call" | custom-call | flops 3489660928 | bytes 5373952 | tf_op jit(solution)/shard_map/project_sort/pallas_call | solution.py:215
  7.1 3.9 %sort_near.1 = (bf16[1152,256]{1,0:T(8,128)(2,1)}, f32[8,128]{1,0:T(8,128)}) custom-call(s32[1]{0:T(128)} %bitcast.me_ref, bf16[2048,256]{1,0:T(8,128)(2,1)} %get-tuple-element.26.yb_ref, s32[16,128]{1,0:T(8,128)} %get-tuple-element.27.target_ref, f32[16,256]{1,0:T(8,128)} %get-tuple-element.28.list_ref, f32[16,256]{1,0:T(8,128)} %get-tuple-element.29.notes_ref), custom_call_target="tpu_custom_call" | custom-call | flops 1207959552 | bytes 1638400 | tf_op jit(solution)/shard_map/sort_near/pallas_call | solution.py:79
  11.0 0.7 copy-done.9
  11.7 5.9 %moments.1 = (bf16[512,1024]{1,0:T(8,128)(2,1)S(1)}, bf16[512,1024]{1,0:T(8,128)(2,1)}) custom-call(s32[1]{0:T(128)} %bitcast.me_ref, f32[1,1024]{1,0:T(1,128)S(1)} %copy-done.10, bf16[2048,1024]{1,0:T(8,128)(2,1)} %e_hbm.3, f32[8,128]{1,0:T(8,128)S(1)} %copy-done.9), custom_call_target="tpu_custom_call" | custom-call | flops 4294967296 | bytes 7340032 | tf_op jit(solution)/shard_map/moments/pallas_call | solution.py:312
  17.6 0.6 collective-permute-start.1
  18.1 4.9 %all-to-all-start = ((bf16[8,144,256]{2,1,0:T(8,128)(2,1)}), bf16[8,144,256]{2,1,0:T(8,128)(2,1)S(1)}, u32[]{:S(2)}, u32[]{:S(2)}) async-start(bf16[8,144,256]{2,1,0:T(8,128)(2,1)} %bitcast.3), calls=%async_computation | async-start | bytes 1179648 | tf_op jit(solution)/shard_map/all_to_all | solution.py:538
  23.0 2.6 %collective-permute-start = (bf16[1152,256]{1,0:T(8,128)(2,1)}, bf16[1152,256]{1,0:T(8,128)(2,1)S(1)}, u32[]{:S(2)}, u32[]{:S(2)}) collective-permute-start(bf16[1152,256]{1,0:T(8,128)(2,1)} %get-tuple-element.31), channel_id=1, source_target_pairs={{0,8},{1,9},{2,10},{3,11},{4,12},{5,13},{6,14},{7,15},{8,0},{9,1},... | collective-permute-start | bytes 1769480 | tf_op jit(solution)/shard_map/ppermute | solution.py:543
  25.6 0.2 add_and_split.3
  25.9 0.8 copy-done.2
  26.6 2.0 %collective-permute-start.2 = (bf16[256,512]{1,0:T(8,128)(2,1)S(1)}, bf16[256,512]{1,0:T(8,128)(2,1)S(1)}, u32[]{:S(2)}, u32[]{:S(2)}) collective-permute-start(bf16[256,512]{1,0:T(8,128)(2,1)S(1)} %get-tuple-element.37), channel_id=1, source_target_pairs={{0,2},{1,3},{2,0},{3,1},{4,6},{5,7},{6,4},{7,5},{8,10},{9,11},{10,... | collective-permute-start | bytes 786440 | tf_op jit(solution)/shard_map/ppermute | solution.py:402
  28.7 8.5 %collective-permute-done.2.refs_0_ = bf16[256,512]{1,0:T(8,128)(2,1)S(1)} collective-permute-done((bf16[256,512]{1,0:T(8,128)(2,1)S(1)}, bf16[256,512]{1,0:T(8,128)(2,1)S(1)}, u32[]{:S(2)}, u32[]{:S(2)}) %collective-permute-start.2) | collective-permute-done | bytes 262176 | tf_op jit(solution)/shard_map/ppermute | solution.py:402
  37.2 0.0 copy-start.4
  37.2 0.6 copy-done.4
  37.8 14.7 %collective-permute-done.refs_0_ = bf16[1152,256]{1,0:T(8,128)(2,1)S(1)} collective-permute-done((bf16[1152,256]{1,0:T(8,128)(2,1)}, bf16[1152,256]{1,0:T(8,128)(2,1)S(1)}, u32[]{:S(2)}, u32[]{:S(2)}) %collective-permute-start) | collective-permute-done | bytes 589856 | tf_op jit(solution)/shard_map/ppermute | solution.py:543
  52.5 0.8 copy-done
  53.4 3.5 %all-to-all-start.1 = ((bf16[8,144,256]{2,1,0:T(8,128)(2,1)}), bf16[8,144,256]{2,1,0:T(8,128)(2,1)S(1)}, u32[]{:S(2)}, u32[]{:S(2)}) async-start(bf16[8,144,256]{2,1,0:T(8,128)(2,1)} %bitcast.7), calls=%async_computation.1 | async-start | bytes 1179648 | tf_op jit(solution)/shard_map/all_to_all | solution.py:538
  56.9 1.9 %collective-permute-start.3 = (bf16[256,512]{1,0:T(8,128)(2,1)S(1)}, bf16[256,512]{1,0:T(8,128)(2,1)S(1)}, u32[]{:S(2)}, u32[]{:S(2)}) collective-permute-start(bf16[256,512]{1,0:T(8,128)(2,1)S(1)} %get-tuple-element.40), channel_id=1, source_target_pairs={{0,2},{1,3},{2,0},{3,1},{4,6},{5,7},{6,4},{7,5},{8,10},{9,11},{10,... | collective-permute-start | bytes 786440 | tf_op jit(solution)/shard_map/ppermute | solution.py:402
  58.8 1.5 %collective-permute-start.5 = (bf16[64,512]{1,0:T(8,128)(2,1)S(1)}, bf16[64,512]{1,0:T(8,128)(2,1)S(1)}, u32[]{:S(2)}, u32[]{:S(2)}) collective-permute-start(bf16[64,512]{1,0:T(8,128)(2,1)S(1)} %get-tuple-element.45), channel_id=1, source_target_pairs={{0,4},{1,5},{2,6},{3,7},{4,0},{5,1},{6,2},{7,3},{8,12},{9,13},{10,... | collective-permute-start | bytes 196616 | tf_op jit(solution)/shard_map/ppermute | solution.py:402
  60.3 3.0 %collective-permute-start.4 = (bf16[64,512]{1,0:T(8,128)(2,1)}, bf16[64,512]{1,0:T(8,128)(2,1)S(1)}, u32[]{:S(2)}, u32[]{:S(2)}) collective-permute-start(bf16[64,512]{1,0:T(8,128)(2,1)} %copy-done.4), channel_id=1, source_target_pairs={{0,8},{1,9},{2,10},{3,11},{4,12},{5,13},{6,14},{7,15},{8,0},{9,1},... | collective-permute-start | bytes 196616 | tf_op jit(solution)/shard_map/ppermute | solution.py:402
  63.3 8.7 %collective-permute-done.3.refs_0_ = bf16[256,512]{1,0:T(8,128)(2,1)S(1)} collective-permute-done((bf16[256,512]{1,0:T(8,128)(2,1)S(1)}, bf16[256,512]{1,0:T(8,128)(2,1)S(1)}, u32[]{:S(2)}, u32[]{:S(2)}) %collective-permute-start.3) | collective-permute-done | bytes 262176 | tf_op jit(solution)/shard_map/ppermute | solution.py:402
  72.0 1.1 %copy-done.1 = bf16[1152,256]{1,0:T(8,128)(2,1)S(1)} copy-done((bf16[1152,256]{1,0:T(8,128)(2,1)S(1)}, bf16[1152,256]{1,0:T(8,128)(2,1)}, u32[]{:S(2)}) %copy-start.1) | copy-done | bytes 589848
  73.0 1.0 %copy-done.3 = f32[256,512]{1,0:T(8,128)S(1)} copy-done((f32[256,512]{1,0:T(8,128)S(1)}, f32[256,512]{1,0:T(8,128)}, u32[]{:S(2)}) %copy-start.3) | copy-done | bytes 524312
  74.1 1.6 %collective-permute-start.8 = (bf16[64,512]{1,0:T(8,128)(2,1)S(1)}, bf16[64,512]{1,0:T(8,128)(2,1)S(1)}, u32[]{:S(2)}, u32[]{:S(2)}) collective-permute-start(bf16[64,512]{1,0:T(8,128)(2,1)S(1)} %get-tuple-element.48), channel_id=1, source_target_pairs={{0,4},{1,5},{2,6},{3,7},{4,0},{5,1},{6,2},{7,3},{8,12},{9,13},{10,... | collective-permute-start | bytes 196616 | tf_op jit(solution)/shard_map/ppermute | solution.py:402
  75.7 3.0 %collective-permute-start.9 = (bf16[64,512]{1,0:T(8,128)(2,1)S(1)}, bf16[64,512]{1,0:T(8,128)(2,1)S(1)}, u32[]{:S(2)}, u32[]{:S(2)}) collective-permute-start(bf16[64,512]{1,0:T(8,128)(2,1)S(1)} %get-tuple-element.49), channel_id=1, source_target_pairs={{0,12},{1,13},{2,14},{3,15},{4,8},{5,9},{6,10},{7,11},{8,4},{9,5},... | collective-permute-start | bytes 196616 | tf_op jit(solution)/shard_map/ppermute | solution.py:402
  78.7 0.0 collective-permute-start.7
  78.7 0.0 copy-start.5
  78.7 0.8 copy-done.5
  79.5 1.0 %copy-done.6 = bf16[1024,256]{1,0:T(8,128)(2,1)S(1)} copy-done((bf16[1024,256]{1,0:T(8,128)(2,1)S(1)}, bf16[1024,256]{1,0:T(8,128)(2,1)}, u32[]{:S(2)}) %copy-start.6) | copy-done | bytes 524312
  80.6 1.0 %copy-done.7 = bf16[1024,256]{1,0:T(8,128)(2,1)S(1)} copy-done((bf16[1024,256]{1,0:T(8,128)(2,1)S(1)}, bf16[1024,256]{1,0:T(8,128)(2,1)}, u32[]{:S(2)}) %copy-start.7) | copy-done | bytes 524312
  81.6 0.9 %copy-done.8 = bf16[256,256]{1,0:T(8,128)(2,1)S(1)} copy-done((bf16[256,256]{1,0:T(8,128)(2,1)S(1)}, bf16[256,256]{1,0:T(8,128)(2,1)}, u32[]{:S(2)}) %copy-start.8) | copy-done | bytes 131096
  82.5 4.0 %encode.1 = (bf16[2048,256]{1,0:T(8,128)(2,1)}, f32[64,1024]{1,0:T(8,128)S(1)}) custom-call(s32[1]{0:T(128)} %bitcast.me_ref, bf16[1152,256]{1,0:T(8,128)(2,1)S(1)} %bitcast.8, bf16[1152,256]{1,0:T(8,128)(2,1)S(1)} %bitcast.9, bf16[1024,256]{1,0:T(8,128)(2,1)S(1)} %copy-done.6, bf16[1024,256]{1,0:T(8,128)(2,1)S(1)} %copy-done.7, ...), custom_call_target="tpu_custom_call" | custom-call | flops 1342177280 | bytes 2097152 | tf_op jit(solution)/shard_map/encode/pallas_call | solution.py:503
  86.6 0.8 finish.1
  (23 shorter events, 0.1 us)
Async XLA Ops:
  7.1 3.9 %copy-start.10 = (f32[1,1024]{1,0:T(1,128)S(1)}, f32[1,1024]{1,0:T(1,128)}, u32[]{:S(2)}) copy-start(f32[1,1024]{1,0:T(1,128)} %get-tuple-element.32.mean_hbm) | copy-start | bytes 12292
  11.0 0.7 copy-start.9
  17.6 8.0 %collective-permute-start.1 = (bf16[512,1024]{1,0:T(8,128)(2,1)}, bf16[512,1024]{1,0:T(8,128)(2,1)S(1)}, u32[]{:S(2)}, u32[]{:S(2)}) collective-permute-start(bf16[512,1024]{1,0:T(8,128)(2,1)} %get-tuple-element.35), channel_id=1, source_target_pairs={{0,1},{1,0},{2,3},{3,2},{4,5},{5,4},{6,7},{7,6},{8,9},{9,8},{10,11... | collective-permute-start | bytes 3145736 | tf_op jit(solution)/shard_map/ppermute | solution.py:402
  18.1 35.2 %all-to-all-start = ((bf16[8,144,256]{2,1,0:T(8,128)(2,1)}), bf16[8,144,256]{2,1,0:T(8,128)(2,1)S(1)}, u32[]{:S(2)}, u32[]{:S(2)}) async-start(bf16[8,144,256]{2,1,0:T(8,128)(2,1)} %bitcast.3), calls=%async_computation | async-start | bytes 1179648 | tf_op jit(solution)/shard_map/all_to_all | solution.py:538
  23.0 29.5 %collective-permute-start = (bf16[1152,256]{1,0:T(8,128)(2,1)}, bf16[1152,256]{1,0:T(8,128)(2,1)S(1)}, u32[]{:S(2)}, u32[]{:S(2)}) collective-permute-start(bf16[1152,256]{1,0:T(8,128)(2,1)} %get-tuple-element.31), channel_id=1, source_target_pairs={{0,8},{1,9},{2,10},{3,11},{4,12},{5,13},{6,14},{7,15},{8,0},{9,1},... | collective-permute-start | bytes 1769480 | tf_op jit(solution)/shard_map/ppermute | solution.py:543
  25.8 0.8 copy-start.2
  26.6 10.5 %collective-permute-start.2 = (bf16[256,512]{1,0:T(8,128)(2,1)S(1)}, bf16[256,512]{1,0:T(8,128)(2,1)S(1)}, u32[]{:S(2)}, u32[]{:S(2)}) collective-permute-start(bf16[256,512]{1,0:T(8,128)(2,1)S(1)} %get-tuple-element.37), channel_id=1, source_target_pairs={{0,2},{1,3},{2,0},{3,1},{4,6},{5,7},{6,4},{7,5},{8,10},{9,11},{10,... | collective-permute-start | bytes 786440 | tf_op jit(solution)/shard_map/ppermute | solution.py:402
  37.2 0.6 copy-start.4
  52.5 0.8 copy-start
  53.4 25.3 %all-to-all-start.1 = ((bf16[8,144,256]{2,1,0:T(8,128)(2,1)}), bf16[8,144,256]{2,1,0:T(8,128)(2,1)S(1)}, u32[]{:S(2)}, u32[]{:S(2)}) async-start(bf16[8,144,256]{2,1,0:T(8,128)(2,1)} %bitcast.7), calls=%async_computation.1 | async-start | bytes 1179648 | tf_op jit(solution)/shard_map/all_to_all | solution.py:538
  56.9 15.1 %collective-permute-start.3 = (bf16[256,512]{1,0:T(8,128)(2,1)S(1)}, bf16[256,512]{1,0:T(8,128)(2,1)S(1)}, u32[]{:S(2)}, u32[]{:S(2)}) collective-permute-start(bf16[256,512]{1,0:T(8,128)(2,1)S(1)} %get-tuple-element.40), channel_id=1, source_target_pairs={{0,2},{1,3},{2,0},{3,1},{4,6},{5,7},{6,4},{7,5},{8,10},{9,11},{10,... | collective-permute-start | bytes 786440 | tf_op jit(solution)/shard_map/ppermute | solution.py:402
  58.8 19.8 %collective-permute-start.5 = (bf16[64,512]{1,0:T(8,128)(2,1)S(1)}, bf16[64,512]{1,0:T(8,128)(2,1)S(1)}, u32[]{:S(2)}, u32[]{:S(2)}) collective-permute-start(bf16[64,512]{1,0:T(8,128)(2,1)S(1)} %get-tuple-element.45), channel_id=1, source_target_pairs={{0,4},{1,5},{2,6},{3,7},{4,0},{5,1},{6,2},{7,3},{8,12},{9,13},{10,... | collective-permute-start | bytes 196616 | tf_op jit(solution)/shard_map/ppermute | solution.py:402
  60.3 26.2 %collective-permute-start.4 = (bf16[64,512]{1,0:T(8,128)(2,1)}, bf16[64,512]{1,0:T(8,128)(2,1)S(1)}, u32[]{:S(2)}, u32[]{:S(2)}) collective-permute-start(bf16[64,512]{1,0:T(8,128)(2,1)} %copy-done.4), channel_id=1, source_target_pairs={{0,8},{1,9},{2,10},{3,11},{4,12},{5,13},{6,14},{7,15},{8,0},{9,1},... | collective-permute-start | bytes 196616 | tf_op jit(solution)/shard_map/ppermute | solution.py:402
  63.3 23.2 %collective-permute-start.6 = (bf16[64,512]{1,0:T(8,128)(2,1)S(1)}, bf16[64,512]{1,0:T(8,128)(2,1)S(1)}, u32[]{:S(2)}, u32[]{:S(2)}) collective-permute-start(bf16[64,512]{1,0:T(8,128)(2,1)S(1)} %get-tuple-element.46), channel_id=1, source_target_pairs={{0,12},{1,13},{2,14},{3,15},{4,8},{5,9},{6,10},{7,11},{8,4},{9,5},... | collective-permute-start | bytes 196616 | tf_op jit(solution)/shard_map/ppermute | solution.py:402
  72.0 1.1 %copy-start.1 = (bf16[1152,256]{1,0:T(8,128)(2,1)S(1)}, bf16[1152,256]{1,0:T(8,128)(2,1)}, u32[]{:S(2)}) copy-start(bf16[1152,256]{1,0:T(8,128)(2,1)} %tie.1.refs_1_) | copy-start | bytes 1769476
  73.0 1.0 %copy-start.3 = (f32[256,512]{1,0:T(8,128)S(1)}, f32[256,512]{1,0:T(8,128)}, u32[]{:S(2)}) copy-start(f32[256,512]{1,0:T(8,128)} %copy-done.2) | copy-start | bytes 1572868
  74.1 12.4 %collective-permute-start.8 = (bf16[64,512]{1,0:T(8,128)(2,1)S(1)}, bf16[64,512]{1,0:T(8,128)(2,1)S(1)}, u32[]{:S(2)}, u32[]{:S(2)}) collective-permute-start(bf16[64,512]{1,0:T(8,128)(2,1)S(1)} %get-tuple-element.48), channel_id=1, source_target_pairs={{0,4},{1,5},{2,6},{3,7},{4,0},{5,1},{6,2},{7,3},{8,12},{9,13},{10,... | collective-permute-start | bytes 196616 | tf_op jit(solution)/shard_map/ppermute | solution.py:402
  75.7 10.9 %collective-permute-start.9 = (bf16[64,512]{1,0:T(8,128)(2,1)S(1)}, bf16[64,512]{1,0:T(8,128)(2,1)S(1)}, u32[]{:S(2)}, u32[]{:S(2)}) collective-permute-start(bf16[64,512]{1,0:T(8,128)(2,1)S(1)} %get-tuple-element.49), channel_id=1, source_target_pairs={{0,12},{1,13},{2,14},{3,15},{4,8},{5,9},{6,10},{7,11},{8,4},{9,5},... | collective-permute-start | bytes 196616 | tf_op jit(solution)/shard_map/ppermute | solution.py:402
  78.7 7.9 %collective-permute-start.7 = (bf16[64,512]{1,0:T(8,128)(2,1)S(1)}, bf16[64,512]{1,0:T(8,128)(2,1)S(1)}, u32[]{:S(2)}, u32[]{:S(2)}) collective-permute-start(bf16[64,512]{1,0:T(8,128)(2,1)S(1)} %get-tuple-element.41.refs_1_), channel_id=1, source_target_pairs={{0,8},{1,9},{2,10},{3,11},{4,12},{5,13},{6,14},{7,15},{8,0},{9,1},... | collective-permute-start | bytes 196616 | tf_op jit(solution)/shard_map/ppermute | solution.py:402
  78.7 0.8 copy-start.5
  79.5 1.0 %copy-start.6 = (bf16[1024,256]{1,0:T(8,128)(2,1)S(1)}, bf16[1024,256]{1,0:T(8,128)(2,1)}, u32[]{:S(2)}) copy-start(bf16[1024,256]{1,0:T(8,128)(2,1)} %basis_ref.1) | copy-start | bytes 1572868
  80.6 1.0 %copy-start.7 = (bf16[1024,256]{1,0:T(8,128)(2,1)S(1)}, bf16[1024,256]{1,0:T(8,128)(2,1)}, u32[]{:S(2)}) copy-start(bf16[1024,256]{1,0:T(8,128)(2,1)} %centroid_ref.1) | copy-start | bytes 1572868
  81.6 0.9 %copy-start.8 = (bf16[256,256]{1,0:T(8,128)(2,1)S(1)}, bf16[256,256]{1,0:T(8,128)(2,1)}, u32[]{:S(2)}) copy-start(bf16[256,256]{1,0:T(8,128)(2,1)} %rotation_ref.1) | copy-start | bytes 393220

commit v18 on v17

--- a/solution.py
+++ b/solution.py
@@ -15,7 +15,8 @@
 TILE = 256
 GROUP = 4
 SHARES = 2
-VMEM_ALL = 60 * 1024 * 1024
+NO_COST = pl.CostEstimate(flops=0, bytes_accessed=0, transcendentals=0)
+VMEM_ALL = 61840 * 1024
 VMEM_SOME = 24 * 1024 * 1024
 VMEM_MOST = 48 * 1024 * 1024
 
@@ -83,9 +84,7 @@
         out_shape=[jax.ShapeDtypeStruct((slots, feats), jnp.bfloat16), jax.ShapeDtypeStruct((8, LANES), jnp.float32)],
         scratch_shapes=[pltpu.VMEM((slots, feats), jnp.bfloat16), pltpu.SemaphoreType.DMA((slots // (GROUP * SPAN),))],
         compiler_params=pltpu.CompilerParams(vmem_limit_bytes=VMEM_ALL),
-        cost_estimate=pl.CostEstimate(
-            flops=2 * rows_here * feats * slots, bytes_accessed=2 * (rows_here + slots) * feats, transcendentals=0
-        ),
+        cost_estimate=NO_COST,
         name="sort_near",
     )(me.reshape(1), yb, targets, lists, notes)
 
@@ -244,9 +243,7 @@
             pltpu.SemaphoreType.DMA((width // GROUP // 2,)),
         ],
         compiler_params=pltpu.CompilerParams(vmem_limit_bytes=VMEM_ALL),
-        cost_estimate=pl.CostEstimate(
-            flops=2 * rows_here * feats * (wide + slots), bytes_accessed=2 * rows_here * wide + 2 * slots * feats, transcendentals=0
-        ),
+        cost_estimate=NO_COST,
         name="project_sort",
     )(me.reshape(1), embeddings, basis, list_owner.reshape(lanes, LANES), list_slot.reshape(lanes, LANES))
 
@@ -325,9 +322,7 @@
             pltpu.SemaphoreType.DMA,
         ],
         compiler_params=pltpu.CompilerParams(vmem_limit_bytes=VMEM_MOST),
-        cost_estimate=pl.CostEstimate(
-            flops=2 * rows_here * wide * wide, bytes_accessed=2 * rows_here * wide + 3 * wide * wide, transcendentals=0
-        ),
+        cost_estimate=NO_COST,
         name="moments",
     )(me.reshape(1), mean, embeddings, after)
 
@@ -358,7 +353,7 @@
         out_specs=[vmem] * (shares * pieces),
         out_shape=[jax.ShapeDtypeStruct(shape, kind) for kind in kinds * shares],
         compiler_params=pltpu.CompilerParams(vmem_limit_bytes=VMEM_SOME),
-        cost_estimate=pl.CostEstimate(flops=2 * rows * columns, bytes_accessed=10 * rows * columns, transcendentals=0),
+        cost_estimate=NO_COST,
         name="add_and_split",
     )(keep, *came, *after)
     return [outs[h * pieces:(h + 1) * pieces] for h in range(shares)]
@@ -385,7 +380,7 @@
         out_specs=vmem,
         out_shape=jax.ShapeDtypeStruct(between.shape, jnp.float32),
         compiler_params=pltpu.CompilerParams(vmem_limit_bytes=VMEM_SOME),
-        cost_estimate=pl.CostEstimate(flops=8 * between.size, bytes_accessed=16 * between.size, transcendentals=0),
+        cost_estimate=NO_COST,
         name="finish",
     )(between, *parts)
 
@@ -515,10 +510,8 @@
             pltpu.VMEM((width, wide), jnp.float32),
             pltpu.SemaphoreType.DMA((width // GROUP,)),
         ],
-        compiler_params=pltpu.CompilerParams(vmem_limit_bytes=VMEM_SOME),
-        cost_estimate=pl.CostEstimate(
-            flops=2 * slots * feats * (owned + feats), bytes_accessed=4 * slots * feats, transcendentals=0
-        ),
+        compiler_params=pltpu.CompilerParams(vmem_limit_bytes=VMEM_ALL),
+        cost_estimate=NO_COST,
         name="encode",
     )(me.reshape(1), near, far, basis, centroids, rotation, *after)
 

time: 87.9 us -> 88 us (level)
  local copies, waits for them, and re-layouts: 8.82 us -> 5.63 us
  Pallas kernels: 21.3 us -> 23.6 us
    unnamed x22 -> x16, local copies, waits for them, and re-layouts: 8.82 us -> 5.63 us
    pallas_call x1, Pallas kernels: 3.99 us -> 6.27 us  [encode(): pl.pallas_call(functools.partial(encode_kernel, total), in_specs=[pl.Bloc...]
    ppermute x1, waiting for transfers between devices: 14.7 us -> 16.4 us  [local(): far = lax.ppermute(far, 'wide', [(i, i ^ half) for i in range(width)])]
  transfers between devices with their start and end apart: 12 -> 12, of which waited for: 3 -> 3; matrix products, arithmetic and copies ran while one was open for 0% -> 0% of each run, Pallas kernels for 5% -> 8%
where the time goes in v18:
time: 88 us; the launch traced here: 87.5 us
  waiting for transfers between devices  32.7 us (37%)
  starting transfers between devices  24.8 us (28%)
  Pallas kernels  23.6 us (27%)
  local copies, waits for them, and re-layouts  5.63 us (6%)
    ppermute x1, waiting for transfers between devices, local(): far = lax.ppermute(far, 'wide', [(i, i ^ half) for i in range(width)])  16.4 us
    ppermute x9, waiting for transfers between devices, exchange(): lax.ppermute(out[p - 1], 'wide', [(i, i ^ apart) for i in range(width)])  16.3 us
    ppermute x9, starting transfers between devices, exchange(): lax.ppermute(out[p - 1], 'wide', [(i, i ^ apart) for i in range(width)])  13.4 us
    all_to_all x2, starting transfers between devices, spread(): lax.all_to_all(blocks.reshape(half, SPAN, feats), 'wide', split_axis=0, c...  8.43 us
    pallas_call x1, Pallas kernels, project_and_sort_far(): pl.pallas_call(functools.partial(rows_kernel, width), grid=(rows_here //...  6.46 us
    pallas_call x1, Pallas kernels, encode(): pl.pallas_call(functools.partial(encode_kernel, total), in_specs=[pl.Bloc...  6.27 us
    pallas_call x1, Pallas kernels, moments(): pl.pallas_call(functools.partial(moments_kernel, width), in_specs=[pl.Blo...  5.84 us
    unnamed x16, local copies, waits for them, and re-layouts  5.63 us
  transfers between devices with their start and end apart: 12, of which 3 were waited for; matrix products, arithmetic and copies ran while one was open for 0% of the time, Pallas kernels for 8%

profile of v18, /device:TPU:0, one launch (start us, length us, event | category | flops | bytes accessed | tf_op | source)
XLA Modules:
  0.0 87.5 jit_solution(511825160619097878)
XLA Ops:
  0.6 6.5 %project_sort.1 = (bf16[1152,256]{1,0:T(8,128)(2,1)}, f32[1,1024]{1,0:T(1,128)}, bf16[2048,256]{1,0:T(8,128)(2,1)}, s32[16,128]{1,0:T(8,128)}, f32[16,256]{1,0:T(8,128)}, /*index=5*/f32[16,256]{1,0:T(8,128)}) custom-call(s32[1]{0:T(128)} %bitcast.me_ref, bf16[2048,1024]{1,0:T(8,128)(2,1)} %e_hbm.3, bf16[1024,256]{1,0:T(8,128)(2,1)} %basis_ref.1, ...), custom_call_target="tpu_custom_call" | custom-call | tf_op jit(solution)/shard_map/project_sort/pallas_call | solution.py:214
  7.1 3.9 %sort_near.1 = (bf16[1152,256]{1,0:T(8,128)(2,1)}, f32[8,128]{1,0:T(8,128)}) custom-call(s32[1]{0:T(128)} %bitcast.me_ref, bf16[2048,256]{1,0:T(8,128)(2,1)} %get-tuple-element.26.yb_ref, s32[16,128]{1,0:T(8,128)} %get-tuple-element.27.target_ref, f32[16,256]{1,0:T(8,128)} %get-tuple-element.28.list_ref, f32[16,256]{1,0:T(8,128)} %get-tuple-element.29.notes_ref), custom_call_target="tpu_custom_call" | custom-call | tf_op jit(solution)/shard_map/sort_near/pallas_call | solution.py:80
  11.1 0.7 copy-done.5
  11.7 0.7 copy-done.6
  12.4 5.8 %moments.1 = (bf16[512,1024]{1,0:T(8,128)(2,1)S(1)}, bf16[512,1024]{1,0:T(8,128)(2,1)}) custom-call(s32[1]{0:T(128)} %bitcast.me_ref, f32[1,1024]{1,0:T(1,128)S(1)} %copy-done.5, bf16[2048,1024]{1,0:T(8,128)(2,1)} %e_hbm.3, f32[8,128]{1,0:T(8,128)S(1)} %copy-done.6), custom_call_target="tpu_custom_call" | custom-call | tf_op jit(solution)/shard_map/moments/pallas_call | solution.py:309
  18.3 0.6 collective-permute-start.1
  18.8 4.9 %all-to-all-start = ((bf16[8,144,256]{2,1,0:T(8,128)(2,1)}), bf16[8,144,256]{2,1,0:T(8,128)(2,1)}, u32[]{:S(2)}, u32[]{:S(2)}) async-start(bf16[8,144,256]{2,1,0:T(8,128)(2,1)} %bitcast.3), calls=%async_computation | async-start | bytes 1179648 | tf_op jit(solution)/shard_map/all_to_all | solution.py:531
  23.7 3.0 %collective-permute-start = (bf16[1152,256]{1,0:T(8,128)(2,1)}, bf16[1152,256]{1,0:T(8,128)(2,1)S(1)}, u32[]{:S(2)}, u32[]{:S(2)}) collective-permute-start(bf16[1152,256]{1,0:T(8,128)(2,1)} %get-tuple-element.31), channel_id=1, source_target_pairs={{0,8},{1,9},{2,10},{3,11},{4,12},{5,13},{6,14},{7,15},{8,0},{9,1},... | collective-permute-start | bytes 1769480 | tf_op jit(solution)/shard_map/ppermute | solution.py:536
  26.7 0.2 add_and_split.3
  26.9 1.9 %collective-permute-start.2 = (bf16[256,512]{1,0:T(8,128)(2,1)S(1)}, bf16[256,512]{1,0:T(8,128)(2,1)S(1)}, u32[]{:S(2)}, u32[]{:S(2)}) collective-permute-start(bf16[256,512]{1,0:T(8,128)(2,1)S(1)} %get-tuple-element.37), channel_id=1, source_target_pairs={{0,2},{1,3},{2,0},{3,1},{4,6},{5,7},{6,4},{7,5},{8,10},{9,11},{10,... | collective-permute-start | bytes 786440 | tf_op jit(solution)/shard_map/ppermute | solution.py:397
  28.8 7.6 %collective-permute-done.2.refs_0_ = bf16[256,512]{1,0:T(8,128)(2,1)S(1)} collective-permute-done((bf16[256,512]{1,0:T(8,128)(2,1)S(1)}, bf16[256,512]{1,0:T(8,128)(2,1)S(1)}, u32[]{:S(2)}, u32[]{:S(2)}) %collective-permute-start.2) | collective-permute-done | bytes 262176 | tf_op jit(solution)/shard_map/ppermute | solution.py:397
  36.5 0.6 copy-done.2
  37.1 16.4 %collective-permute-done.refs_0_ = bf16[1152,256]{1,0:T(8,128)(2,1)S(1)} collective-permute-done((bf16[1152,256]{1,0:T(8,128)(2,1)}, bf16[1152,256]{1,0:T(8,128)(2,1)S(1)}, u32[]{:S(2)}, u32[]{:S(2)}) %collective-permute-start) | collective-permute-done | bytes 589856 | tf_op jit(solution)/shard_map/ppermute | solution.py:536
  53.5 0.8 copy-done
  54.3 0.0 all-to-all-done
  54.3 3.5 %all-to-all-start.1 = ((bf16[8,144,256]{2,1,0:T(8,128)(2,1)}), bf16[8,144,256]{2,1,0:T(8,128)(2,1)S(1)}, u32[]{:S(2)}, u32[]{:S(2)}) async-start(bf16[8,144,256]{2,1,0:T(8,128)(2,1)} %bitcast.7), calls=%async_computation.1 | async-start | bytes 1179648 | tf_op jit(solution)/shard_map/all_to_all | solution.py:531
  57.9 1.9 %collective-permute-start.3 = (bf16[256,512]{1,0:T(8,128)(2,1)S(1)}, bf16[256,512]{1,0:T(8,128)(2,1)S(1)}, u32[]{:S(2)}, u32[]{:S(2)}) collective-permute-start(bf16[256,512]{1,0:T(8,128)(2,1)S(1)} %get-tuple-element.40), channel_id=1, source_target_pairs={{0,2},{1,3},{2,0},{3,1},{4,6},{5,7},{6,4},{7,5},{8,10},{9,11},{10,... | collective-permute-start | bytes 786440 | tf_op jit(solution)/shard_map/ppermute | solution.py:397
  59.8 1.5 %collective-permute-start.5 = (bf16[64,512]{1,0:T(8,128)(2,1)S(1)}, bf16[64,512]{1,0:T(8,128)(2,1)S(1)}, u32[]{:S(2)}, u32[]{:S(2)}) collective-permute-start(bf16[64,512]{1,0:T(8,128)(2,1)S(1)} %get-tuple-element.45), channel_id=1, source_target_pairs={{0,4},{1,5},{2,6},{3,7},{4,0},{5,1},{6,2},{7,3},{8,12},{9,13},{10,... | collective-permute-start | bytes 196616 | tf_op jit(solution)/shard_map/ppermute | solution.py:397
  61.3 3.0 %collective-permute-start.4 = (bf16[64,512]{1,0:T(8,128)(2,1)}, bf16[64,512]{1,0:T(8,128)(2,1)S(1)}, u32[]{:S(2)}, u32[]{:S(2)}) collective-permute-start(bf16[64,512]{1,0:T(8,128)(2,1)} %copy-done.2), channel_id=1, source_target_pairs={{0,8},{1,9},{2,10},{3,11},{4,12},{5,13},{6,14},{7,15},{8,0},{9,1},... | collective-permute-start | bytes 196616 | tf_op jit(solution)/shard_map/ppermute | solution.py:397
  64.3 0.0 collective-permute-start.6
  64.3 8.7 %collective-permute-done.3.refs_0_ = bf16[256,512]{1,0:T(8,128)(2,1)S(1)} collective-permute-done((bf16[256,512]{1,0:T(8,128)(2,1)S(1)}, bf16[256,512]{1,0:T(8,128)(2,1)S(1)}, u32[]{:S(2)}, u32[]{:S(2)}) %collective-permute-start.3) | collective-permute-done | bytes 262176 | tf_op jit(solution)/shard_map/ppermute | solution.py:397
  72.9 1.1 %copy-done.1 = bf16[1152,256]{1,0:T(8,128)(2,1)S(1)} copy-done((bf16[1152,256]{1,0:T(8,128)(2,1)S(1)}, bf16[1152,256]{1,0:T(8,128)(2,1)}, u32[]{:S(2)}) %copy-start.1) | copy-done | bytes 589848
  74.1 1.6 %collective-permute-start.8 = (bf16[64,512]{1,0:T(8,128)(2,1)S(1)}, bf16[64,512]{1,0:T(8,128)(2,1)S(1)}, u32[]{:S(2)}, u32[]{:S(2)}) collective-permute-start(bf16[64,512]{1,0:T(8,128)(2,1)S(1)} %get-tuple-element.48), channel_id=1, source_target_pairs={{0,4},{1,5},{2,6},{3,7},{4,0},{5,1},{6,2},{7,3},{8,12},{9,13},{10,... | collective-permute-start | bytes 196616 | tf_op jit(solution)/shard_map/ppermute | solution.py:397
  75.6 3.0 %collective-permute-start.9 = (bf16[64,512]{1,0:T(8,128)(2,1)S(1)}, bf16[64,512]{1,0:T(8,128)(2,1)S(1)}, u32[]{:S(2)}, u32[]{:S(2)}) collective-permute-start(bf16[64,512]{1,0:T(8,128)(2,1)S(1)} %get-tuple-element.49), channel_id=1, source_target_pairs={{0,12},{1,13},{2,14},{3,15},{4,8},{5,9},{6,10},{7,11},{8,4},{9,5},... | collective-permute-start | bytes 196616 | tf_op jit(solution)/shard_map/ppermute | solution.py:397
  78.6 0.0 collective-permute-done.5.refs_2_
  78.6 0.0 collective-permute-start.7
  78.6 0.0 all-to-all-done.1
  78.6 0.8 copy-done.7
  79.4 6.3 %encode.1 = (bf16[2048,256]{1,0:T(8,128)(2,1)}, f32[64,1024]{1,0:T(8,128)}) custom-call(s32[1]{0:T(128)} %bitcast.me_ref, bf16[1152,256]{1,0:T(8,128)(2,1)} %bitcast.4.near_ref, bf16[1152,256]{1,0:T(8,128)(2,1)} %bitcast.8, bf16[1024,256]{1,0:T(8,128)(2,1)} %basis_ref.1, bf16[1024,256]{1,0:T(8,128)(2,1)} %centroid_ref.1, bf16[256,256]{1,0:T(8,128)(2,1)} %rotation_ref.1, ...), custom_call_target="tpu_custom_call" | custom-call | tf_op jit(solution)/shard_map/encode/pallas_call | solution.py:498
  85.8 0.0 copy-start.3
  85.8 0.9 %copy-done.3 = f32[64,1024]{1,0:T(8,128)S(1)} copy-done((f32[64,1024]{1,0:T(8,128)S(1)}, f32[64,1024]{1,0:T(8,128)}, u32[]{:S(2)}) %copy-start.3) | copy-done | bytes 262168
  86.7 0.8 finish.1
  (17 shorter events, 0.1 us)
Async XLA Ops:
  11.0 0.7 copy-start.5
  11.7 0.7 copy-start.6
  18.3 8.4 %collective-permute-start.1 = (bf16[512,1024]{1,0:T(8,128)(2,1)}, bf16[512,1024]{1,0:T(8,128)(2,1)S(1)}, u32[]{:S(2)}, u32[]{:S(2)}) collective-permute-start(bf16[512,1024]{1,0:T(8,128)(2,1)} %get-tuple-element.35), channel_id=1, source_target_pairs={{0,1},{1,0},{2,3},{3,2},{4,5},{5,4},{6,7},{7,6},{8,9},{9,8},{10,11... | collective-permute-start | bytes 3145736 | tf_op jit(solution)/shard_map/ppermute | solution.py:397
  18.8 35.5 %all-to-all-start = ((bf16[8,144,256]{2,1,0:T(8,128)(2,1)}), bf16[8,144,256]{2,1,0:T(8,128)(2,1)}, u32[]{:S(2)}, u32[]{:S(2)}) async-start(bf16[8,144,256]{2,1,0:T(8,128)(2,1)} %bitcast.3), calls=%async_computation | async-start | bytes 1179648 | tf_op jit(solution)/shard_map/all_to_all | solution.py:531
  23.7 29.8 %collective-permute-start = (bf16[1152,256]{1,0:T(8,128)(2,1)}, bf16[1152,256]{1,0:T(8,128)(2,1)S(1)}, u32[]{:S(2)}, u32[]{:S(2)}) collective-permute-start(bf16[1152,256]{1,0:T(8,128)(2,1)} %get-tuple-element.31), channel_id=1, source_target_pairs={{0,8},{1,9},{2,10},{3,11},{4,12},{5,13},{6,14},{7,15},{8,0},{9,1},... | collective-permute-start | bytes 1769480 | tf_op jit(solution)/shard_map/ppermute | solution.py:536
  26.9 9.5 %collective-permute-start.2 = (bf16[256,512]{1,0:T(8,128)(2,1)S(1)}, bf16[256,512]{1,0:T(8,128)(2,1)S(1)}, u32[]{:S(2)}, u32[]{:S(2)}) collective-permute-start(bf16[256,512]{1,0:T(8,128)(2,1)S(1)} %get-tuple-element.37), channel_id=1, source_target_pairs={{0,2},{1,3},{2,0},{3,1},{4,6},{5,7},{6,4},{7,5},{8,10},{9,11},{10,... | collective-permute-start | bytes 786440 | tf_op jit(solution)/shard_map/ppermute | solution.py:397
  36.5 0.6 copy-start.2
  53.5 0.8 copy-start
  54.3 24.3 %all-to-all-start.1 = ((bf16[8,144,256]{2,1,0:T(8,128)(2,1)}), bf16[8,144,256]{2,1,0:T(8,128)(2,1)S(1)}, u32[]{:S(2)}, u32[]{:S(2)}) async-start(bf16[8,144,256]{2,1,0:T(8,128)(2,1)} %bitcast.7), calls=%async_computation.1 | async-start | bytes 1179648 | tf_op jit(solution)/shard_map/all_to_all | solution.py:531
  57.9 15.1 %collective-permute-start.3 = (bf16[256,512]{1,0:T(8,128)(2,1)S(1)}, bf16[256,512]{1,0:T(8,128)(2,1)S(1)}, u32[]{:S(2)}, u32[]{:S(2)}) collective-permute-start(bf16[256,512]{1,0:T(8,128)(2,1)S(1)} %get-tuple-element.40), channel_id=1, source_target_pairs={{0,2},{1,3},{2,0},{3,1},{4,6},{5,7},{6,4},{7,5},{8,10},{9,11},{10,... | collective-permute-start | bytes 786440 | tf_op jit(solution)/shard_map/ppermute | solution.py:397
  59.8 18.8 %collective-permute-start.5 = (bf16[64,512]{1,0:T(8,128)(2,1)S(1)}, bf16[64,512]{1,0:T(8,128)(2,1)S(1)}, u32[]{:S(2)}, u32[]{:S(2)}) collective-permute-start(bf16[64,512]{1,0:T(8,128)(2,1)S(1)} %get-tuple-element.45), channel_id=1, source_target_pairs={{0,4},{1,5},{2,6},{3,7},{4,0},{5,1},{6,2},{7,3},{8,12},{9,13},{10,... | collective-permute-start | bytes 196616 | tf_op jit(solution)/shard_map/ppermute | solution.py:397
  61.3 24.5 %collective-permute-start.4 = (bf16[64,512]{1,0:T(8,128)(2,1)}, bf16[64,512]{1,0:T(8,128)(2,1)S(1)}, u32[]{:S(2)}, u32[]{:S(2)}) collective-permute-start(bf16[64,512]{1,0:T(8,128)(2,1)} %copy-done.2), channel_id=1, source_target_pairs={{0,8},{1,9},{2,10},{3,11},{4,12},{5,13},{6,14},{7,15},{8,0},{9,1},... | collective-permute-start | bytes 196616 | tf_op jit(solution)/shard_map/ppermute | solution.py:397
  64.3 21.5 %collective-permute-start.6 = (bf16[64,512]{1,0:T(8,128)(2,1)S(1)}, bf16[64,512]{1,0:T(8,128)(2,1)S(1)}, u32[]{:S(2)}, u32[]{:S(2)}) collective-permute-start(bf16[64,512]{1,0:T(8,128)(2,1)S(1)} %get-tuple-element.46), channel_id=1, source_target_pairs={{0,12},{1,13},{2,14},{3,15},{4,8},{5,9},{6,10},{7,11},{8,4},{9,5},... | collective-permute-start | bytes 196616 | tf_op jit(solution)/shard_map/ppermute | solution.py:397
  72.9 1.1 %copy-start.1 = (bf16[1152,256]{1,0:T(8,128)(2,1)S(1)}, bf16[1152,256]{1,0:T(8,128)(2,1)}, u32[]{:S(2)}) copy-start(bf16[1152,256]{1,0:T(8,128)(2,1)} %tie.1.refs_1_) | copy-start | bytes 1769476
  74.0 4.6 %copy-start.4 = (bf16[64,512]{1,0:T(8,128)(2,1)}, bf16[64,512]{1,0:T(8,128)(2,1)S(1)}, u32[]{:S(2)}) copy-start(bf16[64,512]{1,0:T(8,128)(2,1)S(1)} %get-tuple-element.41.refs_1_) | copy-start | bytes 196612
  74.1 11.7 %collective-permute-start.8 = (bf16[64,512]{1,0:T(8,128)(2,1)S(1)}, bf16[64,512]{1,0:T(8,128)(2,1)S(1)}, u32[]{:S(2)}, u32[]{:S(2)}) collective-permute-start(bf16[64,512]{1,0:T(8,128)(2,1)S(1)} %get-tuple-element.48), channel_id=1, source_target_pairs={{0,4},{1,5},{2,6},{3,7},{4,0},{5,1},{6,2},{7,3},{8,12},{9,13},{10,... | collective-permute-start | bytes 196616 | tf_op jit(solution)/shard_map/ppermute | solution.py:397
  75.6 10.2 %collective-permute-start.9 = (bf16[64,512]{1,0:T(8,128)(2,1)S(1)}, bf16[64,512]{1,0:T(8,128)(2,1)S(1)}, u32[]{:S(2)}, u32[]{:S(2)}) collective-permute-start(bf16[64,512]{1,0:T(8,128)(2,1)S(1)} %get-tuple-element.49), channel_id=1, source_target_pairs={{0,12},{1,13},{2,14},{3,15},{4,8},{5,9},{6,10},{7,11},{8,4},{9,5},... | collective-permute-start | bytes 196616 | tf_op jit(solution)/shard_map/ppermute | solution.py:397
  78.6 7.2 %collective-permute-start.7 = (bf16[64,512]{1,0:T(8,128)(2,1)S(1)}, bf16[64,512]{1,0:T(8,128)(2,1)S(1)}, u32[]{:S(2)}, u32[]{:S(2)}) collective-permute-start(bf16[64,512]{1,0:T(8,128)(2,1)S(1)} %get-tuple-element.41.refs_1_), channel_id=1, source_target_pairs={{0,8},{1,9},{2,10},{3,11},{4,12},{5,13},{6,14},{7,15},{8,0},{9,1},... | collective-permute-start | bytes 196616 | tf_op jit(solution)/shard_map/ppermute | solution.py:397
  78.6 0.8 copy-start.7
  85.8 1.0 %copy-start.3 = (f32[64,1024]{1,0:T(8,128)S(1)}, f32[64,1024]{1,0:T(8,128)}, u32[]{:S(2)}) copy-start(f32[64,1024]{1,0:T(8,128)} %get-tuple-element.43.between_ref) | copy-start | bytes 786436

commit v19 on v8

--- a/solution.py
+++ b/solution.py
@@ -197,6 +197,7 @@
     rows_here, wide = e_ref.shape
     block = wide // width
     bits = width.bit_length() - 1
+    tiles = wide // TILE
     mean_copy = pltpu.make_async_copy(mean_hbm, mean_ref, mean_sem)
     mean_copy.start()
     copies = []
@@ -205,10 +206,11 @@
         copies.append(pltpu.make_async_copy(e_hbm.at[at], e_ref.at[at], sem.at[c]))
         copies[c].start()
     me = me_ref[0]
+    odd = (me & 1) == 1
     mean_copy.wait()
     mean = mean_ref[...]
-    for t in range(wide // TILE):
-        rows = slice(t * TILE, (t + 1) * TILE)
+    for t in range(tiles):
+        rows, columns = slice(t * TILE, (t + 1) * TILE), slice(t * TILE, wide)
         if t == 0:
             product = jnp.zeros((TILE, wide), jnp.float32)
             for c in range(rows_here // CHUNK):
@@ -219,12 +221,20 @@
                 )
         else:
             product = lax.dot_general(
-                e_ref[:, rows], e_ref[...], (((0,), (0,)), ((), ())), preferred_element_type=jnp.float32
+                e_ref[:, rows], e_ref[:, columns], (((0,), (0,)), ((), ())), preferred_element_type=jnp.float32
             )
         down = jnp.transpose(jnp.broadcast_to(mean[:, rows] * rows_here, (LANES, TILE)))
-        for j in range(wide // LANES):
-            across = slice(j * LANES, (j + 1) * LANES)
-            m_ref[rows, across] = product[:, across] - down * mean[:, across]
+        for u in range(t, tiles):
+            pieces = []
+            for j in range(u * TILE // LANES, (u + 1) * TILE // LANES):
+                across = slice(j * LANES, (j + 1) * LANES)
+                within = slice(j * LANES - t * TILE, (j + 1) * LANES - t * TILE)
+                pieces.append((product[:, within] - down * mean[:, across]).astype(jnp.bfloat16))
+            piece = jnp.concatenate(pieces, 1)
+            other = slice(u * TILE, (u + 1) * TILE)
+            m_ref[rows, other] = piece
+            if u > t:
+                m_ref[other, rows] = jnp.transpose(piece)
         for pair in range(TILE // block // 2):
             first = t * (TILE // block) + 2 * pair
             apart = (first ^ me) >> 1
@@ -232,10 +242,10 @@
             for k in range(bits - 1):
                 place = place + (((apart >> k) & 1) << (bits - 2 - k))
             to = pl.ds(pl.multiple_of(place * block, block), block)
-            kept = pl.multiple_of((first + (me & 1)) * block, block)
-            sent = pl.multiple_of((first + 1 - (me & 1)) * block, block)
-            keep_ref[to, :] = m_ref[pl.ds(kept, block), :]
-            send_ref[to, :] = m_ref[pl.ds(sent, block), :].astype(jnp.bfloat16)
+            even_rows = m_ref[first * block:(first + 1) * block, :]
+            odd_rows = m_ref[(first + 1) * block:(first + 2) * block, :]
+            keep_ref[to, :] = jnp.where(odd, odd_rows, even_rows)
+            send_ref[to, :] = jnp.where(odd, even_rows, odd_rows)
 
 
 def moments(width, me, embeddings, mean):
@@ -246,13 +256,13 @@
         in_specs=[pl.BlockSpec(memory_space=pltpu.SMEM)] + [pl.BlockSpec(memory_space=pl.ANY)] * 2,
         out_specs=[vmem] * 2,
         out_shape=[
-            jax.ShapeDtypeStruct((wide // 2, wide), jnp.float32),
+            jax.ShapeDtypeStruct((wide // 2, wide), jnp.bfloat16),
             jax.ShapeDtypeStruct((wide // 2, wide), jnp.bfloat16),
         ],
         scratch_shapes=[
             pltpu.VMEM((rows_here, wide), jnp.bfloat16),
             pltpu.VMEM((1, wide), jnp.float32),
-            pltpu.VMEM((wide, wide), jnp.float32),
+            pltpu.VMEM((wide, wide), jnp.bfloat16),
             pltpu.SemaphoreType.DMA((rows_here // CHUNK,)),
             pltpu.SemaphoreType.DMA,
         ],
@@ -272,7 +282,7 @@
         across = slice(h * columns, (h + 1) * columns)
         for p in range(pieces):
             at = slice(p * rows, (p + 1) * rows)
-            held = keep_ref[at, across]
+            held = keep_ref[at, across].astype(jnp.float32)
             for ref in came:
                 held = held + ref[at, across].astype(jnp.float32)
             out = outs[h * pieces + p]
@@ -296,23 +306,24 @@
     return [outs[h * pieces:(h + 1) * pieces] for h in range(shares)]
 
 
-def finish_kernel(total, between_ref, *refs):
+def finish_kernel(total, counts, between_ref, *refs):
     out_ref = refs[-1]
-    each = (len(refs) - 1) // SHARES
     columns = out_ref.shape[1] // SHARES
-    for h in range(SHARES):
+    at = 0
+    for h, count in enumerate(counts):
         across = slice(h * columns, (h + 1) * columns)
-        held = refs[h * each][...]
-        for ref in refs[h * each + 1:(h + 1) * each]:
+        held = refs[at][...]
+        for ref in refs[at + 1:at + count]:
             held = held + ref[...].astype(jnp.float32)
         out_ref[:, across] = (held + between_ref[:, across]) / total
+        at += count
 
 
 def finish(total, between, keeps, came):
     parts = [part for keep, pieces in zip(keeps, came) for part in (keep, *pieces)]
     vmem = pl.BlockSpec(memory_space=pltpu.VMEM)
     return pl.pallas_call(
-        functools.partial(finish_kernel, total),
+        functools.partial(finish_kernel, total, [1 + len(pieces) for pieces in came]),
         in_specs=[vmem] * (1 + len(parts)),
         out_specs=vmem,
         out_shape=jax.ShapeDtypeStruct(between.shape, jnp.float32),
@@ -322,9 +333,9 @@
     )(between, *parts)
 
 
-def halving_stages(width):
+def halving_stages(width, together):
     strides = [1 << k for k in range(width.bit_length() - 1)]
-    return [[s] for s in strides[:-2]] + [strides[-2:]]
+    return [[s] for s in strides[:-together]] + [strides[-together:]]
 
 
 def exchange(width, stage, out):
@@ -348,7 +359,7 @@
     size = width * NOTES
     to = lax.broadcasted_iota(jnp.int32, (size, size), 0)
     of = lax.broadcasted_iota(jnp.int32, (size, size), 1)
-    turn = jnp.where((to % width) * NOTES + to // width == of, 1.0, 0.0).astype(jnp.bfloat16)
+    turn = jnp.where((to & (width - 1)) * NOTES + (to >> (width.bit_length() - 1)) == of, 1.0, 0.0).astype(jnp.bfloat16)
     turned = jnp.dot(turn, notes, preferred_element_type=jnp.float32)
     row = [turned[r * width:(r + 1) * width] for r in range(NOTES)]
     digits = row[NOTES - 1]
@@ -373,8 +384,15 @@
 
     names = lax.broadcasted_iota(jnp.int32, (CAP, owned), 1).astype(jnp.int16)
 
+    groups = width // GROUP
+    if groups <= 4:
+        every = jnp.transpose(list_ref[...])
+
     def encode_group(g):
-        columns = jnp.transpose(list_ref[pl.ds(g * GROUP, GROUP), :])
+        if groups <= 4:
+            columns = every[:, g * GROUP:(g + 1) * GROUP]
+        else:
+            columns = jnp.transpose(list_ref[pl.ds(g * GROUP, GROUP), :])
         hits, projected, held = [], [], []
         for s in range(GROUP):
             listed = jnp.broadcast_to(columns[:, s:s + 1], (CAP, LANES))
@@ -392,7 +410,6 @@
         ).astype(jnp.bfloat16)
         return pltpu.make_async_copy(out_ref.at[at], out_hbm.at[at], sem.at[g])
 
-    groups = width // GROUP
     copies = []
     if groups <= 4:
         for g in range(groups):
@@ -459,20 +476,22 @@
     got = lax.all_to_all(rows.reshape(width, SPAN, feats), "wide", split_axis=0, concat_axis=0, tiled=True)
 
     keep, send = moments(width, me, embeddings, mean)
-    stages = halving_stages(width)
-    came = exchange(width, stages[0], [send])
-    shares = add_and_split(keep, came, SHARES, 1 << len(stages[1]))
-    last = []
-    for share in shares:
-        for n in range(1, len(stages) - 1):
-            came = exchange(width, stages[n], share[1:])
-            (share,) = add_and_split(share[0], came, 1, 1 << len(stages[n + 1]))
-        last.append(share)
-    came = [exchange(width, stages[-1], share[1:]) for share in last]
+    came = exchange(width, [1], [send])
+    shares = add_and_split(keep, came, SHARES, 2)
+    keeps, ends, sends = [], [], []
+    for together, (keep, *out) in zip((1, 2), shares):
+        stages = halving_stages(width, together)[1:]
+        for n, stage in enumerate(stages):
+            sends.append(out[0])
+            came = exchange(width, stage, out)
+            if n + 1 < len(stages):
+                ((keep, *out),) = add_and_split(keep, came, 1, 1 << len(stages[n + 1]))
+        keeps.append(keep)
+        ends.append(came)
     encoded, between = encode(
-        width, total, me, got.reshape(width * SPAN, feats), basis, centroids, rotation, [share[1] for share in last]
+        width, total, me, got.reshape(width * SPAN, feats), basis, centroids, rotation, sends
     )
-    covariance = finish(total, between, [share[0] for share in last], came)
+    covariance = finish(total, between, keeps, ends)
     return (encoded, covariance)
 
 

time: 57 us -> 59.5 us (1.044)
  waiting for transfers between devices: 14.8 us -> 19 us
  Pallas kernels: 19.5 us -> 18.5 us
  starting transfers between devices: 21.7 us -> 21 us
    ppermute x9 -> x8, waiting for transfers between devices: 14.8 us -> 19 us  [exchange(): lax.ppermute(out[p - 1], 'wide', [(i, i ^ apart) for i in range(width)])]
    pallas_call x1, Pallas kernels: 7.16 us -> 4.93 us  [moments(): pl.pallas_call(functools.partial(moments_kernel, width), in_specs=[pl.Blo...]
    pallas_call x3 -> x4, Pallas kernels: 0.26 us -> 1.63 us  [add_and_split(): pl.pallas_call(functools.partial(add_kernel, shares, pieces), in_specs=[v...]
    ppermute x9 -> x8, starting transfers between devices: 14.3 us -> 13.6 us  [exchange(): lax.ppermute(out[p - 1], 'wide', [(i, i ^ apart) for i in range(width)])]
  transfers between devices with their start and end apart: 10 -> 9, of which waited for: 4 -> 5; matrix products, arithmetic and copies ran while one was open for 0% -> 0% of each run, Pallas kernels for 20% -> 18%
where the time goes in v19:
time: 59.5 us; the launch traced here: 59.3 us
  starting transfers between devices  21 us (35%)
  waiting for transfers between devices  19 us (32%)
  Pallas kernels  18.5 us (31%)
  between operations  0.75 us (1%)
    ppermute x8, waiting for transfers between devices, exchange(): lax.ppermute(out[p - 1], 'wide', [(i, i ^ apart) for i in range(width)])  19 us
    ppermute x8, starting transfers between devices, exchange(): lax.ppermute(out[p - 1], 'wide', [(i, i ^ apart) for i in range(width)])  13.6 us
    all_to_all x1, starting transfers between devices, local(): lax.all_to_all(rows.reshape(width, SPAN, feats), 'wide', split_axis=0, co...  7.4 us
    pallas_call x1, Pallas kernels, project_and_sort(): pl.pallas_call(functools.partial(rows_kernel, width), grid=(rows_here //...  7.27 us
    pallas_call x1, Pallas kernels, moments(): pl.pallas_call(functools.partial(moments_kernel, width), in_specs=[pl.Blo...  4.93 us
    pallas_call x1, Pallas kernels, encode(): pl.pallas_call(functools.partial(encode_kernel, total), in_specs=[pl.Bloc...  3.9 us
    pallas_call x4, Pallas kernels, add_and_split(): pl.pallas_call(functools.partial(add_kernel, shares, pieces), in_specs=[v...  1.63 us
  transfers between devices with their start and end apart: 9, of which 5 were waited for; matrix products, arithmetic and copies ran while one was open for 0% of the time, Pallas kernels for 18%

profile of v19, /device:TPU:0, one launch (start us, length us, event | category | flops | bytes accessed | tf_op | source)
XLA Modules:
  0.0 59.3 jit_solution(2457069572569463321)
XLA Ops:
  0.6 7.3 %project_sort.1 = (bf16[2304,256]{1,0:T(8,128)(2,1)}, f32[1,1024]{1,0:T(1,128)}) custom-call(bf16[2048,1024]{1,0:T(8,128)(2,1)} %e_hbm.3, bf16[1024,256]{1,0:T(8,128)(2,1)} %basis_ref.1, s32[16,128]{1,0:T(8,128)} %bitcast.7, s32[16,128]{1,0:T(8,128)} %bitcast.8), custom_call_target="tpu_custom_call" | custom-call | flops 3489660928 | bytes 5373952 | tf_op jit(solution)/shard_map/project_sort/pallas_call | solution.py:162
  7.9 0.0 copy-start.3
  7.9 7.4 %all-to-all-start = ((bf16[16,144,256]{2,1,0:T(8,128)(2,1)}), bf16[16,144,256]{2,1,0:T(8,128)(2,1)S(1)}, u32[]{:S(2)}, u32[]{:S(2)}) async-start(bf16[16,144,256]{2,1,0:T(8,128)(2,1)} %bitcast.6), calls=%async_computation | async-start | bytes 2359296 | tf_op jit(solution)/shard_map/all_to_all | solution.py:476
  15.3 0.0 copy-done.3
  15.3 4.9 %moments.1 = (bf16[512,1024]{1,0:T(8,128)(2,1)S(1)}, bf16[512,1024]{1,0:T(8,128)(2,1)S(1)}) custom-call(s32[1]{0:T(128)} %bitcast.me_ref, f32[1,1024]{1,0:T(1,128)S(1)} %copy-done.3, bf16[2048,1024]{1,0:T(8,128)(2,1)} %e_hbm.3), custom_call_target="tpu_custom_call" | custom-call | flops 4294967296 | bytes 7340032 | tf_op jit(solution)/shard_map/moments/pallas_call | solution.py:254
  20.3 0.5 collective-permute-start
  20.7 2.3 %collective-permute-done.refs_0_ = bf16[512,1024]{1,0:T(8,128)(2,1)S(1)} collective-permute-done((bf16[512,1024]{1,0:T(8,128)(2,1)S(1)}, bf16[512,1024]{1,0:T(8,128)(2,1)S(1)}, u32[]{:S(2)}, u32[]{:S(2)}) %collective-permute-start) | collective-permute-done | bytes 1048608 | tf_op jit(solution)/shard_map/ppermute | solution.py:345
  23.0 0.2 add_and_split.4
  23.3 0.0 copy-start
  23.3 0.0 copy-start.1
  23.3 0.0 copy-start.2
  23.3 2.0 %collective-permute-start.1 = (bf16[256,512]{1,0:T(8,128)(2,1)S(1)}, bf16[256,512]{1,0:T(8,128)(2,1)S(1)}, u32[]{:S(2)}, u32[]{:S(2)}) collective-permute-start(bf16[256,512]{1,0:T(8,128)(2,1)S(1)} %get-tuple-element.24.refs_0_), channel_id=1, source_target_pairs={{0,2},{1,3},{2,0},{3,1},{4,6},{5,7},{6,4},{7,5},{8,10},{9,11},{10,... | collective-permute-start | bytes 786440 | tf_op jit(solution)/shard_map/ppermute | solution.py:345
  25.2 0.2 collective-permute-start.3
  25.4 11.0 %collective-permute-done.1.refs_0_ = bf16[256,512]{1,0:T(8,128)(2,1)S(1)} collective-permute-done((bf16[256,512]{1,0:T(8,128)(2,1)S(1)}, bf16[256,512]{1,0:T(8,128)(2,1)S(1)}, u32[]{:S(2)}, u32[]{:S(2)}) %collective-permute-start.1) | collective-permute-done | bytes 262176 | tf_op jit(solution)/shard_map/ppermute | solution.py:345
  36.5 3.6 %collective-permute-start.2 = (bf16[128,512]{1,0:T(8,128)(2,1)S(1)}, bf16[128,512]{1,0:T(8,128)(2,1)S(1)}, u32[]{:S(2)}, u32[]{:S(2)}) collective-permute-start(bf16[128,512]{1,0:T(8,128)(2,1)S(1)} %get-tuple-element.26.refs_1_), channel_id=1, source_target_pairs={{0,4},{1,5},{2,6},{3,7},{4,0},{5,1},{6,2},{7,3},{8,12},{9,13},{10,... | collective-permute-start | bytes 393224 | tf_op jit(solution)/shard_map/ppermute | solution.py:345
  40.1 3.3 %collective-permute-done.3.refs_0_ = bf16[256,512]{1,0:T(8,128)(2,1)S(1)} collective-permute-done((bf16[256,512]{1,0:T(8,128)(2,1)S(1)}, bf16[256,512]{1,0:T(8,128)(2,1)S(1)}, u32[]{:S(2)}, u32[]{:S(2)}) %collective-permute-start.3) | collective-permute-done | bytes 262176 | tf_op jit(solution)/shard_map/ppermute | solution.py:345
  43.4 0.7 %add_and_split.7 = (f32[64,512]{1,0:T(8,128)S(1)}, bf16[64,512]{1,0:T(8,128)(2,1)}, bf16[64,512]{1,0:T(8,128)(2,1)}, bf16[64,512]{1,0:T(8,128)(2,1)}) custom-call(f32[256,512]{1,0:T(8,128)S(1)} %get-tuple-element.30.keep_ref, bf16[256,512]{1,0:T(8,128)(2,1)S(1)} %collective-permute-done.3.refs_0_), custom_call_target="tpu_custom_call" | custom-call | flops 262144 | bytes 1310720 | tf_op jit(solution)/shard_map/add_and_split/pallas_call | solution.py:297
  44.1 3.5 %collective-permute-start.6 = (bf16[64,512]{1,0:T(8,128)(2,1)}, bf16[64,512]{1,0:T(8,128)(2,1)S(1)}, u32[]{:S(2)}, u32[]{:S(2)}) collective-permute-start(bf16[64,512]{1,0:T(8,128)(2,1)} %get-tuple-element.36), channel_id=1, source_target_pairs={{0,4},{1,5},{2,6},{3,7},{4,0},{5,1},{6,2},{7,3},{8,12},{9,13},{10,... | collective-permute-start | bytes 196616 | tf_op jit(solution)/shard_map/ppermute | solution.py:345
  47.6 1.1 %collective-permute-start.7 = (bf16[64,512]{1,0:T(8,128)(2,1)}, bf16[64,512]{1,0:T(8,128)(2,1)S(1)}, u32[]{:S(2)}, u32[]{:S(2)}) collective-permute-start(bf16[64,512]{1,0:T(8,128)(2,1)} %get-tuple-element.37), channel_id=1, source_target_pairs={{0,12},{1,13},{2,14},{3,15},{4,8},{5,9},{6,10},{7,11},{8,4},{9,5},... | collective-permute-start | bytes 196616 | tf_op jit(solution)/shard_map/ppermute | solution.py:345
  48.6 0.4 collective-permute-start.5
  49.0 0.0 collective-permute-done.2.refs_0_
  49.0 0.6 %add_and_split.6 = (f32[64,512]{1,0:T(8,128)S(1)}, bf16[64,512]{1,0:T(8,128)(2,1)}) custom-call(f32[128,512]{1,0:T(8,128)S(1)} %get-tuple-element.27.keep_ref, bf16[128,512]{1,0:T(8,128)(2,1)S(1)} %collective-permute-done.2.refs_0_), custom_call_target="tpu_custom_call" | custom-call | flops 131072 | bytes 655360 | tf_op jit(solution)/shard_map/add_and_split/pallas_call | solution.py:297
  49.7 2.5 %collective-permute-start.4 = (bf16[64,512]{1,0:T(8,128)(2,1)}, bf16[64,512]{1,0:T(8,128)(2,1)S(1)}, u32[]{:S(2)}, u32[]{:S(2)}) collective-permute-start(bf16[64,512]{1,0:T(8,128)(2,1)} %get-tuple-element.28.refs_2_), channel_id=1, source_target_pairs={{0,8},{1,9},{2,10},{3,11},{4,12},{5,13},{6,14},{7,15},{8,0},{9,1},... | collective-permute-start | bytes 196616 | tf_op jit(solution)/shard_map/ppermute | solution.py:345
  52.2 0.0 all-to-all-done
  52.2 0.0 copy-done
  52.2 0.0 copy-done.2
  52.2 3.9 %encode.1 = (bf16[2048,256]{1,0:T(8,128)(2,1)}, f32[64,1024]{1,0:T(8,128)S(1)}) custom-call(s32[1]{0:T(128)} %bitcast.me_ref, bf16[2304,256]{1,0:T(8,128)(2,1)S(1)} %bitcast.5, bf16[1024,256]{1,0:T(8,128)(2,1)S(1)} %copy-done, bf16[1024,256]{1,0:T(8,128)(2,1)S(1)} %copy-done.1, bf16[256,256]{1,0:T(8,128)(2,1)S(1)} %copy-done.2, ...), custom_call_target="tpu_custom_call" | custom-call | flops 1342177280 | bytes 2097152 | tf_op jit(solution)/shard_map/encode/pallas_call | solution.py:445
  56.1 0.0 collective-permute-done.6.refs_4_
  56.1 0.0 collective-permute-done.7.refs_5_
  56.2 1.6 %collective-permute-done.5.refs_3_ = bf16[64,512]{1,0:T(8,128)(2,1)S(1)} collective-permute-done((bf16[64,512]{1,0:T(8,128)(2,1)}, bf16[64,512]{1,0:T(8,128)(2,1)S(1)}, u32[]{:S(2)}, u32[]{:S(2)}) %collective-permute-start.5) | collective-permute-done | bytes 65568 | tf_op jit(solution)/shard_map/ppermute | solution.py:345
  57.8 0.7 %collective-permute-done.4.refs_1_ = bf16[64,512]{1,0:T(8,128)(2,1)S(1)} collective-permute-done((bf16[64,512]{1,0:T(8,128)(2,1)}, bf16[64,512]{1,0:T(8,128)(2,1)S(1)}, u32[]{:S(2)}, u32[]{:S(2)}) %collective-permute-start.4) | collective-permute-done | bytes 65568 | tf_op jit(solution)/shard_map/ppermute | solution.py:345
  58.5 0.8 %finish.1 = f32[64,1024]{1,0:T(8,128)} custom-call(f32[64,1024]{1,0:T(8,128)S(1)} %get-tuple-element.33.between_ref, f32[64,512]{1,0:T(8,128)S(1)} %get-tuple-element.34.refs_0_, bf16[64,512]{1,0:T(8,128)(2,1)S(1)} %collective-permute-done.4.refs_1_, f32[64,512]{1,0:T(8,128)S(1)} %get-tuple-element.35.refs_2_, ...), custom_call_target="tpu_custom_call" | custom-call | flops 524288 | bytes 1048576 | tf_op jit(solution)/shard_map/finish/pallas_call | solution.py:325
  (2 shorter events, 0.0 us)
Async XLA Ops:
  7.9 7.4 %copy-start.3 = (f32[1,1024]{1,0:T(1,128)S(1)}, f32[1,1024]{1,0:T(1,128)}, u32[]{:S(2)}) copy-start(f32[1,1024]{1,0:T(1,128)} %get-tuple-element.21.mean_hbm) | copy-start | bytes 12292
  7.9 44.3 %all-to-all-start = ((bf16[16,144,256]{2,1,0:T(8,128)(2,1)}), bf16[16,144,256]{2,1,0:T(8,128)(2,1)S(1)}, u32[]{:S(2)}, u32[]{:S(2)}) async-start(bf16[16,144,256]{2,1,0:T(8,128)(2,1)} %bitcast.6), calls=%async_computation | async-start | bytes 2359296 | tf_op jit(solution)/shard_map/all_to_all | solution.py:476
  20.3 2.8 %collective-permute-start = (bf16[512,1024]{1,0:T(8,128)(2,1)S(1)}, bf16[512,1024]{1,0:T(8,128)(2,1)S(1)}, u32[]{:S(2)}, u32[]{:S(2)}) collective-permute-start(bf16[512,1024]{1,0:T(8,128)(2,1)S(1)} %get-tuple-element.23), channel_id=1, source_target_pairs={{0,1},{1,0},{2,3},{3,2},{4,5},{5,4},{6,7},{7,6},{8,9},{9,8},{10,11... | collective-permute-start | bytes 3145736 | tf_op jit(solution)/shard_map/ppermute | solution.py:345
  23.3 28.9 %copy-start = (bf16[1024,256]{1,0:T(8,128)(2,1)S(1)}, bf16[1024,256]{1,0:T(8,128)(2,1)}, u32[]{:S(2)}) copy-start(bf16[1024,256]{1,0:T(8,128)(2,1)} %basis_ref.1) | copy-start | bytes 1572868
  23.3 28.9 %copy-start.1 = (bf16[1024,256]{1,0:T(8,128)(2,1)S(1)}, bf16[1024,256]{1,0:T(8,128)(2,1)}, u32[]{:S(2)}) copy-start(bf16[1024,256]{1,0:T(8,128)(2,1)} %centroid_ref.1) | copy-start | bytes 1572868
  23.3 28.9 %copy-start.2 = (bf16[256,256]{1,0:T(8,128)(2,1)S(1)}, bf16[256,256]{1,0:T(8,128)(2,1)}, u32[]{:S(2)}) copy-start(bf16[256,256]{1,0:T(8,128)(2,1)} %rotation_ref.1) | copy-start | bytes 393220
  23.3 13.2 %collective-permute-start.1 = (bf16[256,512]{1,0:T(8,128)(2,1)S(1)}, bf16[256,512]{1,0:T(8,128)(2,1)S(1)}, u32[]{:S(2)}, u32[]{:S(2)}) collective-permute-start(bf16[256,512]{1,0:T(8,128)(2,1)S(1)} %get-tuple-element.24.refs_0_), channel_id=1, source_target_pairs={{0,2},{1,3},{2,0},{3,1},{4,6},{5,7},{6,4},{7,5},{8,10},{9,11},{10,... | collective-permute-start | bytes 786440 | tf_op jit(solution)/shard_map/ppermute | solution.py:345
  25.2 18.1 %collective-permute-start.3 = (bf16[256,512]{1,0:T(8,128)(2,1)S(1)}, bf16[256,512]{1,0:T(8,128)(2,1)S(1)}, u32[]{:S(2)}, u32[]{:S(2)}) collective-permute-start(bf16[256,512]{1,0:T(8,128)(2,1)S(1)} %get-tuple-element.29.refs_3_), channel_id=1, source_target_pairs={{0,2},{1,3},{2,0},{3,1},{4,6},{5,7},{6,4},{7,5},{8,10},{9,11},{10,... | collective-permute-start | bytes 786440 | tf_op jit(solution)/shard_map/ppermute | solution.py:345
  36.5 12.5 %collective-permute-start.2 = (bf16[128,512]{1,0:T(8,128)(2,1)S(1)}, bf16[128,512]{1,0:T(8,128)(2,1)S(1)}, u32[]{:S(2)}, u32[]{:S(2)}) collective-permute-start(bf16[128,512]{1,0:T(8,128)(2,1)S(1)} %get-tuple-element.26.refs_1_), channel_id=1, source_target_pairs={{0,4},{1,5},{2,6},{3,7},{4,0},{5,1},{6,2},{7,3},{8,12},{9,13},{10,... | collective-permute-start | bytes 393224 | tf_op jit(solution)/shard_map/ppermute | solution.py:345
  44.1 12.0 %collective-permute-start.6 = (bf16[64,512]{1,0:T(8,128)(2,1)}, bf16[64,512]{1,0:T(8,128)(2,1)S(1)}, u32[]{:S(2)}, u32[]{:S(2)}) collective-permute-start(bf16[64,512]{1,0:T(8,128)(2,1)} %get-tuple-element.36), channel_id=1, source_target_pairs={{0,4},{1,5},{2,6},{3,7},{4,0},{5,1},{6,2},{7,3},{8,12},{9,13},{10,... | collective-permute-start | bytes 196616 | tf_op jit(solution)/shard_map/ppermute | solution.py:345
  47.6 8.6 %collective-permute-start.7 = (bf16[64,512]{1,0:T(8,128)(2,1)}, bf16[64,512]{1,0:T(8,128)(2,1)S(1)}, u32[]{:S(2)}, u32[]{:S(2)}) collective-permute-start(bf16[64,512]{1,0:T(8,128)(2,1)} %get-tuple-element.37), channel_id=1, source_target_pairs={{0,12},{1,13},{2,14},{3,15},{4,8},{5,9},{6,10},{7,11},{8,4},{9,5},... | collective-permute-start | bytes 196616 | tf_op jit(solution)/shard_map/ppermute | solution.py:345
  48.6 9.1 %collective-permute-start.5 = (bf16[64,512]{1,0:T(8,128)(2,1)}, bf16[64,512]{1,0:T(8,128)(2,1)S(1)}, u32[]{:S(2)}, u32[]{:S(2)}) collective-permute-start(bf16[64,512]{1,0:T(8,128)(2,1)} %get-tuple-element.31.refs_4_), channel_id=1, source_target_pairs={{0,8},{1,9},{2,10},{3,11},{4,12},{5,13},{6,14},{7,15},{8,0},{9,1},... | collective-permute-start | bytes 196616 | tf_op jit(solution)/shard_map/ppermute | solution.py:345
  49.7 8.8 %collective-permute-start.4 = (bf16[64,512]{1,0:T(8,128)(2,1)}, bf16[64,512]{1,0:T(8,128)(2,1)S(1)}, u32[]{:S(2)}, u32[]{:S(2)}) collective-permute-start(bf16[64,512]{1,0:T(8,128)(2,1)} %get-tuple-element.28.refs_2_), channel_id=1, source_target_pairs={{0,8},{1,9},{2,10},{3,11},{4,12},{5,13},{6,14},{7,15},{8,0},{9,1},... | collective-permute-start | bytes 196616 | tf_op jit(solution)/shard_map/ppermute | solution.py:345

commit v20 on v8

--- a/solution.py
+++ b/solution.py
@@ -15,9 +15,18 @@
 TILE = 256
 GROUP = 4
 SHARES = 2
+PLANE = 4
 VMEM_ALL = 60 * 1024 * 1024
 VMEM_SOME = 24 * 1024 * 1024
 VMEM_MOST = 48 * 1024 * 1024
+
+
+def place_of(width, device):
+    return (device & (PLANE - 1)) * (width // PLANE) + device // PLANE
+
+
+def device_at(width, place):
+    return (place & (width // PLANE - 1)) * PLANE + place // (width // PLANE)
 
 
 def in_three(x):
@@ -55,7 +64,7 @@
         owner_copy.wait()
         sum_ref[...] = jnp.zeros_like(sum_ref)
         total_ref[...] = jnp.zeros_like(total_ref)
-        owner = owner_ref[...]
+        owner = place_of(width, owner_ref[...])
         wanted = lax.broadcasted_iota(jnp.int32, (width, LANES), 0)
         hits = [jnp.where(owner[c:c + 1, :] == wanted, 1.0, 0.0) for c in range(chunks)]
         flat = jnp.concatenate(hits, 0).astype(jnp.bfloat16)
@@ -197,6 +206,7 @@
     rows_here, wide = e_ref.shape
     block = wide // width
     bits = width.bit_length() - 1
+    tiles = wide // TILE
     mean_copy = pltpu.make_async_copy(mean_hbm, mean_ref, mean_sem)
     mean_copy.start()
     copies = []
@@ -205,10 +215,11 @@
         copies.append(pltpu.make_async_copy(e_hbm.at[at], e_ref.at[at], sem.at[c]))
         copies[c].start()
     me = me_ref[0]
+    odd = (me & 1) == 1
     mean_copy.wait()
     mean = mean_ref[...]
-    for t in range(wide // TILE):
-        rows = slice(t * TILE, (t + 1) * TILE)
+    for t in range(tiles):
+        rows, columns = slice(t * TILE, (t + 1) * TILE), slice(t * TILE, wide)
         if t == 0:
             product = jnp.zeros((TILE, wide), jnp.float32)
             for c in range(rows_here // CHUNK):
@@ -219,12 +230,20 @@
                 )
         else:
             product = lax.dot_general(
-                e_ref[:, rows], e_ref[...], (((0,), (0,)), ((), ())), preferred_element_type=jnp.float32
+                e_ref[:, rows], e_ref[:, columns], (((0,), (0,)), ((), ())), preferred_element_type=jnp.float32
             )
         down = jnp.transpose(jnp.broadcast_to(mean[:, rows] * rows_here, (LANES, TILE)))
-        for j in range(wide // LANES):
-            across = slice(j * LANES, (j + 1) * LANES)
-            m_ref[rows, across] = product[:, across] - down * mean[:, across]
+        for u in range(t, tiles):
+            pieces = []
+            for j in range(u * TILE // LANES, (u + 1) * TILE // LANES):
+                across = slice(j * LANES, (j + 1) * LANES)
+                within = slice(j * LANES - t * TILE, (j + 1) * LANES - t * TILE)
+                pieces.append((product[:, within] - down * mean[:, across]).astype(jnp.bfloat16))
+            piece = jnp.concatenate(pieces, 1)
+            other = slice(u * TILE, (u + 1) * TILE)
+            m_ref[rows, other] = piece
+            if u > t:
+                m_ref[other, rows] = jnp.transpose(piece)
         for pair in range(TILE // block // 2):
             first = t * (TILE // block) + 2 * pair
             apart = (first ^ me) >> 1
@@ -232,10 +251,10 @@
             for k in range(bits - 1):
                 place = place + (((apart >> k) & 1) << (bits - 2 - k))
             to = pl.ds(pl.multiple_of(place * block, block), block)
-            kept = pl.multiple_of((first + (me & 1)) * block, block)
-            sent = pl.multiple_of((first + 1 - (me & 1)) * block, block)
-            keep_ref[to, :] = m_ref[pl.ds(kept, block), :]
-            send_ref[to, :] = m_ref[pl.ds(sent, block), :].astype(jnp.bfloat16)
+            even_rows = m_ref[first * block:(first + 1) * block, :]
+            odd_rows = m_ref[(first + 1) * block:(first + 2) * block, :]
+            keep_ref[to, :] = jnp.where(odd, odd_rows, even_rows)
+            send_ref[to, :] = jnp.where(odd, even_rows, odd_rows)
 
 
 def moments(width, me, embeddings, mean):
@@ -246,13 +265,13 @@
         in_specs=[pl.BlockSpec(memory_space=pltpu.SMEM)] + [pl.BlockSpec(memory_space=pl.ANY)] * 2,
         out_specs=[vmem] * 2,
         out_shape=[
-            jax.ShapeDtypeStruct((wide // 2, wide), jnp.float32),
+            jax.ShapeDtypeStruct((wide // 2, wide), jnp.bfloat16),
             jax.ShapeDtypeStruct((wide // 2, wide), jnp.bfloat16),
         ],
         scratch_shapes=[
             pltpu.VMEM((rows_here, wide), jnp.bfloat16),
             pltpu.VMEM((1, wide), jnp.float32),
-            pltpu.VMEM((wide, wide), jnp.float32),
+            pltpu.VMEM((wide, wide), jnp.bfloat16),
             pltpu.SemaphoreType.DMA((rows_here // CHUNK,)),
             pltpu.SemaphoreType.DMA,
         ],
@@ -272,7 +291,7 @@
         across = slice(h * columns, (h + 1) * columns)
         for p in range(pieces):
             at = slice(p * rows, (p + 1) * rows)
-            held = keep_ref[at, across]
+            held = keep_ref[at, across].astype(jnp.float32)
             for ref in came:
                 held = held + ref[at, across].astype(jnp.float32)
             out = outs[h * pieces + p]
@@ -390,21 +409,30 @@
         out_ref[at, :] = jnp.dot(
             residual.astype(jnp.bfloat16), rotation_ref[...], preferred_element_type=jnp.float32
         ).astype(jnp.bfloat16)
-        return pltpu.make_async_copy(out_ref.at[at], out_hbm.at[at], sem.at[g])
+        copies = []
+        for s in range(GROUP):
+            place = g * GROUP + s
+            here = pl.ds(pl.multiple_of(place * CAP, CAP), CAP)
+            there = pl.ds(pl.multiple_of(device_at(width, place) * CAP, CAP), CAP)
+            copies.append(pltpu.make_async_copy(out_ref.at[here], out_hbm.at[there], sem.at[place]))
+        return copies
 
     groups = width // GROUP
     copies = []
     if groups <= 4:
         for g in range(groups):
-            copies.append(encode_group(g))
-            copies[g].start()
+            for copy in encode_group(g):
+                copy.start()
+                copies.append(copy)
     else:
 
         @pl.loop(0, groups)
         def _(g):
-            copy = encode_group(g)
-            copy.start()
-            copy.wait()
+            for copy in encode_group(g):
+                copy.start()
+            for s in range(GROUP):
+                at = pl.ds(pl.multiple_of((g * GROUP + s) * CAP, CAP), CAP)
+                pltpu.make_async_copy(out_ref.at[at], out_hbm.at[at], sem.at[g * GROUP + s]).wait()
 
     first = me_ref[0] * block
     near = apart_ref[:, pl.ds(pl.multiple_of(first // LANES * LANES, LANES), LANES)]
@@ -438,7 +466,7 @@
             pltpu.VMEM((width, feats), jnp.float32),
             pltpu.VMEM((width, CAP), jnp.float32),
             pltpu.VMEM((width, wide), jnp.float32),
-            pltpu.SemaphoreType.DMA((width // GROUP,)),
+            pltpu.SemaphoreType.DMA((width,)),
         ],
         compiler_params=pltpu.CompilerParams(vmem_limit_bytes=VMEM_SOME),
         cost_estimate=pl.CostEstimate(
@@ -456,7 +484,10 @@
     total = rows_here * width
 
     rows, mean = project_and_sort(width, embeddings, basis, list_owner, list_slot)
-    got = lax.all_to_all(rows.reshape(width, SPAN, feats), "wide", split_axis=0, concat_axis=0, tiled=True)
+    order = [[device_at(width, place) for place in range(width)]]
+    got = lax.all_to_all(
+        rows.reshape(width, SPAN, feats), "wide", split_axis=0, concat_axis=0, tiled=True, axis_index_groups=order
+    )
 
     keep, send = moments(width, me, embeddings, mean)
     stages = halving_stages(width)

time: 57 us -> 56.9 us (level)
  waiting for transfers between devices: 14.8 us -> 17.1 us
  Pallas kernels: 19.5 us -> 17.4 us
    ppermute x9, waiting for transfers between devices: 14.8 us -> 17.1 us  [exchange(): lax.ppermute(out[p - 1], 'wide', [(i, i ^ apart) for i in range(width)])]
    pallas_call x1, Pallas kernels: 7.16 us -> 4.93 us  [moments(): pl.pallas_call(functools.partial(moments_kernel, width), in_specs=[pl.Blo...]
  transfers between devices with their start and end apart: 10 -> 10, of which waited for: 4 -> 4; matrix products, arithmetic and copies ran while one was open for 0% -> 0% of each run, Pallas kernels for 20% -> 16%
where the time goes in v20:
time: 56.9 us; the launch traced here: 56.7 us
  starting transfers between devices  21.4 us (38%)
  Pallas kernels  17.4 us (31%)
  waiting for transfers between devices  17.1 us (30%)
  between operations  0.74 us (1%)
    ppermute x9, waiting for transfers between devices, exchange(): lax.ppermute(out[p - 1], 'wide', [(i, i ^ apart) for i in range(width)])  17.1 us
    ppermute x9, starting transfers between devices, exchange(): lax.ppermute(out[p - 1], 'wide', [(i, i ^ apart) for i in range(width)])  14 us
    all_to_all x1, starting transfers between devices, local(): lax.all_to_all(rows.reshape(width, SPAN, feats), 'wide', split_axis=0, co...  7.4 us
    pallas_call x1, Pallas kernels, project_and_sort(): pl.pallas_call(functools.partial(rows_kernel, width), grid=(rows_here //...  7.27 us
    pallas_call x1, Pallas kernels, moments(): pl.pallas_call(functools.partial(moments_kernel, width), in_specs=[pl.Blo...  4.93 us
    pallas_call x1, Pallas kernels, encode(): pl.pallas_call(functools.partial(encode_kernel, total), in_specs=[pl.Bloc...  4.09 us
  transfers between devices with their start and end apart: 10, of which 4 were waited for; matrix products, arithmetic and copies ran while one was open for 0% of the time, Pallas kernels for 16%

profile of v20, /device:TPU:0, one launch (start us, length us, event | category | flops | bytes accessed | tf_op | source)
XLA Modules:
  0.0 56.7 jit_solution(12799554283968048381)
XLA Ops:
  0.6 7.3 %project_sort.1 = (bf16[2304,256]{1,0:T(8,128)(2,1)}, f32[1,1024]{1,0:T(1,128)}) custom-call(bf16[2048,1024]{1,0:T(8,128)(2,1)} %e_hbm.3, bf16[1024,256]{1,0:T(8,128)(2,1)} %basis_ref.1, s32[16,128]{1,0:T(8,128)} %bitcast.7, s32[16,128]{1,0:T(8,128)} %bitcast.8), custom_call_target="tpu_custom_call" | custom-call | flops 3489660928 | bytes 5373952 | tf_op jit(solution)/shard_map/project_sort/pallas_call | solution.py:171
  7.9 0.0 copy-start.3
  7.9 7.4 %all-to-all-start = ((bf16[16,144,256]{2,1,0:T(8,128)(2,1)}), bf16[16,144,256]{2,1,0:T(8,128)(2,1)S(1)}, u32[]{:S(2)}, u32[]{:S(2)}) async-start(bf16[16,144,256]{2,1,0:T(8,128)(2,1)} %bitcast.6), calls=%async_computation | async-start | bytes 2359296 | tf_op jit(solution)/shard_map/all_to_all | solution.py:488
  15.3 0.0 copy-done.3
  15.3 4.9 %moments.1 = (bf16[512,1024]{1,0:T(8,128)(2,1)S(1)}, bf16[512,1024]{1,0:T(8,128)(2,1)S(1)}) custom-call(s32[1]{0:T(128)} %bitcast.me_ref, f32[1,1024]{1,0:T(1,128)S(1)} %copy-done.3, bf16[2048,1024]{1,0:T(8,128)(2,1)} %e_hbm.3), custom_call_target="tpu_custom_call" | custom-call | flops 4294967296 | bytes 7340032 | tf_op jit(solution)/shard_map/moments/pallas_call | solution.py:263
  20.3 0.5 collective-permute-start
  20.7 2.3 %collective-permute-done.refs_0_ = bf16[512,1024]{1,0:T(8,128)(2,1)S(1)} collective-permute-done((bf16[512,1024]{1,0:T(8,128)(2,1)S(1)}, bf16[512,1024]{1,0:T(8,128)(2,1)S(1)}, u32[]{:S(2)}, u32[]{:S(2)}) %collective-permute-start) | collective-permute-done | bytes 1048608 | tf_op jit(solution)/shard_map/ppermute | solution.py:353
  23.0 0.2 add_and_split.3
  23.3 0.0 copy-start
  23.3 0.0 copy-start.1
  23.3 0.0 copy-start.2
  23.3 2.0 %collective-permute-start.1 = (bf16[256,512]{1,0:T(8,128)(2,1)S(1)}, bf16[256,512]{1,0:T(8,128)(2,1)S(1)}, u32[]{:S(2)}, u32[]{:S(2)}) collective-permute-start(bf16[256,512]{1,0:T(8,128)(2,1)S(1)} %get-tuple-element.25), channel_id=1, source_target_pairs={{0,2},{1,3},{2,0},{3,1},{4,6},{5,7},{6,4},{7,5},{8,10},{9,11},{10,... | collective-permute-start | bytes 786440 | tf_op jit(solution)/shard_map/ppermute | solution.py:353
  25.2 0.2 collective-permute-start.2
  25.4 11.0 %collective-permute-done.1.refs_0_ = bf16[256,512]{1,0:T(8,128)(2,1)S(1)} collective-permute-done((bf16[256,512]{1,0:T(8,128)(2,1)S(1)}, bf16[256,512]{1,0:T(8,128)(2,1)S(1)}, u32[]{:S(2)}, u32[]{:S(2)}) %collective-permute-start.1) | collective-permute-done | bytes 262176 | tf_op jit(solution)/shard_map/ppermute | solution.py:353
  36.4 1.4 %collective-permute-start.4 = (bf16[64,512]{1,0:T(8,128)(2,1)S(1)}, bf16[64,512]{1,0:T(8,128)(2,1)S(1)}, u32[]{:S(2)}, u32[]{:S(2)}) collective-permute-start(bf16[64,512]{1,0:T(8,128)(2,1)S(1)} %get-tuple-element.33), channel_id=1, source_target_pairs={{0,4},{1,5},{2,6},{3,7},{4,0},{5,1},{6,2},{7,3},{8,12},{9,13},{10,... | collective-permute-start | bytes 196616 | tf_op jit(solution)/shard_map/ppermute | solution.py:353
  37.8 4.3 %collective-permute-start.5 = (bf16[64,512]{1,0:T(8,128)(2,1)S(1)}, bf16[64,512]{1,0:T(8,128)(2,1)S(1)}, u32[]{:S(2)}, u32[]{:S(2)}) collective-permute-start(bf16[64,512]{1,0:T(8,128)(2,1)S(1)} %get-tuple-element.34), channel_id=1, source_target_pairs={{0,12},{1,13},{2,14},{3,15},{4,8},{5,9},{6,10},{7,11},{8,4},{9,5},... | collective-permute-start | bytes 196616 | tf_op jit(solution)/shard_map/ppermute | solution.py:353
  42.1 0.5 collective-permute-start.3
  42.6 0.0 collective-permute-done.2.refs_0_
  42.7 3.5 %collective-permute-start.7 = (bf16[64,512]{1,0:T(8,128)(2,1)S(1)}, bf16[64,512]{1,0:T(8,128)(2,1)S(1)}, u32[]{:S(2)}, u32[]{:S(2)}) collective-permute-start(bf16[64,512]{1,0:T(8,128)(2,1)S(1)} %get-tuple-element.36), channel_id=1, source_target_pairs={{0,4},{1,5},{2,6},{3,7},{4,0},{5,1},{6,2},{7,3},{8,12},{9,13},{10,... | collective-permute-start | bytes 196616 | tf_op jit(solution)/shard_map/ppermute | solution.py:353
  46.1 1.3 %collective-permute-start.8 = (bf16[64,512]{1,0:T(8,128)(2,1)S(1)}, bf16[64,512]{1,0:T(8,128)(2,1)S(1)}, u32[]{:S(2)}, u32[]{:S(2)}) collective-permute-start(bf16[64,512]{1,0:T(8,128)(2,1)S(1)} %get-tuple-element.37), channel_id=1, source_target_pairs={{0,12},{1,13},{2,14},{3,15},{4,8},{5,9},{6,10},{7,11},{8,4},{9,5},... | collective-permute-start | bytes 196616 | tf_op jit(solution)/shard_map/ppermute | solution.py:353
  47.4 0.0 collective-permute-done.4.refs_2_
  47.4 0.5 collective-permute-start.6
  47.9 0.0 all-to-all-done
  47.9 0.0 copy-done
  47.9 0.0 copy-done.1
  47.9 4.1 %encode.1 = (bf16[2048,256]{1,0:T(8,128)(2,1)}, f32[64,1024]{1,0:T(8,128)S(1)}) custom-call(s32[1]{0:T(128)} %bitcast.me_ref, bf16[2304,256]{1,0:T(8,128)(2,1)S(1)} %bitcast.5, bf16[1024,256]{1,0:T(8,128)(2,1)S(1)} %copy-done, bf16[1024,256]{1,0:T(8,128)(2,1)S(1)} %copy-done.1, bf16[256,256]{1,0:T(8,128)(2,1)S(1)} %copy-done.2, ...), custom_call_target="tpu_custom_call" | custom-call | flops 1342177280 | bytes 2097152 | tf_op jit(solution)/shard_map/encode/pallas_call | solution.py:456
  52.0 0.0 collective-permute-done.5.refs_3_
  52.1 1.5 %collective-permute-done.3.refs_1_ = bf16[64,512]{1,0:T(8,128)(2,1)S(1)} collective-permute-done((bf16[64,512]{1,0:T(8,128)(2,1)S(1)}, bf16[64,512]{1,0:T(8,128)(2,1)S(1)}, u32[]{:S(2)}, u32[]{:S(2)}) %collective-permute-start.3) | collective-permute-done | bytes 65568 | tf_op jit(solution)/shard_map/ppermute | solution.py:353
  53.6 0.0 collective-permute-done.7.refs_6_
  53.6 0.0 collective-permute-done.8.refs_7_
  53.6 2.3 %collective-permute-done.6.refs_5_ = bf16[64,512]{1,0:T(8,128)(2,1)S(1)} collective-permute-done((bf16[64,512]{1,0:T(8,128)(2,1)S(1)}, bf16[64,512]{1,0:T(8,128)(2,1)S(1)}, u32[]{:S(2)}, u32[]{:S(2)}) %collective-permute-start.6) | collective-permute-done | bytes 65568 | tf_op jit(solution)/shard_map/ppermute | solution.py:353
  55.9 0.8 %finish.1 = f32[64,1024]{1,0:T(8,128)} custom-call(f32[64,1024]{1,0:T(8,128)S(1)} %get-tuple-element.31.between_ref, f32[64,512]{1,0:T(8,128)S(1)} %get-tuple-element.32.refs_0_, bf16[64,512]{1,0:T(8,128)(2,1)S(1)} %collective-permute-done.3.refs_1_, bf16[64,512]{1,0:T(8,128)(2,1)S(1)} %collective-permute-done.4.refs_2_, ...), custom_call_target="tpu_custom_call" | custom-call | flops 524288 | bytes 1048576 | tf_op jit(solution)/shard_map/finish/pallas_call | solution.py:333
  (3 shorter events, 0.1 us)
Async XLA Ops:
  7.9 7.4 %copy-start.3 = (f32[1,1024]{1,0:T(1,128)S(1)}, f32[1,1024]{1,0:T(1,128)}, u32[]{:S(2)}) copy-start(f32[1,1024]{1,0:T(1,128)} %get-tuple-element.21.mean_hbm) | copy-start | bytes 12292
  7.9 40.0 %all-to-all-start = ((bf16[16,144,256]{2,1,0:T(8,128)(2,1)}), bf16[16,144,256]{2,1,0:T(8,128)(2,1)S(1)}, u32[]{:S(2)}, u32[]{:S(2)}) async-start(bf16[16,144,256]{2,1,0:T(8,128)(2,1)} %bitcast.6), calls=%async_computation | async-start | bytes 2359296 | tf_op jit(solution)/shard_map/all_to_all | solution.py:488
  20.3 2.8 %collective-permute-start = (bf16[512,1024]{1,0:T(8,128)(2,1)S(1)}, bf16[512,1024]{1,0:T(8,128)(2,1)S(1)}, u32[]{:S(2)}, u32[]{:S(2)}) collective-permute-start(bf16[512,1024]{1,0:T(8,128)(2,1)S(1)} %get-tuple-element.23), channel_id=1, source_target_pairs={{0,1},{1,0},{2,3},{3,2},{4,5},{5,4},{6,7},{7,6},{8,9},{9,8},{10,11... | collective-permute-start | bytes 3145736 | tf_op jit(solution)/shard_map/ppermute | solution.py:353
  23.3 24.7 %copy-start = (bf16[1024,256]{1,0:T(8,128)(2,1)S(1)}, bf16[1024,256]{1,0:T(8,128)(2,1)}, u32[]{:S(2)}) copy-start(bf16[1024,256]{1,0:T(8,128)(2,1)} %basis_ref.1) | copy-start | bytes 1572868
  23.3 24.7 %copy-start.1 = (bf16[1024,256]{1,0:T(8,128)(2,1)S(1)}, bf16[1024,256]{1,0:T(8,128)(2,1)}, u32[]{:S(2)}) copy-start(bf16[1024,256]{1,0:T(8,128)(2,1)} %centroid_ref.1) | copy-start | bytes 1572868
  23.3 24.7 %copy-start.2 = (bf16[256,256]{1,0:T(8,128)(2,1)S(1)}, bf16[256,256]{1,0:T(8,128)(2,1)}, u32[]{:S(2)}) copy-start(bf16[256,256]{1,0:T(8,128)(2,1)} %rotation_ref.1) | copy-start | bytes 393220
  23.3 13.1 %collective-permute-start.1 = (bf16[256,512]{1,0:T(8,128)(2,1)S(1)}, bf16[256,512]{1,0:T(8,128)(2,1)S(1)}, u32[]{:S(2)}, u32[]{:S(2)}) collective-permute-start(bf16[256,512]{1,0:T(8,128)(2,1)S(1)} %get-tuple-element.25), channel_id=1, source_target_pairs={{0,2},{1,3},{2,0},{3,1},{4,6},{5,7},{6,4},{7,5},{8,10},{9,11},{10,... | collective-permute-start | bytes 786440 | tf_op jit(solution)/shard_map/ppermute | solution.py:353
  25.2 17.4 %collective-permute-start.2 = (bf16[256,512]{1,0:T(8,128)(2,1)S(1)}, bf16[256,512]{1,0:T(8,128)(2,1)S(1)}, u32[]{:S(2)}, u32[]{:S(2)}) collective-permute-start(bf16[256,512]{1,0:T(8,128)(2,1)S(1)} %get-tuple-element.28), channel_id=1, source_target_pairs={{0,2},{1,3},{2,0},{3,1},{4,6},{5,7},{6,4},{7,5},{8,10},{9,11},{10,... | collective-permute-start | bytes 786440 | tf_op jit(solution)/shard_map/ppermute | solution.py:353
  36.4 11.0 %collective-permute-start.4 = (bf16[64,512]{1,0:T(8,128)(2,1)S(1)}, bf16[64,512]{1,0:T(8,128)(2,1)S(1)}, u32[]{:S(2)}, u32[]{:S(2)}) collective-permute-start(bf16[64,512]{1,0:T(8,128)(2,1)S(1)} %get-tuple-element.33), channel_id=1, source_target_pairs={{0,4},{1,5},{2,6},{3,7},{4,0},{5,1},{6,2},{7,3},{8,12},{9,13},{10,... | collective-permute-start | bytes 196616 | tf_op jit(solution)/shard_map/ppermute | solution.py:353
  37.8 14.3 %collective-permute-start.5 = (bf16[64,512]{1,0:T(8,128)(2,1)S(1)}, bf16[64,512]{1,0:T(8,128)(2,1)S(1)}, u32[]{:S(2)}, u32[]{:S(2)}) collective-permute-start(bf16[64,512]{1,0:T(8,128)(2,1)S(1)} %get-tuple-element.34), channel_id=1, source_target_pairs={{0,12},{1,13},{2,14},{3,15},{4,8},{5,9},{6,10},{7,11},{8,4},{9,5},... | collective-permute-start | bytes 196616 | tf_op jit(solution)/shard_map/ppermute | solution.py:353
  42.1 11.5 %collective-permute-start.3 = (bf16[64,512]{1,0:T(8,128)(2,1)S(1)}, bf16[64,512]{1,0:T(8,128)(2,1)S(1)}, u32[]{:S(2)}, u32[]{:S(2)}) collective-permute-start(bf16[64,512]{1,0:T(8,128)(2,1)S(1)} %get-tuple-element.26.refs_0_), channel_id=1, source_target_pairs={{0,8},{1,9},{2,10},{3,11},{4,12},{5,13},{6,14},{7,15},{8,0},{9,1},... | collective-permute-start | bytes 196616 | tf_op jit(solution)/shard_map/ppermute | solution.py:353
  42.7 10.9 %collective-permute-start.7 = (bf16[64,512]{1,0:T(8,128)(2,1)S(1)}, bf16[64,512]{1,0:T(8,128)(2,1)S(1)}, u32[]{:S(2)}, u32[]{:S(2)}) collective-permute-start(bf16[64,512]{1,0:T(8,128)(2,1)S(1)} %get-tuple-element.36), channel_id=1, source_target_pairs={{0,4},{1,5},{2,6},{3,7},{4,0},{5,1},{6,2},{7,3},{8,12},{9,13},{10,... | collective-permute-start | bytes 196616 | tf_op jit(solution)/shard_map/ppermute | solution.py:353
  46.1 7.5 %collective-permute-start.8 = (bf16[64,512]{1,0:T(8,128)(2,1)S(1)}, bf16[64,512]{1,0:T(8,128)(2,1)S(1)}, u32[]{:S(2)}, u32[]{:S(2)}) collective-permute-start(bf16[64,512]{1,0:T(8,128)(2,1)S(1)} %get-tuple-element.37), channel_id=1, source_target_pairs={{0,12},{1,13},{2,14},{3,15},{4,8},{5,9},{6,10},{7,11},{8,4},{9,5},... | collective-permute-start | bytes 196616 | tf_op jit(solution)/shard_map/ppermute | solution.py:353
  47.4 8.5 %collective-permute-start.6 = (bf16[64,512]{1,0:T(8,128)(2,1)S(1)}, bf16[64,512]{1,0:T(8,128)(2,1)S(1)}, u32[]{:S(2)}, u32[]{:S(2)}) collective-permute-start(bf16[64,512]{1,0:T(8,128)(2,1)S(1)} %get-tuple-element.29.refs_1_), channel_id=1, source_target_pairs={{0,8},{1,9},{2,10},{3,11},{4,12},{5,13},{6,14},{7,15},{8,0},{9,1},... | collective-permute-start | bytes 196616 | tf_op jit(solution)/shard_map/ppermute | solution.py:353

commit v21 on v20

--- a/solution.py
+++ b/solution.py
@@ -348,7 +348,7 @@
 
 def exchange(width, stage, out):
     came = []
-    for p in range(1, 1 << len(stage)):
+    for p in (2, 1, 3) if len(stage) == 2 else (1,):
         apart = sum(s for k, s in enumerate(stage) if (p >> (len(stage) - 1 - k)) & 1)
         came.append(lax.ppermute(out[p - 1], "wide", [(i, i ^ apart) for i in range(width)]))
     return came

time: 56.9 us -> 56.9 us (level)
  no operation moved by 1% of the time
where the time goes in v21:
time: 56.9 us; the launch traced here: 56.7 us
  starting transfers between devices  21.4 us (38%)
  Pallas kernels  17.4 us (31%)
  waiting for transfers between devices  17.1 us (30%)
  between operations  0.74 us (1%)
    ppermute x9, waiting for transfers between devices, exchange(): lax.ppermute(out[p - 1], 'wide', [(i, i ^ apart) for i in range(width)])  17.1 us
    ppermute x9, starting transfers between devices, exchange(): lax.ppermute(out[p - 1], 'wide', [(i, i ^ apart) for i in range(width)])  14 us
    all_to_all x1, starting transfers between devices, local(): lax.all_to_all(rows.reshape(width, SPAN, feats), 'wide', split_axis=0, co...  7.4 us
    pallas_call x1, Pallas kernels, project_and_sort(): pl.pallas_call(functools.partial(rows_kernel, width), grid=(rows_here //...  7.27 us
    pallas_call x1, Pallas kernels, moments(): pl.pallas_call(functools.partial(moments_kernel, width), in_specs=[pl.Blo...  4.93 us
    pallas_call x1, Pallas kernels, encode(): pl.pallas_call(functools.partial(encode_kernel, total), in_specs=[pl.Bloc...  4.09 us
  transfers between devices with their start and end apart: 10, of which 4 were waited for; matrix products, arithmetic and copies ran while one was open for 0% of the time, Pallas kernels for 16%

profile of v21, /device:TPU:0, one launch (start us, length us, event | category | flops | bytes accessed | tf_op | source)
XLA Modules:
  0.0 56.7 jit_solution(1337651097436292670)
XLA Ops:
  0.6 7.3 %project_sort.1 = (bf16[2304,256]{1,0:T(8,128)(2,1)}, f32[1,1024]{1,0:T(1,128)}) custom-call(bf16[2048,1024]{1,0:T(8,128)(2,1)} %e_hbm.3, bf16[1024,256]{1,0:T(8,128)(2,1)} %basis_ref.1, s32[16,128]{1,0:T(8,128)} %bitcast.7, s32[16,128]{1,0:T(8,128)} %bitcast.8), custom_call_target="tpu_custom_call" | custom-call | flops 3489660928 | bytes 5373952 | tf_op jit(solution)/shard_map/project_sort/pallas_call | solution.py:171
  7.9 0.0 copy-start.3
  7.9 7.4 %all-to-all-start = ((bf16[16,144,256]{2,1,0:T(8,128)(2,1)}), bf16[16,144,256]{2,1,0:T(8,128)(2,1)S(1)}, u32[]{:S(2)}, u32[]{:S(2)}) async-start(bf16[16,144,256]{2,1,0:T(8,128)(2,1)} %bitcast.6), calls=%async_computation | async-start | bytes 2359296 | tf_op jit(solution)/shard_map/all_to_all | solution.py:488
  15.3 0.0 copy-done.3
  15.3 4.9 %moments.1 = (bf16[512,1024]{1,0:T(8,128)(2,1)S(1)}, bf16[512,1024]{1,0:T(8,128)(2,1)S(1)}) custom-call(s32[1]{0:T(128)} %bitcast.me_ref, f32[1,1024]{1,0:T(1,128)S(1)} %copy-done.3, bf16[2048,1024]{1,0:T(8,128)(2,1)} %e_hbm.3), custom_call_target="tpu_custom_call" | custom-call | flops 4294967296 | bytes 7340032 | tf_op jit(solution)/shard_map/moments/pallas_call | solution.py:263
  20.3 0.5 collective-permute-start
  20.7 2.3 %collective-permute-done.refs_0_ = bf16[512,1024]{1,0:T(8,128)(2,1)S(1)} collective-permute-done((bf16[512,1024]{1,0:T(8,128)(2,1)S(1)}, bf16[512,1024]{1,0:T(8,128)(2,1)S(1)}, u32[]{:S(2)}, u32[]{:S(2)}) %collective-permute-start) | collective-permute-done | bytes 1048608 | tf_op jit(solution)/shard_map/ppermute | solution.py:353
  23.0 0.2 add_and_split.3
  23.3 0.0 copy-start
  23.3 0.0 copy-start.1
  23.3 0.0 copy-start.2
  23.3 2.0 %collective-permute-start.1 = (bf16[256,512]{1,0:T(8,128)(2,1)S(1)}, bf16[256,512]{1,0:T(8,128)(2,1)S(1)}, u32[]{:S(2)}, u32[]{:S(2)}) collective-permute-start(bf16[256,512]{1,0:T(8,128)(2,1)S(1)} %get-tuple-element.25), channel_id=1, source_target_pairs={{0,2},{1,3},{2,0},{3,1},{4,6},{5,7},{6,4},{7,5},{8,10},{9,11},{10,... | collective-permute-start | bytes 786440 | tf_op jit(solution)/shard_map/ppermute | solution.py:353
  25.2 0.2 collective-permute-start.2
  25.4 11.0 %collective-permute-done.1.refs_0_ = bf16[256,512]{1,0:T(8,128)(2,1)S(1)} collective-permute-done((bf16[256,512]{1,0:T(8,128)(2,1)S(1)}, bf16[256,512]{1,0:T(8,128)(2,1)S(1)}, u32[]{:S(2)}, u32[]{:S(2)}) %collective-permute-start.1) | collective-permute-done | bytes 262176 | tf_op jit(solution)/shard_map/ppermute | solution.py:353
  36.4 1.4 %collective-permute-start.3 = (bf16[64,512]{1,0:T(8,128)(2,1)S(1)}, bf16[64,512]{1,0:T(8,128)(2,1)S(1)}, u32[]{:S(2)}, u32[]{:S(2)}) collective-permute-start(bf16[64,512]{1,0:T(8,128)(2,1)S(1)} %get-tuple-element.33), channel_id=1, source_target_pairs={{0,4},{1,5},{2,6},{3,7},{4,0},{5,1},{6,2},{7,3},{8,12},{9,13},{10,... | collective-permute-start | bytes 196616 | tf_op jit(solution)/shard_map/ppermute | solution.py:353
  37.8 4.3 %collective-permute-start.5 = (bf16[64,512]{1,0:T(8,128)(2,1)S(1)}, bf16[64,512]{1,0:T(8,128)(2,1)S(1)}, u32[]{:S(2)}, u32[]{:S(2)}) collective-permute-start(bf16[64,512]{1,0:T(8,128)(2,1)S(1)} %get-tuple-element.34), channel_id=1, source_target_pairs={{0,12},{1,13},{2,14},{3,15},{4,8},{5,9},{6,10},{7,11},{8,4},{9,5},... | collective-permute-start | bytes 196616 | tf_op jit(solution)/shard_map/ppermute | solution.py:353
  42.1 0.5 collective-permute-start.4
  42.6 0.0 collective-permute-done.2.refs_0_
  42.7 3.5 %collective-permute-start.6 = (bf16[64,512]{1,0:T(8,128)(2,1)S(1)}, bf16[64,512]{1,0:T(8,128)(2,1)S(1)}, u32[]{:S(2)}, u32[]{:S(2)}) collective-permute-start(bf16[64,512]{1,0:T(8,128)(2,1)S(1)} %get-tuple-element.36), channel_id=1, source_target_pairs={{0,4},{1,5},{2,6},{3,7},{4,0},{5,1},{6,2},{7,3},{8,12},{9,13},{10,... | collective-permute-start | bytes 196616 | tf_op jit(solution)/shard_map/ppermute | solution.py:353
  46.1 1.3 %collective-permute-start.8 = (bf16[64,512]{1,0:T(8,128)(2,1)S(1)}, bf16[64,512]{1,0:T(8,128)(2,1)S(1)}, u32[]{:S(2)}, u32[]{:S(2)}) collective-permute-start(bf16[64,512]{1,0:T(8,128)(2,1)S(1)} %get-tuple-element.37), channel_id=1, source_target_pairs={{0,12},{1,13},{2,14},{3,15},{4,8},{5,9},{6,10},{7,11},{8,4},{9,5},... | collective-permute-start | bytes 196616 | tf_op jit(solution)/shard_map/ppermute | solution.py:353
  47.4 0.0 collective-permute-done.3.refs_1_
  47.4 0.5 collective-permute-start.7
  47.9 0.0 all-to-all-done
  47.9 0.0 copy-done
  47.9 0.0 copy-done.1
  47.9 4.1 %encode.1 = (bf16[2048,256]{1,0:T(8,128)(2,1)}, f32[64,1024]{1,0:T(8,128)S(1)}) custom-call(s32[1]{0:T(128)} %bitcast.me_ref, bf16[2304,256]{1,0:T(8,128)(2,1)S(1)} %bitcast.5, bf16[1024,256]{1,0:T(8,128)(2,1)S(1)} %copy-done, bf16[1024,256]{1,0:T(8,128)(2,1)S(1)} %copy-done.1, bf16[256,256]{1,0:T(8,128)(2,1)S(1)} %copy-done.2, ...), custom_call_target="tpu_custom_call" | custom-call | flops 1342177280 | bytes 2097152 | tf_op jit(solution)/shard_map/encode/pallas_call | solution.py:456
  52.0 0.0 collective-permute-done.5.refs_3_
  52.1 1.5 %collective-permute-done.4.refs_2_ = bf16[64,512]{1,0:T(8,128)(2,1)S(1)} collective-permute-done((bf16[64,512]{1,0:T(8,128)(2,1)S(1)}, bf16[64,512]{1,0:T(8,128)(2,1)S(1)}, u32[]{:S(2)}, u32[]{:S(2)}) %collective-permute-start.4) | collective-permute-done | bytes 65568 | tf_op jit(solution)/shard_map/ppermute | solution.py:353
  53.6 0.0 collective-permute-done.6.refs_5_
  53.6 0.0 collective-permute-done.8.refs_7_
  53.6 2.3 %collective-permute-done.7.refs_6_ = bf16[64,512]{1,0:T(8,128)(2,1)S(1)} collective-permute-done((bf16[64,512]{1,0:T(8,128)(2,1)S(1)}, bf16[64,512]{1,0:T(8,128)(2,1)S(1)}, u32[]{:S(2)}, u32[]{:S(2)}) %collective-permute-start.7) | collective-permute-done | bytes 65568 | tf_op jit(solution)/shard_map/ppermute | solution.py:353
  55.9 0.8 %finish.1 = f32[64,1024]{1,0:T(8,128)} custom-call(f32[64,1024]{1,0:T(8,128)S(1)} %get-tuple-element.31.between_ref, f32[64,512]{1,0:T(8,128)S(1)} %get-tuple-element.32.refs_0_, bf16[64,512]{1,0:T(8,128)(2,1)S(1)} %collective-permute-done.3.refs_1_, bf16[64,512]{1,0:T(8,128)(2,1)S(1)} %collective-permute-done.4.refs_2_, ...), custom_call_target="tpu_custom_call" | custom-call | flops 524288 | bytes 1048576 | tf_op jit(solution)/shard_map/finish/pallas_call | solution.py:333
  (3 shorter events, 0.1 us)
Async XLA Ops:
  7.9 7.4 %copy-start.3 = (f32[1,1024]{1,0:T(1,128)S(1)}, f32[1,1024]{1,0:T(1,128)}, u32[]{:S(2)}) copy-start(f32[1,1024]{1,0:T(1,128)} %get-tuple-element.21.mean_hbm) | copy-start | bytes 12292
  7.9 40.0 %all-to-all-start = ((bf16[16,144,256]{2,1,0:T(8,128)(2,1)}), bf16[16,144,256]{2,1,0:T(8,128)(2,1)S(1)}, u32[]{:S(2)}, u32[]{:S(2)}) async-start(bf16[16,144,256]{2,1,0:T(8,128)(2,1)} %bitcast.6), calls=%async_computation | async-start | bytes 2359296 | tf_op jit(solution)/shard_map/all_to_all | solution.py:488
  20.3 2.8 %collective-permute-start = (bf16[512,1024]{1,0:T(8,128)(2,1)S(1)}, bf16[512,1024]{1,0:T(8,128)(2,1)S(1)}, u32[]{:S(2)}, u32[]{:S(2)}) collective-permute-start(bf16[512,1024]{1,0:T(8,128)(2,1)S(1)} %get-tuple-element.23), channel_id=1, source_target_pairs={{0,1},{1,0},{2,3},{3,2},{4,5},{5,4},{6,7},{7,6},{8,9},{9,8},{10,11... | collective-permute-start | bytes 3145736 | tf_op jit(solution)/shard_map/ppermute | solution.py:353
  23.3 24.7 %copy-start = (bf16[1024,256]{1,0:T(8,128)(2,1)S(1)}, bf16[1024,256]{1,0:T(8,128)(2,1)}, u32[]{:S(2)}) copy-start(bf16[1024,256]{1,0:T(8,128)(2,1)} %basis_ref.1) | copy-start | bytes 1572868
  23.3 24.7 %copy-start.1 = (bf16[1024,256]{1,0:T(8,128)(2,1)S(1)}, bf16[1024,256]{1,0:T(8,128)(2,1)}, u32[]{:S(2)}) copy-start(bf16[1024,256]{1,0:T(8,128)(2,1)} %centroid_ref.1) | copy-start | bytes 1572868
  23.3 24.7 %copy-start.2 = (bf16[256,256]{1,0:T(8,128)(2,1)S(1)}, bf16[256,256]{1,0:T(8,128)(2,1)}, u32[]{:S(2)}) copy-start(bf16[256,256]{1,0:T(8,128)(2,1)} %rotation_ref.1) | copy-start | bytes 393220
  23.3 13.1 %collective-permute-start.1 = (bf16[256,512]{1,0:T(8,128)(2,1)S(1)}, bf16[256,512]{1,0:T(8,128)(2,1)S(1)}, u32[]{:S(2)}, u32[]{:S(2)}) collective-permute-start(bf16[256,512]{1,0:T(8,128)(2,1)S(1)} %get-tuple-element.25), channel_id=1, source_target_pairs={{0,2},{1,3},{2,0},{3,1},{4,6},{5,7},{6,4},{7,5},{8,10},{9,11},{10,... | collective-permute-start | bytes 786440 | tf_op jit(solution)/shard_map/ppermute | solution.py:353
  25.2 17.4 %collective-permute-start.2 = (bf16[256,512]{1,0:T(8,128)(2,1)S(1)}, bf16[256,512]{1,0:T(8,128)(2,1)S(1)}, u32[]{:S(2)}, u32[]{:S(2)}) collective-permute-start(bf16[256,512]{1,0:T(8,128)(2,1)S(1)} %get-tuple-element.28), channel_id=1, source_target_pairs={{0,2},{1,3},{2,0},{3,1},{4,6},{5,7},{6,4},{7,5},{8,10},{9,11},{10,... | collective-permute-start | bytes 786440 | tf_op jit(solution)/shard_map/ppermute | solution.py:353
  36.4 11.0 %collective-permute-start.3 = (bf16[64,512]{1,0:T(8,128)(2,1)S(1)}, bf16[64,512]{1,0:T(8,128)(2,1)S(1)}, u32[]{:S(2)}, u32[]{:S(2)}) collective-permute-start(bf16[64,512]{1,0:T(8,128)(2,1)S(1)} %get-tuple-element.33), channel_id=1, source_target_pairs={{0,4},{1,5},{2,6},{3,7},{4,0},{5,1},{6,2},{7,3},{8,12},{9,13},{10,... | collective-permute-start | bytes 196616 | tf_op jit(solution)/shard_map/ppermute | solution.py:353
  37.8 14.3 %collective-permute-start.5 = (bf16[64,512]{1,0:T(8,128)(2,1)S(1)}, bf16[64,512]{1,0:T(8,128)(2,1)S(1)}, u32[]{:S(2)}, u32[]{:S(2)}) collective-permute-start(bf16[64,512]{1,0:T(8,128)(2,1)S(1)} %get-tuple-element.34), channel_id=1, source_target_pairs={{0,12},{1,13},{2,14},{3,15},{4,8},{5,9},{6,10},{7,11},{8,4},{9,5},... | collective-permute-start | bytes 196616 | tf_op jit(solution)/shard_map/ppermute | solution.py:353
  42.1 11.5 %collective-permute-start.4 = (bf16[64,512]{1,0:T(8,128)(2,1)S(1)}, bf16[64,512]{1,0:T(8,128)(2,1)S(1)}, u32[]{:S(2)}, u32[]{:S(2)}) collective-permute-start(bf16[64,512]{1,0:T(8,128)(2,1)S(1)} %get-tuple-element.26.refs_0_), channel_id=1, source_target_pairs={{0,8},{1,9},{2,10},{3,11},{4,12},{5,13},{6,14},{7,15},{8,0},{9,1},... | collective-permute-start | bytes 196616 | tf_op jit(solution)/shard_map/ppermute | solution.py:353
  42.7 10.9 %collective-permute-start.6 = (bf16[64,512]{1,0:T(8,128)(2,1)S(1)}, bf16[64,512]{1,0:T(8,128)(2,1)S(1)}, u32[]{:S(2)}, u32[]{:S(2)}) collective-permute-start(bf16[64,512]{1,0:T(8,128)(2,1)S(1)} %get-tuple-element.36), channel_id=1, source_target_pairs={{0,4},{1,5},{2,6},{3,7},{4,0},{5,1},{6,2},{7,3},{8,12},{9,13},{10,... | collective-permute-start | bytes 196616 | tf_op jit(solution)/shard_map/ppermute | solution.py:353
  46.1 7.5 %collective-permute-start.8 = (bf16[64,512]{1,0:T(8,128)(2,1)S(1)}, bf16[64,512]{1,0:T(8,128)(2,1)S(1)}, u32[]{:S(2)}, u32[]{:S(2)}) collective-permute-start(bf16[64,512]{1,0:T(8,128)(2,1)S(1)} %get-tuple-element.37), channel_id=1, source_target_pairs={{0,12},{1,13},{2,14},{3,15},{4,8},{5,9},{6,10},{7,11},{8,4},{9,5},... | collective-permute-start | bytes 196616 | tf_op jit(solution)/shard_map/ppermute | solution.py:353
  47.4 8.5 %collective-permute-start.7 = (bf16[64,512]{1,0:T(8,128)(2,1)S(1)}, bf16[64,512]{1,0:T(8,128)(2,1)S(1)}, u32[]{:S(2)}, u32[]{:S(2)}) collective-permute-start(bf16[64,512]{1,0:T(8,128)(2,1)S(1)} %get-tuple-element.29.refs_1_), channel_id=1, source_target_pairs={{0,8},{1,9},{2,10},{3,11},{4,12},{5,13},{6,14},{7,15},{8,0},{9,1},... | collective-permute-start | bytes 196616 | tf_op jit(solution)/shard_map/ppermute | solution.py:353

commit v22 on v21

--- a/solution.py
+++ b/solution.py
@@ -200,6 +200,11 @@
         ),
         name="project_sort",
     )(embeddings, basis, list_owner.reshape(lanes, LANES), list_slot.reshape(lanes, LANES))
+
+
+def strides_after_core(width):
+    strides = [1 << k for k in range(1, width.bit_length() - 1)]
+    return strides[:-2] + strides[:-3:-1]
 
 
 def moments_kernel(width, me_ref, mean_hbm, e_hbm, keep_ref, send_ref, e_ref, mean_ref, m_ref, sem, mean_sem):
@@ -246,10 +251,9 @@
                 m_ref[other, rows] = jnp.transpose(piece)
         for pair in range(TILE // block // 2):
             first = t * (TILE // block) + 2 * pair
-            apart = (first ^ me) >> 1
             place = 0
-            for k in range(bits - 1):
-                place = place + (((apart >> k) & 1) << (bits - 2 - k))
+            for n, stride in enumerate(strides_after_core(width)):
+                place = place + jnp.where(((first ^ me) & stride) != 0, 1 << (bits - 2 - n), 0)
             to = pl.ds(pl.multiple_of(place * block, block), block)
             even_rows = m_ref[first * block:(first + 1) * block, :]
             odd_rows = m_ref[(first + 1) * block:(first + 2) * block, :]
@@ -341,17 +345,8 @@
     )(between, *parts)
 
 
-def halving_stages(width):
-    strides = [1 << k for k in range(width.bit_length() - 1)]
-    return [[s] for s in strides[:-2]] + [strides[-2:]]
-
-
-def exchange(width, stage, out):
-    came = []
-    for p in (2, 1, 3) if len(stage) == 2 else (1,):
-        apart = sum(s for k, s in enumerate(stage) if (p >> (len(stage) - 1 - k)) & 1)
-        came.append(lax.ppermute(out[p - 1], "wide", [(i, i ^ apart) for i in range(width)]))
-    return came
+def exchange(width, stride, out):
+    return lax.ppermute(out, "wide", [(i, i ^ stride) for i in range(width)])
 
 
 def encode_kernel(total, me_ref, got_ref, basis_ref, centroid_ref, rotation_ref, *refs):
@@ -490,20 +485,23 @@
     )
 
     keep, send = moments(width, me, embeddings, mean)
-    stages = halving_stages(width)
-    came = exchange(width, stages[0], [send])
-    shares = add_and_split(keep, came, SHARES, 1 << len(stages[1]))
-    last = []
-    for share in shares:
-        for n in range(1, len(stages) - 1):
-            came = exchange(width, stages[n], share[1:])
-            (share,) = add_and_split(share[0], came, 1, 1 << len(stages[n + 1]))
-        last.append(share)
-    came = [exchange(width, stages[-1], share[1:]) for share in last]
+    came = exchange(width, 1, send)
+    shares = add_and_split(keep, [came], SHARES, 2)
+    strides = strides_after_core(width)
+    sends, keeps, ends = [], [], []
+    for keep, send in shares:
+        for n, stride in enumerate(strides):
+            came = exchange(width, stride, send)
+            if n + 1 < len(strides):
+                ((keep, send),) = add_and_split(keep, [came], 1, 2)
+            if n == len(strides) - 3:
+                sends.append(send)
+        keeps.append(keep)
+        ends.append([came])
     encoded, between = encode(
-        width, total, me, got.reshape(width * SPAN, feats), basis, centroids, rotation, [share[1] for share in last]
+        width, total, me, got.reshape(width * SPAN, feats), basis, centroids, rotation, sends
     )
-    covariance = finish(total, between, [share[0] for share in last], came)
+    covariance = finish(total, between, keeps, ends)
     return (encoded, covariance)
 
 

time: 56.9 us -> 61.3 us (1.077)
  waiting for transfers between devices: 17.1 us -> 29.1 us
  starting transfers between devices: 21.4 us -> 13.9 us
    ppermute x9 -> x7, waiting for transfers between devices: 17.1 us -> 29 us  [exchange(): return lax.ppermute(out, 'wide', [(i, i ^ stride) for i in range(width)])]
    ppermute x9 -> x7, starting transfers between devices: 14 us -> 6.46 us  [exchange(): return lax.ppermute(out, 'wide', [(i, i ^ stride) for i in range(width)])]
  transfers between devices with their start and end apart: 10 -> 8, of which waited for: 4 -> 6; matrix products, arithmetic and copies ran while one was open for 0% -> 0% of each run, Pallas kernels for 16% -> 15%
where the time goes in v22:
time: 61.3 us; the launch traced here: 61.1 us
  waiting for transfers between devices  29.1 us (47%)
  Pallas kernels  17.4 us (28%)
  starting transfers between devices  13.9 us (23%)
  between operations  0.76 us (1%)
    ppermute x7, waiting for transfers between devices, exchange(): return lax.ppermute(out, 'wide', [(i, i ^ stride) for i in range(width)])  29 us
    all_to_all x1, starting transfers between devices, local(): lax.all_to_all(rows.reshape(width, SPAN, feats), 'wide', split_axis=0, co...  7.4 us
    pallas_call x1, Pallas kernels, project_and_sort(): pl.pallas_call(functools.partial(rows_kernel, width), grid=(rows_here //...  7.27 us
    ppermute x7, starting transfers between devices, exchange(): return lax.ppermute(out, 'wide', [(i, i ^ stride) for i in range(width)])  6.46 us
    pallas_call x1, Pallas kernels, moments(): pl.pallas_call(functools.partial(moments_kernel, width), in_specs=[pl.Blo...  4.93 us
    pallas_call x1, Pallas kernels, encode(): pl.pallas_call(functools.partial(encode_kernel, total), in_specs=[pl.Bloc...  4.09 us
  transfers between devices with their start and end apart: 8, of which 6 were waited for; matrix products, arithmetic and copies ran while one was open for 0% of the time, Pallas kernels for 15%

profile of v22, /device:TPU:0, one launch (start us, length us, event | category | flops | bytes accessed | tf_op | source)
XLA Modules:
  0.0 61.1 jit_solution(12106178327994315551)
XLA Ops:
  0.6 7.3 %project_sort.1 = (bf16[2304,256]{1,0:T(8,128)(2,1)}, f32[1,1024]{1,0:T(1,128)}) custom-call(bf16[2048,1024]{1,0:T(8,128)(2,1)} %e_hbm.3, bf16[1024,256]{1,0:T(8,128)(2,1)} %basis_ref.1, s32[16,128]{1,0:T(8,128)} %bitcast.7, s32[16,128]{1,0:T(8,128)} %bitcast.8), custom_call_target="tpu_custom_call" | custom-call | flops 3489660928 | bytes 5373952 | tf_op jit(solution)/shard_map/project_sort/pallas_call | solution.py:171
  7.9 0.0 copy-start.3
  7.9 7.4 %all-to-all-start = ((bf16[16,144,256]{2,1,0:T(8,128)(2,1)}), bf16[16,144,256]{2,1,0:T(8,128)(2,1)S(1)}, u32[]{:S(2)}, u32[]{:S(2)}) async-start(bf16[16,144,256]{2,1,0:T(8,128)(2,1)} %bitcast.6), calls=%async_computation | async-start | bytes 2359296 | tf_op jit(solution)/shard_map/all_to_all | solution.py:483
  15.3 0.0 copy-done.3
  15.3 4.9 %moments.1 = (bf16[512,1024]{1,0:T(8,128)(2,1)S(1)}, bf16[512,1024]{1,0:T(8,128)(2,1)S(1)}) custom-call(s32[1]{0:T(128)} %bitcast.me_ref, f32[1,1024]{1,0:T(1,128)S(1)} %copy-done.3, bf16[2048,1024]{1,0:T(8,128)(2,1)} %e_hbm.3), custom_call_target="tpu_custom_call" | custom-call | flops 4294967296 | bytes 7340032 | tf_op jit(solution)/shard_map/moments/pallas_call | solution.py:267
  20.3 0.5 collective-permute-start
  20.7 2.3 %collective-permute-done.refs_0_ = bf16[512,1024]{1,0:T(8,128)(2,1)S(1)} collective-permute-done((bf16[512,1024]{1,0:T(8,128)(2,1)S(1)}, bf16[512,1024]{1,0:T(8,128)(2,1)S(1)}, u32[]{:S(2)}, u32[]{:S(2)}) %collective-permute-start) | collective-permute-done | bytes 1048608 | tf_op jit(solution)/shard_map/ppermute | solution.py:349
  23.0 0.2 add_and_split.5
  23.2 2.0 %collective-permute-start.1 = (bf16[256,512]{1,0:T(8,128)(2,1)S(1)}, bf16[256,512]{1,0:T(8,128)(2,1)S(1)}, u32[]{:S(2)}, u32[]{:S(2)}) collective-permute-start(bf16[256,512]{1,0:T(8,128)(2,1)S(1)} %get-tuple-element.25), channel_id=1, source_target_pairs={{0,2},{1,3},{2,0},{3,1},{4,6},{5,7},{6,4},{7,5},{8,10},{9,11},{10,... | collective-permute-start | bytes 786440 | tf_op jit(solution)/shard_map/ppermute | solution.py:349
  25.2 0.2 collective-permute-start.2
  25.4 11.0 %collective-permute-done.1.refs_0_ = bf16[256,512]{1,0:T(8,128)(2,1)S(1)} collective-permute-done((bf16[256,512]{1,0:T(8,128)(2,1)S(1)}, bf16[256,512]{1,0:T(8,128)(2,1)S(1)}, u32[]{:S(2)}, u32[]{:S(2)}) %collective-permute-start.1) | collective-permute-done | bytes 262176 | tf_op jit(solution)/shard_map/ppermute | solution.py:349
  36.3 0.0 copy-start
  36.4 0.0 copy-start.1
  36.4 0.0 copy-start.2
  36.4 1.4 %collective-permute-start.3 = (bf16[128,512]{1,0:T(8,128)(2,1)S(1)}, bf16[128,512]{1,0:T(8,128)(2,1)S(1)}, u32[]{:S(2)}, u32[]{:S(2)}) collective-permute-start(bf16[128,512]{1,0:T(8,128)(2,1)S(1)} %get-tuple-element.26.refs_0_), channel_id=1, source_target_pairs={{0,8},{1,9},{2,10},{3,11},{4,12},{5,13},{6,14},{7,15},{8,0},{9,1},... | collective-permute-start | bytes 393224 | tf_op jit(solution)/shard_map/ppermute | solution.py:349
  37.8 3.9 %collective-permute-done.2.refs_0_ = bf16[256,512]{1,0:T(8,128)(2,1)S(1)} collective-permute-done((bf16[256,512]{1,0:T(8,128)(2,1)S(1)}, bf16[256,512]{1,0:T(8,128)(2,1)S(1)}, u32[]{:S(2)}, u32[]{:S(2)}) %collective-permute-start.2) | collective-permute-done | bytes 262176 | tf_op jit(solution)/shard_map/ppermute | solution.py:349
  41.7 2.4 %collective-permute-start.5 = (bf16[128,512]{1,0:T(8,128)(2,1)S(1)}, bf16[128,512]{1,0:T(8,128)(2,1)S(1)}, u32[]{:S(2)}, u32[]{:S(2)}) collective-permute-start(bf16[128,512]{1,0:T(8,128)(2,1)S(1)} %get-tuple-element.29.refs_1_), channel_id=1, source_target_pairs={{0,8},{1,9},{2,10},{3,11},{4,12},{5,13},{6,14},{7,15},{8,0},{9,1},... | collective-permute-start | bytes 393224 | tf_op jit(solution)/shard_map/ppermute | solution.py:349
  44.1 9.5 %collective-permute-done.3.refs_0_ = bf16[128,512]{1,0:T(8,128)(2,1)S(1)} collective-permute-done((bf16[128,512]{1,0:T(8,128)(2,1)S(1)}, bf16[128,512]{1,0:T(8,128)(2,1)S(1)}, u32[]{:S(2)}, u32[]{:S(2)}) %collective-permute-start.3) | collective-permute-done | bytes 131104 | tf_op jit(solution)/shard_map/ppermute | solution.py:349
  53.6 0.1 collective-permute-start.4
  53.7 2.3 %collective-permute-done.5.refs_0_ = bf16[128,512]{1,0:T(8,128)(2,1)S(1)} collective-permute-done((bf16[128,512]{1,0:T(8,128)(2,1)S(1)}, bf16[128,512]{1,0:T(8,128)(2,1)S(1)}, u32[]{:S(2)}, u32[]{:S(2)}) %collective-permute-start.5) | collective-permute-done | bytes 131104 | tf_op jit(solution)/shard_map/ppermute | solution.py:349
  56.0 0.1 collective-permute-start.6
  56.1 0.0 all-to-all-done
  56.1 0.0 copy-done
  56.1 0.0 copy-done.1
  56.1 0.0 copy-done.2
  56.1 4.1 %encode.1 = (bf16[2048,256]{1,0:T(8,128)(2,1)}, f32[64,1024]{1,0:T(8,128)S(1)}) custom-call(s32[1]{0:T(128)} %bitcast.me_ref, bf16[2304,256]{1,0:T(8,128)(2,1)S(1)} %bitcast.5, bf16[1024,256]{1,0:T(8,128)(2,1)S(1)} %copy-done, bf16[1024,256]{1,0:T(8,128)(2,1)S(1)} %copy-done.1, bf16[256,256]{1,0:T(8,128)(2,1)S(1)} %copy-done.2, ...), custom_call_target="tpu_custom_call" | custom-call | flops 1342177280 | bytes 2097152 | tf_op jit(solution)/shard_map/encode/pallas_call | solution.py:451
  60.2 0.0 collective-permute-done.4.refs_1_
  60.2 0.1 collective-permute-done.6.refs_3_
  60.3 0.7 %finish.1 = f32[64,1024]{1,0:T(8,128)} custom-call(f32[64,1024]{1,0:T(8,128)S(1)} %get-tuple-element.31.between_ref, f32[64,512]{1,0:T(8,128)S(1)} %get-tuple-element.33.refs_0_, bf16[64,512]{1,0:T(8,128)(2,1)S(1)} %collective-permute-done.4.refs_1_, f32[64,512]{1,0:T(8,128)S(1)} %get-tuple-element.36.refs_2_, bf16[64,512]{1,0:T(8,128)(2,1)S(1)} %collective-permute-done.6.refs_3_), custom_call_target="tpu_custom_call" | custom-call | flops 524288 | bytes 1048576 | tf_op jit(solution)/shard_map/finish/pallas_call | solution.py:337
  (4 shorter events, 0.1 us)
Async XLA Ops:
  7.9 7.4 %copy-start.3 = (f32[1,1024]{1,0:T(1,128)S(1)}, f32[1,1024]{1,0:T(1,128)}, u32[]{:S(2)}) copy-start(f32[1,1024]{1,0:T(1,128)} %get-tuple-element.21.mean_hbm) | copy-start | bytes 12292
  7.9 48.2 %all-to-all-start = ((bf16[16,144,256]{2,1,0:T(8,128)(2,1)}), bf16[16,144,256]{2,1,0:T(8,128)(2,1)S(1)}, u32[]{:S(2)}, u32[]{:S(2)}) async-start(bf16[16,144,256]{2,1,0:T(8,128)(2,1)} %bitcast.6), calls=%async_computation | async-start | bytes 2359296 | tf_op jit(solution)/shard_map/all_to_all | solution.py:483
  20.3 2.8 %collective-permute-start = (bf16[512,1024]{1,0:T(8,128)(2,1)S(1)}, bf16[512,1024]{1,0:T(8,128)(2,1)S(1)}, u32[]{:S(2)}, u32[]{:S(2)}) collective-permute-start(bf16[512,1024]{1,0:T(8,128)(2,1)S(1)} %get-tuple-element.23), channel_id=1, source_target_pairs={{0,1},{1,0},{2,3},{3,2},{4,5},{5,4},{6,7},{7,6},{8,9},{9,8},{10,11... | collective-permute-start | bytes 3145736 | tf_op jit(solution)/shard_map/ppermute | solution.py:349
  23.2 13.1 %collective-permute-start.1 = (bf16[256,512]{1,0:T(8,128)(2,1)S(1)}, bf16[256,512]{1,0:T(8,128)(2,1)S(1)}, u32[]{:S(2)}, u32[]{:S(2)}) collective-permute-start(bf16[256,512]{1,0:T(8,128)(2,1)S(1)} %get-tuple-element.25), channel_id=1, source_target_pairs={{0,2},{1,3},{2,0},{3,1},{4,6},{5,7},{6,4},{7,5},{8,10},{9,11},{10,... | collective-permute-start | bytes 786440 | tf_op jit(solution)/shard_map/ppermute | solution.py:349
  25.2 16.5 %collective-permute-start.2 = (bf16[256,512]{1,0:T(8,128)(2,1)S(1)}, bf16[256,512]{1,0:T(8,128)(2,1)S(1)}, u32[]{:S(2)}, u32[]{:S(2)}) collective-permute-start(bf16[256,512]{1,0:T(8,128)(2,1)S(1)} %get-tuple-element.28), channel_id=1, source_target_pairs={{0,2},{1,3},{2,0},{3,1},{4,6},{5,7},{6,4},{7,5},{8,10},{9,11},{10,... | collective-permute-start | bytes 786440 | tf_op jit(solution)/shard_map/ppermute | solution.py:349
  36.3 19.8 %copy-start = (bf16[1024,256]{1,0:T(8,128)(2,1)S(1)}, bf16[1024,256]{1,0:T(8,128)(2,1)}, u32[]{:S(2)}) copy-start(bf16[1024,256]{1,0:T(8,128)(2,1)} %basis_ref.1) | copy-start | bytes 1572868
  36.4 19.8 %copy-start.1 = (bf16[1024,256]{1,0:T(8,128)(2,1)S(1)}, bf16[1024,256]{1,0:T(8,128)(2,1)}, u32[]{:S(2)}) copy-start(bf16[1024,256]{1,0:T(8,128)(2,1)} %centroid_ref.1) | copy-start | bytes 1572868
  36.4 19.8 %copy-start.2 = (bf16[256,256]{1,0:T(8,128)(2,1)S(1)}, bf16[256,256]{1,0:T(8,128)(2,1)}, u32[]{:S(2)}) copy-start(bf16[256,256]{1,0:T(8,128)(2,1)} %rotation_ref.1) | copy-start | bytes 393220
  36.4 17.2 %collective-permute-start.3 = (bf16[128,512]{1,0:T(8,128)(2,1)S(1)}, bf16[128,512]{1,0:T(8,128)(2,1)S(1)}, u32[]{:S(2)}, u32[]{:S(2)}) collective-permute-start(bf16[128,512]{1,0:T(8,128)(2,1)S(1)} %get-tuple-element.26.refs_0_), channel_id=1, source_target_pairs={{0,8},{1,9},{2,10},{3,11},{4,12},{5,13},{6,14},{7,15},{8,0},{9,1},... | collective-permute-start | bytes 393224 | tf_op jit(solution)/shard_map/ppermute | solution.py:349
  41.7 14.3 %collective-permute-start.5 = (bf16[128,512]{1,0:T(8,128)(2,1)S(1)}, bf16[128,512]{1,0:T(8,128)(2,1)S(1)}, u32[]{:S(2)}, u32[]{:S(2)}) collective-permute-start(bf16[128,512]{1,0:T(8,128)(2,1)S(1)} %get-tuple-element.29.refs_1_), channel_id=1, source_target_pairs={{0,8},{1,9},{2,10},{3,11},{4,12},{5,13},{6,14},{7,15},{8,0},{9,1},... | collective-permute-start | bytes 393224 | tf_op jit(solution)/shard_map/ppermute | solution.py:349
  53.6 6.6 %collective-permute-start.4 = (bf16[64,512]{1,0:T(8,128)(2,1)S(1)}, bf16[64,512]{1,0:T(8,128)(2,1)S(1)}, u32[]{:S(2)}, u32[]{:S(2)}) collective-permute-start(bf16[64,512]{1,0:T(8,128)(2,1)S(1)} %get-tuple-element.34), channel_id=1, source_target_pairs={{0,4},{1,5},{2,6},{3,7},{4,0},{5,1},{6,2},{7,3},{8,12},{9,13},{10,... | collective-permute-start | bytes 196616 | tf_op jit(solution)/shard_map/ppermute | solution.py:349
  56.0 4.3 %collective-permute-start.6 = (bf16[64,512]{1,0:T(8,128)(2,1)S(1)}, bf16[64,512]{1,0:T(8,128)(2,1)S(1)}, u32[]{:S(2)}, u32[]{:S(2)}) collective-permute-start(bf16[64,512]{1,0:T(8,128)(2,1)S(1)} %get-tuple-element.37), channel_id=1, source_target_pairs={{0,4},{1,5},{2,6},{3,7},{4,0},{5,1},{6,2},{7,3},{8,12},{9,13},{10,... | collective-permute-start | bytes 196616 | tf_op jit(solution)/shard_map/ppermute | solution.py:349

commit v23 on v19

--- a/solution.py
+++ b/solution.py
@@ -274,9 +274,9 @@
     )(me.reshape(1), mean, embeddings)
 
 
-def add_kernel(shares, pieces, keep_ref, *refs):
+def add_kernel(shares, pieces, arrived, keep_ref, *refs):
     outs = refs[len(refs) - shares * pieces:]
-    came = refs[:len(refs) - shares * pieces]
+    came = refs[:arrived]
     rows, columns = outs[0].shape
     for h in range(shares):
         across = slice(h * columns, (h + 1) * columns)
@@ -289,20 +289,20 @@
             out[...] = held.astype(out.dtype)
 
 
-def add_and_split(keep, came, shares, pieces):
+def add_and_split(keep, came, shares, pieces, after=()):
     rows, columns = keep.shape
     vmem = pl.BlockSpec(memory_space=pltpu.VMEM)
     shape = (rows // pieces, columns // shares)
     kinds = [jnp.float32] + [jnp.bfloat16] * (pieces - 1)
     outs = pl.pallas_call(
-        functools.partial(add_kernel, shares, pieces),
-        in_specs=[vmem] * (1 + len(came)),
+        functools.partial(add_kernel, shares, pieces, len(came)),
+        in_specs=[vmem] * (1 + len(came)) + [pl.BlockSpec(memory_space=pl.ANY)] * len(after),
         out_specs=[vmem] * (shares * pieces),
         out_shape=[jax.ShapeDtypeStruct(shape, kind) for kind in kinds * shares],
         compiler_params=pltpu.CompilerParams(vmem_limit_bytes=VMEM_SOME),
         cost_estimate=pl.CostEstimate(flops=2 * rows * columns, bytes_accessed=10 * rows * columns, transcendentals=0),
         name="add_and_split",
-    )(keep, *came)
+    )(keep, *came, *after)
     return [outs[h * pieces:(h + 1) * pieces] for h in range(shares)]
 
 
@@ -478,19 +478,17 @@
     keep, send = moments(width, me, embeddings, mean)
     came = exchange(width, [1], [send])
     shares = add_and_split(keep, came, SHARES, 2)
-    keeps, ends, sends = [], [], []
+    keeps, ends, last = [], [], []
     for together, (keep, *out) in zip((1, 2), shares):
         stages = halving_stages(width, together)[1:]
         for n, stage in enumerate(stages):
-            sends.append(out[0])
             came = exchange(width, stage, out)
             if n + 1 < len(stages):
-                ((keep, *out),) = add_and_split(keep, came, 1, 1 << len(stages[n + 1]))
+                ((keep, *out),) = add_and_split(keep, came, 1, 1 << len(stages[n + 1]), last if n == 0 else [])
         keeps.append(keep)
         ends.append(came)
-    encoded, between = encode(
-        width, total, me, got.reshape(width * SPAN, feats), basis, centroids, rotation, sends
-    )
+        last = last + [out[0]]
+    encoded, between = encode(width, total, me, got.reshape(width * SPAN, feats), basis, centroids, rotation, last)
     covariance = finish(total, between, keeps, ends)
     return (encoded, covariance)
 

time: 59.5 us -> 57.4 us (0.965)
  starting transfers between devices: 21 us -> 19.4 us
  Pallas kernels: 18.5 us -> 17.2 us
  waiting for transfers between devices: 19 us -> 19.8 us
    ppermute x8, starting transfers between devices: 13.6 us -> 12 us  [exchange(): lax.ppermute(out[p - 1], 'wide', [(i, i ^ apart) for i in range(width)])]
    pallas_call x4, Pallas kernels: 1.63 us -> 0.34 us  [add_and_split(): pl.pallas_call(functools.partial(add_kernel, shares, pieces, len(came)),...]
    ppermute x8, waiting for transfers between devices: 19 us -> 19.8 us  [exchange(): lax.ppermute(out[p - 1], 'wide', [(i, i ^ apart) for i in range(width)])]
  transfers between devices with their start and end apart: 9 -> 9, of which waited for: 5 -> 5; matrix products, arithmetic and copies ran while one was open for 0% -> 0% of each run, Pallas kernels for 18% -> 16%
where the time goes in v23:
time: 57.4 us; the launch traced here: 57.2 us
  waiting for transfers between devices  19.8 us (34%)
  starting transfers between devices  19.4 us (34%)
  Pallas kernels  17.2 us (30%)
  between operations  0.75 us (1%)
    ppermute x8, waiting for transfers between devices, exchange(): lax.ppermute(out[p - 1], 'wide', [(i, i ^ apart) for i in range(width)])  19.8 us
    ppermute x8, starting transfers between devices, exchange(): lax.ppermute(out[p - 1], 'wide', [(i, i ^ apart) for i in range(width)])  12 us
    all_to_all x1, starting transfers between devices, local(): lax.all_to_all(rows.reshape(width, SPAN, feats), 'wide', split_axis=0, co...  7.4 us
    pallas_call x1, Pallas kernels, project_and_sort(): pl.pallas_call(functools.partial(rows_kernel, width), grid=(rows_here //...  7.27 us
    pallas_call x1, Pallas kernels, moments(): pl.pallas_call(functools.partial(moments_kernel, width), in_specs=[pl.Blo...  4.93 us
    pallas_call x1, Pallas kernels, encode(): pl.pallas_call(functools.partial(encode_kernel, total), in_specs=[pl.Bloc...  3.9 us
  transfers between devices with their start and end apart: 9, of which 5 were waited for; matrix products, arithmetic and copies ran while one was open for 0% of the time, Pallas kernels for 16%

profile of v23, /device:TPU:0, one launch (start us, length us, event | category | flops | bytes accessed | tf_op | source)
XLA Modules:
  0.0 57.2 jit_solution(309599000963165802)
XLA Ops:
  0.6 7.3 %project_sort.1 = (bf16[2304,256]{1,0:T(8,128)(2,1)}, f32[1,1024]{1,0:T(1,128)}) custom-call(bf16[2048,1024]{1,0:T(8,128)(2,1)} %e_hbm.3, bf16[1024,256]{1,0:T(8,128)(2,1)} %basis_ref.1, s32[16,128]{1,0:T(8,128)} %bitcast.7, s32[16,128]{1,0:T(8,128)} %bitcast.8), custom_call_target="tpu_custom_call" | custom-call | flops 3489660928 | bytes 5373952 | tf_op jit(solution)/shard_map/project_sort/pallas_call | solution.py:162
  7.9 0.0 copy-start.3
  7.9 7.4 %all-to-all-start = ((bf16[16,144,256]{2,1,0:T(8,128)(2,1)}), bf16[16,144,256]{2,1,0:T(8,128)(2,1)S(1)}, u32[]{:S(2)}, u32[]{:S(2)}) async-start(bf16[16,144,256]{2,1,0:T(8,128)(2,1)} %bitcast.6), calls=%async_computation | async-start | bytes 2359296 | tf_op jit(solution)/shard_map/all_to_all | solution.py:476
  15.3 0.0 copy-done.3
  15.3 4.9 %moments.1 = (bf16[512,1024]{1,0:T(8,128)(2,1)S(1)}, bf16[512,1024]{1,0:T(8,128)(2,1)S(1)}) custom-call(s32[1]{0:T(128)} %bitcast.me_ref, f32[1,1024]{1,0:T(1,128)S(1)} %copy-done.3, bf16[2048,1024]{1,0:T(8,128)(2,1)} %e_hbm.3), custom_call_target="tpu_custom_call" | custom-call | flops 4294967296 | bytes 7340032 | tf_op jit(solution)/shard_map/moments/pallas_call | solution.py:254
  20.3 0.5 collective-permute-start
  20.7 2.3 %collective-permute-done.refs_0_ = bf16[512,1024]{1,0:T(8,128)(2,1)S(1)} collective-permute-done((bf16[512,1024]{1,0:T(8,128)(2,1)S(1)}, bf16[512,1024]{1,0:T(8,128)(2,1)S(1)}, u32[]{:S(2)}, u32[]{:S(2)}) %collective-permute-start) | collective-permute-done | bytes 1048608 | tf_op jit(solution)/shard_map/ppermute | solution.py:345
  23.0 0.2 add_and_split.4
  23.3 0.0 copy-start
  23.3 0.0 copy-start.1
  23.3 0.0 copy-start.2
  23.3 2.0 %collective-permute-start.1 = (bf16[256,512]{1,0:T(8,128)(2,1)S(1)}, bf16[256,512]{1,0:T(8,128)(2,1)S(1)}, u32[]{:S(2)}, u32[]{:S(2)}) collective-permute-start(bf16[256,512]{1,0:T(8,128)(2,1)S(1)} %get-tuple-element.25), channel_id=1, source_target_pairs={{0,2},{1,3},{2,0},{3,1},{4,6},{5,7},{6,4},{7,5},{8,10},{9,11},{10,... | collective-permute-start | bytes 786440 | tf_op jit(solution)/shard_map/ppermute | solution.py:345
  25.2 0.2 collective-permute-start.3
  25.4 11.0 %collective-permute-done.1.refs_0_ = bf16[256,512]{1,0:T(8,128)(2,1)S(1)} collective-permute-done((bf16[256,512]{1,0:T(8,128)(2,1)S(1)}, bf16[256,512]{1,0:T(8,128)(2,1)S(1)}, u32[]{:S(2)}, u32[]{:S(2)}) %collective-permute-start.1) | collective-permute-done | bytes 262176 | tf_op jit(solution)/shard_map/ppermute | solution.py:345
  36.5 3.6 %collective-permute-start.2 = (bf16[128,512]{1,0:T(8,128)(2,1)S(1)}, bf16[128,512]{1,0:T(8,128)(2,1)S(1)}, u32[]{:S(2)}, u32[]{:S(2)}) collective-permute-start(bf16[128,512]{1,0:T(8,128)(2,1)S(1)} %get-tuple-element.27), channel_id=1, source_target_pairs={{0,4},{1,5},{2,6},{3,7},{4,0},{5,1},{6,2},{7,3},{8,12},{9,13},{10,... | collective-permute-start | bytes 393224 | tf_op jit(solution)/shard_map/ppermute | solution.py:345
  40.1 4.3 %collective-permute-done.2.refs_0_ = bf16[128,512]{1,0:T(8,128)(2,1)S(1)} collective-permute-done((bf16[128,512]{1,0:T(8,128)(2,1)S(1)}, bf16[128,512]{1,0:T(8,128)(2,1)S(1)}, u32[]{:S(2)}, u32[]{:S(2)}) %collective-permute-start.2) | collective-permute-done | bytes 131104 | tf_op jit(solution)/shard_map/ppermute | solution.py:345
  44.4 1.8 %collective-permute-start.4 = (bf16[64,512]{1,0:T(8,128)(2,1)S(1)}, bf16[64,512]{1,0:T(8,128)(2,1)S(1)}, u32[]{:S(2)}, u32[]{:S(2)}) collective-permute-start(bf16[64,512]{1,0:T(8,128)(2,1)S(1)} %get-tuple-element.28.refs_1_.refs_0_), channel_id=1, source_target_pairs={{0,8},{1,9},{2,10},{3,11},{4,12},{5,13},{6,14},{7,15},{8,0},{9,1},... | collective-permute-start | bytes 196616 | tf_op jit(solution)/shard_map/ppermute | solution.py:345
  46.2 0.0 collective-permute-done.3.refs_0_
  46.2 2.5 %collective-permute-start.6 = (bf16[64,512]{1,0:T(8,128)(2,1)S(1)}, bf16[64,512]{1,0:T(8,128)(2,1)S(1)}, u32[]{:S(2)}, u32[]{:S(2)}) collective-permute-start(bf16[64,512]{1,0:T(8,128)(2,1)S(1)} %get-tuple-element.36), channel_id=1, source_target_pairs={{0,4},{1,5},{2,6},{3,7},{4,0},{5,1},{6,2},{7,3},{8,12},{9,13},{10,... | collective-permute-start | bytes 196616 | tf_op jit(solution)/shard_map/ppermute | solution.py:345
  48.8 0.2 collective-permute-start.7
  49.0 1.3 %collective-permute-start.5 = (bf16[64,512]{1,0:T(8,128)(2,1)S(1)}, bf16[64,512]{1,0:T(8,128)(2,1)S(1)}, u32[]{:S(2)}, u32[]{:S(2)}) collective-permute-start(bf16[64,512]{1,0:T(8,128)(2,1)S(1)} %get-tuple-element.31.refs_1_), channel_id=1, source_target_pairs={{0,8},{1,9},{2,10},{3,11},{4,12},{5,13},{6,14},{7,15},{8,0},{9,1},... | collective-permute-start | bytes 196616 | tf_op jit(solution)/shard_map/ppermute | solution.py:345
  50.3 0.0 all-to-all-done
  50.3 0.0 copy-done
  50.3 0.0 copy-done.1
  50.3 0.0 copy-done.2
  50.3 3.9 %encode.1 = (bf16[2048,256]{1,0:T(8,128)(2,1)}, f32[64,1024]{1,0:T(8,128)S(1)}) custom-call(s32[1]{0:T(128)} %bitcast.me_ref, bf16[2304,256]{1,0:T(8,128)(2,1)S(1)} %bitcast.5, bf16[1024,256]{1,0:T(8,128)(2,1)S(1)} %copy-done, bf16[1024,256]{1,0:T(8,128)(2,1)S(1)} %copy-done.1, bf16[256,256]{1,0:T(8,128)(2,1)S(1)} %copy-done.2, ...), custom_call_target="tpu_custom_call" | custom-call | flops 1342177280 | bytes 2097152 | tf_op jit(solution)/shard_map/encode/pallas_call | solution.py:445
  54.2 0.0 collective-permute-done.4.refs_1_
  54.3 0.0 collective-permute-done.6.refs_4_
  54.3 0.7 %collective-permute-done.7.refs_5_ = bf16[64,512]{1,0:T(8,128)(2,1)S(1)} collective-permute-done((bf16[64,512]{1,0:T(8,128)(2,1)S(1)}, bf16[64,512]{1,0:T(8,128)(2,1)S(1)}, u32[]{:S(2)}, u32[]{:S(2)}) %collective-permute-start.7) | collective-permute-done | bytes 65568 | tf_op jit(solution)/shard_map/ppermute | solution.py:345
  54.9 1.5 %collective-permute-done.5.refs_3_ = bf16[64,512]{1,0:T(8,128)(2,1)S(1)} collective-permute-done((bf16[64,512]{1,0:T(8,128)(2,1)S(1)}, bf16[64,512]{1,0:T(8,128)(2,1)S(1)}, u32[]{:S(2)}, u32[]{:S(2)}) %collective-permute-start.5) | collective-permute-done | bytes 65568 | tf_op jit(solution)/shard_map/ppermute | solution.py:345
  56.4 0.8 %finish.1 = f32[64,1024]{1,0:T(8,128)} custom-call(f32[64,1024]{1,0:T(8,128)S(1)} %get-tuple-element.33.between_ref, f32[64,512]{1,0:T(8,128)S(1)} %get-tuple-element.34.refs_0_, bf16[64,512]{1,0:T(8,128)(2,1)S(1)} %collective-permute-done.4.refs_1_, f32[64,512]{1,0:T(8,128)S(1)} %get-tuple-element.35.refs_2_, ...), custom_call_target="tpu_custom_call" | custom-call | flops 524288 | bytes 1048576 | tf_op jit(solution)/shard_map/finish/pallas_call | solution.py:325
  (3 shorter events, 0.1 us)
Async XLA Ops:
  7.9 7.4 %copy-start.3 = (f32[1,1024]{1,0:T(1,128)S(1)}, f32[1,1024]{1,0:T(1,128)}, u32[]{:S(2)}) copy-start(f32[1,1024]{1,0:T(1,128)} %get-tuple-element.21.mean_hbm) | copy-start | bytes 12292
  7.9 42.4 %all-to-all-start = ((bf16[16,144,256]{2,1,0:T(8,128)(2,1)}), bf16[16,144,256]{2,1,0:T(8,128)(2,1)S(1)}, u32[]{:S(2)}, u32[]{:S(2)}) async-start(bf16[16,144,256]{2,1,0:T(8,128)(2,1)} %bitcast.6), calls=%async_computation | async-start | bytes 2359296 | tf_op jit(solution)/shard_map/all_to_all | solution.py:476
  20.3 2.8 %collective-permute-start = (bf16[512,1024]{1,0:T(8,128)(2,1)S(1)}, bf16[512,1024]{1,0:T(8,128)(2,1)S(1)}, u32[]{:S(2)}, u32[]{:S(2)}) collective-permute-start(bf16[512,1024]{1,0:T(8,128)(2,1)S(1)} %get-tuple-element.23), channel_id=1, source_target_pairs={{0,1},{1,0},{2,3},{3,2},{4,5},{5,4},{6,7},{7,6},{8,9},{9,8},{10,11... | collective-permute-start | bytes 3145736 | tf_op jit(solution)/shard_map/ppermute | solution.py:345
  23.3 27.1 %copy-start = (bf16[1024,256]{1,0:T(8,128)(2,1)S(1)}, bf16[1024,256]{1,0:T(8,128)(2,1)}, u32[]{:S(2)}) copy-start(bf16[1024,256]{1,0:T(8,128)(2,1)} %basis_ref.1) | copy-start | bytes 1572868
  23.3 27.1 %copy-start.1 = (bf16[1024,256]{1,0:T(8,128)(2,1)S(1)}, bf16[1024,256]{1,0:T(8,128)(2,1)}, u32[]{:S(2)}) copy-start(bf16[1024,256]{1,0:T(8,128)(2,1)} %centroid_ref.1) | copy-start | bytes 1572868
  23.3 27.0 %copy-start.2 = (bf16[256,256]{1,0:T(8,128)(2,1)S(1)}, bf16[256,256]{1,0:T(8,128)(2,1)}, u32[]{:S(2)}) copy-start(bf16[256,256]{1,0:T(8,128)(2,1)} %rotation_ref.1) | copy-start | bytes 393220
  23.3 13.2 %collective-permute-start.1 = (bf16[256,512]{1,0:T(8,128)(2,1)S(1)}, bf16[256,512]{1,0:T(8,128)(2,1)S(1)}, u32[]{:S(2)}, u32[]{:S(2)}) collective-permute-start(bf16[256,512]{1,0:T(8,128)(2,1)S(1)} %get-tuple-element.25), channel_id=1, source_target_pairs={{0,2},{1,3},{2,0},{3,1},{4,6},{5,7},{6,4},{7,5},{8,10},{9,11},{10,... | collective-permute-start | bytes 786440 | tf_op jit(solution)/shard_map/ppermute | solution.py:345
  25.2 20.9 %collective-permute-start.3 = (bf16[256,512]{1,0:T(8,128)(2,1)S(1)}, bf16[256,512]{1,0:T(8,128)(2,1)S(1)}, u32[]{:S(2)}, u32[]{:S(2)}) collective-permute-start(bf16[256,512]{1,0:T(8,128)(2,1)S(1)} %get-tuple-element.30), channel_id=1, source_target_pairs={{0,2},{1,3},{2,0},{3,1},{4,6},{5,7},{6,4},{7,5},{8,10},{9,11},{10,... | collective-permute-start | bytes 786440 | tf_op jit(solution)/shard_map/ppermute | solution.py:345
  36.5 7.9 %collective-permute-start.2 = (bf16[128,512]{1,0:T(8,128)(2,1)S(1)}, bf16[128,512]{1,0:T(8,128)(2,1)S(1)}, u32[]{:S(2)}, u32[]{:S(2)}) collective-permute-start(bf16[128,512]{1,0:T(8,128)(2,1)S(1)} %get-tuple-element.27), channel_id=1, source_target_pairs={{0,4},{1,5},{2,6},{3,7},{4,0},{5,1},{6,2},{7,3},{8,12},{9,13},{10,... | collective-permute-start | bytes 393224 | tf_op jit(solution)/shard_map/ppermute | solution.py:345
  44.4 9.8 %collective-permute-start.4 = (bf16[64,512]{1,0:T(8,128)(2,1)S(1)}, bf16[64,512]{1,0:T(8,128)(2,1)S(1)}, u32[]{:S(2)}, u32[]{:S(2)}) collective-permute-start(bf16[64,512]{1,0:T(8,128)(2,1)S(1)} %get-tuple-element.28.refs_1_.refs_0_), channel_id=1, source_target_pairs={{0,8},{1,9},{2,10},{3,11},{4,12},{5,13},{6,14},{7,15},{8,0},{9,1},... | collective-permute-start | bytes 196616 | tf_op jit(solution)/shard_map/ppermute | solution.py:345
  46.2 8.0 %collective-permute-start.6 = (bf16[64,512]{1,0:T(8,128)(2,1)S(1)}, bf16[64,512]{1,0:T(8,128)(2,1)S(1)}, u32[]{:S(2)}, u32[]{:S(2)}) collective-permute-start(bf16[64,512]{1,0:T(8,128)(2,1)S(1)} %get-tuple-element.36), channel_id=1, source_target_pairs={{0,4},{1,5},{2,6},{3,7},{4,0},{5,1},{6,2},{7,3},{8,12},{9,13},{10,... | collective-permute-start | bytes 196616 | tf_op jit(solution)/shard_map/ppermute | solution.py:345
  48.8 6.2 %collective-permute-start.7 = (bf16[64,512]{1,0:T(8,128)(2,1)S(1)}, bf16[64,512]{1,0:T(8,128)(2,1)S(1)}, u32[]{:S(2)}, u32[]{:S(2)}) collective-permute-start(bf16[64,512]{1,0:T(8,128)(2,1)S(1)} %get-tuple-element.37), channel_id=1, source_target_pairs={{0,12},{1,13},{2,14},{3,15},{4,8},{5,9},{6,10},{7,11},{8,4},{9,5},... | collective-permute-start | bytes 196616 | tf_op jit(solution)/shard_map/ppermute | solution.py:345
  49.0 7.4 %collective-permute-start.5 = (bf16[64,512]{1,0:T(8,128)(2,1)S(1)}, bf16[64,512]{1,0:T(8,128)(2,1)S(1)}, u32[]{:S(2)}, u32[]{:S(2)}) collective-permute-start(bf16[64,512]{1,0:T(8,128)(2,1)S(1)} %get-tuple-element.31.refs_1_), channel_id=1, source_target_pairs={{0,8},{1,9},{2,10},{3,11},{4,12},{5,13},{6,14},{7,15},{8,0},{9,1},... | collective-permute-start | bytes 196616 | tf_op jit(solution)/shard_map/ppermute | solution.py:345

commit v24 on v21

--- a/solution.py
+++ b/solution.py
@@ -315,30 +315,50 @@
     return [outs[h * pieces:(h + 1) * pieces] for h in range(shares)]
 
 
-def finish_kernel(total, between_ref, *refs):
+def join_kernel(first_ref, second_ref, *refs):
+    out_ref = refs[-1]
+    columns = first_ref.shape[1]
+    out_ref[:, :columns] = first_ref[...]
+    out_ref[:, columns:] = second_ref[...]
+
+
+def join(first, second, after):
+    rows, columns = first.shape
+    vmem = pl.BlockSpec(memory_space=pltpu.VMEM)
+    return pl.pallas_call(
+        join_kernel,
+        in_specs=[vmem] * 2 + [pl.BlockSpec(memory_space=pl.ANY)] * len(after),
+        out_specs=vmem,
+        out_shape=jax.ShapeDtypeStruct((rows, 2 * columns), first.dtype),
+        compiler_params=pltpu.CompilerParams(vmem_limit_bytes=VMEM_SOME),
+        name="join",
+    )(first, second, *after)
+
+
+def finish_kernel(total, between_ref, near_ref, *refs):
     out_ref = refs[-1]
     each = (len(refs) - 1) // SHARES
     columns = out_ref.shape[1] // SHARES
     for h in range(SHARES):
         across = slice(h * columns, (h + 1) * columns)
-        held = refs[h * each][...]
+        held = refs[h * each][...] + near_ref[:, across].astype(jnp.float32)
         for ref in refs[h * each + 1:(h + 1) * each]:
             held = held + ref[...].astype(jnp.float32)
         out_ref[:, across] = (held + between_ref[:, across]) / total
 
 
-def finish(total, between, keeps, came):
+def finish(total, between, near, keeps, came):
     parts = [part for keep, pieces in zip(keeps, came) for part in (keep, *pieces)]
     vmem = pl.BlockSpec(memory_space=pltpu.VMEM)
     return pl.pallas_call(
         functools.partial(finish_kernel, total),
-        in_specs=[vmem] * (1 + len(parts)),
+        in_specs=[vmem] * (2 + len(parts)),
         out_specs=vmem,
         out_shape=jax.ShapeDtypeStruct(between.shape, jnp.float32),
         compiler_params=pltpu.CompilerParams(vmem_limit_bytes=VMEM_SOME),
         cost_estimate=pl.CostEstimate(flops=8 * between.size, bytes_accessed=16 * between.size, transcendentals=0),
         name="finish",
-    )(between, *parts)
+    )(between, near, *parts)
 
 
 def halving_stages(width):
@@ -346,12 +366,8 @@
     return [[s] for s in strides[:-2]] + [strides[-2:]]
 
 
-def exchange(width, stage, out):
-    came = []
-    for p in (2, 1, 3) if len(stage) == 2 else (1,):
-        apart = sum(s for k, s in enumerate(stage) if (p >> (len(stage) - 1 - k)) & 1)
-        came.append(lax.ppermute(out[p - 1], "wide", [(i, i ^ apart) for i in range(width)]))
-    return came
+def exchange(width, apart, piece):
+    return lax.ppermute(piece, "wide", [(i, i ^ apart) for i in range(width)])
 
 
 def encode_kernel(total, me_ref, got_ref, basis_ref, centroid_ref, rotation_ref, *refs):
@@ -491,19 +507,20 @@
 
     keep, send = moments(width, me, embeddings, mean)
     stages = halving_stages(width)
-    came = exchange(width, stages[0], [send])
-    shares = add_and_split(keep, came, SHARES, 1 << len(stages[1]))
+    came = exchange(width, 1, send)
     last = []
-    for share in shares:
+    for share in add_and_split(keep, [came], SHARES, 1 << len(stages[1])):
         for n in range(1, len(stages) - 1):
-            came = exchange(width, stages[n], share[1:])
-            (share,) = add_and_split(share[0], came, 1, 1 << len(stages[n + 1]))
+            came = exchange(width, stages[n][0], share[1])
+            (share,) = add_and_split(share[0], [came], 1, 1 << len(stages[n + 1]))
         last.append(share)
-    came = [exchange(width, stages[-1], share[1:]) for share in last]
+    near, far = stages[-1]
+    came = [[exchange(width, far, share[1]), exchange(width, near + far, share[3])] for share in last]
     encoded, between = encode(
         width, total, me, got.reshape(width * SPAN, feats), basis, centroids, rotation, [share[1] for share in last]
     )
-    covariance = finish(total, between, [share[0] for share in last], came)
+    came_near = exchange(width, near, join(last[0][2], last[1][2], came[1]))
+    covariance = finish(total, between, came_near, [share[0] for share in last], came)
     return (encoded, covariance)
 
 

time: 56.9 us -> 60.8 us (1.069)
  waiting for transfers between devices: 17.1 us -> 23.3 us
  starting transfers between devices: 21.4 us -> 19.1 us
    ppermute x9 -> x8, waiting for transfers between devices: 17.1 us -> 23.3 us  [exchange(): return lax.ppermute(piece, 'wide', [(i, i ^ apart) for i in range(width)])]
    ppermute x9 -> x8, starting transfers between devices: 14 us -> 11.7 us  [exchange(): return lax.ppermute(piece, 'wide', [(i, i ^ apart) for i in range(width)])]
  transfers between devices with their start and end apart: 10 -> 9, of which waited for: 4 -> 5; matrix products, arithmetic and copies ran while one was open for 0% -> 0% of each run, Pallas kernels for 16% -> 15%
where the time goes in v24:
time: 60.8 us; the launch traced here: 60.6 us
  waiting for transfers between devices  23.3 us (38%)
  starting transfers between devices  19.1 us (31%)
  Pallas kernels  17.4 us (29%)
  between operations  0.75 us (1%)
    ppermute x8, waiting for transfers between devices, exchange(): return lax.ppermute(piece, 'wide', [(i, i ^ apart) for i in range(width)])  23.3 us
    ppermute x8, starting transfers between devices, exchange(): return lax.ppermute(piece, 'wide', [(i, i ^ apart) for i in range(width)])  11.7 us
    all_to_all x1, starting transfers between devices, local(): lax.all_to_all(rows.reshape(width, SPAN, feats), 'wide', split_axis=0, co...  7.4 us
    pallas_call x1, Pallas kernels, project_and_sort(): pl.pallas_call(functools.partial(rows_kernel, width), grid=(rows_here //...  7.26 us
    pallas_call x1, Pallas kernels, moments(): pl.pallas_call(functools.partial(moments_kernel, width), in_specs=[pl.Blo...  4.93 us
    pallas_call x1, Pallas kernels, encode(): pl.pallas_call(functools.partial(encode_kernel, total), in_specs=[pl.Bloc...  4.09 us
  transfers between devices with their start and end apart: 9, of which 5 were waited for; matrix products, arithmetic and copies ran while one was open for 0% of the time, Pallas kernels for 15%

profile of v24, /device:TPU:0, one launch (start us, length us, event | category | flops | bytes accessed | tf_op | source)
XLA Modules:
  0.0 60.6 jit_solution(15044883985034041989)
XLA Ops:
  0.6 7.3 %project_sort.1 = (bf16[2304,256]{1,0:T(8,128)(2,1)}, f32[1,1024]{1,0:T(1,128)}) custom-call(bf16[2048,1024]{1,0:T(8,128)(2,1)} %e_hbm.3, bf16[1024,256]{1,0:T(8,128)(2,1)} %basis_ref.1, s32[16,128]{1,0:T(8,128)} %bitcast.7, s32[16,128]{1,0:T(8,128)} %bitcast.8), custom_call_target="tpu_custom_call" | custom-call | flops 3489660928 | bytes 5373952 | tf_op jit(solution)/shard_map/project_sort/pallas_call | solution.py:171
  7.9 0.0 copy-start.3
  7.9 7.4 %all-to-all-start = ((bf16[16,144,256]{2,1,0:T(8,128)(2,1)}), bf16[16,144,256]{2,1,0:T(8,128)(2,1)S(1)}, u32[]{:S(2)}, u32[]{:S(2)}) async-start(bf16[16,144,256]{2,1,0:T(8,128)(2,1)} %bitcast.6), calls=%async_computation | async-start | bytes 2359296 | tf_op jit(solution)/shard_map/all_to_all | solution.py:504
  15.3 0.0 copy-done.3
  15.3 4.9 %moments.1 = (bf16[512,1024]{1,0:T(8,128)(2,1)S(1)}, bf16[512,1024]{1,0:T(8,128)(2,1)S(1)}) custom-call(s32[1]{0:T(128)} %bitcast.me_ref, f32[1,1024]{1,0:T(1,128)S(1)} %copy-done.3, bf16[2048,1024]{1,0:T(8,128)(2,1)} %e_hbm.3), custom_call_target="tpu_custom_call" | custom-call | flops 4294967296 | bytes 7340032 | tf_op jit(solution)/shard_map/moments/pallas_call | solution.py:263
  20.3 0.5 collective-permute-start
  20.7 2.3 %collective-permute-done.refs_0_ = bf16[512,1024]{1,0:T(8,128)(2,1)S(1)} collective-permute-done((bf16[512,1024]{1,0:T(8,128)(2,1)S(1)}, bf16[512,1024]{1,0:T(8,128)(2,1)S(1)}, u32[]{:S(2)}, u32[]{:S(2)}) %collective-permute-start) | collective-permute-done | bytes 1048608 | tf_op jit(solution)/shard_map/ppermute | solution.py:370
  23.0 0.2 add_and_split.3
  23.3 0.0 copy-start
  23.3 0.0 copy-start.1
  23.3 0.0 copy-start.2
  23.3 2.0 %collective-permute-start.2 = (bf16[256,512]{1,0:T(8,128)(2,1)S(1)}, bf16[256,512]{1,0:T(8,128)(2,1)S(1)}, u32[]{:S(2)}, u32[]{:S(2)}) collective-permute-start(bf16[256,512]{1,0:T(8,128)(2,1)S(1)} %get-tuple-element.28), channel_id=1, source_target_pairs={{0,2},{1,3},{2,0},{3,1},{4,6},{5,7},{6,4},{7,5},{8,10},{9,11},{10,... | collective-permute-start | bytes 786440 | tf_op jit(solution)/shard_map/ppermute | solution.py:370
  25.3 0.1 collective-permute-start.1
  25.4 11.0 %collective-permute-done.2.refs_0_ = bf16[256,512]{1,0:T(8,128)(2,1)S(1)} collective-permute-done((bf16[256,512]{1,0:T(8,128)(2,1)S(1)}, bf16[256,512]{1,0:T(8,128)(2,1)S(1)}, u32[]{:S(2)}, u32[]{:S(2)}) %collective-permute-start.2) | collective-permute-done | bytes 262176 | tf_op jit(solution)/shard_map/ppermute | solution.py:370
  36.4 5.6 %collective-permute-start.4 = (bf16[64,512]{1,0:T(8,128)(2,1)S(1)}, bf16[64,512]{1,0:T(8,128)(2,1)S(1)}, u32[]{:S(2)}, u32[]{:S(2)}) collective-permute-start(bf16[64,512]{1,0:T(8,128)(2,1)S(1)} %get-tuple-element.34), channel_id=1, source_target_pairs={{0,12},{1,13},{2,14},{3,15},{4,8},{5,9},{6,10},{7,11},{8,4},{9,5},... | collective-permute-start | bytes 196616 | tf_op jit(solution)/shard_map/ppermute | solution.py:370
  42.0 0.0 collective-permute-start.3
  42.0 0.0 collective-permute-done.1.refs_0_
  42.1 2.5 %collective-permute-done.4.refs_1_.refs_5_ = bf16[64,512]{1,0:T(8,128)(2,1)S(1)} collective-permute-done((bf16[64,512]{1,0:T(8,128)(2,1)S(1)}, bf16[64,512]{1,0:T(8,128)(2,1)S(1)}, u32[]{:S(2)}, u32[]{:S(2)}) %collective-permute-start.4) | collective-permute-done | bytes 65568 | tf_op jit(solution)/shard_map/ppermute | solution.py:370
  44.6 5.7 %collective-permute-done.3.refs_0_.refs_4_ = bf16[64,512]{1,0:T(8,128)(2,1)S(1)} collective-permute-done((bf16[64,512]{1,0:T(8,128)(2,1)S(1)}, bf16[64,512]{1,0:T(8,128)(2,1)S(1)}, u32[]{:S(2)}, u32[]{:S(2)}) %collective-permute-start.3) | collective-permute-done | bytes 65568 | tf_op jit(solution)/shard_map/ppermute | solution.py:370
  50.3 0.1 collective-permute-start.5
  50.4 1.4 %collective-permute-start.7 = (bf16[64,512]{1,0:T(8,128)(2,1)S(1)}, bf16[64,512]{1,0:T(8,128)(2,1)S(1)}, u32[]{:S(2)}, u32[]{:S(2)}) collective-permute-start(bf16[64,512]{1,0:T(8,128)(2,1)S(1)} %get-tuple-element.36), channel_id=1, source_target_pairs={{0,12},{1,13},{2,14},{3,15},{4,8},{5,9},{6,10},{7,11},{8,4},{9,5},... | collective-permute-start | bytes 196616 | tf_op jit(solution)/shard_map/ppermute | solution.py:370
  51.7 2.1 %collective-permute-start.6 = (bf16[64,512]{1,0:T(8,128)(2,1)S(1)}, bf16[64,512]{1,0:T(8,128)(2,1)S(1)}, u32[]{:S(2)}, u32[]{:S(2)}) collective-permute-start(bf16[64,512]{1,0:T(8,128)(2,1)S(1)} %get-tuple-element.26.refs_0_), channel_id=1, source_target_pairs={{0,8},{1,9},{2,10},{3,11},{4,12},{5,13},{6,14},{7,15},{8,0},{9,1},... | collective-permute-start | bytes 196616 | tf_op jit(solution)/shard_map/ppermute | solution.py:370
  53.9 0.0 all-to-all-done
  53.9 0.0 copy-done
  53.9 0.0 copy-done.1
  53.9 0.0 copy-done.2
  53.9 4.1 %encode.1 = (bf16[2048,256]{1,0:T(8,128)(2,1)}, f32[64,1024]{1,0:T(8,128)S(1)}) custom-call(s32[1]{0:T(128)} %bitcast.me_ref, bf16[2304,256]{1,0:T(8,128)(2,1)S(1)} %bitcast.5, bf16[1024,256]{1,0:T(8,128)(2,1)S(1)} %copy-done, bf16[1024,256]{1,0:T(8,128)(2,1)S(1)} %copy-done.1, bf16[256,256]{1,0:T(8,128)(2,1)S(1)} %copy-done.2, ...), custom_call_target="tpu_custom_call" | custom-call | flops 1342177280 | bytes 2097152 | tf_op jit(solution)/shard_map/encode/pallas_call | solution.py:472
  58.0 0.0 collective-permute-done.7.refs_2_
  58.0 1.8 %collective-permute-done.6.refs_1_ = bf16[64,512]{1,0:T(8,128)(2,1)S(1)} collective-permute-done((bf16[64,512]{1,0:T(8,128)(2,1)S(1)}, bf16[64,512]{1,0:T(8,128)(2,1)S(1)}, u32[]{:S(2)}, u32[]{:S(2)}) %collective-permute-start.6) | collective-permute-done | bytes 65568 | tf_op jit(solution)/shard_map/ppermute | solution.py:370
  59.8 0.0 collective-permute-done.5.near_ref
  59.8 0.8 %finish.1 = f32[64,1024]{1,0:T(8,128)} custom-call(f32[64,1024]{1,0:T(8,128)S(1)} %get-tuple-element.31.between_ref, bf16[64,1024]{1,0:T(8,128)(2,1)S(1)} %collective-permute-done.5.near_ref, f32[64,512]{1,0:T(8,128)S(1)} %get-tuple-element.35.refs_0_, bf16[64,512]{1,0:T(8,128)(2,1)S(1)} %collective-permute-done.6.refs_1_, ...), custom_call_target="tpu_custom_call" | custom-call | flops 524288 | bytes 1048576 | tf_op jit(solution)/shard_map/finish/pallas_call | solution.py:353
  (3 shorter events, 0.1 us)
Async XLA Ops:
  7.9 7.4 %copy-start.3 = (f32[1,1024]{1,0:T(1,128)S(1)}, f32[1,1024]{1,0:T(1,128)}, u32[]{:S(2)}) copy-start(f32[1,1024]{1,0:T(1,128)} %get-tuple-element.21.mean_hbm) | copy-start | bytes 12292
  7.9 46.0 %all-to-all-start = ((bf16[16,144,256]{2,1,0:T(8,128)(2,1)}), bf16[16,144,256]{2,1,0:T(8,128)(2,1)S(1)}, u32[]{:S(2)}, u32[]{:S(2)}) async-start(bf16[16,144,256]{2,1,0:T(8,128)(2,1)} %bitcast.6), calls=%async_computation | async-start | bytes 2359296 | tf_op jit(solution)/shard_map/all_to_all | solution.py:504
  20.3 2.8 %collective-permute-start = (bf16[512,1024]{1,0:T(8,128)(2,1)S(1)}, bf16[512,1024]{1,0:T(8,128)(2,1)S(1)}, u32[]{:S(2)}, u32[]{:S(2)}) collective-permute-start(bf16[512,1024]{1,0:T(8,128)(2,1)S(1)} %get-tuple-element.23), channel_id=1, source_target_pairs={{0,1},{1,0},{2,3},{3,2},{4,5},{5,4},{6,7},{7,6},{8,9},{9,8},{10,11... | collective-permute-start | bytes 3145736 | tf_op jit(solution)/shard_map/ppermute | solution.py:370
  23.3 30.6 %copy-start = (bf16[1024,256]{1,0:T(8,128)(2,1)S(1)}, bf16[1024,256]{1,0:T(8,128)(2,1)}, u32[]{:S(2)}) copy-start(bf16[1024,256]{1,0:T(8,128)(2,1)} %basis_ref.1) | copy-start | bytes 1572868
  23.3 30.6 %copy-start.1 = (bf16[1024,256]{1,0:T(8,128)(2,1)S(1)}, bf16[1024,256]{1,0:T(8,128)(2,1)}, u32[]{:S(2)}) copy-start(bf16[1024,256]{1,0:T(8,128)(2,1)} %centroid_ref.1) | copy-start | bytes 1572868
  23.3 30.6 %copy-start.2 = (bf16[256,256]{1,0:T(8,128)(2,1)S(1)}, bf16[256,256]{1,0:T(8,128)(2,1)}, u32[]{:S(2)}) copy-start(bf16[256,256]{1,0:T(8,128)(2,1)} %rotation_ref.1) | copy-start | bytes 393220
  23.3 13.1 %collective-permute-start.2 = (bf16[256,512]{1,0:T(8,128)(2,1)S(1)}, bf16[256,512]{1,0:T(8,128)(2,1)S(1)}, u32[]{:S(2)}, u32[]{:S(2)}) collective-permute-start(bf16[256,512]{1,0:T(8,128)(2,1)S(1)} %get-tuple-element.28), channel_id=1, source_target_pairs={{0,2},{1,3},{2,0},{3,1},{4,6},{5,7},{6,4},{7,5},{8,10},{9,11},{10,... | collective-permute-start | bytes 786440 | tf_op jit(solution)/shard_map/ppermute | solution.py:370
  25.3 16.8 %collective-permute-start.1 = (bf16[256,512]{1,0:T(8,128)(2,1)S(1)}, bf16[256,512]{1,0:T(8,128)(2,1)S(1)}, u32[]{:S(2)}, u32[]{:S(2)}) collective-permute-start(bf16[256,512]{1,0:T(8,128)(2,1)S(1)} %get-tuple-element.25), channel_id=1, source_target_pairs={{0,2},{1,3},{2,0},{3,1},{4,6},{5,7},{6,4},{7,5},{8,10},{9,11},{10,... | collective-permute-start | bytes 786440 | tf_op jit(solution)/shard_map/ppermute | solution.py:370
  36.4 8.2 %collective-permute-start.4 = (bf16[64,512]{1,0:T(8,128)(2,1)S(1)}, bf16[64,512]{1,0:T(8,128)(2,1)S(1)}, u32[]{:S(2)}, u32[]{:S(2)}) collective-permute-start(bf16[64,512]{1,0:T(8,128)(2,1)S(1)} %get-tuple-element.34), channel_id=1, source_target_pairs={{0,12},{1,13},{2,14},{3,15},{4,8},{5,9},{6,10},{7,11},{8,4},{9,5},... | collective-permute-start | bytes 196616 | tf_op jit(solution)/shard_map/ppermute | solution.py:370
  42.0 8.3 %collective-permute-start.3 = (bf16[64,512]{1,0:T(8,128)(2,1)S(1)}, bf16[64,512]{1,0:T(8,128)(2,1)S(1)}, u32[]{:S(2)}, u32[]{:S(2)}) collective-permute-start(bf16[64,512]{1,0:T(8,128)(2,1)S(1)} %get-tuple-element.29.refs_1_), channel_id=1, source_target_pairs={{0,8},{1,9},{2,10},{3,11},{4,12},{5,13},{6,14},{7,15},{8,0},{9,1},... | collective-permute-start | bytes 196616 | tf_op jit(solution)/shard_map/ppermute | solution.py:370
  50.3 9.5 %collective-permute-start.5 = (bf16[64,1024]{1,0:T(8,128)(2,1)S(1)}, bf16[64,1024]{1,0:T(8,128)(2,1)S(1)}, u32[]{:S(2)}, u32[]{:S(2)}) collective-permute-start(bf16[64,1024]{1,0:T(8,128)(2,1)S(1)} %join.1), channel_id=1, source_target_pairs={{0,4},{1,5},{2,6},{3,7},{4,0},{5,1},{6,2},{7,3},{8,12},{9,13},{10,... | collective-permute-start | bytes 393224 | tf_op jit(solution)/shard_map/ppermute | solution.py:370
  50.4 7.6 %collective-permute-start.7 = (bf16[64,512]{1,0:T(8,128)(2,1)S(1)}, bf16[64,512]{1,0:T(8,128)(2,1)S(1)}, u32[]{:S(2)}, u32[]{:S(2)}) collective-permute-start(bf16[64,512]{1,0:T(8,128)(2,1)S(1)} %get-tuple-element.36), channel_id=1, source_target_pairs={{0,12},{1,13},{2,14},{3,15},{4,8},{5,9},{6,10},{7,11},{8,4},{9,5},... | collective-permute-start | bytes 196616 | tf_op jit(solution)/shard_map/ppermute | solution.py:370
  51.7 8.1 %collective-permute-start.6 = (bf16[64,512]{1,0:T(8,128)(2,1)S(1)}, bf16[64,512]{1,0:T(8,128)(2,1)S(1)}, u32[]{:S(2)}, u32[]{:S(2)}) collective-permute-start(bf16[64,512]{1,0:T(8,128)(2,1)S(1)} %get-tuple-element.26.refs_0_), channel_id=1, source_target_pairs={{0,8},{1,9},{2,10},{3,11},{4,12},{5,13},{6,14},{7,15},{8,0},{9,1},... | collective-permute-start | bytes 196616 | tf_op jit(solution)/shard_map/ppermute | solution.py:370

commit v25 on v24

--- a/solution.py
+++ b/solution.py
@@ -519,7 +519,7 @@
     encoded, between = encode(
         width, total, me, got.reshape(width * SPAN, feats), basis, centroids, rotation, [share[1] for share in last]
     )
-    came_near = exchange(width, near, join(last[0][2], last[1][2], came[1]))
+    came_near = exchange(width, near, join(last[0][2], last[1][2], came[0] + came[1] + [between]))
     covariance = finish(total, between, came_near, [share[0] for share in last], came)
     return (encoded, covariance)
 

time: 60.8 us -> 62 us (1.020)
  starting transfers between devices: 19.1 us -> 21.1 us
  waiting for transfers between devices: 23.3 us -> 22.6 us
    ppermute x8, starting transfers between devices: 11.7 us -> 13.7 us  [exchange(): return lax.ppermute(piece, 'wide', [(i, i ^ apart) for i in range(width)])]
    ppermute x8, waiting for transfers between devices: 23.3 us -> 22.2 us  [exchange(): return lax.ppermute(piece, 'wide', [(i, i ^ apart) for i in range(width)])]
  transfers between devices with their start and end apart: 9 -> 9, of which waited for: 5 -> 6; matrix products, arithmetic and copies ran while one was open for 0% -> 0% of each run, Pallas kernels for 15% -> 15%
where the time goes in v25:
time: 62 us; the launch traced here: 61.8 us
  waiting for transfers between devices  22.6 us (36%)
  starting transfers between devices  21.1 us (34%)
  Pallas kernels  17.4 us (28%)
  between operations  0.75 us (1%)
    ppermute x8, waiting for transfers between devices, exchange(): return lax.ppermute(piece, 'wide', [(i, i ^ apart) for i in range(width)])  22.2 us
    ppermute x8, starting transfers between devices, exchange(): return lax.ppermute(piece, 'wide', [(i, i ^ apart) for i in range(width)])  13.7 us
    all_to_all x1, starting transfers between devices, local(): lax.all_to_all(rows.reshape(width, SPAN, feats), 'wide', split_axis=0, co...  7.4 us
    pallas_call x1, Pallas kernels, project_and_sort(): pl.pallas_call(functools.partial(rows_kernel, width), grid=(rows_here //...  7.26 us
    pallas_call x1, Pallas kernels, moments(): pl.pallas_call(functools.partial(moments_kernel, width), in_specs=[pl.Blo...  4.93 us
    pallas_call x1, Pallas kernels, encode(): pl.pallas_call(functools.partial(encode_kernel, total), in_specs=[pl.Bloc...  4.09 us
  transfers between devices with their start and end apart: 9, of which 6 were waited for; matrix products, arithmetic and copies ran while one was open for 0% of the time, Pallas kernels for 15%

profile of v25, /device:TPU:0, one launch (start us, length us, event | category | flops | bytes accessed | tf_op | source)
XLA Modules:
  0.0 61.8 jit_solution(14988299937730944897)
XLA Ops:
  0.6 7.3 %project_sort.1 = (bf16[2304,256]{1,0:T(8,128)(2,1)}, f32[1,1024]{1,0:T(1,128)}) custom-call(bf16[2048,1024]{1,0:T(8,128)(2,1)} %e_hbm.3, bf16[1024,256]{1,0:T(8,128)(2,1)} %basis_ref.1, s32[16,128]{1,0:T(8,128)} %bitcast.7, s32[16,128]{1,0:T(8,128)} %bitcast.8), custom_call_target="tpu_custom_call" | custom-call | flops 3489660928 | bytes 5373952 | tf_op jit(solution)/shard_map/project_sort/pallas_call | solution.py:171
  7.9 0.0 copy-start.3
  7.9 7.4 %all-to-all-start = ((bf16[16,144,256]{2,1,0:T(8,128)(2,1)}), bf16[16,144,256]{2,1,0:T(8,128)(2,1)S(1)}, u32[]{:S(2)}, u32[]{:S(2)}) async-start(bf16[16,144,256]{2,1,0:T(8,128)(2,1)} %bitcast.6), calls=%async_computation | async-start | bytes 2359296 | tf_op jit(solution)/shard_map/all_to_all | solution.py:504
  15.3 0.0 copy-done.3
  15.3 4.9 %moments.1 = (bf16[512,1024]{1,0:T(8,128)(2,1)S(1)}, bf16[512,1024]{1,0:T(8,128)(2,1)S(1)}) custom-call(s32[1]{0:T(128)} %bitcast.me_ref, f32[1,1024]{1,0:T(1,128)S(1)} %copy-done.3, bf16[2048,1024]{1,0:T(8,128)(2,1)} %e_hbm.3), custom_call_target="tpu_custom_call" | custom-call | flops 4294967296 | bytes 7340032 | tf_op jit(solution)/shard_map/moments/pallas_call | solution.py:263
  20.3 0.5 collective-permute-start
  20.7 2.3 %collective-permute-done.refs_0_ = bf16[512,1024]{1,0:T(8,128)(2,1)S(1)} collective-permute-done((bf16[512,1024]{1,0:T(8,128)(2,1)S(1)}, bf16[512,1024]{1,0:T(8,128)(2,1)S(1)}, u32[]{:S(2)}, u32[]{:S(2)}) %collective-permute-start) | collective-permute-done | bytes 1048608 | tf_op jit(solution)/shard_map/ppermute | solution.py:370
  23.0 0.2 add_and_split.3
  23.2 0.0 copy-start
  23.3 0.0 copy-start.1
  23.3 0.0 copy-start.2
  23.3 2.0 %collective-permute-start.1 = (bf16[256,512]{1,0:T(8,128)(2,1)S(1)}, bf16[256,512]{1,0:T(8,128)(2,1)S(1)}, u32[]{:S(2)}, u32[]{:S(2)}) collective-permute-start(bf16[256,512]{1,0:T(8,128)(2,1)S(1)} %get-tuple-element.25), channel_id=1, source_target_pairs={{0,2},{1,3},{2,0},{3,1},{4,6},{5,7},{6,4},{7,5},{8,10},{9,11},{10,... | collective-permute-start | bytes 786440 | tf_op jit(solution)/shard_map/ppermute | solution.py:370
  25.2 0.1 collective-permute-start.2
  25.4 11.0 %collective-permute-done.1.refs_0_ = bf16[256,512]{1,0:T(8,128)(2,1)S(1)} collective-permute-done((bf16[256,512]{1,0:T(8,128)(2,1)S(1)}, bf16[256,512]{1,0:T(8,128)(2,1)S(1)}, u32[]{:S(2)}, u32[]{:S(2)}) %collective-permute-start.1) | collective-permute-done | bytes 262176 | tf_op jit(solution)/shard_map/ppermute | solution.py:370
  36.4 5.6 %collective-permute-start.4 = (bf16[64,512]{1,0:T(8,128)(2,1)S(1)}, bf16[64,512]{1,0:T(8,128)(2,1)S(1)}, u32[]{:S(2)}, u32[]{:S(2)}) collective-permute-start(bf16[64,512]{1,0:T(8,128)(2,1)S(1)} %get-tuple-element.34), channel_id=1, source_target_pairs={{0,12},{1,13},{2,14},{3,15},{4,8},{5,9},{6,10},{7,11},{8,4},{9,5},... | collective-permute-start | bytes 196616 | tf_op jit(solution)/shard_map/ppermute | solution.py:370
  42.0 0.0 collective-permute-start.3
  42.0 0.0 collective-permute-done.2.refs_0_
  42.1 5.3 %collective-permute-start.6 = (bf16[64,512]{1,0:T(8,128)(2,1)S(1)}, bf16[64,512]{1,0:T(8,128)(2,1)S(1)}, u32[]{:S(2)}, u32[]{:S(2)}) collective-permute-start(bf16[64,512]{1,0:T(8,128)(2,1)S(1)} %get-tuple-element.35), channel_id=1, source_target_pairs={{0,12},{1,13},{2,14},{3,15},{4,8},{5,9},{6,10},{7,11},{8,4},{9,5},... | collective-permute-start | bytes 196616 | tf_op jit(solution)/shard_map/ppermute | solution.py:370
  47.3 0.2 collective-permute-start.5
  47.5 0.4 all-to-all-done
  47.9 0.0 copy-done
  47.9 0.0 copy-done.1
  47.9 0.0 copy-done.2
  47.9 4.1 %encode.1 = (bf16[2048,256]{1,0:T(8,128)(2,1)}, f32[64,1024]{1,0:T(8,128)S(1)}) custom-call(s32[1]{0:T(128)} %bitcast.me_ref, bf16[2304,256]{1,0:T(8,128)(2,1)S(1)} %bitcast.5, bf16[1024,256]{1,0:T(8,128)(2,1)S(1)} %copy-done, bf16[1024,256]{1,0:T(8,128)(2,1)S(1)} %copy-done.1, bf16[256,256]{1,0:T(8,128)(2,1)S(1)} %copy-done.2, ...), custom_call_target="tpu_custom_call" | custom-call | flops 1342177280 | bytes 2097152 | tf_op jit(solution)/shard_map/encode/pallas_call | solution.py:472
  52.0 0.0 collective-permute-done.4.refs_1_.refs_2_
  52.0 1.5 %collective-permute-done.3.refs_0_.refs_1_ = bf16[64,512]{1,0:T(8,128)(2,1)S(1)} collective-permute-done((bf16[64,512]{1,0:T(8,128)(2,1)S(1)}, bf16[64,512]{1,0:T(8,128)(2,1)S(1)}, u32[]{:S(2)}, u32[]{:S(2)}) %collective-permute-start.3) | collective-permute-done | bytes 65568 | tf_op jit(solution)/shard_map/ppermute | solution.py:370
  53.6 0.0 collective-permute-done.6.refs_3_.refs_5_
  53.6 2.3 %collective-permute-done.5.refs_2_.refs_4_ = bf16[64,512]{1,0:T(8,128)(2,1)S(1)} collective-permute-done((bf16[64,512]{1,0:T(8,128)(2,1)S(1)}, bf16[64,512]{1,0:T(8,128)(2,1)S(1)}, u32[]{:S(2)}, u32[]{:S(2)}) %collective-permute-start.5) | collective-permute-done | bytes 65568 | tf_op jit(solution)/shard_map/ppermute | solution.py:370
  55.9 0.1 collective-permute-start.7
  56.0 5.0 %collective-permute-done.7.near_ref = bf16[64,1024]{1,0:T(8,128)(2,1)S(1)} collective-permute-done((bf16[64,1024]{1,0:T(8,128)(2,1)S(1)}, bf16[64,1024]{1,0:T(8,128)(2,1)S(1)}, u32[]{:S(2)}, u32[]{:S(2)}) %collective-permute-start.7) | collective-permute-done | bytes 131104 | tf_op jit(solution)/shard_map/ppermute | solution.py:370
  61.0 0.8 %finish.1 = f32[64,1024]{1,0:T(8,128)} custom-call(f32[64,1024]{1,0:T(8,128)S(1)} %get-tuple-element.31.refs_4_.between_ref, bf16[64,1024]{1,0:T(8,128)(2,1)S(1)} %collective-permute-done.7.near_ref, f32[64,512]{1,0:T(8,128)S(1)} %get-tuple-element.36.refs_0_, bf16[64,512]{1,0:T(8,128)(2,1)S(1)} %collective-permute-done.3.refs_0_.refs_1_, ...), custom_call_target="tpu_custom_call" | custom-call | flops 524288 | bytes 1048576 | tf_op jit(solution)/shard_map/finish/pallas_call | solution.py:353
  (3 shorter events, 0.1 us)
Async XLA Ops:
  7.9 7.4 %copy-start.3 = (f32[1,1024]{1,0:T(1,128)S(1)}, f32[1,1024]{1,0:T(1,128)}, u32[]{:S(2)}) copy-start(f32[1,1024]{1,0:T(1,128)} %get-tuple-element.21.mean_hbm) | copy-start | bytes 12292
  7.9 40.0 %all-to-all-start = ((bf16[16,144,256]{2,1,0:T(8,128)(2,1)}), bf16[16,144,256]{2,1,0:T(8,128)(2,1)S(1)}, u32[]{:S(2)}, u32[]{:S(2)}) async-start(bf16[16,144,256]{2,1,0:T(8,128)(2,1)} %bitcast.6), calls=%async_computation | async-start | bytes 2359296 | tf_op jit(solution)/shard_map/all_to_all | solution.py:504
  20.3 2.8 %collective-permute-start = (bf16[512,1024]{1,0:T(8,128)(2,1)S(1)}, bf16[512,1024]{1,0:T(8,128)(2,1)S(1)}, u32[]{:S(2)}, u32[]{:S(2)}) collective-permute-start(bf16[512,1024]{1,0:T(8,128)(2,1)S(1)} %get-tuple-element.23), channel_id=1, source_target_pairs={{0,1},{1,0},{2,3},{3,2},{4,5},{5,4},{6,7},{7,6},{8,9},{9,8},{10,11... | collective-permute-start | bytes 3145736 | tf_op jit(solution)/shard_map/ppermute | solution.py:370
  23.2 24.7 %copy-start = (bf16[1024,256]{1,0:T(8,128)(2,1)S(1)}, bf16[1024,256]{1,0:T(8,128)(2,1)}, u32[]{:S(2)}) copy-start(bf16[1024,256]{1,0:T(8,128)(2,1)} %basis_ref.1) | copy-start | bytes 1572868
  23.3 24.7 %copy-start.1 = (bf16[1024,256]{1,0:T(8,128)(2,1)S(1)}, bf16[1024,256]{1,0:T(8,128)(2,1)}, u32[]{:S(2)}) copy-start(bf16[1024,256]{1,0:T(8,128)(2,1)} %centroid_ref.1) | copy-start | bytes 1572868
  23.3 24.7 %copy-start.2 = (bf16[256,256]{1,0:T(8,128)(2,1)S(1)}, bf16[256,256]{1,0:T(8,128)(2,1)}, u32[]{:S(2)}) copy-start(bf16[256,256]{1,0:T(8,128)(2,1)} %rotation_ref.1) | copy-start | bytes 393220
  23.3 13.1 %collective-permute-start.1 = (bf16[256,512]{1,0:T(8,128)(2,1)S(1)}, bf16[256,512]{1,0:T(8,128)(2,1)S(1)}, u32[]{:S(2)}, u32[]{:S(2)}) collective-permute-start(bf16[256,512]{1,0:T(8,128)(2,1)S(1)} %get-tuple-element.25), channel_id=1, source_target_pairs={{0,2},{1,3},{2,0},{3,1},{4,6},{5,7},{6,4},{7,5},{8,10},{9,11},{10,... | collective-permute-start | bytes 786440 | tf_op jit(solution)/shard_map/ppermute | solution.py:370
  25.2 16.8 %collective-permute-start.2 = (bf16[256,512]{1,0:T(8,128)(2,1)S(1)}, bf16[256,512]{1,0:T(8,128)(2,1)S(1)}, u32[]{:S(2)}, u32[]{:S(2)}) collective-permute-start(bf16[256,512]{1,0:T(8,128)(2,1)S(1)} %get-tuple-element.28), channel_id=1, source_target_pairs={{0,2},{1,3},{2,0},{3,1},{4,6},{5,7},{6,4},{7,5},{8,10},{9,11},{10,... | collective-permute-start | bytes 786440 | tf_op jit(solution)/shard_map/ppermute | solution.py:370
  36.4 15.6 %collective-permute-start.4 = (bf16[64,512]{1,0:T(8,128)(2,1)S(1)}, bf16[64,512]{1,0:T(8,128)(2,1)S(1)}, u32[]{:S(2)}, u32[]{:S(2)}) collective-permute-start(bf16[64,512]{1,0:T(8,128)(2,1)S(1)} %get-tuple-element.34), channel_id=1, source_target_pairs={{0,12},{1,13},{2,14},{3,15},{4,8},{5,9},{6,10},{7,11},{8,4},{9,5},... | collective-permute-start | bytes 196616 | tf_op jit(solution)/shard_map/ppermute | solution.py:370
  42.0 11.6 %collective-permute-start.3 = (bf16[64,512]{1,0:T(8,128)(2,1)S(1)}, bf16[64,512]{1,0:T(8,128)(2,1)S(1)}, u32[]{:S(2)}, u32[]{:S(2)}) collective-permute-start(bf16[64,512]{1,0:T(8,128)(2,1)S(1)} %get-tuple-element.26.refs_0_), channel_id=1, source_target_pairs={{0,8},{1,9},{2,10},{3,11},{4,12},{5,13},{6,14},{7,15},{8,0},{9,1},... | collective-permute-start | bytes 196616 | tf_op jit(solution)/shard_map/ppermute | solution.py:370
  42.1 11.5 %collective-permute-start.6 = (bf16[64,512]{1,0:T(8,128)(2,1)S(1)}, bf16[64,512]{1,0:T(8,128)(2,1)S(1)}, u32[]{:S(2)}, u32[]{:S(2)}) collective-permute-start(bf16[64,512]{1,0:T(8,128)(2,1)S(1)} %get-tuple-element.35), channel_id=1, source_target_pairs={{0,12},{1,13},{2,14},{3,15},{4,8},{5,9},{6,10},{7,11},{8,4},{9,5},... | collective-permute-start | bytes 196616 | tf_op jit(solution)/shard_map/ppermute | solution.py:370
  47.3 8.6 %collective-permute-start.5 = (bf16[64,512]{1,0:T(8,128)(2,1)S(1)}, bf16[64,512]{1,0:T(8,128)(2,1)S(1)}, u32[]{:S(2)}, u32[]{:S(2)}) collective-permute-start(bf16[64,512]{1,0:T(8,128)(2,1)S(1)} %get-tuple-element.29.refs_1_), channel_id=1, source_target_pairs={{0,8},{1,9},{2,10},{3,11},{4,12},{5,13},{6,14},{7,15},{8,0},{9,1},... | collective-permute-start | bytes 196616 | tf_op jit(solution)/shard_map/ppermute | solution.py:370
  55.9 5.1 %collective-permute-start.7 = (bf16[64,1024]{1,0:T(8,128)(2,1)S(1)}, bf16[64,1024]{1,0:T(8,128)(2,1)S(1)}, u32[]{:S(2)}, u32[]{:S(2)}) collective-permute-start(bf16[64,1024]{1,0:T(8,128)(2,1)S(1)} %join.1), channel_id=1, source_target_pairs={{0,4},{1,5},{2,6},{3,7},{4,0},{5,1},{6,2},{7,3},{8,12},{9,13},{10,... | collective-permute-start | bytes 393224 | tf_op jit(solution)/shard_map/ppermute | solution.py:370

commit v26 on v21

--- a/solution.py
+++ b/solution.py
@@ -12,6 +12,7 @@
 NOTES = 16
 SPAN = CAP + NOTES
 CHUNK = 512
+STEP = 1024
 TILE = 256
 GROUP = 4
 SHARES = 2
@@ -47,7 +48,7 @@
     chunks = rows_here // LANES
 
     def e_copy(c):
-        at = pl.ds(pl.multiple_of(c * CHUNK, CHUNK), CHUNK)
+        at = pl.ds(pl.multiple_of(c * STEP, STEP), STEP)
         return pltpu.make_async_copy(e_hbm.at[at], e_ref.at[at], e_sem.at[c])
 
     @pl.when(step == 0)
@@ -59,7 +60,7 @@
         e_copy(0).start()
         slot_copy.start()
         basis_copy.start()
-        for c in range(1, rows_here // CHUNK):
+        for c in range(1, rows_here // STEP):
             e_copy(c).start()
         owner_copy.wait()
         sum_ref[...] = jnp.zeros_like(sum_ref)
@@ -100,21 +101,21 @@
         basis_copy.wait()
 
     e_copy(step).wait()
-    here = pl.ds(pl.multiple_of(step * CHUNK, CHUNK), CHUNK)
+    here = pl.ds(pl.multiple_of(step * STEP, STEP), STEP)
     rows = e_ref[here, :]
     y = jnp.dot(rows, basis_ref[...], preferred_element_type=jnp.float32)
     y_ref[here, :] = y
-    sum_ref[...] += jnp.sum(y.reshape(CHUNK // 8, 8, feats), 0)
-    total_ref[...] += jnp.sum(rows.astype(jnp.float32).reshape(CHUNK // 8, 8, wide), 0)
+    sum_ref[...] += jnp.sum(y.reshape(STEP // 8, 8, feats), 0)
+    total_ref[...] += jnp.sum(rows.astype(jnp.float32).reshape(STEP // 8, 8, wide), 0)
 
     @pl.when(step == pl.num_programs(0) - 1)
     def _():
         mean_y = jnp.sum(sum_ref[...], 0, keepdims=True) / rows_here
         square = jnp.zeros((8, feats), jnp.float32)
-        for c in range(rows_here // CHUNK):
-            at = slice(c * CHUNK, (c + 1) * CHUNK)
+        for c in range(rows_here // STEP):
+            at = slice(c * STEP, (c + 1) * STEP)
             centred = y_ref[at, :] - mean_y
-            square = square + jnp.sum((centred * centred).reshape(CHUNK // 8, 8, feats), 0)
+            square = square + jnp.sum((centred * centred).reshape(STEP // 8, 8, feats), 0)
             yb_ref[at, :] = centred.astype(jnp.bfloat16)
         mean = jnp.sum(total_ref[...], 0, keepdims=True) / rows_here
         mean_ref[...] = mean
@@ -170,7 +171,7 @@
     slots = width * SPAN
     return pl.pallas_call(
         functools.partial(rows_kernel, width),
-        grid=(rows_here // CHUNK,),
+        grid=(rows_here // STEP,),
         in_specs=[pl.BlockSpec(memory_space=pl.ANY)] * 4,
         out_specs=[pl.BlockSpec(memory_space=pl.ANY)] * 2,
         out_shape=[
@@ -190,7 +191,7 @@
             pltpu.VMEM((8, wide), jnp.float32),
             pltpu.VMEM((lanes, LANES), jnp.int32),
             pltpu.VMEM((width, 2 * CAP), jnp.float32),
-            pltpu.SemaphoreType.DMA((rows_here // CHUNK,)),
+            pltpu.SemaphoreType.DMA((rows_here // STEP,)),
             pltpu.SemaphoreType.DMA((4,)),
             pltpu.SemaphoreType.DMA((width // GROUP,)),
         ],

time: 56.9 us -> 56.2 us (0.988)
  Pallas kernels: 17.4 us -> 16.6 us
    pallas_call x1, Pallas kernels: 7.27 us -> 6.51 us  [project_and_sort(): pl.pallas_call(functools.partial(rows_kernel, width), grid=(rows_here //...]
  transfers between devices with their start and end apart: 10 -> 10, of which waited for: 4 -> 4; matrix products, arithmetic and copies ran while one was open for 0% -> 0% of each run, Pallas kernels for 16% -> 17%
where the time goes in v26:
time: 56.2 us; the launch traced here: 55.9 us
  starting transfers between devices  21.4 us (38%)
  waiting for transfers between devices  17.2 us (31%)
  Pallas kernels  16.6 us (30%)
  between operations  0.74 us (1%)
    ppermute x9, waiting for transfers between devices, exchange(): lax.ppermute(out[p - 1], 'wide', [(i, i ^ apart) for i in range(width)])  17.1 us
    ppermute x9, starting transfers between devices, exchange(): lax.ppermute(out[p - 1], 'wide', [(i, i ^ apart) for i in range(width)])  14 us
    all_to_all x1, starting transfers between devices, local(): lax.all_to_all(rows.reshape(width, SPAN, feats), 'wide', split_axis=0, co...  7.4 us
    pallas_call x1, Pallas kernels, project_and_sort(): pl.pallas_call(functools.partial(rows_kernel, width), grid=(rows_here //...  6.51 us
    pallas_call x1, Pallas kernels, moments(): pl.pallas_call(functools.partial(moments_kernel, width), in_specs=[pl.Blo...  4.92 us
    pallas_call x1, Pallas kernels, encode(): pl.pallas_call(functools.partial(encode_kernel, total), in_specs=[pl.Bloc...  4.09 us
  transfers between devices with their start and end apart: 10, of which 4 were waited for; matrix products, arithmetic and copies ran while one was open for 0% of the time, Pallas kernels for 17%

profile of v26, /device:TPU:0, one launch (start us, length us, event | category | flops | bytes accessed | tf_op | source)
XLA Modules:
  0.0 55.9 jit_solution(6042430264323954238)
XLA Ops:
  0.6 6.5 %project_sort.1 = (bf16[2304,256]{1,0:T(8,128)(2,1)}, f32[1,1024]{1,0:T(1,128)}) custom-call(bf16[2048,1024]{1,0:T(8,128)(2,1)} %e_hbm.3, bf16[1024,256]{1,0:T(8,128)(2,1)} %basis_ref.1, s32[16,128]{1,0:T(8,128)} %bitcast.7, s32[16,128]{1,0:T(8,128)} %bitcast.8), custom_call_target="tpu_custom_call" | custom-call | flops 3489660928 | bytes 5373952 | tf_op jit(solution)/shard_map/project_sort/pallas_call | solution.py:172
  7.1 0.0 copy-start.3
  7.2 7.4 %all-to-all-start = ((bf16[16,144,256]{2,1,0:T(8,128)(2,1)}), bf16[16,144,256]{2,1,0:T(8,128)(2,1)S(1)}, u32[]{:S(2)}, u32[]{:S(2)}) async-start(bf16[16,144,256]{2,1,0:T(8,128)(2,1)} %bitcast.6), calls=%async_computation | async-start | bytes 2359296 | tf_op jit(solution)/shard_map/all_to_all | solution.py:489
  14.6 0.0 copy-done.3
  14.6 4.9 %moments.1 = (bf16[512,1024]{1,0:T(8,128)(2,1)S(1)}, bf16[512,1024]{1,0:T(8,128)(2,1)S(1)}) custom-call(s32[1]{0:T(128)} %bitcast.me_ref, f32[1,1024]{1,0:T(1,128)S(1)} %copy-done.3, bf16[2048,1024]{1,0:T(8,128)(2,1)} %e_hbm.3), custom_call_target="tpu_custom_call" | custom-call | flops 4294967296 | bytes 7340032 | tf_op jit(solution)/shard_map/moments/pallas_call | solution.py:264
  19.5 0.5 collective-permute-start
  20.0 2.3 %collective-permute-done.refs_0_ = bf16[512,1024]{1,0:T(8,128)(2,1)S(1)} collective-permute-done((bf16[512,1024]{1,0:T(8,128)(2,1)S(1)}, bf16[512,1024]{1,0:T(8,128)(2,1)S(1)}, u32[]{:S(2)}, u32[]{:S(2)}) %collective-permute-start) | collective-permute-done | bytes 1048608 | tf_op jit(solution)/shard_map/ppermute | solution.py:354
  22.3 0.2 add_and_split.3
  22.5 0.0 copy-start
  22.5 0.0 copy-start.1
  22.5 0.0 copy-start.2
  22.5 2.0 %collective-permute-start.1 = (bf16[256,512]{1,0:T(8,128)(2,1)S(1)}, bf16[256,512]{1,0:T(8,128)(2,1)S(1)}, u32[]{:S(2)}, u32[]{:S(2)}) collective-permute-start(bf16[256,512]{1,0:T(8,128)(2,1)S(1)} %get-tuple-element.25), channel_id=1, source_target_pairs={{0,2},{1,3},{2,0},{3,1},{4,6},{5,7},{6,4},{7,5},{8,10},{9,11},{10,... | collective-permute-start | bytes 786440 | tf_op jit(solution)/shard_map/ppermute | solution.py:354
  24.5 0.1 collective-permute-start.2
  24.6 11.0 %collective-permute-done.1.refs_0_ = bf16[256,512]{1,0:T(8,128)(2,1)S(1)} collective-permute-done((bf16[256,512]{1,0:T(8,128)(2,1)S(1)}, bf16[256,512]{1,0:T(8,128)(2,1)S(1)}, u32[]{:S(2)}, u32[]{:S(2)}) %collective-permute-start.1) | collective-permute-done | bytes 262176 | tf_op jit(solution)/shard_map/ppermute | solution.py:354
  35.7 1.4 %collective-permute-start.3 = (bf16[64,512]{1,0:T(8,128)(2,1)S(1)}, bf16[64,512]{1,0:T(8,128)(2,1)S(1)}, u32[]{:S(2)}, u32[]{:S(2)}) collective-permute-start(bf16[64,512]{1,0:T(8,128)(2,1)S(1)} %get-tuple-element.33), channel_id=1, source_target_pairs={{0,4},{1,5},{2,6},{3,7},{4,0},{5,1},{6,2},{7,3},{8,12},{9,13},{10,... | collective-permute-start | bytes 196616 | tf_op jit(solution)/shard_map/ppermute | solution.py:354
  37.0 4.3 %collective-permute-start.5 = (bf16[64,512]{1,0:T(8,128)(2,1)S(1)}, bf16[64,512]{1,0:T(8,128)(2,1)S(1)}, u32[]{:S(2)}, u32[]{:S(2)}) collective-permute-start(bf16[64,512]{1,0:T(8,128)(2,1)S(1)} %get-tuple-element.34), channel_id=1, source_target_pairs={{0,12},{1,13},{2,14},{3,15},{4,8},{5,9},{6,10},{7,11},{8,4},{9,5},... | collective-permute-start | bytes 196616 | tf_op jit(solution)/shard_map/ppermute | solution.py:354
  41.3 0.5 collective-permute-start.4
  41.8 0.0 collective-permute-done.2.refs_0_
  41.9 3.5 %collective-permute-start.6 = (bf16[64,512]{1,0:T(8,128)(2,1)S(1)}, bf16[64,512]{1,0:T(8,128)(2,1)S(1)}, u32[]{:S(2)}, u32[]{:S(2)}) collective-permute-start(bf16[64,512]{1,0:T(8,128)(2,1)S(1)} %get-tuple-element.36), channel_id=1, source_target_pairs={{0,4},{1,5},{2,6},{3,7},{4,0},{5,1},{6,2},{7,3},{8,12},{9,13},{10,... | collective-permute-start | bytes 196616 | tf_op jit(solution)/shard_map/ppermute | solution.py:354
  45.4 1.3 %collective-permute-start.8 = (bf16[64,512]{1,0:T(8,128)(2,1)S(1)}, bf16[64,512]{1,0:T(8,128)(2,1)S(1)}, u32[]{:S(2)}, u32[]{:S(2)}) collective-permute-start(bf16[64,512]{1,0:T(8,128)(2,1)S(1)} %get-tuple-element.37), channel_id=1, source_target_pairs={{0,12},{1,13},{2,14},{3,15},{4,8},{5,9},{6,10},{7,11},{8,4},{9,5},... | collective-permute-start | bytes 196616 | tf_op jit(solution)/shard_map/ppermute | solution.py:354
  46.7 0.0 collective-permute-done.3.refs_1_
  46.7 0.5 collective-permute-start.7
  47.2 0.0 all-to-all-done
  47.2 0.0 copy-done
  47.2 0.0 copy-done.1
  47.2 4.1 %encode.1 = (bf16[2048,256]{1,0:T(8,128)(2,1)}, f32[64,1024]{1,0:T(8,128)S(1)}) custom-call(s32[1]{0:T(128)} %bitcast.me_ref, bf16[2304,256]{1,0:T(8,128)(2,1)S(1)} %bitcast.5, bf16[1024,256]{1,0:T(8,128)(2,1)S(1)} %copy-done, bf16[1024,256]{1,0:T(8,128)(2,1)S(1)} %copy-done.1, bf16[256,256]{1,0:T(8,128)(2,1)S(1)} %copy-done.2, ...), custom_call_target="tpu_custom_call" | custom-call | flops 1342177280 | bytes 2097152 | tf_op jit(solution)/shard_map/encode/pallas_call | solution.py:457
  51.3 0.0 collective-permute-done.5.refs_3_
  51.3 1.5 %collective-permute-done.4.refs_2_ = bf16[64,512]{1,0:T(8,128)(2,1)S(1)} collective-permute-done((bf16[64,512]{1,0:T(8,128)(2,1)S(1)}, bf16[64,512]{1,0:T(8,128)(2,1)S(1)}, u32[]{:S(2)}, u32[]{:S(2)}) %collective-permute-start.4) | collective-permute-done | bytes 65568 | tf_op jit(solution)/shard_map/ppermute | solution.py:354
  52.8 0.0 collective-permute-done.6.refs_5_
  52.8 0.0 collective-permute-done.8.refs_7_
  52.8 2.3 %collective-permute-done.7.refs_6_ = bf16[64,512]{1,0:T(8,128)(2,1)S(1)} collective-permute-done((bf16[64,512]{1,0:T(8,128)(2,1)S(1)}, bf16[64,512]{1,0:T(8,128)(2,1)S(1)}, u32[]{:S(2)}, u32[]{:S(2)}) %collective-permute-start.7) | collective-permute-done | bytes 65568 | tf_op jit(solution)/shard_map/ppermute | solution.py:354
  55.2 0.8 %finish.1 = f32[64,1024]{1,0:T(8,128)} custom-call(f32[64,1024]{1,0:T(8,128)S(1)} %get-tuple-element.31.between_ref, f32[64,512]{1,0:T(8,128)S(1)} %get-tuple-element.32.refs_0_, bf16[64,512]{1,0:T(8,128)(2,1)S(1)} %collective-permute-done.3.refs_1_, bf16[64,512]{1,0:T(8,128)(2,1)S(1)} %collective-permute-done.4.refs_2_, ...), custom_call_target="tpu_custom_call" | custom-call | flops 524288 | bytes 1048576 | tf_op jit(solution)/shard_map/finish/pallas_call | solution.py:334
  (3 shorter events, 0.1 us)
Async XLA Ops:
  7.1 7.4 %copy-start.3 = (f32[1,1024]{1,0:T(1,128)S(1)}, f32[1,1024]{1,0:T(1,128)}, u32[]{:S(2)}) copy-start(f32[1,1024]{1,0:T(1,128)} %get-tuple-element.21.mean_hbm) | copy-start | bytes 12292
  7.2 40.0 %all-to-all-start = ((bf16[16,144,256]{2,1,0:T(8,128)(2,1)}), bf16[16,144,256]{2,1,0:T(8,128)(2,1)S(1)}, u32[]{:S(2)}, u32[]{:S(2)}) async-start(bf16[16,144,256]{2,1,0:T(8,128)(2,1)} %bitcast.6), calls=%async_computation | async-start | bytes 2359296 | tf_op jit(solution)/shard_map/all_to_all | solution.py:489
  19.5 2.8 %collective-permute-start = (bf16[512,1024]{1,0:T(8,128)(2,1)S(1)}, bf16[512,1024]{1,0:T(8,128)(2,1)S(1)}, u32[]{:S(2)}, u32[]{:S(2)}) collective-permute-start(bf16[512,1024]{1,0:T(8,128)(2,1)S(1)} %get-tuple-element.23), channel_id=1, source_target_pairs={{0,1},{1,0},{2,3},{3,2},{4,5},{5,4},{6,7},{7,6},{8,9},{9,8},{10,11... | collective-permute-start | bytes 3145736 | tf_op jit(solution)/shard_map/ppermute | solution.py:354
  22.5 24.7 %copy-start = (bf16[1024,256]{1,0:T(8,128)(2,1)S(1)}, bf16[1024,256]{1,0:T(8,128)(2,1)}, u32[]{:S(2)}) copy-start(bf16[1024,256]{1,0:T(8,128)(2,1)} %basis_ref.1) | copy-start | bytes 1572868
  22.5 24.7 %copy-start.1 = (bf16[1024,256]{1,0:T(8,128)(2,1)S(1)}, bf16[1024,256]{1,0:T(8,128)(2,1)}, u32[]{:S(2)}) copy-start(bf16[1024,256]{1,0:T(8,128)(2,1)} %centroid_ref.1) | copy-start | bytes 1572868
  22.5 24.7 %copy-start.2 = (bf16[256,256]{1,0:T(8,128)(2,1)S(1)}, bf16[256,256]{1,0:T(8,128)(2,1)}, u32[]{:S(2)}) copy-start(bf16[256,256]{1,0:T(8,128)(2,1)} %rotation_ref.1) | copy-start | bytes 393220
  22.5 13.1 %collective-permute-start.1 = (bf16[256,512]{1,0:T(8,128)(2,1)S(1)}, bf16[256,512]{1,0:T(8,128)(2,1)S(1)}, u32[]{:S(2)}, u32[]{:S(2)}) collective-permute-start(bf16[256,512]{1,0:T(8,128)(2,1)S(1)} %get-tuple-element.25), channel_id=1, source_target_pairs={{0,2},{1,3},{2,0},{3,1},{4,6},{5,7},{6,4},{7,5},{8,10},{9,11},{10,... | collective-permute-start | bytes 786440 | tf_op jit(solution)/shard_map/ppermute | solution.py:354
  24.5 17.4 %collective-permute-start.2 = (bf16[256,512]{1,0:T(8,128)(2,1)S(1)}, bf16[256,512]{1,0:T(8,128)(2,1)S(1)}, u32[]{:S(2)}, u32[]{:S(2)}) collective-permute-start(bf16[256,512]{1,0:T(8,128)(2,1)S(1)} %get-tuple-element.28), channel_id=1, source_target_pairs={{0,2},{1,3},{2,0},{3,1},{4,6},{5,7},{6,4},{7,5},{8,10},{9,11},{10,... | collective-permute-start | bytes 786440 | tf_op jit(solution)/shard_map/ppermute | solution.py:354
  35.7 11.0 %collective-permute-start.3 = (bf16[64,512]{1,0:T(8,128)(2,1)S(1)}, bf16[64,512]{1,0:T(8,128)(2,1)S(1)}, u32[]{:S(2)}, u32[]{:S(2)}) collective-permute-start(bf16[64,512]{1,0:T(8,128)(2,1)S(1)} %get-tuple-element.33), channel_id=1, source_target_pairs={{0,4},{1,5},{2,6},{3,7},{4,0},{5,1},{6,2},{7,3},{8,12},{9,13},{10,... | collective-permute-start | bytes 196616 | tf_op jit(solution)/shard_map/ppermute | solution.py:354
  37.0 14.3 %collective-permute-start.5 = (bf16[64,512]{1,0:T(8,128)(2,1)S(1)}, bf16[64,512]{1,0:T(8,128)(2,1)S(1)}, u32[]{:S(2)}, u32[]{:S(2)}) collective-permute-start(bf16[64,512]{1,0:T(8,128)(2,1)S(1)} %get-tuple-element.34), channel_id=1, source_target_pairs={{0,12},{1,13},{2,14},{3,15},{4,8},{5,9},{6,10},{7,11},{8,4},{9,5},... | collective-permute-start | bytes 196616 | tf_op jit(solution)/shard_map/ppermute | solution.py:354
  41.3 11.5 %collective-permute-start.4 = (bf16[64,512]{1,0:T(8,128)(2,1)S(1)}, bf16[64,512]{1,0:T(8,128)(2,1)S(1)}, u32[]{:S(2)}, u32[]{:S(2)}) collective-permute-start(bf16[64,512]{1,0:T(8,128)(2,1)S(1)} %get-tuple-element.26.refs_0_), channel_id=1, source_target_pairs={{0,8},{1,9},{2,10},{3,11},{4,12},{5,13},{6,14},{7,15},{8,0},{9,1},... | collective-permute-start | bytes 196616 | tf_op jit(solution)/shard_map/ppermute | solution.py:354
  41.9 10.9 %collective-permute-start.6 = (bf16[64,512]{1,0:T(8,128)(2,1)S(1)}, bf16[64,512]{1,0:T(8,128)(2,1)S(1)}, u32[]{:S(2)}, u32[]{:S(2)}) collective-permute-start(bf16[64,512]{1,0:T(8,128)(2,1)S(1)} %get-tuple-element.36), channel_id=1, source_target_pairs={{0,4},{1,5},{2,6},{3,7},{4,0},{5,1},{6,2},{7,3},{8,12},{9,13},{10,... | collective-permute-start | bytes 196616 | tf_op jit(solution)/shard_map/ppermute | solution.py:354
  45.4 7.5 %collective-permute-start.8 = (bf16[64,512]{1,0:T(8,128)(2,1)S(1)}, bf16[64,512]{1,0:T(8,128)(2,1)S(1)}, u32[]{:S(2)}, u32[]{:S(2)}) collective-permute-start(bf16[64,512]{1,0:T(8,128)(2,1)S(1)} %get-tuple-element.37), channel_id=1, source_target_pairs={{0,12},{1,13},{2,14},{3,15},{4,8},{5,9},{6,10},{7,11},{8,4},{9,5},... | collective-permute-start | bytes 196616 | tf_op jit(solution)/shard_map/ppermute | solution.py:354
  46.7 8.5 %collective-permute-start.7 = (bf16[64,512]{1,0:T(8,128)(2,1)S(1)}, bf16[64,512]{1,0:T(8,128)(2,1)S(1)}, u32[]{:S(2)}, u32[]{:S(2)}) collective-permute-start(bf16[64,512]{1,0:T(8,128)(2,1)S(1)} %get-tuple-element.29.refs_1_), channel_id=1, source_target_pairs={{0,8},{1,9},{2,10},{3,11},{4,12},{5,13},{6,14},{7,15},{8,0},{9,1},... | collective-permute-start | bytes 196616 | tf_op jit(solution)/shard_map/ppermute | solution.py:354

commit v27 on v26

--- a/solution.py
+++ b/solution.py
@@ -12,7 +12,7 @@
 NOTES = 16
 SPAN = CAP + NOTES
 CHUNK = 512
-STEP = 1024
+STEP = 2048
 TILE = 256
 GROUP = 4
 SHARES = 2

time: 56.2 us -> 58.6 us (1.043)
  Pallas kernels: 16.6 us -> 19 us
    pallas_call x1, Pallas kernels: 6.51 us -> 8.94 us  [project_and_sort(): pl.pallas_call(functools.partial(rows_kernel, width), grid=(rows_here //...]
  transfers between devices with their start and end apart: 10 -> 10, of which waited for: 4 -> 4; matrix products, arithmetic and copies ran while one was open for 0% -> 0% of each run, Pallas kernels for 17% -> 16%
where the time goes in v27:
time: 58.6 us; the launch traced here: 58.4 us
  starting transfers between devices  21.4 us (37%)
  Pallas kernels  19 us (32%)
  waiting for transfers between devices  17.1 us (29%)
  between operations  0.74 us (1%)
    ppermute x9, waiting for transfers between devices, exchange(): lax.ppermute(out[p - 1], 'wide', [(i, i ^ apart) for i in range(width)])  17.1 us
    ppermute x9, starting transfers between devices, exchange(): lax.ppermute(out[p - 1], 'wide', [(i, i ^ apart) for i in range(width)])  14 us
    pallas_call x1, Pallas kernels, project_and_sort(): pl.pallas_call(functools.partial(rows_kernel, width), grid=(rows_here //...  8.94 us
    all_to_all x1, starting transfers between devices, local(): lax.all_to_all(rows.reshape(width, SPAN, feats), 'wide', split_axis=0, co...  7.4 us
    pallas_call x1, Pallas kernels, moments(): pl.pallas_call(functools.partial(moments_kernel, width), in_specs=[pl.Blo...  4.92 us
    pallas_call x1, Pallas kernels, encode(): pl.pallas_call(functools.partial(encode_kernel, total), in_specs=[pl.Bloc...  4.09 us
  transfers between devices with their start and end apart: 10, of which 4 were waited for; matrix products, arithmetic and copies ran while one was open for 0% of the time, Pallas kernels for 16%

profile of v27, /device:TPU:0, one launch (start us, length us, event | category | flops | bytes accessed | tf_op | source)
XLA Modules:
  0.0 58.4 jit_solution(7525871743019503725)
XLA Ops:
  0.6 8.9 %project_sort.1 = (bf16[2304,256]{1,0:T(8,128)(2,1)}, f32[1,1024]{1,0:T(1,128)}) custom-call(bf16[2048,1024]{1,0:T(8,128)(2,1)} %e_hbm.3, bf16[1024,256]{1,0:T(8,128)(2,1)} %basis_ref.1, s32[16,128]{1,0:T(8,128)} %bitcast.7, s32[16,128]{1,0:T(8,128)} %bitcast.8), custom_call_target="tpu_custom_call" | custom-call | flops 3489660928 | bytes 5373952 | tf_op jit(solution)/shard_map/project_sort/pallas_call | solution.py:172
  9.6 0.0 copy-start.3
  9.6 7.4 %all-to-all-start = ((bf16[16,144,256]{2,1,0:T(8,128)(2,1)}), bf16[16,144,256]{2,1,0:T(8,128)(2,1)S(1)}, u32[]{:S(2)}, u32[]{:S(2)}) async-start(bf16[16,144,256]{2,1,0:T(8,128)(2,1)} %bitcast.6), calls=%async_computation | async-start | bytes 2359296 | tf_op jit(solution)/shard_map/all_to_all | solution.py:489
  17.0 0.0 copy-done.3
  17.0 4.9 %moments.1 = (bf16[512,1024]{1,0:T(8,128)(2,1)S(1)}, bf16[512,1024]{1,0:T(8,128)(2,1)S(1)}) custom-call(s32[1]{0:T(128)} %bitcast.me_ref, f32[1,1024]{1,0:T(1,128)S(1)} %copy-done.3, bf16[2048,1024]{1,0:T(8,128)(2,1)} %e_hbm.3), custom_call_target="tpu_custom_call" | custom-call | flops 4294967296 | bytes 7340032 | tf_op jit(solution)/shard_map/moments/pallas_call | solution.py:264
  21.9 0.5 collective-permute-start
  22.4 2.3 %collective-permute-done.refs_0_ = bf16[512,1024]{1,0:T(8,128)(2,1)S(1)} collective-permute-done((bf16[512,1024]{1,0:T(8,128)(2,1)S(1)}, bf16[512,1024]{1,0:T(8,128)(2,1)S(1)}, u32[]{:S(2)}, u32[]{:S(2)}) %collective-permute-start) | collective-permute-done | bytes 1048608 | tf_op jit(solution)/shard_map/ppermute | solution.py:354
  24.7 0.2 add_and_split.3
  24.9 0.0 copy-start
  24.9 0.0 copy-start.1
  25.0 0.0 copy-start.2
  25.0 1.9 %collective-permute-start.1 = (bf16[256,512]{1,0:T(8,128)(2,1)S(1)}, bf16[256,512]{1,0:T(8,128)(2,1)S(1)}, u32[]{:S(2)}, u32[]{:S(2)}) collective-permute-start(bf16[256,512]{1,0:T(8,128)(2,1)S(1)} %get-tuple-element.25), channel_id=1, source_target_pairs={{0,2},{1,3},{2,0},{3,1},{4,6},{5,7},{6,4},{7,5},{8,10},{9,11},{10,... | collective-permute-start | bytes 786440 | tf_op jit(solution)/shard_map/ppermute | solution.py:354
  26.9 0.2 collective-permute-start.2
  27.1 11.0 %collective-permute-done.1.refs_0_ = bf16[256,512]{1,0:T(8,128)(2,1)S(1)} collective-permute-done((bf16[256,512]{1,0:T(8,128)(2,1)S(1)}, bf16[256,512]{1,0:T(8,128)(2,1)S(1)}, u32[]{:S(2)}, u32[]{:S(2)}) %collective-permute-start.1) | collective-permute-done | bytes 262176 | tf_op jit(solution)/shard_map/ppermute | solution.py:354
  38.1 1.4 %collective-permute-start.3 = (bf16[64,512]{1,0:T(8,128)(2,1)S(1)}, bf16[64,512]{1,0:T(8,128)(2,1)S(1)}, u32[]{:S(2)}, u32[]{:S(2)}) collective-permute-start(bf16[64,512]{1,0:T(8,128)(2,1)S(1)} %get-tuple-element.33), channel_id=1, source_target_pairs={{0,4},{1,5},{2,6},{3,7},{4,0},{5,1},{6,2},{7,3},{8,12},{9,13},{10,... | collective-permute-start | bytes 196616 | tf_op jit(solution)/shard_map/ppermute | solution.py:354
  39.5 4.3 %collective-permute-start.5 = (bf16[64,512]{1,0:T(8,128)(2,1)S(1)}, bf16[64,512]{1,0:T(8,128)(2,1)S(1)}, u32[]{:S(2)}, u32[]{:S(2)}) collective-permute-start(bf16[64,512]{1,0:T(8,128)(2,1)S(1)} %get-tuple-element.34), channel_id=1, source_target_pairs={{0,12},{1,13},{2,14},{3,15},{4,8},{5,9},{6,10},{7,11},{8,4},{9,5},... | collective-permute-start | bytes 196616 | tf_op jit(solution)/shard_map/ppermute | solution.py:354
  43.8 0.5 collective-permute-start.4
  44.3 0.0 collective-permute-done.2.refs_0_
  44.3 3.5 %collective-permute-start.6 = (bf16[64,512]{1,0:T(8,128)(2,1)S(1)}, bf16[64,512]{1,0:T(8,128)(2,1)S(1)}, u32[]{:S(2)}, u32[]{:S(2)}) collective-permute-start(bf16[64,512]{1,0:T(8,128)(2,1)S(1)} %get-tuple-element.36), channel_id=1, source_target_pairs={{0,4},{1,5},{2,6},{3,7},{4,0},{5,1},{6,2},{7,3},{8,12},{9,13},{10,... | collective-permute-start | bytes 196616 | tf_op jit(solution)/shard_map/ppermute | solution.py:354
  47.8 1.3 %collective-permute-start.8 = (bf16[64,512]{1,0:T(8,128)(2,1)S(1)}, bf16[64,512]{1,0:T(8,128)(2,1)S(1)}, u32[]{:S(2)}, u32[]{:S(2)}) collective-permute-start(bf16[64,512]{1,0:T(8,128)(2,1)S(1)} %get-tuple-element.37), channel_id=1, source_target_pairs={{0,12},{1,13},{2,14},{3,15},{4,8},{5,9},{6,10},{7,11},{8,4},{9,5},... | collective-permute-start | bytes 196616 | tf_op jit(solution)/shard_map/ppermute | solution.py:354
  49.1 0.0 collective-permute-done.3.refs_1_
  49.1 0.5 collective-permute-start.7
  49.6 0.0 all-to-all-done
  49.6 0.0 copy-done
  49.6 0.0 copy-done.1
  49.6 4.1 %encode.1 = (bf16[2048,256]{1,0:T(8,128)(2,1)}, f32[64,1024]{1,0:T(8,128)S(1)}) custom-call(s32[1]{0:T(128)} %bitcast.me_ref, bf16[2304,256]{1,0:T(8,128)(2,1)S(1)} %bitcast.5, bf16[1024,256]{1,0:T(8,128)(2,1)S(1)} %copy-done, bf16[1024,256]{1,0:T(8,128)(2,1)S(1)} %copy-done.1, bf16[256,256]{1,0:T(8,128)(2,1)S(1)} %copy-done.2, ...), custom_call_target="tpu_custom_call" | custom-call | flops 1342177280 | bytes 2097152 | tf_op jit(solution)/shard_map/encode/pallas_call | solution.py:457
  53.7 0.0 collective-permute-done.5.refs_3_
  53.7 1.5 %collective-permute-done.4.refs_2_ = bf16[64,512]{1,0:T(8,128)(2,1)S(1)} collective-permute-done((bf16[64,512]{1,0:T(8,128)(2,1)S(1)}, bf16[64,512]{1,0:T(8,128)(2,1)S(1)}, u32[]{:S(2)}, u32[]{:S(2)}) %collective-permute-start.4) | collective-permute-done | bytes 65568 | tf_op jit(solution)/shard_map/ppermute | solution.py:354
  55.3 0.0 collective-permute-done.6.refs_5_
  55.3 0.0 collective-permute-done.8.refs_7_
  55.3 2.3 %collective-permute-done.7.refs_6_ = bf16[64,512]{1,0:T(8,128)(2,1)S(1)} collective-permute-done((bf16[64,512]{1,0:T(8,128)(2,1)S(1)}, bf16[64,512]{1,0:T(8,128)(2,1)S(1)}, u32[]{:S(2)}, u32[]{:S(2)}) %collective-permute-start.7) | collective-permute-done | bytes 65568 | tf_op jit(solution)/shard_map/ppermute | solution.py:354
  57.6 0.8 %finish.1 = f32[64,1024]{1,0:T(8,128)} custom-call(f32[64,1024]{1,0:T(8,128)S(1)} %get-tuple-element.31.between_ref, f32[64,512]{1,0:T(8,128)S(1)} %get-tuple-element.32.refs_0_, bf16[64,512]{1,0:T(8,128)(2,1)S(1)} %collective-permute-done.3.refs_1_, bf16[64,512]{1,0:T(8,128)(2,1)S(1)} %collective-permute-done.4.refs_2_, ...), custom_call_target="tpu_custom_call" | custom-call | flops 524288 | bytes 1048576 | tf_op jit(solution)/shard_map/finish/pallas_call | solution.py:334
  (3 shorter events, 0.1 us)
Async XLA Ops:
  9.6 7.4 %copy-start.3 = (f32[1,1024]{1,0:T(1,128)S(1)}, f32[1,1024]{1,0:T(1,128)}, u32[]{:S(2)}) copy-start(f32[1,1024]{1,0:T(1,128)} %get-tuple-element.21.mean_hbm) | copy-start | bytes 12292
  9.6 40.0 %all-to-all-start = ((bf16[16,144,256]{2,1,0:T(8,128)(2,1)}), bf16[16,144,256]{2,1,0:T(8,128)(2,1)S(1)}, u32[]{:S(2)}, u32[]{:S(2)}) async-start(bf16[16,144,256]{2,1,0:T(8,128)(2,1)} %bitcast.6), calls=%async_computation | async-start | bytes 2359296 | tf_op jit(solution)/shard_map/all_to_all | solution.py:489
  21.9 2.8 %collective-permute-start = (bf16[512,1024]{1,0:T(8,128)(2,1)S(1)}, bf16[512,1024]{1,0:T(8,128)(2,1)S(1)}, u32[]{:S(2)}, u32[]{:S(2)}) collective-permute-start(bf16[512,1024]{1,0:T(8,128)(2,1)S(1)} %get-tuple-element.23), channel_id=1, source_target_pairs={{0,1},{1,0},{2,3},{3,2},{4,5},{5,4},{6,7},{7,6},{8,9},{9,8},{10,11... | collective-permute-start | bytes 3145736 | tf_op jit(solution)/shard_map/ppermute | solution.py:354
  24.9 24.7 %copy-start = (bf16[1024,256]{1,0:T(8,128)(2,1)S(1)}, bf16[1024,256]{1,0:T(8,128)(2,1)}, u32[]{:S(2)}) copy-start(bf16[1024,256]{1,0:T(8,128)(2,1)} %basis_ref.1) | copy-start | bytes 1572868
  24.9 24.7 %copy-start.1 = (bf16[1024,256]{1,0:T(8,128)(2,1)S(1)}, bf16[1024,256]{1,0:T(8,128)(2,1)}, u32[]{:S(2)}) copy-start(bf16[1024,256]{1,0:T(8,128)(2,1)} %centroid_ref.1) | copy-start | bytes 1572868
  25.0 24.7 %copy-start.2 = (bf16[256,256]{1,0:T(8,128)(2,1)S(1)}, bf16[256,256]{1,0:T(8,128)(2,1)}, u32[]{:S(2)}) copy-start(bf16[256,256]{1,0:T(8,128)(2,1)} %rotation_ref.1) | copy-start | bytes 393220
  25.0 13.1 %collective-permute-start.1 = (bf16[256,512]{1,0:T(8,128)(2,1)S(1)}, bf16[256,512]{1,0:T(8,128)(2,1)S(1)}, u32[]{:S(2)}, u32[]{:S(2)}) collective-permute-start(bf16[256,512]{1,0:T(8,128)(2,1)S(1)} %get-tuple-element.25), channel_id=1, source_target_pairs={{0,2},{1,3},{2,0},{3,1},{4,6},{5,7},{6,4},{7,5},{8,10},{9,11},{10,... | collective-permute-start | bytes 786440 | tf_op jit(solution)/shard_map/ppermute | solution.py:354
  26.9 17.4 %collective-permute-start.2 = (bf16[256,512]{1,0:T(8,128)(2,1)S(1)}, bf16[256,512]{1,0:T(8,128)(2,1)S(1)}, u32[]{:S(2)}, u32[]{:S(2)}) collective-permute-start(bf16[256,512]{1,0:T(8,128)(2,1)S(1)} %get-tuple-element.28), channel_id=1, source_target_pairs={{0,2},{1,3},{2,0},{3,1},{4,6},{5,7},{6,4},{7,5},{8,10},{9,11},{10,... | collective-permute-start | bytes 786440 | tf_op jit(solution)/shard_map/ppermute | solution.py:354
  38.1 11.0 %collective-permute-start.3 = (bf16[64,512]{1,0:T(8,128)(2,1)S(1)}, bf16[64,512]{1,0:T(8,128)(2,1)S(1)}, u32[]{:S(2)}, u32[]{:S(2)}) collective-permute-start(bf16[64,512]{1,0:T(8,128)(2,1)S(1)} %get-tuple-element.33), channel_id=1, source_target_pairs={{0,4},{1,5},{2,6},{3,7},{4,0},{5,1},{6,2},{7,3},{8,12},{9,13},{10,... | collective-permute-start | bytes 196616 | tf_op jit(solution)/shard_map/ppermute | solution.py:354
  39.5 14.3 %collective-permute-start.5 = (bf16[64,512]{1,0:T(8,128)(2,1)S(1)}, bf16[64,512]{1,0:T(8,128)(2,1)S(1)}, u32[]{:S(2)}, u32[]{:S(2)}) collective-permute-start(bf16[64,512]{1,0:T(8,128)(2,1)S(1)} %get-tuple-element.34), channel_id=1, source_target_pairs={{0,12},{1,13},{2,14},{3,15},{4,8},{5,9},{6,10},{7,11},{8,4},{9,5},... | collective-permute-start | bytes 196616 | tf_op jit(solution)/shard_map/ppermute | solution.py:354
  43.8 11.5 %collective-permute-start.4 = (bf16[64,512]{1,0:T(8,128)(2,1)S(1)}, bf16[64,512]{1,0:T(8,128)(2,1)S(1)}, u32[]{:S(2)}, u32[]{:S(2)}) collective-permute-start(bf16[64,512]{1,0:T(8,128)(2,1)S(1)} %get-tuple-element.26.refs_0_), channel_id=1, source_target_pairs={{0,8},{1,9},{2,10},{3,11},{4,12},{5,13},{6,14},{7,15},{8,0},{9,1},... | collective-permute-start | bytes 196616 | tf_op jit(solution)/shard_map/ppermute | solution.py:354
  44.3 10.9 %collective-permute-start.6 = (bf16[64,512]{1,0:T(8,128)(2,1)S(1)}, bf16[64,512]{1,0:T(8,128)(2,1)S(1)}, u32[]{:S(2)}, u32[]{:S(2)}) collective-permute-start(bf16[64,512]{1,0:T(8,128)(2,1)S(1)} %get-tuple-element.36), channel_id=1, source_target_pairs={{0,4},{1,5},{2,6},{3,7},{4,0},{5,1},{6,2},{7,3},{8,12},{9,13},{10,... | collective-permute-start | bytes 196616 | tf_op jit(solution)/shard_map/ppermute | solution.py:354
  47.8 7.5 %collective-permute-start.8 = (bf16[64,512]{1,0:T(8,128)(2,1)S(1)}, bf16[64,512]{1,0:T(8,128)(2,1)S(1)}, u32[]{:S(2)}, u32[]{:S(2)}) collective-permute-start(bf16[64,512]{1,0:T(8,128)(2,1)S(1)} %get-tuple-element.37), channel_id=1, source_target_pairs={{0,12},{1,13},{2,14},{3,15},{4,8},{5,9},{6,10},{7,11},{8,4},{9,5},... | collective-permute-start | bytes 196616 | tf_op jit(solution)/shard_map/ppermute | solution.py:354
  49.1 8.5 %collective-permute-start.7 = (bf16[64,512]{1,0:T(8,128)(2,1)S(1)}, bf16[64,512]{1,0:T(8,128)(2,1)S(1)}, u32[]{:S(2)}, u32[]{:S(2)}) collective-permute-start(bf16[64,512]{1,0:T(8,128)(2,1)S(1)} %get-tuple-element.29.refs_1_), channel_id=1, source_target_pairs={{0,8},{1,9},{2,10},{3,11},{4,12},{5,13},{6,14},{7,15},{8,0},{9,1},... | collective-permute-start | bytes 196616 | tf_op jit(solution)/shard_map/ppermute | solution.py:354

commit v28 on v26

--- a/solution.py
+++ b/solution.py
@@ -48,7 +48,7 @@
     chunks = rows_here // LANES
 
     def e_copy(c):
-        at = pl.ds(pl.multiple_of(c * STEP, STEP), STEP)
+        at = pl.ds(pl.multiple_of(c * CHUNK, CHUNK), CHUNK)
         return pltpu.make_async_copy(e_hbm.at[at], e_ref.at[at], e_sem.at[c])
 
     @pl.when(step == 0)
@@ -60,7 +60,7 @@
         e_copy(0).start()
         slot_copy.start()
         basis_copy.start()
-        for c in range(1, rows_here // STEP):
+        for c in range(1, rows_here // CHUNK):
             e_copy(c).start()
         owner_copy.wait()
         sum_ref[...] = jnp.zeros_like(sum_ref)
@@ -100,7 +100,8 @@
         list_ref[:, CAP:] = found[width:]
         basis_copy.wait()
 
-    e_copy(step).wait()
+    for c in range(STEP // CHUNK):
+        e_copy(step * (STEP // CHUNK) + c).wait()
     here = pl.ds(pl.multiple_of(step * STEP, STEP), STEP)
     rows = e_ref[here, :]
     y = jnp.dot(rows, basis_ref[...], preferred_element_type=jnp.float32)
@@ -191,7 +192,7 @@
             pltpu.VMEM((8, wide), jnp.float32),
             pltpu.VMEM((lanes, LANES), jnp.int32),
             pltpu.VMEM((width, 2 * CAP), jnp.float32),
-            pltpu.SemaphoreType.DMA((rows_here // STEP,)),
+            pltpu.SemaphoreType.DMA((rows_here // CHUNK,)),
             pltpu.SemaphoreType.DMA((4,)),
             pltpu.SemaphoreType.DMA((width // GROUP,)),
         ],

time: 56.2 us -> 56.5 us (level)
  no operation moved by 1% of the time
where the time goes in v28:
time: 56.5 us; the launch traced here: 56.3 us
  starting transfers between devices  21.4 us (38%)
  waiting for transfers between devices  17.1 us (30%)
  Pallas kernels  17 us (30%)
  between operations  0.74 us (1%)
    ppermute x9, waiting for transfers between devices, exchange(): lax.ppermute(out[p - 1], 'wide', [(i, i ^ apart) for i in range(width)])  17.1 us
    ppermute x9, starting transfers between devices, exchange(): lax.ppermute(out[p - 1], 'wide', [(i, i ^ apart) for i in range(width)])  14 us
    all_to_all x1, starting transfers between devices, local(): lax.all_to_all(rows.reshape(width, SPAN, feats), 'wide', split_axis=0, co...  7.4 us
    pallas_call x1, Pallas kernels, project_and_sort(): pl.pallas_call(functools.partial(rows_kernel, width), grid=(rows_here //...  6.85 us
    pallas_call x1, Pallas kernels, moments(): pl.pallas_call(functools.partial(moments_kernel, width), in_specs=[pl.Blo...  4.92 us
    pallas_call x1, Pallas kernels, encode(): pl.pallas_call(functools.partial(encode_kernel, total), in_specs=[pl.Bloc...  4.09 us
  transfers between devices with their start and end apart: 10, of which 4 were waited for; matrix products, arithmetic and copies ran while one was open for 0% of the time, Pallas kernels for 17%

profile of v28, /device:TPU:0, one launch (start us, length us, event | category | flops | bytes accessed | tf_op | source)
XLA Modules:
  0.0 56.3 jit_solution(15225627661607636657)
XLA Ops:
  0.6 6.8 %project_sort.1 = (bf16[2304,256]{1,0:T(8,128)(2,1)}, f32[1,1024]{1,0:T(1,128)}) custom-call(bf16[2048,1024]{1,0:T(8,128)(2,1)} %e_hbm.3, bf16[1024,256]{1,0:T(8,128)(2,1)} %basis_ref.1, s32[16,128]{1,0:T(8,128)} %bitcast.7, s32[16,128]{1,0:T(8,128)} %bitcast.8), custom_call_target="tpu_custom_call" | custom-call | flops 3489660928 | bytes 5373952 | tf_op jit(solution)/shard_map/project_sort/pallas_call | solution.py:173
  7.5 0.0 copy-start.3
  7.5 7.4 %all-to-all-start = ((bf16[16,144,256]{2,1,0:T(8,128)(2,1)}), bf16[16,144,256]{2,1,0:T(8,128)(2,1)S(1)}, u32[]{:S(2)}, u32[]{:S(2)}) async-start(bf16[16,144,256]{2,1,0:T(8,128)(2,1)} %bitcast.6), calls=%async_computation | async-start | bytes 2359296 | tf_op jit(solution)/shard_map/all_to_all | solution.py:490
  14.9 0.0 copy-done.3
  14.9 4.9 %moments.1 = (bf16[512,1024]{1,0:T(8,128)(2,1)S(1)}, bf16[512,1024]{1,0:T(8,128)(2,1)S(1)}) custom-call(s32[1]{0:T(128)} %bitcast.me_ref, f32[1,1024]{1,0:T(1,128)S(1)} %copy-done.3, bf16[2048,1024]{1,0:T(8,128)(2,1)} %e_hbm.3), custom_call_target="tpu_custom_call" | custom-call | flops 4294967296 | bytes 7340032 | tf_op jit(solution)/shard_map/moments/pallas_call | solution.py:265
  19.8 0.5 collective-permute-start
  20.3 2.3 %collective-permute-done.refs_0_ = bf16[512,1024]{1,0:T(8,128)(2,1)S(1)} collective-permute-done((bf16[512,1024]{1,0:T(8,128)(2,1)S(1)}, bf16[512,1024]{1,0:T(8,128)(2,1)S(1)}, u32[]{:S(2)}, u32[]{:S(2)}) %collective-permute-start) | collective-permute-done | bytes 1048608 | tf_op jit(solution)/shard_map/ppermute | solution.py:355
  22.6 0.2 add_and_split.3
  22.8 0.0 copy-start
  22.8 0.0 copy-start.1
  22.9 0.0 copy-start.2
  22.9 2.0 %collective-permute-start.1 = (bf16[256,512]{1,0:T(8,128)(2,1)S(1)}, bf16[256,512]{1,0:T(8,128)(2,1)S(1)}, u32[]{:S(2)}, u32[]{:S(2)}) collective-permute-start(bf16[256,512]{1,0:T(8,128)(2,1)S(1)} %get-tuple-element.25), channel_id=1, source_target_pairs={{0,2},{1,3},{2,0},{3,1},{4,6},{5,7},{6,4},{7,5},{8,10},{9,11},{10,... | collective-permute-start | bytes 786440 | tf_op jit(solution)/shard_map/ppermute | solution.py:355
  24.8 0.1 collective-permute-start.2
  25.0 11.0 %collective-permute-done.1.refs_0_ = bf16[256,512]{1,0:T(8,128)(2,1)S(1)} collective-permute-done((bf16[256,512]{1,0:T(8,128)(2,1)S(1)}, bf16[256,512]{1,0:T(8,128)(2,1)S(1)}, u32[]{:S(2)}, u32[]{:S(2)}) %collective-permute-start.1) | collective-permute-done | bytes 262176 | tf_op jit(solution)/shard_map/ppermute | solution.py:355
  36.0 1.4 %collective-permute-start.3 = (bf16[64,512]{1,0:T(8,128)(2,1)S(1)}, bf16[64,512]{1,0:T(8,128)(2,1)S(1)}, u32[]{:S(2)}, u32[]{:S(2)}) collective-permute-start(bf16[64,512]{1,0:T(8,128)(2,1)S(1)} %get-tuple-element.33), channel_id=1, source_target_pairs={{0,4},{1,5},{2,6},{3,7},{4,0},{5,1},{6,2},{7,3},{8,12},{9,13},{10,... | collective-permute-start | bytes 196616 | tf_op jit(solution)/shard_map/ppermute | solution.py:355
  37.4 4.3 %collective-permute-start.5 = (bf16[64,512]{1,0:T(8,128)(2,1)S(1)}, bf16[64,512]{1,0:T(8,128)(2,1)S(1)}, u32[]{:S(2)}, u32[]{:S(2)}) collective-permute-start(bf16[64,512]{1,0:T(8,128)(2,1)S(1)} %get-tuple-element.34), channel_id=1, source_target_pairs={{0,12},{1,13},{2,14},{3,15},{4,8},{5,9},{6,10},{7,11},{8,4},{9,5},... | collective-permute-start | bytes 196616 | tf_op jit(solution)/shard_map/ppermute | solution.py:355
  41.7 0.5 collective-permute-start.4
  42.2 0.0 collective-permute-done.2.refs_0_
  42.2 3.5 %collective-permute-start.6 = (bf16[64,512]{1,0:T(8,128)(2,1)S(1)}, bf16[64,512]{1,0:T(8,128)(2,1)S(1)}, u32[]{:S(2)}, u32[]{:S(2)}) collective-permute-start(bf16[64,512]{1,0:T(8,128)(2,1)S(1)} %get-tuple-element.36), channel_id=1, source_target_pairs={{0,4},{1,5},{2,6},{3,7},{4,0},{5,1},{6,2},{7,3},{8,12},{9,13},{10,... | collective-permute-start | bytes 196616 | tf_op jit(solution)/shard_map/ppermute | solution.py:355
  45.7 1.3 %collective-permute-start.8 = (bf16[64,512]{1,0:T(8,128)(2,1)S(1)}, bf16[64,512]{1,0:T(8,128)(2,1)S(1)}, u32[]{:S(2)}, u32[]{:S(2)}) collective-permute-start(bf16[64,512]{1,0:T(8,128)(2,1)S(1)} %get-tuple-element.37), channel_id=1, source_target_pairs={{0,12},{1,13},{2,14},{3,15},{4,8},{5,9},{6,10},{7,11},{8,4},{9,5},... | collective-permute-start | bytes 196616 | tf_op jit(solution)/shard_map/ppermute | solution.py:355
  47.0 0.0 collective-permute-done.3.refs_1_
  47.0 0.5 collective-permute-start.7
  47.5 0.0 all-to-all-done
  47.5 0.0 copy-done
  47.5 0.0 copy-done.2
  47.5 4.1 %encode.1 = (bf16[2048,256]{1,0:T(8,128)(2,1)}, f32[64,1024]{1,0:T(8,128)S(1)}) custom-call(s32[1]{0:T(128)} %bitcast.me_ref, bf16[2304,256]{1,0:T(8,128)(2,1)S(1)} %bitcast.5, bf16[1024,256]{1,0:T(8,128)(2,1)S(1)} %copy-done, bf16[1024,256]{1,0:T(8,128)(2,1)S(1)} %copy-done.1, bf16[256,256]{1,0:T(8,128)(2,1)S(1)} %copy-done.2, ...), custom_call_target="tpu_custom_call" | custom-call | flops 1342177280 | bytes 2097152 | tf_op jit(solution)/shard_map/encode/pallas_call | solution.py:458
  51.6 0.0 collective-permute-done.5.refs_3_
  51.6 1.5 %collective-permute-done.4.refs_2_ = bf16[64,512]{1,0:T(8,128)(2,1)S(1)} collective-permute-done((bf16[64,512]{1,0:T(8,128)(2,1)S(1)}, bf16[64,512]{1,0:T(8,128)(2,1)S(1)}, u32[]{:S(2)}, u32[]{:S(2)}) %collective-permute-start.4) | collective-permute-done | bytes 65568 | tf_op jit(solution)/shard_map/ppermute | solution.py:355
  53.2 0.0 collective-permute-done.6.refs_5_
  53.2 0.0 collective-permute-done.8.refs_7_
  53.2 2.3 %collective-permute-done.7.refs_6_ = bf16[64,512]{1,0:T(8,128)(2,1)S(1)} collective-permute-done((bf16[64,512]{1,0:T(8,128)(2,1)S(1)}, bf16[64,512]{1,0:T(8,128)(2,1)S(1)}, u32[]{:S(2)}, u32[]{:S(2)}) %collective-permute-start.7) | collective-permute-done | bytes 65568 | tf_op jit(solution)/shard_map/ppermute | solution.py:355
  55.5 0.8 %finish.1 = f32[64,1024]{1,0:T(8,128)} custom-call(f32[64,1024]{1,0:T(8,128)S(1)} %get-tuple-element.31.between_ref, f32[64,512]{1,0:T(8,128)S(1)} %get-tuple-element.32.refs_0_, bf16[64,512]{1,0:T(8,128)(2,1)S(1)} %collective-permute-done.3.refs_1_, bf16[64,512]{1,0:T(8,128)(2,1)S(1)} %collective-permute-done.4.refs_2_, ...), custom_call_target="tpu_custom_call" | custom-call | flops 524288 | bytes 1048576 | tf_op jit(solution)/shard_map/finish/pallas_call | solution.py:335
  (3 shorter events, 0.1 us)
Async XLA Ops:
  7.5 7.4 %copy-start.3 = (f32[1,1024]{1,0:T(1,128)S(1)}, f32[1,1024]{1,0:T(1,128)}, u32[]{:S(2)}) copy-start(f32[1,1024]{1,0:T(1,128)} %get-tuple-element.21.mean_hbm) | copy-start | bytes 12292
  7.5 40.0 %all-to-all-start = ((bf16[16,144,256]{2,1,0:T(8,128)(2,1)}), bf16[16,144,256]{2,1,0:T(8,128)(2,1)S(1)}, u32[]{:S(2)}, u32[]{:S(2)}) async-start(bf16[16,144,256]{2,1,0:T(8,128)(2,1)} %bitcast.6), calls=%async_computation | async-start | bytes 2359296 | tf_op jit(solution)/shard_map/all_to_all | solution.py:490
  19.8 2.8 %collective-permute-start = (bf16[512,1024]{1,0:T(8,128)(2,1)S(1)}, bf16[512,1024]{1,0:T(8,128)(2,1)S(1)}, u32[]{:S(2)}, u32[]{:S(2)}) collective-permute-start(bf16[512,1024]{1,0:T(8,128)(2,1)S(1)} %get-tuple-element.23), channel_id=1, source_target_pairs={{0,1},{1,0},{2,3},{3,2},{4,5},{5,4},{6,7},{7,6},{8,9},{9,8},{10,11... | collective-permute-start | bytes 3145736 | tf_op jit(solution)/shard_map/ppermute | solution.py:355
  22.8 24.7 %copy-start = (bf16[1024,256]{1,0:T(8,128)(2,1)S(1)}, bf16[1024,256]{1,0:T(8,128)(2,1)}, u32[]{:S(2)}) copy-start(bf16[1024,256]{1,0:T(8,128)(2,1)} %basis_ref.1) | copy-start | bytes 1572868
  22.8 24.7 %copy-start.1 = (bf16[1024,256]{1,0:T(8,128)(2,1)S(1)}, bf16[1024,256]{1,0:T(8,128)(2,1)}, u32[]{:S(2)}) copy-start(bf16[1024,256]{1,0:T(8,128)(2,1)} %centroid_ref.1) | copy-start | bytes 1572868
  22.9 24.7 %copy-start.2 = (bf16[256,256]{1,0:T(8,128)(2,1)S(1)}, bf16[256,256]{1,0:T(8,128)(2,1)}, u32[]{:S(2)}) copy-start(bf16[256,256]{1,0:T(8,128)(2,1)} %rotation_ref.1) | copy-start | bytes 393220
  22.9 13.1 %collective-permute-start.1 = (bf16[256,512]{1,0:T(8,128)(2,1)S(1)}, bf16[256,512]{1,0:T(8,128)(2,1)S(1)}, u32[]{:S(2)}, u32[]{:S(2)}) collective-permute-start(bf16[256,512]{1,0:T(8,128)(2,1)S(1)} %get-tuple-element.25), channel_id=1, source_target_pairs={{0,2},{1,3},{2,0},{3,1},{4,6},{5,7},{6,4},{7,5},{8,10},{9,11},{10,... | collective-permute-start | bytes 786440 | tf_op jit(solution)/shard_map/ppermute | solution.py:355
  24.8 17.4 %collective-permute-start.2 = (bf16[256,512]{1,0:T(8,128)(2,1)S(1)}, bf16[256,512]{1,0:T(8,128)(2,1)S(1)}, u32[]{:S(2)}, u32[]{:S(2)}) collective-permute-start(bf16[256,512]{1,0:T(8,128)(2,1)S(1)} %get-tuple-element.28), channel_id=1, source_target_pairs={{0,2},{1,3},{2,0},{3,1},{4,6},{5,7},{6,4},{7,5},{8,10},{9,11},{10,... | collective-permute-start | bytes 786440 | tf_op jit(solution)/shard_map/ppermute | solution.py:355
  36.0 11.0 %collective-permute-start.3 = (bf16[64,512]{1,0:T(8,128)(2,1)S(1)}, bf16[64,512]{1,0:T(8,128)(2,1)S(1)}, u32[]{:S(2)}, u32[]{:S(2)}) collective-permute-start(bf16[64,512]{1,0:T(8,128)(2,1)S(1)} %get-tuple-element.33), channel_id=1, source_target_pairs={{0,4},{1,5},{2,6},{3,7},{4,0},{5,1},{6,2},{7,3},{8,12},{9,13},{10,... | collective-permute-start | bytes 196616 | tf_op jit(solution)/shard_map/ppermute | solution.py:355
  37.4 14.3 %collective-permute-start.5 = (bf16[64,512]{1,0:T(8,128)(2,1)S(1)}, bf16[64,512]{1,0:T(8,128)(2,1)S(1)}, u32[]{:S(2)}, u32[]{:S(2)}) collective-permute-start(bf16[64,512]{1,0:T(8,128)(2,1)S(1)} %get-tuple-element.34), channel_id=1, source_target_pairs={{0,12},{1,13},{2,14},{3,15},{4,8},{5,9},{6,10},{7,11},{8,4},{9,5},... | collective-permute-start | bytes 196616 | tf_op jit(solution)/shard_map/ppermute | solution.py:355
  41.7 11.5 %collective-permute-start.4 = (bf16[64,512]{1,0:T(8,128)(2,1)S(1)}, bf16[64,512]{1,0:T(8,128)(2,1)S(1)}, u32[]{:S(2)}, u32[]{:S(2)}) collective-permute-start(bf16[64,512]{1,0:T(8,128)(2,1)S(1)} %get-tuple-element.26.refs_0_), channel_id=1, source_target_pairs={{0,8},{1,9},{2,10},{3,11},{4,12},{5,13},{6,14},{7,15},{8,0},{9,1},... | collective-permute-start | bytes 196616 | tf_op jit(solution)/shard_map/ppermute | solution.py:355
  42.2 10.9 %collective-permute-start.6 = (bf16[64,512]{1,0:T(8,128)(2,1)S(1)}, bf16[64,512]{1,0:T(8,128)(2,1)S(1)}, u32[]{:S(2)}, u32[]{:S(2)}) collective-permute-start(bf16[64,512]{1,0:T(8,128)(2,1)S(1)} %get-tuple-element.36), channel_id=1, source_target_pairs={{0,4},{1,5},{2,6},{3,7},{4,0},{5,1},{6,2},{7,3},{8,12},{9,13},{10,... | collective-permute-start | bytes 196616 | tf_op jit(solution)/shard_map/ppermute | solution.py:355
  45.7 7.5 %collective-permute-start.8 = (bf16[64,512]{1,0:T(8,128)(2,1)S(1)}, bf16[64,512]{1,0:T(8,128)(2,1)S(1)}, u32[]{:S(2)}, u32[]{:S(2)}) collective-permute-start(bf16[64,512]{1,0:T(8,128)(2,1)S(1)} %get-tuple-element.37), channel_id=1, source_target_pairs={{0,12},{1,13},{2,14},{3,15},{4,8},{5,9},{6,10},{7,11},{8,4},{9,5},... | collective-permute-start | bytes 196616 | tf_op jit(solution)/shard_map/ppermute | solution.py:355
  47.0 8.5 %collective-permute-start.7 = (bf16[64,512]{1,0:T(8,128)(2,1)S(1)}, bf16[64,512]{1,0:T(8,128)(2,1)S(1)}, u32[]{:S(2)}, u32[]{:S(2)}) collective-permute-start(bf16[64,512]{1,0:T(8,128)(2,1)S(1)} %get-tuple-element.29.refs_1_), channel_id=1, source_target_pairs={{0,8},{1,9},{2,10},{3,11},{4,12},{5,13},{6,14},{7,15},{8,0},{9,1},... | collective-permute-start | bytes 196616 | tf_op jit(solution)/shard_map/ppermute | solution.py:355
